TPU v7x, 32 devices: a whole 2x2x4 slice. The times are simulated.
32 devices in a mesh: parts: 2 (over y), sect: 4 (over z), tp: 2 (over x), sub: 2 (over core).
Axes of the slice: x: 2, y: 2, z: 4, core: 2. Of those that a mesh axis runs over, the one named last changes fastest.
Arguments:
- prompt_keys: bfloat16 [8, 8192, 1024], P(('parts', 'sect'), 'sub', 'tp'), parts along dimension 0, may hold values from -6 to 6
- prompt_values: bfloat16 [8, 8192, 1024], P(('parts', 'sect'), 'sub', 'tp'), parts along dimension 0, may hold values from -6 to 6
- lengths: int32 [8], P(('parts', 'sect')), parts along dimension 0, may hold values from 2048 to 8192, as said below
- feature_weight: bfloat16 [8, 128, 128], P('tp'), may hold values from -3 to 3
- queries: bfloat16 [64, 8192], P(('parts', 'sect', 'sub'), 'tp'), parts along dimension 0, may hold values from -6 to 6
- new_keys: bfloat16 [64, 1024], P(('parts', 'sect', 'sub'), 'tp'), parts along dimension 0, may hold values from -6 to 6
- new_values: bfloat16 [64, 1024], P(('parts', 'sect', 'sub'), 'tp'), parts along dimension 0, may hold values from -6 to 6
- row_prompt: int32 [64], P('parts'), parts along dimension 0, may hold values from 0 to 3, as said below
Outputs:
- decoded: bfloat16 [64, 8192], P(('parts', 'sect', 'sub'), 'tp'), parts along dimension 0
There are 2 independent parts, one for each index of `parts`. A program takes and returns all parts, laid end to end along the dimension named above; an argument that names none is the same for every part. Nothing has to cross between parts.
Inputs may be any that keep to these rules, and one draw needn't show every extreme that they name: `lengths`: each prompt holds 2048 to 8192 tokens; some prompt holds exactly 8192. `row_prompt`: every prompt is continued by at least one decode row; the rows are spread unevenly over the prompts.
All inputs are finite; a program needn't handle non-finite values.
Results may differ from a plain program's by a relative error of at most 0.0045.
Values may be sent and summed in bfloat16 or wider, within the bound.
No kernel may reach another device: no remote copies, remote signals or barrier semaphores. Data moves between devices by JAX's collectives and lax.ppermute only.
A program may use at most 64 MiB of HBM per device.

v0:
```python
import jax
import jax.numpy as jnp
from jax import lax
from jax.sharding import PartitionSpec as P

WINDOW = 64


TAU = 10.0
EPS = 1e-06


def unit_rows(values):
    wide = values.astype(jnp.float32)
    return wide * lax.rsqrt(jnp.mean(wide * wide, axis=-1, keepdims=True) + EPS)


def featurize(values, weight, form):
    proj = jnp.einsum(form, values, weight, preferred_element_type=jnp.float32)
    return ((jax.nn.elu(proj) + 1.0) / weight.shape[2]).astype(jnp.bfloat16)


def respond(rows, own_keys, own_values, weight, state, norms, near_keys, near_values):
    head_size = rows.shape[-1]
    forms = ("rgqf,rgfd->rgqd", "rgqf,rgf->rgq", "rgqd,rwgd->rgqw", "rgqw,rwgd->rgqd")
    mapped = featurize(rows, weight, "rgqd,gdf->rgqf")
    mapped = lax.optimization_barrier(mapped).astype(jnp.float32)
    unit_query = unit_rows(rows)
    own_score = (
        TAU
        / head_size
        * jnp.einsum(
            "rgqd,rgd->rgq", unit_query, unit_rows(own_keys), precision=lax.Precision.HIGHEST
        )
    )
    linear_num = jnp.einsum(forms[0], mapped, state, precision=lax.Precision.HIGHEST)
    linear_den = jnp.einsum(forms[1], mapped, norms, precision=lax.Precision.HIGHEST)
    scores = (
        TAU
        / head_size
        * jnp.einsum(forms[2], unit_query, near_keys, precision=lax.Precision.HIGHEST)
    )
    weights = jnp.exp(scores)
    own_weight = jnp.exp(own_score)
    denominator = linear_den + jnp.sum(weights, axis=-1) + own_weight
    numerator = linear_num + jnp.einsum(
        forms[3], weights.astype(jnp.bfloat16), near_values, preferred_element_type=jnp.float32
    )
    own_rounded = lax.optimization_barrier(own_weight.astype(jnp.bfloat16)).astype(jnp.float32)
    numerator = numerator + own_rounded[..., None] * own_values.astype(jnp.float32)[:, :, None, :]
    return numerator / denominator[..., None]


def body(
    prompt_keys, prompt_values, lengths, feature_weight, queries, new_keys, new_values, row_prompt
):
    heads_kv, head_size, features = feature_weight.shape
    span = prompt_keys.shape[1]
    window = WINDOW
    sub_index = lax.axis_index("sub")
    length = lengths[0]
    position = sub_index * span + jnp.arange(span, dtype=jnp.int32)
    keys_local = prompt_keys[0].reshape(span, heads_kv, head_size)
    values_local = prompt_values[0].reshape(span, heads_kv, head_size)
    mapped = featurize(keys_local, feature_weight, "tgd,gdf->tgf")
    mapped = jnp.where((position < length - window)[:, None, None], mapped, jnp.zeros_like(mapped))
    state_part = jnp.einsum(
        "tgf,tgd->gfd", mapped, values_local, preferred_element_type=jnp.float32
    )
    norm_part = jnp.sum(mapped.astype(jnp.float32), axis=0)
    offset_start = jnp.clip(length - sub_index * span, 0, span + window)
    padding = ((window, window), (0, 0))
    window_keys = lax.dynamic_slice_in_dim(
        jnp.pad(prompt_keys[0], padding), offset_start, window, 0
    )
    window_values = lax.dynamic_slice_in_dim(
        jnp.pad(prompt_values[0], padding), offset_start, window, 0
    )
    state, norms = (
        lax.psum(state_part.astype(jnp.bfloat16), "sub").astype(jnp.float32),
        lax.psum(norm_part.astype(jnp.bfloat16), "sub").astype(jnp.float32),
    )
    recent_keys, recent_values = (
        lax.psum(window_keys.astype(jnp.float32).astype(jnp.bfloat16), "sub").astype(jnp.float32),
        lax.psum(window_values.astype(jnp.float32).astype(jnp.bfloat16), "sub").astype(jnp.float32),
    )
    count = queries.shape[0]
    group = queries.shape[1] // (heads_kv * head_size)
    first_row = lax.axis_index(("sect", "sub")) * count
    mine = lax.dynamic_slice_in_dim(row_prompt, first_row, count, 0)

    def selector(number, dtype):
        return (mine[:, None] == jnp.arange(number, dtype=jnp.int32)[None, :]).astype(dtype)

    initial = (
        jnp.zeros((count, heads_kv, features, head_size), jnp.float32),
        jnp.zeros((count, heads_kv, features), jnp.float32),
    )
    piece = (
        lax.all_gather(state[None].astype(jnp.bfloat16), "sect", axis=0, tiled=True).astype(
            jnp.float32
        ),
        lax.all_gather(norms[None].astype(jnp.bfloat16), "sect", axis=0, tiled=True).astype(
            jnp.float32
        ),
    )
    onehot = selector(piece[0].shape[0], jnp.float32)
    collect_piece = (
        lax.all_gather(recent_keys.astype(jnp.bfloat16)[None], "sect", axis=0, tiled=True),
        lax.all_gather(recent_values.astype(jnp.bfloat16)[None], "sect", axis=0, tiled=True),
    )
    collect_onehot = selector(collect_piece[0].shape[0], jnp.bfloat16)
    rows = queries.reshape(count, heads_kv, group, head_size)
    near_keys = unit_rows(
        jnp.einsum(
            "rc,cwe->rwe", collect_onehot, collect_piece[0], preferred_element_type=jnp.float32
        ).reshape(count, window, heads_kv, head_size)
    )
    near_values = (
        jnp.einsum(
            "rc,cwe->rwe", collect_onehot, collect_piece[1], preferred_element_type=jnp.float32
        )
        .reshape(count, window, heads_kv, head_size)
        .astype(jnp.bfloat16)
    )
    result = respond(
        rows,
        new_keys.reshape(count, heads_kv, head_size),
        new_values.reshape(count, heads_kv, head_size),
        feature_weight,
        initial[0] + jnp.einsum("rc,cgfd->rgfd", onehot, piece[0], precision=lax.Precision.HIGHEST),
        initial[1] + jnp.einsum("rc,cgf->rgf", onehot, piece[1], precision=lax.Precision.HIGHEST),
        near_keys,
        near_values,
    )
    return result.reshape(count, -1).astype(jnp.bfloat16)


def solution(mesh):
    placed = (
        P(("parts", "sect"), "sub", "tp"),
        P(("parts", "sect"), "sub", "tp"),
        P(("parts", "sect")),
        P("tp", None, None),
        P(("parts", "sect", "sub"), "tp"),
        P(("parts", "sect", "sub"), "tp"),
        P(("parts", "sect", "sub"), "tp"),
        P("parts"),
    )
    return jax.shard_map(
        body,
        mesh=mesh,
        in_specs=placed,
        out_specs=P(("parts", "sect", "sub"), "tp"),
        check_vma=False,
    )
```

profile of v0, /device:TPU:0, one launch (start us, length us, event | category | flops | bytes accessed | tf_op | source)
XLA Modules:
  0.0 109.9 jit_solution(15652719407297374227)
XLA Ops:
  6.5 0.0 copy-start
  6.5 0.0 all-reduce.5.cloned.1.call-start
  7.2 6.9 %reshape_squeeze.6 = bf16[4096,4,128]{2,1,0:T(4,128)(2,1)} reshape(bf16[1,4096,512]{2,1,0:T(8,128)(2,1)} %param.8) | data formatting | bytes 8388608 | tf_op jit(solution)/shard_map/reshape;squeeze | solution.py:63
  14.2 6.9 %reshape_squeeze.7 = bf16[4096,4,128]{2,1,0:T(4,128)(2,1)} reshape(bf16[1,4096,512]{2,1,0:T(8,128)(2,1)} %param.9) | data formatting | bytes 8388608 | tf_op jit(solution)/shard_map/reshape;squeeze | solution.py:64
  21.1 0.0 copy-done
  21.1 0.0 copy-start.1
  21.1 7.6 %fusion.62 = (bf16[4,128]{1,0:T(4,128)(2,1)S(1)}, bf16[4096,4,128]{0,2,1:T(8,128)(2,1)S(1)}) fusion(bf16[4,128,128]{2,1,0:T(8,128)(2,1)S(1)} %copy-done, bf16[4096,4,128]{2,1,0:T(4,128)(2,1)} %reshape_squeeze.6, pred[4096]{0:T(1024)(128)(4,1)S(1)} %add_compare_fusion), kind=kOutput, calls=%fused_computation.72 | convolution fusion | flops 553647616 | bytes 8524800 | tf_op jit(solution)/shard_map/tgd,gdf->tgf/dot_general | solution.py:19
  28.7 0.0 copy-done.1
  28.7 1.9 %fusion.11 = bf16[1,4,128,128]{3,2,1,0:T(8,128)(2,1)} fusion(bf16[4096,4,128]{0,2,1:T(8,128)(2,1)S(1)} %get-tuple-element.11, bf16[4096,4,128]{2,1,0:T(4,128)(2,1)S(1)} %copy-done.1), kind=kOutput, calls=%fused_computation.14 | convolution fusion | flops 536936448 | bytes 8519680 | tf_op jit(solution)/shard_map/tgf,tgd->gfd/dot_general | solution.py:67
  30.7 0.0 copy-start.3
  30.7 0.0 copy-start.5
  30.7 0.0 copy-start.7
  30.7 0.0 copy-start.6
  30.7 0.7 fusion.43
  31.4 0.0 all-reduce.5.cloned.1.call-update
  31.4 0.0 copy-done.3
  31.4 0.1 fusion.30
  31.5 0.2 fusion.40
  31.7 3.5 %psum.31 = bf16[1,4,128]{2,1,0:T(4,128)(2,1)S(1)} all-reduce(bf16[1,4,128]{2,1,0:T(4,128)(2,1)S(1)} %bitcast.97), channel_id=1, replica_groups=mesh['parts'=2,'sect'=4,'tp'=2,'sub'=2] {'sub'}, use_global_device_ids=true, to_apply=%region_7.8 | all-reduce | flops 512 | bytes 2048 | tf_op jit(solution)/shard_map/psum | solution.py:81
  35.3 12.0 %all_gather.15 = bf16[4,4,128]{2,1,0:T(4,128)(2,1)S(1)} all-gather(bf16[1,4,128]{2,1,0:T(4,128)(2,1)S(1)} %psum.31), channel_id=1, replica_groups=mesh['parts'=2,'sect'=4,'tp'=2,'sub'=2] {'sect'}, dimensions={0}, use_global_device_ids=true | all-gather | bytes 5120 | tf_op jit(solution)/shard_map/all_gather | solution.py:103
  47.2 0.0 copy-done.5
  47.3 0.1 multiply_reduce_fusion.1
  47.4 0.1 broadcast_multiply_fusion.1
  47.4 0.0 copy-done.7
  47.4 0.1 dynamic_slice.9
  47.5 0.2 convolution_bitcast_fusion.1
  47.7 0.2 fusion.49
  47.9 0.0 copy-done.6
  47.9 0.3 fusion.29
  48.3 4.9 %all-reduce.5.cloned.1.call-done = (bf16[1,4,128,128]{3,2,1,0:T(8,128)(2,1)}, bf16[1,64,512]{2,1,0:T(8,128)(2,1)}, bf16[1,64,512]{2,1,0:T(8,128)(2,1)}) async-done(((bf16[1,4,128,128]{3,2,1,0:T(8,128)(2,1)}, bf16[1,64,512]{2,1,0:T(8,128)(2,1)}, bf16[1,64,512]{2,1,0:T(8,128)(2,1)}), (bf16[1,4,128,128]{3,2,1,0:T(8,128)(2,1)}, bf16[1,64,512]{2,1,0:T(8,128)(2,1)}, ...) | async-done | bytes 262160 | tf_op jit(solution)/shard_map/psum | solution.py:80
  53.2 0.0 copy-start.2
  53.2 0.0 copy-start.4
  53.2 14.6 %all_gather.13 = bf16[4,64,512]{2,1,0:T(8,128)(2,1)S(1)} all-gather(bf16[1,64,512]{2,1,0:T(8,128)(2,1)} %get-tuple-element.7), channel_id=1, replica_groups=mesh['parts'=2,'sect'=4,'tp'=2,'sub'=2] {'sect'}, dimensions={0}, use_global_device_ids=true | all-gather | bytes 327680 | tf_op jit(solution)/shard_map/all_gather | solution.py:109
  67.8 0.3 fusion.26
  68.1 0.3 reshape.56
  68.4 0.4 multiply_reduce_fusion
  68.9 0.1 copy.45
  69.0 0.1 copy.46
  69.2 0.3 broadcast_multiply_fusion
  69.5 1.1 fusion.63
  70.6 0.0 copy-done.2
  70.6 16.0 %all_gather.12 = bf16[4,4,128,128]{3,2,1,0:T(8,128)(2,1)S(1)} all-gather(bf16[1,4,128,128]{3,2,1,0:T(8,128)(2,1)S(1)} %copy-done.2), channel_id=1, replica_groups=mesh['parts'=2,'sect'=4,'tp'=2,'sub'=2] {'sect'}, dimensions={0}, use_global_device_ids=true | all-gather | bytes 655360 | tf_op jit(solution)/shard_map/all_gather | solution.py:100
  86.7 0.5 fusion.22
  87.2 0.6 fusion.19
  87.8 0.0 copy-done.4
  87.8 13.9 %all_gather.14 = bf16[4,64,512]{2,1,0:T(8,128)(2,1)S(1)} all-gather(bf16[1,64,512]{2,1,0:T(8,128)(2,1)S(1)} %copy-done.4), channel_id=1, replica_groups=mesh['parts'=2,'sect'=4,'tp'=2,'sub'=2] {'sect'}, dimensions={0}, use_global_device_ids=true | all-gather | bytes 327680 | tf_op jit(solution)/shard_map/all_gather | solution.py:110
  101.8 0.4 convolution_convert_fusion
  102.1 0.1 convert_element_type.84
  102.2 0.2 fusion.18
  102.4 0.6 copy.108
  (8 shorter events, 0.1 us)
Async XLA Ops:
  6.5 14.6 %copy-start = (bf16[4,128,128]{2,1,0:T(8,128)(2,1)S(1)}, bf16[4,128,128]{2,1,0:T(8,128)(2,1)}, u32[]{:S(2)}) copy-start(bf16[4,128,128]{2,1,0:T(8,128)(2,1)} %param.11) | copy-start | bytes 393220
  6.5 46.7 %all-reduce.5.cloned.1.call-start = ((), (), s32[]{:S(2)}) async-start(), calls=%async_computation | async-start | bytes 524288 | tf_op jit(solution)/shard_map/psum | solution.py:80
  21.1 7.6 %copy-start.1 = (bf16[4096,4,128]{2,1,0:T(4,128)(2,1)S(1)}, bf16[4096,4,128]{2,1,0:T(4,128)(2,1)}, u32[]{:S(2)}) copy-start(bf16[4096,4,128]{2,1,0:T(4,128)(2,1)} %reshape_squeeze.7) | copy-start | bytes 12582916
  30.7 0.8 copy-start.3
  30.7 16.6 %copy-start.5 = (bf16[4,512]{1,0:T(4,128)(2,1)S(1)}, bf16[4,512]{1,0:T(4,128)(2,1)}, u32[]{:S(2)}) copy-start(bf16[4,512]{1,0:T(4,128)(2,1)} %param.13) | copy-start | bytes 12292
  30.7 16.8 %copy-start.7 = (s32[32]{0:T(128)S(1)}, s32[32]{0:T(128)}, u32[]{:S(2)}) copy-start(s32[32]{0:T(128)} %param.15) | copy-start | bytes 388
  30.7 17.2 %copy-start.6 = (bf16[4,512]{1,0:T(4,128)(2,1)S(1)}, bf16[4,512]{1,0:T(4,128)(2,1)}, u32[]{:S(2)}) copy-start(bf16[4,512]{1,0:T(4,128)(2,1)} %param.14) | copy-start | bytes 12292
  53.2 17.4 %copy-start.2 = (bf16[1,4,128,128]{3,2,1,0:T(8,128)(2,1)S(1)}, bf16[1,4,128,128]{3,2,1,0:T(8,128)(2,1)}, u32[]{:S(2)}) copy-start(bf16[1,4,128,128]{3,2,1,0:T(8,128)(2,1)} %get-tuple-element.5) | copy-start | bytes 393220
  53.2 34.6 %copy-start.4 = (bf16[1,64,512]{2,1,0:T(8,128)(2,1)S(1)}, bf16[1,64,512]{2,1,0:T(8,128)(2,1)}, u32[]{:S(2)}) copy-start(bf16[1,64,512]{2,1,0:T(8,128)(2,1)} %get-tuple-element.6) | copy-start | bytes 196612
Sparse Core Ops, SparseCore 0:
  31.6 21.6 all-reduce.4
where the time goes:
time: 111 us; the launch traced here: 110 us
  blocking collectives  60 us (54%)
  local copies, waits for them, and re-layouts  16 us (14%)
  between operations  14.3 us (13%)
  matrix products  13.6 us (12%)
  waiting for transfers between devices  4.96 us (4%)
  other arithmetic  1.12 us (1%)
    all_gather x1, blocking collectives, body(): lax.all_gather(state[None].astype(jnp.bfloat16), 'sect', axis=0, tiled=True)  16 us
    all_gather x1, blocking collectives, body(): lax.all_gather(recent_keys.astype(jnp.bfloat16)[None], 'sect', axis=0, ti...  14.6 us
    all_gather x1, blocking collectives, body(): lax.all_gather(recent_values.astype(jnp.bfloat16)[None], 'sect', axis=0,...  13.9 us
    all_gather x1, blocking collectives, body(): lax.all_gather(norms[None].astype(jnp.bfloat16), 'sect', axis=0, tiled=True)  12 us
    dot_general x2, matrix products, featurize(): proj = jnp.einsum(form, values, weight, preferred_element_type=jnp.float32)  7.78 us
    another operation x1, local copies, waits for them, and re-layouts, body(): keys_local = prompt_keys[0].reshape(span, heads_kv, head_size)  6.93 us
    another operation x1, local copies, waits for them, and re-layouts, body(): values_local = prompt_values[0].reshape(span, heads_kv, head_size)  6.92 us
    psum x1, waiting for transfers between devices, body(): lax.psum(state_part.astype(jnp.bfloat16), 'sub').astype(jnp.float32)  4.94 us
  transfers between devices with their start and end apart: 1, of which 1 were waited for; matrix products, arithmetic and copies ran while one was open for 1% of the time, Pallas kernels for 0%

commit v1 on v0

v1 whole, which is shorter than its diff:
```python
import functools

import jax
import jax.numpy as jnp
from jax import lax
from jax.experimental import pallas as pl
from jax.experimental.pallas import tpu as pltpu
from jax.sharding import PartitionSpec as P

WINDOW = 64
TAU = 10.0
EPS = 1e-06
BLOCK = 512
NT = (((1,), (1,)), ((), ()))


def feature(proj):
    return jnp.maximum(proj, 0.0) + jnp.exp(jnp.minimum(proj, 0.0))


def prefill_kernel(limit_ref, keys_ref, values_ref, weight_ref, out_ref, wide_ref, state_ref, norm_ref):
    step = pl.program_id(0)
    heads, head_size, feats = weight_ref.shape
    pairs = heads // 2
    block = keys_ref.shape[1]

    @pl.when(step == 0)
    def _():
        wide_ref[...] = jnp.zeros_like(wide_ref)
        state_ref[...] = jnp.zeros_like(state_ref)
        norm_ref[...] = jnp.zeros_like(norm_ref)
        for g in range(heads):
            half = g % 2
            turned = weight_ref[g].astype(jnp.float32).T.astype(jnp.bfloat16)
            wide_ref[g // 2, half * feats : (half + 1) * feats, half * head_size : (half + 1) * head_size] = turned

    position = step * block + lax.broadcasted_iota(jnp.int32, (1, block), 1)
    live = position < limit_ref[0]
    for j in range(pairs):
        cols = slice(j * 2 * head_size, (j + 1) * 2 * head_size)
        proj = lax.dot_general(wide_ref[j], keys_ref[0, :, cols], NT, preferred_element_type=jnp.float32)
        mapped = jnp.where(live, feature(proj), 0.0)
        total = norm_ref[j]
        for c in range(block // 128):
            total = total + mapped[:, c * 128 : (c + 1) * 128]
        norm_ref[j] = total
        state_ref[j] += jnp.dot(
            mapped.astype(jnp.bfloat16), values_ref[0, :, cols], preferred_element_type=jnp.float32
        )

    @pl.when(step == pl.num_programs(0) - 1)
    def _():
        out_ref[heads * feats :, :] = jnp.zeros((out_ref.shape[0] - heads * feats, head_size), jnp.bfloat16)
        rows = []
        for g in range(heads):
            half = g % 2
            part = state_ref[g // 2, half * feats : (half + 1) * feats, half * head_size : (half + 1) * head_size]
            out_ref[g * feats : (g + 1) * feats, :] = part.astype(jnp.bfloat16)
            sums = norm_ref[g // 2, half * feats : (half + 1) * feats, :]
            rows.append(jnp.sum(sums.T, axis=0, keepdims=True))
        pad = out_ref.shape[0] - heads * feats - heads
        rows.append(jnp.zeros((pad, head_size), jnp.float32))
        out_ref[heads * feats :, :] = jnp.concatenate(rows, axis=0).astype(jnp.bfloat16)


def prefill(keys, values, weight, limit):
    heads, head_size, feats = weight.shape
    span, width = keys.shape[1:]
    spec = pl.BlockSpec((1, BLOCK, width), lambda i: (0, i, 0))
    return pl.pallas_call(
        prefill_kernel,
        grid=(span // BLOCK,),
        in_specs=[
            pl.BlockSpec(memory_space=pltpu.SMEM),
            spec,
            spec,
            pl.BlockSpec(memory_space=pltpu.VMEM),
        ],
        out_specs=pl.BlockSpec(memory_space=pltpu.VMEM),
        out_shape=jax.ShapeDtypeStruct((heads * feats + 16, head_size), jnp.bfloat16),
        scratch_shapes=[
            pltpu.VMEM((heads // 2, 2 * feats, 2 * head_size), jnp.bfloat16),
            pltpu.VMEM((heads // 2, 2 * feats, 2 * head_size), jnp.float32),
            pltpu.VMEM((heads // 2, 2 * feats, 128), jnp.float32),
        ],
        compiler_params=pltpu.CompilerParams(vmem_limit_bytes=32 * 1024 * 1024),
        cost_estimate=pl.CostEstimate(
            flops=4 * span * width * feats, bytes_accessed=4 * span * width, transcendentals=span * width
        ),
        name="prefill",
    )(limit, keys, values, weight)


def decode_kernel(
    info_ref, rows_ref, weight_ref, state_a_ref, state_b_ref, near_a_ref, near_b_ref, *out_refs
):
    heads, head_size, feats = weight_ref.shape
    count = rows_ref.shape[0]
    group = (rows_ref.shape[1] - 2 * heads * head_size) // (heads * head_size)
    keys_at = heads * group * head_size
    values_at = keys_at + heads * head_size
    each = count // len(out_refs)
    window = near_a_ref.shape[1]
    slot = lax.broadcasted_iota(jnp.int32, (1, 2 * window), 1)
    place = jnp.where(slot < window, slot + info_ref[0], slot - window + info_ref[1])
    seen = (place >= info_ref[2] - window) & (place < info_ref[2])
    for g in range(heads):
        cols = slice(g * head_size, (g + 1) * head_size)
        query = jnp.concatenate(
            [
                rows_ref[:, (g * group + h) * head_size : (g * group + h + 1) * head_size]
                for h in range(group)
            ],
            axis=0,
        )
        wide = query.astype(jnp.float32)
        phi = feature(jnp.dot(query, weight_ref[g], preferred_element_type=jnp.float32)).astype(jnp.bfloat16)
        span = slice(g * feats, (g + 1) * feats)
        linear = jnp.dot(phi, state_a_ref[span, :], preferred_element_type=jnp.float32) + jnp.dot(
            phi, state_b_ref[span, :], preferred_element_type=jnp.float32
        )
        at = heads * feats
        norm = (
            state_a_ref[at : at + 16, :].astype(jnp.float32) + state_b_ref[at : at + 16, :].astype(jnp.float32)
        )[g : g + 1]
        den = jnp.sum(phi.astype(jnp.float32) * norm, axis=-1, keepdims=True)
        scale = (TAU / head_size) * lax.rsqrt(jnp.mean(wide * wide, axis=-1, keepdims=True) + EPS)
        keys = jnp.concatenate([near_a_ref[0, :, cols], near_b_ref[0, :, cols]], axis=0)
        values = jnp.concatenate([near_a_ref[1, :, cols], near_b_ref[1, :, cols]], axis=0)
        keys_wide = keys.astype(jnp.float32)
        key_scale = lax.rsqrt(jnp.mean((keys_wide * keys_wide).T, axis=0, keepdims=True) + EPS)
        score = lax.dot_general(query, keys, NT, preferred_element_type=jnp.float32) * scale * key_scale
        weights = jnp.where(seen, jnp.exp(score), 0.0)
        own_key = rows_ref[:, keys_at + g * head_size : keys_at + (g + 1) * head_size].astype(jnp.float32)
        own_value = rows_ref[:, values_at + g * head_size : values_at + (g + 1) * head_size].astype(jnp.float32)
        own_key = own_key * lax.rsqrt(jnp.mean(own_key * own_key, axis=-1, keepdims=True) + EPS)
        own_score = jnp.sum(wide * jnp.concatenate([own_key] * group, axis=0), axis=-1, keepdims=True) * scale
        own_weight = jnp.exp(own_score)
        num = (
            linear * (1.0 / (feats * feats))
            + jnp.dot(weights.astype(jnp.bfloat16), values, preferred_element_type=jnp.float32)
            + own_weight.astype(jnp.bfloat16).astype(jnp.float32) * jnp.concatenate([own_value] * group, axis=0)
        )
        den = den * (1.0 / (feats * feats)) + jnp.sum(weights, axis=-1, keepdims=True) + own_weight
        result = (num / den).astype(jnp.bfloat16)
        for h in range(group):
            at = (g * group + h) * head_size
            for k, out_ref in enumerate(out_refs):
                first = h * count + k * each
                out_ref[:, at : at + head_size] = result[first : first + each]


def decode(info, rows, weight, state_a, state_b, near_a, near_b, parts):
    heads, head_size, feats = weight.shape
    count = rows.shape[0]
    width = rows.shape[1] - 2 * heads * head_size
    vmem = pl.BlockSpec(memory_space=pltpu.VMEM)
    return pl.pallas_call(
        decode_kernel,
        in_specs=[pl.BlockSpec(memory_space=pltpu.SMEM)] + [vmem] * 6,
        out_specs=[vmem] * parts,
        out_shape=[jax.ShapeDtypeStruct((count // parts, width), jnp.bfloat16)] * parts,
        compiler_params=pltpu.CompilerParams(vmem_limit_bytes=32 * 1024 * 1024),
        cost_estimate=pl.CostEstimate(
            flops=10 * count * width * feats, bytes_accessed=4 * count * width, transcendentals=2 * count * width
        ),
        name="decode",
    )(info, rows, weight, state_a, state_b, near_a, near_b)


def body(
    sects, prompt_keys, prompt_values, lengths, feature_weight, queries, new_keys, new_values, row_prompt
):
    span = prompt_keys.shape[1]
    sub = lax.axis_index("sub")
    sect = lax.axis_index("sect")
    length = lengths[0]
    swap = [(0, 1), (1, 0)]

    mine = jnp.concatenate([queries, new_keys, new_values], axis=1)
    blocks = [mine] + [
        lax.ppermute(mine, "sect", [(i, (i + k) % sects) for i in range(sects)]) for k in range(1, sects)
    ]

    def first(half):
        return jnp.clip(length - WINDOW - half * span, 0, span - WINDOW)

    near = jnp.concatenate(
        [
            lax.dynamic_slice_in_dim(prompt_keys, first(sub), WINDOW, 1),
            lax.dynamic_slice_in_dim(prompt_values, first(sub), WINDOW, 1),
        ],
        axis=0,
    )
    far = lax.ppermute(near, "sub", swap)
    info = jnp.stack([sub * span + first(sub), (1 - sub) * span + first(1 - sub), length]).astype(jnp.int32)

    limit = (length - WINDOW - sub * span).reshape(1)
    state = prefill(prompt_keys, prompt_values, feature_weight, limit)
    other = lax.ppermute(state, "sub", swap)
    results = decode(info, jnp.concatenate(blocks, axis=0), feature_weight, state, other, near, far, sects)

    count = queries.shape[0]
    first_row = (sect * lax.axis_size("sub") + sub) * count
    prompts = lax.dynamic_slice_in_dim(row_prompt, first_row, count, 0)
    out = jnp.zeros_like(queries)
    for k, result in enumerate(results):
        if k > 0:
            result = lax.ppermute(result, "sect", [(i, (i - k) % sects) for i in range(sects)])
        out = jnp.where((prompts == (sect + k) % sects)[:, None], result, out)
    return out


def solution(mesh):
    placed = (
        P(("parts", "sect"), "sub", "tp"),
        P(("parts", "sect"), "sub", "tp"),
        P(("parts", "sect")),
        P("tp", None, None),
        P(("parts", "sect", "sub"), "tp"),
        P(("parts", "sect", "sub"), "tp"),
        P(("parts", "sect", "sub"), "tp"),
        P("parts"),
    )
    return jax.shard_map(
        functools.partial(body, mesh.shape["sect"]),
        mesh=mesh,
        in_specs=placed,
        out_specs=P(("parts", "sect", "sub"), "tp"),
        check_vma=False,
    )
```

time: 111 us -> 31.8 us (0.29)
  blocking collectives: 60 us -> 0 us
  matrix products: 13.6 us -> 0 us
  between operations: 14.3 us -> 0.74 us
  starting transfers between devices: 0.01 us -> 11.7 us
  local copies, waits for them, and re-layouts: 16 us -> 8.36 us
  Pallas kernels: 0 us -> 6.22 us
  waiting for transfers between devices: 4.96 us -> 3.46 us
    all_gather x4 -> x0, blocking collectives: 56.5 us -> none  [the longest x1 16 us: body(): lax.all_gather(state[None].astype(jnp.bfloat16), 'sect', axis=0, tiled=True)]
    another operation x2 -> x0, local copies, waits for them, and re-layouts: 13.9 us -> none  [the longest x1 6.93 us: body(): keys_local = prompt_keys[0].reshape(span, heads_kv, head_size)]
    dot_general x12 -> x0, matrix products: 13.6 us -> none  [the longest x2 7.78 us: featurize(): proj = jnp.einsum(form, values, weight, preferred_element_type=jnp.float32)]
    ppermute x0 -> x8, starting transfers between devices: none -> 11.7 us  [the longest x3 6.06 us: body(): lax.ppermute(mine, 'sect', [(i, (i + k) % sects) for i in range(sects)])]
    pallas_call x0 -> x2, Pallas kernels: none -> 6.22 us  [the longest x1 4.99 us: prefill(): pl.pallas_call(prefill_kernel, grid=(span // BLOCK,), in_specs=[pl.BlockS...]
    unnamed x17 -> x12, local copies, waits for them, and re-layouts: 0.67 us -> 6.75 us
    psum x1 -> x0, waiting for transfers between devices: 4.94 us -> none  [body(): lax.psum(state_part.astype(jnp.bfloat16), 'sub').astype(jnp.float32)]
    psum x1 -> x0, blocking collectives: 3.54 us -> none  [body(): lax.psum(norm_part.astype(jnp.bfloat16), 'sub').astype(jnp.float32)]
  transfers between devices with their start and end apart: 1 -> 8, of which waited for: 1 -> 3; matrix products, arithmetic and copies ran while one was open for 1% -> 4% of each run, Pallas kernels for 0% -> 16%
where the time goes in v1:
time: 31.8 us; the launch traced here: 31.4 us
  starting transfers between devices  11.7 us (37%)
  local copies, waits for them, and re-layouts  8.36 us (26%)
  Pallas kernels  6.22 us (20%)
  waiting for transfers between devices  3.46 us (11%)
  other arithmetic  0.99 us (3%)
  between operations  0.74 us (2%)
    unnamed x12, local copies, waits for them, and re-layouts  6.75 us
    ppermute x3, starting transfers between devices, body(): lax.ppermute(mine, 'sect', [(i, (i + k) % sects) for i in range(sects)])  6.06 us
    pallas_call x1, Pallas kernels, prefill(): pl.pallas_call(prefill_kernel, grid=(span // BLOCK,), in_specs=[pl.BlockS...  4.99 us
    ppermute x3, starting transfers between devices, body(): lax.ppermute(result, 'sect', [(i, (i - k) % sects) for i in range(sects)])  4.93 us
    ppermute x3, waiting for transfers between devices, body(): lax.ppermute(result, 'sect', [(i, (i - k) % sects) for i in range(sects)])  2.74 us
    pallas_call x1, Pallas kernels, decode(): pl.pallas_call(decode_kernel, in_specs=[pl.BlockSpec(memory_space=pltpu.S...  1.23 us
    dynamic_slice x1, local copies, waits for them, and re-layouts, body(): lax.dynamic_slice_in_dim(prompt_values, first(sub), WINDOW, 1)  0.91 us
    select_n x1, other arithmetic, body(): out = jnp.where((prompts == (sect + k) % sects)[:, None], result, out)  0.71 us
  transfers between devices with their start and end apart: 8, of which 3 were waited for; matrix products, arithmetic and copies ran while one was open for 4% of the time, Pallas kernels for 16%

profile of v1, /device:TPU:0, one launch (start us, length us, event | category | flops | bytes accessed | tf_op | source)
XLA Modules:
  0.0 31.4 jit_solution(17483606996187451790)
XLA Ops:
  0.0 0.8 %constant_dynamic-update-slice_fusion.2 = bf16[4,5120]{1,0:T(4,128)(2,1)S(1)} fusion(bf16[4,4096]{1,0:T(4,128)(2,1)} %param.12), kind=kLoop, calls=%fused_computation.5 | loop fusion | bytes 65536
  0.8 0.7 %constant_dynamic-update-slice_fusion.1 = bf16[4,5120]{1,0:T(4,128)(2,1)S(1)} fusion(bf16[4,5120]{1,0:T(4,128)(2,1)S(1)} %constant_dynamic-update-slice_fusion.2, bf16[4,512]{1,0:T(4,128)(2,1)} %param.13), kind=kLoop, calls=%fused_computation.4 | loop fusion | bytes 8192
  1.5 0.7 %constant_dynamic-update-slice_fusion = bf16[4,5120]{1,0:T(4,128)(2,1)S(1)} fusion(bf16[4,5120]{1,0:T(4,128)(2,1)S(1)} %constant_dynamic-update-slice_fusion.1, bf16[4,512]{1,0:T(4,128)(2,1)} %param.14), kind=kLoop, calls=%fused_computation.3 | loop fusion | bytes 8192 | tf_op jit(solution)/shard_map/concatenate | solution.py:180
  2.2 5.0 %collective-permute-start.2 = (bf16[4,5120]{1,0:T(4,128)(2,1)S(1)}, bf16[4,5120]{1,0:T(4,128)(2,1)S(1)}, u32[]{:S(2)}, u32[]{:S(2)}) collective-permute-start(bf16[4,5120]{1,0:T(4,128)(2,1)S(1)} %constant_dynamic-update-slice_fusion), channel_id=1, source_target_pairs={{0,12},{4,0},{8,4},{12,8},{1,13},{5,1},{9,5},{13,9},{2,14},{6,2},{... | collective-permute-start | bytes 122888 | tf_op jit(solution)/shard_map/ppermute | solution.py:182
  7.2 0.0 collective-permute-start.1
  7.2 1.0 %collective-permute-start = (bf16[4,5120]{1,0:T(4,128)(2,1)S(1)}, bf16[4,5120]{1,0:T(4,128)(2,1)S(1)}, u32[]{:S(2)}, u32[]{:S(2)}) collective-permute-start(bf16[4,5120]{1,0:T(4,128)(2,1)S(1)} %constant_dynamic-update-slice_fusion), channel_id=1, source_target_pairs={{0,4},{4,8},{8,12},{12,0},{1,5},{5,9},{9,13},{13,1},{2,6},{6,10},{... | collective-permute-start | bytes 122888 | tf_op jit(solution)/shard_map/ppermute | solution.py:182
  8.9 0.0 copy-start
  8.9 2.2 %copy-done = bf16[1,4096,512]{2,1,0:T(8,128)(2,1)S(1)} copy-done((bf16[1,4096,512]{2,1,0:T(8,128)(2,1)S(1)}, bf16[1,4096,512]{2,1,0:T(8,128)(2,1)}, u32[]{:S(2)}) %copy-start) | copy-done | bytes 4194328
  11.1 0.0 copy-start.1
  11.1 2.2 %copy-done.1 = bf16[1,4096,512]{2,1,0:T(8,128)(2,1)S(1)} copy-done((bf16[1,4096,512]{2,1,0:T(8,128)(2,1)S(1)}, bf16[1,4096,512]{2,1,0:T(8,128)(2,1)}, u32[]{:S(2)}) %copy-start.1) | copy-done | bytes 4194328
  13.3 0.0 copy-start.2
  13.3 0.9 %copy-done.2 = bf16[4,128,128]{2,1,0:T(8,128)(2,1)S(1)} copy-done((bf16[4,128,128]{2,1,0:T(8,128)(2,1)S(1)}, bf16[4,128,128]{2,1,0:T(8,128)(2,1)}, u32[]{:S(2)}) %copy-start.2) | copy-done | bytes 131096
  14.2 0.0 copy-start.4
  14.2 0.0 copy-start.3
  14.2 5.0 %prefill.1.state_a_ref = bf16[528,128]{1,0:T(8,128)(2,1)S(1)} custom-call(s32[1]{0:T(128)} %bitcast.3.limit_ref, bf16[1,4096,512]{2,1,0:T(8,128)(2,1)S(1)} %copy-done, bf16[1,4096,512]{2,1,0:T(8,128)(2,1)S(1)} %copy-done.1, bf16[4,128,128]{2,1,0:T(8,128)(2,1)S(1)} %copy-done.2), custom_call_target="tpu_custom_call" | custom-call | flops 1073741824 | bytes 8388608 | tf_op jit(solution)/shard_map/prefill/pallas_call | solution.py:70
  19.2 0.1 collective-permute-start.3
  19.3 0.9 %constant_dynamic-slice_fusion = (bf16[1,64,512]{2,1,0:T(8,128)(2,1)S(1)}, bf16[1,64,512]{2,1,0:T(8,128)(2,1)S(1)}) fusion(bf16[1,4096,512]{2,1,0:T(8,128)(2,1)} %values_ref.1, s32[]{:T(128)S(6)} %min.9, bf16[1,4096,512]{2,1,0:T(8,128)(2,1)} %keys_ref.1), kind=kLoop, calls=%fused_computation.7 | loop fusion | bytes 262148 | tf_op jit(solution)/shard_map/dynamic_slice | solution.py:191
  20.2 0.6 %collective-permute-start.4 = (bf16[2,64,512]{2,1,0:T(8,128)(2,1)S(1)}, bf16[2,64,512]{2,1,0:T(8,128)(2,1)S(1)}, u32[]{:S(2)}, u32[]{:S(2)}) collective-permute-start(bf16[2,64,512]{2,1,0:T(8,128)(2,1)S(1)} %pad_maximum_fusion.1.near_a_ref), channel_id=1, source_target_pairs={{0,1},{1,0},{2,3},{3,2},{4,5},{5,4},{6,7},{7,6},{8,9},{9,8},{10,11... | collective-permute-start | bytes 393224 | tf_op jit(solution)/shard_map/ppermute | solution.py:195
  20.8 0.0 copy-done.4
  20.8 0.1 broadcast_compare_fusion.3
  20.9 0.1 pad_add_fusion.info_ref
  21.0 0.0 collective-permute-done.2
  21.0 0.0 collective-permute-done.1
  21.0 0.0 collective-permute-done
  21.0 0.1 pad_maximum_fusion.rows_ref
  21.1 0.7 %collective-permute-done.4.near_b_ref = bf16[2,64,512]{2,1,0:T(8,128)(2,1)S(1)} collective-permute-done((bf16[2,64,512]{2,1,0:T(8,128)(2,1)S(1)}, bf16[2,64,512]{2,1,0:T(8,128)(2,1)S(1)}, u32[]{:S(2)}, u32[]{:S(2)}) %collective-permute-start.4) | collective-permute-done | bytes 131104 | tf_op jit(solution)/shard_map/ppermute | solution.py:195
  21.8 0.0 collective-permute-done.3.state_b_ref
  21.8 0.0 copy-done.3
  21.8 1.2 %decode.1 = (bf16[4,4096]{1,0:T(4,128)(2,1)S(1)}, bf16[4,4096]{1,0:T(4,128)(2,1)S(1)}, bf16[4,4096]{1,0:T(4,128)(2,1)S(1)}, bf16[4,4096]{1,0:T(4,128)(2,1)S(1)}) custom-call(s32[3]{0:T(128)S(1)} %pad_add_fusion.info_ref, bf16[16,5120]{1,0:T(8,128)(2,1)S(1)} %pad_maximum_fusion.rows_ref, bf16[4,128,128]{2,1,0:T(8,128)(2,1)S(1)} %copy-done.3, ...), custom_call_target="tpu_custom_call" | custom-call | flops 83886080 | bytes 262144 | tf_op jit(solution)/shard_map/decode/pallas_call | solution.py:158
  23.0 2.5 %collective-permute-start.5 = (bf16[4,4096]{1,0:T(4,128)(2,1)S(1)}, bf16[4,4096]{1,0:T(4,128)(2,1)S(1)}, u32[]{:S(2)}, u32[]{:S(2)}) collective-permute-start(bf16[4,4096]{1,0:T(4,128)(2,1)S(1)} %get-tuple-element.9), channel_id=1, source_target_pairs={{0,4},{4,8},{8,12},{12,0},{1,5},{5,9},{9,13},{13,1},{2,6},{6,10},{... | collective-permute-start | bytes 98312 | tf_op jit(solution)/shard_map/ppermute | solution.py:209
  25.5 1.0 %collective-permute-start.6 = (bf16[4,4096]{1,0:T(4,128)(2,1)S(1)}, bf16[4,4096]{1,0:T(4,128)(2,1)S(1)}, u32[]{:S(2)}, u32[]{:S(2)}) collective-permute-start(bf16[4,4096]{1,0:T(4,128)(2,1)S(1)} %get-tuple-element.10), channel_id=1, source_target_pairs={{0,8},{4,12},{8,0},{12,4},{1,9},{5,13},{9,1},{13,5},{2,10},{6,14},... | collective-permute-start | bytes 98312 | tf_op jit(solution)/shard_map/ppermute | solution.py:209
  26.5 1.5 %collective-permute-start.7 = (bf16[4,4096]{1,0:T(4,128)(2,1)S(1)}, bf16[4,4096]{1,0:T(4,128)(2,1)S(1)}, u32[]{:S(2)}, u32[]{:S(2)}) collective-permute-start(bf16[4,4096]{1,0:T(4,128)(2,1)S(1)} %get-tuple-element.11), channel_id=1, source_target_pairs={{0,12},{4,0},{8,4},{12,8},{1,13},{5,1},{9,5},{13,9},{2,14},{6,2},{... | collective-permute-start | bytes 98312 | tf_op jit(solution)/shard_map/ppermute | solution.py:209
  28.0 0.8 %collective-permute-done.5 = bf16[4,4096]{1,0:T(4,128)(2,1)S(1)} collective-permute-done((bf16[4,4096]{1,0:T(4,128)(2,1)S(1)}, bf16[4,4096]{1,0:T(4,128)(2,1)S(1)}, u32[]{:S(2)}, u32[]{:S(2)}) %collective-permute-start.5) | collective-permute-done | bytes 32800 | tf_op jit(solution)/shard_map/ppermute | solution.py:209
  28.8 1.9 %collective-permute-done.6 = bf16[4,4096]{1,0:T(4,128)(2,1)S(1)} collective-permute-done((bf16[4,4096]{1,0:T(4,128)(2,1)S(1)}, bf16[4,4096]{1,0:T(4,128)(2,1)S(1)}, u32[]{:S(2)}, u32[]{:S(2)}) %collective-permute-start.6) | collective-permute-done | bytes 32800 | tf_op jit(solution)/shard_map/ppermute | solution.py:209
  30.7 0.0 collective-permute-done.7
  30.7 0.7 %select_select_fusion = bf16[4,4096]{1,0:T(4,128)(2,1)} fusion(bf16[4,4096]{1,0:T(4,128)(2,1)S(1)} %collective-permute-done.5, bf16[4,4096]{1,0:T(4,128)(2,1)S(1)} %collective-permute-done.6, bf16[4,4096]{1,0:T(4,128)(2,1)S(1)} %collective-permute-done.7, bf16[4,4096]{1,0:T(4,128)(2,1)S(1)} %get-tuple-element.12, pred[4]{0:T(512)(128)(4,1)S(1)} %get-tuple-element.17, ...), kind=kLoop, calls=%fused_computation.2 | loop fusion | flops 65536 | bytes 163856 | tf_op jit(solution)/shard_map/jit(_where)/select_n | solution.py:210
  (2 shorter events, 0.0 us)
Async XLA Ops:
  2.2 18.8 %collective-permute-start.2 = (bf16[4,5120]{1,0:T(4,128)(2,1)S(1)}, bf16[4,5120]{1,0:T(4,128)(2,1)S(1)}, u32[]{:S(2)}, u32[]{:S(2)}) collective-permute-start(bf16[4,5120]{1,0:T(4,128)(2,1)S(1)} %constant_dynamic-update-slice_fusion), channel_id=1, source_target_pairs={{0,12},{4,0},{8,4},{12,8},{1,13},{5,1},{9,5},{13,9},{2,14},{6,2},{... | collective-permute-start | bytes 122888 | tf_op jit(solution)/shard_map/ppermute | solution.py:182
  7.2 13.7 %collective-permute-start.1 = (bf16[4,5120]{1,0:T(4,128)(2,1)S(1)}, bf16[4,5120]{1,0:T(4,128)(2,1)S(1)}, u32[]{:S(2)}, u32[]{:S(2)}) collective-permute-start(bf16[4,5120]{1,0:T(4,128)(2,1)S(1)} %constant_dynamic-update-slice_fusion), channel_id=1, source_target_pairs={{0,8},{4,12},{8,0},{12,4},{1,9},{5,13},{9,1},{13,5},{2,10},{6,14},... | collective-permute-start | bytes 122888 | tf_op jit(solution)/shard_map/ppermute | solution.py:182
  7.2 13.7 %collective-permute-start = (bf16[4,5120]{1,0:T(4,128)(2,1)S(1)}, bf16[4,5120]{1,0:T(4,128)(2,1)S(1)}, u32[]{:S(2)}, u32[]{:S(2)}) collective-permute-start(bf16[4,5120]{1,0:T(4,128)(2,1)S(1)} %constant_dynamic-update-slice_fusion), channel_id=1, source_target_pairs={{0,4},{4,8},{8,12},{12,0},{1,5},{5,9},{9,13},{13,1},{2,6},{6,10},{... | collective-permute-start | bytes 122888 | tf_op jit(solution)/shard_map/ppermute | solution.py:182
  8.9 2.2 %copy-start = (bf16[1,4096,512]{2,1,0:T(8,128)(2,1)S(1)}, bf16[1,4096,512]{2,1,0:T(8,128)(2,1)}, u32[]{:S(2)}) copy-start(bf16[1,4096,512]{2,1,0:T(8,128)(2,1)} %keys_ref.1) | copy-start | bytes 12582916
  11.1 2.2 %copy-start.1 = (bf16[1,4096,512]{2,1,0:T(8,128)(2,1)S(1)}, bf16[1,4096,512]{2,1,0:T(8,128)(2,1)}, u32[]{:S(2)}) copy-start(bf16[1,4096,512]{2,1,0:T(8,128)(2,1)} %values_ref.1) | copy-start | bytes 12582916
  13.3 0.9 %copy-start.2 = (bf16[4,128,128]{2,1,0:T(8,128)(2,1)S(1)}, bf16[4,128,128]{2,1,0:T(8,128)(2,1)}, u32[]{:S(2)}) copy-start(bf16[4,128,128]{2,1,0:T(8,128)(2,1)} %weight_ref.3) | copy-start | bytes 393220
  14.2 6.6 %copy-start.4 = (s32[32]{0:T(128)S(1)}, s32[32]{0:T(128)}, u32[]{:S(2)}) copy-start(s32[32]{0:T(128)} %param.15) | copy-start | bytes 388
  14.2 7.6 %copy-start.3 = (bf16[4,128,128]{2,1,0:T(8,128)(2,1)S(1)}, bf16[4,128,128]{2,1,0:T(8,128)(2,1)}, u32[]{:S(2)}) copy-start(bf16[4,128,128]{2,1,0:T(8,128)(2,1)} %weight_ref.3) | copy-start | bytes 393220
  19.2 2.6 %collective-permute-start.3 = (bf16[528,128]{1,0:T(8,128)(2,1)S(1)}, bf16[528,128]{1,0:T(8,128)(2,1)S(1)}, u32[]{:S(2)}, u32[]{:S(2)}) collective-permute-start(bf16[528,128]{1,0:T(8,128)(2,1)S(1)} %prefill.1.state_a_ref), channel_id=1, source_target_pairs={{0,1},{1,0},{2,3},{3,2},{4,5},{5,4},{6,7},{7,6},{8,9},{9,8},{10,11... | collective-permute-start | bytes 405512 | tf_op jit(solution)/shard_map/ppermute | solution.py:200
  20.2 1.6 %collective-permute-start.4 = (bf16[2,64,512]{2,1,0:T(8,128)(2,1)S(1)}, bf16[2,64,512]{2,1,0:T(8,128)(2,1)S(1)}, u32[]{:S(2)}, u32[]{:S(2)}) collective-permute-start(bf16[2,64,512]{2,1,0:T(8,128)(2,1)S(1)} %pad_maximum_fusion.1.near_a_ref), channel_id=1, source_target_pairs={{0,1},{1,0},{2,3},{3,2},{4,5},{5,4},{6,7},{7,6},{8,9},{9,8},{10,11... | collective-permute-start | bytes 393224 | tf_op jit(solution)/shard_map/ppermute | solution.py:195
  23.0 5.8 %collective-permute-start.5 = (bf16[4,4096]{1,0:T(4,128)(2,1)S(1)}, bf16[4,4096]{1,0:T(4,128)(2,1)S(1)}, u32[]{:S(2)}, u32[]{:S(2)}) collective-permute-start(bf16[4,4096]{1,0:T(4,128)(2,1)S(1)} %get-tuple-element.9), channel_id=1, source_target_pairs={{0,4},{4,8},{8,12},{12,0},{1,5},{5,9},{9,13},{13,1},{2,6},{6,10},{... | collective-permute-start | bytes 98312 | tf_op jit(solution)/shard_map/ppermute | solution.py:209
  25.5 5.2 %collective-permute-start.6 = (bf16[4,4096]{1,0:T(4,128)(2,1)S(1)}, bf16[4,4096]{1,0:T(4,128)(2,1)S(1)}, u32[]{:S(2)}, u32[]{:S(2)}) collective-permute-start(bf16[4,4096]{1,0:T(4,128)(2,1)S(1)} %get-tuple-element.10), channel_id=1, source_target_pairs={{0,8},{4,12},{8,0},{12,4},{1,9},{5,13},{9,1},{13,5},{2,10},{6,14},... | collective-permute-start | bytes 98312 | tf_op jit(solution)/shard_map/ppermute | solution.py:209
  26.5 4.2 %collective-permute-start.7 = (bf16[4,4096]{1,0:T(4,128)(2,1)S(1)}, bf16[4,4096]{1,0:T(4,128)(2,1)S(1)}, u32[]{:S(2)}, u32[]{:S(2)}) collective-permute-start(bf16[4,4096]{1,0:T(4,128)(2,1)S(1)} %get-tuple-element.11), channel_id=1, source_target_pairs={{0,12},{4,0},{8,4},{12,8},{1,13},{5,1},{9,5},{13,9},{2,14},{6,2},{... | collective-permute-start | bytes 98312 | tf_op jit(solution)/shard_map/ppermute | solution.py:209

commit v2 on v1

v2 whole, which is shorter than its diff:
```python
import functools

import jax
import jax.numpy as jnp
from jax import lax
from jax.experimental import pallas as pl
from jax.experimental.pallas import tpu as pltpu
from jax.sharding import PartitionSpec as P

WINDOW = 64
TAU = 10.0
EPS = 1e-06
BLOCK = 512
NT = (((1,), (1,)), ((), ()))


def feature(proj):
    return jnp.maximum(proj, 0.0) + jnp.exp(jnp.minimum(proj, 0.0))


def pack_kernel(queries_ref, keys_ref, values_ref, out_ref):
    width, each = queries_ref.shape[1], keys_ref.shape[1]
    out_ref[:, :width] = queries_ref[...]
    out_ref[:, width : width + each] = keys_ref[...]
    out_ref[:, width + each :] = values_ref[...]


def pack(queries, new_keys, new_values):
    vmem = pl.BlockSpec(memory_space=pltpu.VMEM)
    width = queries.shape[1] + 2 * new_keys.shape[1]
    return pl.pallas_call(
        pack_kernel,
        in_specs=[vmem] * 3,
        out_specs=vmem,
        out_shape=jax.ShapeDtypeStruct((queries.shape[0], width), jnp.bfloat16),
        name="pack",
    )(queries, new_keys, new_values)


SLAB = WINDOW + 16
MASK_ROW = 8


def prefill_kernel(
    lengths_ref, keys_ref, values_ref, weight_ref, out_ref,
    keys_at, values_at, weight_at, wide_ref, state_ref, norm_ref, weight_sem, load_sem, slab_sem,
):
    heads, head_size, feats = weight_ref.shape
    pairs = heads // 2
    span = keys_ref.shape[1]
    chunks = span // BLOCK
    get_weight = pltpu.make_async_copy(weight_ref, weight_at, weight_sem)
    get_weight.start()
    loads = []
    for c in range(chunks):
        rows = pl.ds(c * BLOCK, BLOCK)
        loads.append(
            [
                pltpu.make_async_copy(keys_ref.at[0, rows, :], keys_at.at[rows, :], load_sem.at[0, c]),
                pltpu.make_async_copy(values_ref.at[0, rows, :], values_at.at[rows, :], load_sem.at[1, c]),
            ]
        )
        for load in loads[-1]:
            load.start()

    state_ref[...] = jnp.zeros_like(state_ref)
    norm_ref[...] = jnp.zeros_like(norm_ref)
    wide_ref[...] = jnp.zeros_like(wide_ref)
    get_weight.wait()
    for g in range(heads):
        half = g % 2
        turned = weight_at[g].astype(jnp.float32).T.astype(jnp.bfloat16)
        wide_ref[g // 2, half * feats : (half + 1) * feats, half * head_size : (half + 1) * head_size] = turned

    begin = lengths_ref[0] - WINDOW - lax.axis_index("sub") * span
    first = jnp.clip(begin, 0, span - SLAB)
    first = pl.multiple_of(first - lax.rem(first, 16), 16)
    slabs = []
    for i, source in enumerate((keys_ref, values_ref)):
        for g in range(heads):
            at = heads * feats + 16 + (i * heads + g) * SLAB
            slabs.append(
                pltpu.make_async_copy(
                    source.at[0, pl.ds(first, SLAB), g * head_size : (g + 1) * head_size],
                    out_ref.at[at : at + SLAB, :],
                    slab_sem.at[i, g],
                )
            )
            slabs[-1].start()

    for c in range(chunks):
        rows = slice(c * BLOCK, (c + 1) * BLOCK)
        for load in loads[c]:
            load.wait()
        position = c * BLOCK + lax.broadcasted_iota(jnp.int32, (1, BLOCK), 1)
        live = position < begin
        for j in range(pairs):
            cols = slice(j * 2 * head_size, (j + 1) * 2 * head_size)
            proj = lax.dot_general(wide_ref[j], keys_at[rows, cols], NT, preferred_element_type=jnp.float32)
            mapped = jnp.where(live, feature(proj), 0.0)
            total = norm_ref[j]
            for k in range(BLOCK // 128):
                total = total + mapped[:, k * 128 : (k + 1) * 128]
            norm_ref[j] = total
            state_ref[j] += jnp.dot(
                mapped.astype(jnp.bfloat16), values_at[rows, cols], preferred_element_type=jnp.float32
            )

    tile = []
    for g in range(heads):
        half = g % 2
        part = state_ref[g // 2, half * feats : (half + 1) * feats, half * head_size : (half + 1) * head_size]
        out_ref[g * feats : (g + 1) * feats, :] = part.astype(jnp.bfloat16)
        sums = norm_ref[g // 2, half * feats : (half + 1) * feats, :]
        tile.append(jnp.sum(sums.T, axis=0, keepdims=True))
    slot = first + lax.broadcasted_iota(jnp.int32, (1, head_size), 1)
    tile.append(jnp.zeros((MASK_ROW - heads, head_size), jnp.float32))
    tile.append(jnp.where((slot >= begin) & (slot < begin + WINDOW), 1.0, 0.0))
    tile.append(jnp.zeros((15 - MASK_ROW, head_size), jnp.float32))
    out_ref[heads * feats : heads * feats + 16, :] = jnp.concatenate(tile, axis=0).astype(jnp.bfloat16)
    for slab in slabs:
        slab.wait()


def prefill(keys, values, weight, lengths):
    heads, head_size, feats = weight.shape
    span, width = keys.shape[1:]
    hbm = pl.BlockSpec(memory_space=pltpu.MemorySpace.HBM)
    vmem = pl.BlockSpec(memory_space=pltpu.VMEM)
    return pl.pallas_call(
        prefill_kernel,
        in_specs=[pl.BlockSpec(memory_space=pltpu.SMEM), hbm, hbm, hbm],
        out_specs=vmem,
        out_shape=jax.ShapeDtypeStruct((heads * feats + 16 + 2 * heads * SLAB, head_size), jnp.bfloat16),
        scratch_shapes=[
            pltpu.VMEM((span, width), jnp.bfloat16),
            pltpu.VMEM((span, width), jnp.bfloat16),
            pltpu.VMEM(weight.shape, jnp.bfloat16),
            pltpu.VMEM((heads // 2, 2 * feats, 2 * head_size), jnp.bfloat16),
            pltpu.VMEM((heads // 2, 2 * feats, 2 * head_size), jnp.float32),
            pltpu.VMEM((heads // 2, 2 * feats, 128), jnp.float32),
            pltpu.SemaphoreType.DMA,
            pltpu.SemaphoreType.DMA((2, span // BLOCK)),
            pltpu.SemaphoreType.DMA((2, heads)),
        ],
        compiler_params=pltpu.CompilerParams(vmem_limit_bytes=52 * 1024 * 1024),
        cost_estimate=pl.CostEstimate(
            flops=4 * span * width * feats, bytes_accessed=4 * span * width, transcendentals=span * width
        ),
        name="prefill",
    )(lengths, keys, values, weight)


def decode_kernel(rows_ref, weight_ref, near_ref, far_ref, *out_refs):
    heads, head_size, feats = weight_ref.shape
    count = rows_ref.shape[0]
    group = (rows_ref.shape[1] - 2 * heads * head_size) // (heads * head_size)
    keys_at = heads * group * head_size
    values_at = keys_at + heads * head_size
    each = count // len(out_refs)
    tile_at = heads * feats
    halves = (near_ref, far_ref)
    tiles = [ref[tile_at : tile_at + 16, :].astype(jnp.float32) for ref in halves]
    for g in range(heads):
        query = jnp.concatenate(
            [
                rows_ref[:, (g * group + h) * head_size : (g * group + h + 1) * head_size]
                for h in range(group)
            ],
            axis=0,
        )
        wide = query.astype(jnp.float32)
        phi = feature(jnp.dot(query, weight_ref[g], preferred_element_type=jnp.float32)).astype(jnp.bfloat16)
        scale = (TAU / head_size) * lax.rsqrt(jnp.mean(wide * wide, axis=-1, keepdims=True) + EPS)
        own_key = rows_ref[:, keys_at + g * head_size : keys_at + (g + 1) * head_size].astype(jnp.float32)
        own_value = rows_ref[:, values_at + g * head_size : values_at + (g + 1) * head_size].astype(jnp.float32)
        own_key = own_key * lax.rsqrt(jnp.mean(own_key * own_key, axis=-1, keepdims=True) + EPS)
        own_score = jnp.sum(wide * jnp.concatenate([own_key] * group, axis=0), axis=-1, keepdims=True) * scale
        own_weight = jnp.exp(own_score)
        num = own_weight.astype(jnp.bfloat16).astype(jnp.float32) * jnp.concatenate([own_value] * group, axis=0)
        den = own_weight
        linear = jnp.zeros_like(num)
        for ref, tile in zip(halves, tiles):
            linear += jnp.dot(phi, ref[g * feats : (g + 1) * feats, :], preferred_element_type=jnp.float32)
            at = tile_at + 16 + g * SLAB
            keys = ref[at : at + SLAB, :]
            at += heads * SLAB
            values = ref[at : at + SLAB, :]
            keys_wide = keys.astype(jnp.float32)
            key_scale = lax.rsqrt(jnp.mean((keys_wide * keys_wide).T, axis=0, keepdims=True) + EPS)
            score = lax.dot_general(query, keys, NT, preferred_element_type=jnp.float32) * scale * key_scale
            weights = jnp.exp(score) * tile[MASK_ROW : MASK_ROW + 1, :SLAB]
            num += jnp.dot(weights.astype(jnp.bfloat16), values, preferred_element_type=jnp.float32)
            den += jnp.sum(weights, axis=-1, keepdims=True)
        norm = (tiles[0] + tiles[1])[g : g + 1]
        back = 1.0 / (feats * feats)
        den += jnp.sum(phi.astype(jnp.float32) * norm, axis=-1, keepdims=True) * back
        result = ((linear * back + num) / den).astype(jnp.bfloat16)
        for h in range(group):
            at = (g * group + h) * head_size
            for k, out_ref in enumerate(out_refs):
                start = h * count + k * each
                out_ref[:, at : at + head_size] = result[start : start + each]


def decode(rows, weight, near, far, parts):
    heads, head_size, feats = weight.shape
    count = rows.shape[0]
    width = rows.shape[1] - 2 * heads * head_size
    vmem = pl.BlockSpec(memory_space=pltpu.VMEM)
    return pl.pallas_call(
        decode_kernel,
        in_specs=[vmem] * 4,
        out_specs=[vmem] * parts,
        out_shape=[jax.ShapeDtypeStruct((count // parts, width), jnp.bfloat16)] * parts,
        compiler_params=pltpu.CompilerParams(vmem_limit_bytes=32 * 1024 * 1024),
        cost_estimate=pl.CostEstimate(
            flops=10 * count * width * feats, bytes_accessed=4 * count * width, transcendentals=2 * count * width
        ),
        name="decode",
    )(rows, weight, near, far)


def body(
    sects, prompt_keys, prompt_values, lengths, feature_weight, queries, new_keys, new_values, row_prompt
):
    sub = lax.axis_index("sub")
    sect = lax.axis_index("sect")
    mine = pack(queries, new_keys, new_values)
    blocks = [mine] + [
        lax.ppermute(mine, "sect", [(i, (i + k) % sects) for i in range(sects)]) for k in range(1, sects)
    ]
    near = prefill(prompt_keys, prompt_values, feature_weight, lengths)
    far = lax.ppermute(near, "sub", [(0, 1), (1, 0)])
    results = decode(jnp.concatenate(blocks, axis=0), feature_weight, near, far, sects)

    count = queries.shape[0]
    first_row = (sect * lax.axis_size("sub") + sub) * count
    prompts = lax.dynamic_slice_in_dim(row_prompt, first_row, count, 0)
    out = jnp.zeros_like(queries)
    for k, result in enumerate(results):
        if k > 0:
            result = lax.ppermute(result, "sect", [(i, (i - k) % sects) for i in range(sects)])
        out = jnp.where((prompts == (sect + k) % sects)[:, None], result, out)
    return out


def solution(mesh):
    placed = (
        P(("parts", "sect"), "sub", "tp"),
        P(("parts", "sect"), "sub", "tp"),
        P(("parts", "sect")),
        P("tp", None, None),
        P(("parts", "sect", "sub"), "tp"),
        P(("parts", "sect", "sub"), "tp"),
        P(("parts", "sect", "sub"), "tp"),
        P("parts"),
    )
    return jax.shard_map(
        functools.partial(body, mesh.shape["sect"]),
        mesh=mesh,
        in_specs=placed,
        out_specs=P(("parts", "sect", "sub"), "tp"),
        check_vma=False,
    )
```

time: 31.8 us -> 25.9 us (0.81)
  local copies, waits for them, and re-layouts: 8.36 us -> 0.91 us
  Pallas kernels: 6.22 us -> 8.01 us
  starting transfers between devices: 11.7 us -> 11.1 us
  waiting for transfers between devices: 3.46 us -> 4.06 us
    unnamed x12 -> x8, local copies, waits for them, and re-layouts: 6.75 us -> 0.91 us
    pallas_call x2 -> x3, Pallas kernels: 6.22 us -> 8.01 us  [the longest x1 5.47 us: prefill(): pl.pallas_call(prefill_kernel, in_specs=[pl.BlockSpec(memory_space=pltpu....]
    dynamic_slice x1 -> x0, local copies, waits for them, and re-layouts: 0.91 us -> none  [body(): lax.dynamic_slice_in_dim(prompt_values, first(sub), WINDOW, 1)]
    concatenate x1 -> x0, local copies, waits for them, and re-layouts: 0.7 us -> none  [body(): mine = jnp.concatenate([queries, new_keys, new_values], axis=1)]
    ppermute x2 -> x1, waiting for transfers between devices: 0.71 us -> 1.34 us  [body(): far = lax.ppermute(near, 'sub', [(0, 1), (1, 0)])]
    ppermute x2 -> x1, starting transfers between devices: 0.67 us -> 0.07 us  [body(): far = lax.ppermute(near, 'sub', [(0, 1), (1, 0)])]
  transfers between devices with their start and end apart: 8 -> 7, of which waited for: 3 -> 4; matrix products, arithmetic and copies ran while one was open for 4% -> 1% of each run, Pallas kernels for 16% -> 21%
where the time goes in v2:
time: 25.9 us; the launch traced here: 25.7 us
  starting transfers between devices  11.1 us (43%)
  Pallas kernels  8.01 us (31%)
  waiting for transfers between devices  4.06 us (16%)
  local copies, waits for them, and re-layouts  0.91 us (4%)
  other arithmetic  0.9 us (3%)
  between operations  0.74 us (3%)
    ppermute x3, starting transfers between devices, body(): lax.ppermute(mine, 'sect', [(i, (i + k) % sects) for i in range(sects)])  6.06 us
    pallas_call x1, Pallas kernels, prefill(): pl.pallas_call(prefill_kernel, in_specs=[pl.BlockSpec(memory_space=pltpu....  5.47 us
    ppermute x3, starting transfers between devices, body(): lax.ppermute(result, 'sect', [(i, (i - k) % sects) for i in range(sects)])  4.97 us
    ppermute x3, waiting for transfers between devices, body(): lax.ppermute(result, 'sect', [(i, (i - k) % sects) for i in range(sects)])  2.72 us
    pallas_call x1, Pallas kernels, pack(): pl.pallas_call(pack_kernel, in_specs=[vmem] * 3, out_specs=vmem, out_shap...  1.39 us
    ppermute x1, waiting for transfers between devices, body(): far = lax.ppermute(near, 'sub', [(0, 1), (1, 0)])  1.34 us
    pallas_call x1, Pallas kernels, decode(): pl.pallas_call(decode_kernel, in_specs=[vmem] * 4, out_specs=[vmem] * par...  1.14 us
    unnamed x8, local copies, waits for them, and re-layouts  0.91 us
  transfers between devices with their start and end apart: 7, of which 4 were waited for; matrix products, arithmetic and copies ran while one was open for 1% of the time, Pallas kernels for 21%

profile of v2, /device:TPU:0, one launch (start us, length us, event | category | flops | bytes accessed | tf_op | source)
XLA Modules:
  0.0 25.7 jit_solution(7152564222424679974)
XLA Ops:
  0.0 1.4 %pack.1 = bf16[4,5120]{1,0:T(4,128)(2,1)} custom-call(bf16[4,4096]{1,0:T(4,128)(2,1)} %queries_ref.1, bf16[4,512]{1,0:T(4,128)(2,1)} %keys_ref.2, bf16[4,512]{1,0:T(4,128)(2,1)} %values_ref.2), custom_call_target="tpu_custom_call" | custom-call | tf_op jit(solution)/shard_map/pack/pallas_call | solution.py:31
  1.4 5.0 %collective-permute-start.2 = (bf16[4,5120]{1,0:T(4,128)(2,1)}, bf16[4,5120]{1,0:T(4,128)(2,1)S(1)}, u32[]{:S(2)}, u32[]{:S(2)}) collective-permute-start(bf16[4,5120]{1,0:T(4,128)(2,1)} %pack.1), channel_id=1, source_target_pairs={{0,12},{4,0},{8,4},{12,8},{1,13},{5,1},{9,5},{13,9},{2,14},{6,2},{... | collective-permute-start | bytes 122888 | tf_op jit(solution)/shard_map/ppermute | solution.py:231
  6.4 0.0 collective-permute-start.1
  6.4 1.0 %collective-permute-start = (bf16[4,5120]{1,0:T(4,128)(2,1)}, bf16[4,5120]{1,0:T(4,128)(2,1)S(1)}, u32[]{:S(2)}, u32[]{:S(2)}) collective-permute-start(bf16[4,5120]{1,0:T(4,128)(2,1)} %pack.1), channel_id=1, source_target_pairs={{0,4},{4,8},{8,12},{12,0},{1,5},{5,9},{9,13},{13,1},{2,6},{6,10},{... | collective-permute-start | bytes 122888 | tf_op jit(solution)/shard_map/ppermute | solution.py:231
  8.1 0.0 copy-start
  8.1 0.9 %copy-done = bf16[4,128,128]{2,1,0:T(8,128)(2,1)S(1)} copy-done((bf16[4,128,128]{2,1,0:T(8,128)(2,1)S(1)}, bf16[4,128,128]{2,1,0:T(8,128)(2,1)}, u32[]{:S(2)}) %copy-start) | copy-done | bytes 131096
  9.0 0.0 copy-start.3
  9.0 0.0 copy-start.2
  9.0 0.0 copy-start.1
  9.0 5.5 %prefill.1.near_ref = bf16[1168,128]{1,0:T(8,128)(2,1)S(1)} custom-call(s32[1]{0:T(128)S(6)} %copy.9.lengths_ref, bf16[1,4096,512]{2,1,0:T(8,128)(2,1)} %keys_ref.3, bf16[1,4096,512]{2,1,0:T(8,128)(2,1)} %values_ref.3, bf16[4,128,128]{2,1,0:T(8,128)(2,1)S(1)} %copy-done), custom_call_target="tpu_custom_call" | custom-call | flops 1073741824 | bytes 8388608 | tf_op jit(solution)/shard_map/prefill/pallas_call | solution.py:130
  14.5 0.1 collective-permute-start.3
  14.6 0.0 copy-done.3
  14.6 0.1 broadcast_compare_fusion.3
  14.7 0.0 collective-permute-done.2
  14.7 0.0 collective-permute-done.1
  14.7 0.0 collective-permute-done
  14.7 0.0 copy-done.2
  14.7 0.1 pad_maximum_fusion.rows_ref
  14.8 1.3 %collective-permute-done.3.far_ref = bf16[1168,128]{1,0:T(8,128)(2,1)S(1)} collective-permute-done((bf16[1168,128]{1,0:T(8,128)(2,1)S(1)}, bf16[1168,128]{1,0:T(8,128)(2,1)S(1)}, u32[]{:S(2)}, u32[]{:S(2)}) %collective-permute-start.3) | collective-permute-done | bytes 299040 | tf_op jit(solution)/shard_map/ppermute | solution.py:234
  16.2 0.0 copy-done.1
  16.2 1.1 %decode.1 = (bf16[4,4096]{1,0:T(4,128)(2,1)S(1)}, bf16[4,4096]{1,0:T(4,128)(2,1)S(1)}, bf16[4,4096]{1,0:T(4,128)(2,1)S(1)}, bf16[4,4096]{1,0:T(4,128)(2,1)S(1)}) custom-call(bf16[16,5120]{1,0:T(8,128)(2,1)S(1)} %pad_maximum_fusion.rows_ref, bf16[4,128,128]{2,1,0:T(8,128)(2,1)S(1)} %copy-done.1, bf16[1168,128]{1,0:T(8,128)(2,1)S(1)} %prefill.1.near_ref, ...), custom_call_target="tpu_custom_call" | custom-call | flops 83886080 | bytes 262144 | tf_op jit(solution)/shard_map/decode/pallas_call | solution.py:211
  17.3 2.5 %collective-permute-start.4 = (bf16[4,4096]{1,0:T(4,128)(2,1)S(1)}, bf16[4,4096]{1,0:T(4,128)(2,1)S(1)}, u32[]{:S(2)}, u32[]{:S(2)}) collective-permute-start(bf16[4,4096]{1,0:T(4,128)(2,1)S(1)} %get-tuple-element.9), channel_id=1, source_target_pairs={{0,4},{4,8},{8,12},{12,0},{1,5},{5,9},{9,13},{13,1},{2,6},{6,10},{... | collective-permute-start | bytes 98312 | tf_op jit(solution)/shard_map/ppermute | solution.py:243
  19.8 0.9 %collective-permute-start.5 = (bf16[4,4096]{1,0:T(4,128)(2,1)S(1)}, bf16[4,4096]{1,0:T(4,128)(2,1)S(1)}, u32[]{:S(2)}, u32[]{:S(2)}) collective-permute-start(bf16[4,4096]{1,0:T(4,128)(2,1)S(1)} %get-tuple-element.10), channel_id=1, source_target_pairs={{0,8},{4,12},{8,0},{12,4},{1,9},{5,13},{9,1},{13,5},{2,10},{6,14},... | collective-permute-start | bytes 98312 | tf_op jit(solution)/shard_map/ppermute | solution.py:243
  20.7 1.5 %collective-permute-start.6 = (bf16[4,4096]{1,0:T(4,128)(2,1)S(1)}, bf16[4,4096]{1,0:T(4,128)(2,1)S(1)}, u32[]{:S(2)}, u32[]{:S(2)}) collective-permute-start(bf16[4,4096]{1,0:T(4,128)(2,1)S(1)} %get-tuple-element.11), channel_id=1, source_target_pairs={{0,12},{4,0},{8,4},{12,8},{1,13},{5,1},{9,5},{13,9},{2,14},{6,2},{... | collective-permute-start | bytes 98312 | tf_op jit(solution)/shard_map/ppermute | solution.py:243
  22.3 0.9 %collective-permute-done.4 = bf16[4,4096]{1,0:T(4,128)(2,1)S(1)} collective-permute-done((bf16[4,4096]{1,0:T(4,128)(2,1)S(1)}, bf16[4,4096]{1,0:T(4,128)(2,1)S(1)}, u32[]{:S(2)}, u32[]{:S(2)}) %collective-permute-start.4) | collective-permute-done | bytes 32800 | tf_op jit(solution)/shard_map/ppermute | solution.py:243
  23.2 1.8 %collective-permute-done.5 = bf16[4,4096]{1,0:T(4,128)(2,1)S(1)} collective-permute-done((bf16[4,4096]{1,0:T(4,128)(2,1)S(1)}, bf16[4,4096]{1,0:T(4,128)(2,1)S(1)}, u32[]{:S(2)}, u32[]{:S(2)}) %collective-permute-start.5) | collective-permute-done | bytes 32800 | tf_op jit(solution)/shard_map/ppermute | solution.py:243
  24.9 0.1 collective-permute-done.6
  25.0 0.7 %select_select_fusion = bf16[4,4096]{1,0:T(4,128)(2,1)} fusion(bf16[4,4096]{1,0:T(4,128)(2,1)S(1)} %collective-permute-done.4, bf16[4,4096]{1,0:T(4,128)(2,1)S(1)} %collective-permute-done.5, bf16[4,4096]{1,0:T(4,128)(2,1)S(1)} %collective-permute-done.6, bf16[4,4096]{1,0:T(4,128)(2,1)S(1)} %get-tuple-element.12, pred[4]{0:T(512)(128)(4,1)S(1)} %get-tuple-element.17, ...), kind=kLoop, calls=%fused_computation.1 | loop fusion | flops 65536 | bytes 163856 | tf_op jit(solution)/shard_map/jit(_where)/select_n | solution.py:244
  (1 shorter events, 0.0 us)
Async XLA Ops:
  1.4 13.3 %collective-permute-start.2 = (bf16[4,5120]{1,0:T(4,128)(2,1)}, bf16[4,5120]{1,0:T(4,128)(2,1)S(1)}, u32[]{:S(2)}, u32[]{:S(2)}) collective-permute-start(bf16[4,5120]{1,0:T(4,128)(2,1)} %pack.1), channel_id=1, source_target_pairs={{0,12},{4,0},{8,4},{12,8},{1,13},{5,1},{9,5},{13,9},{2,14},{6,2},{... | collective-permute-start | bytes 122888 | tf_op jit(solution)/shard_map/ppermute | solution.py:231
  6.4 8.3 %collective-permute-start.1 = (bf16[4,5120]{1,0:T(4,128)(2,1)}, bf16[4,5120]{1,0:T(4,128)(2,1)S(1)}, u32[]{:S(2)}, u32[]{:S(2)}) collective-permute-start(bf16[4,5120]{1,0:T(4,128)(2,1)} %pack.1), channel_id=1, source_target_pairs={{0,8},{4,12},{8,0},{12,4},{1,9},{5,13},{9,1},{13,5},{2,10},{6,14},... | collective-permute-start | bytes 122888 | tf_op jit(solution)/shard_map/ppermute | solution.py:231
  6.4 8.3 %collective-permute-start = (bf16[4,5120]{1,0:T(4,128)(2,1)}, bf16[4,5120]{1,0:T(4,128)(2,1)S(1)}, u32[]{:S(2)}, u32[]{:S(2)}) collective-permute-start(bf16[4,5120]{1,0:T(4,128)(2,1)} %pack.1), channel_id=1, source_target_pairs={{0,4},{4,8},{8,12},{12,0},{1,5},{5,9},{9,13},{13,1},{2,6},{6,10},{... | collective-permute-start | bytes 122888 | tf_op jit(solution)/shard_map/ppermute | solution.py:231
  8.1 0.9 %copy-start = (bf16[4,128,128]{2,1,0:T(8,128)(2,1)S(1)}, bf16[4,128,128]{2,1,0:T(8,128)(2,1)}, u32[]{:S(2)}) copy-start(bf16[4,128,128]{2,1,0:T(8,128)(2,1)} %weight_ref.3) | copy-start | bytes 393220
  9.0 5.6 %copy-start.3 = (s32[32]{0:T(128)S(1)}, s32[32]{0:T(128)}, u32[]{:S(2)}) copy-start(s32[32]{0:T(128)} %param.15) | copy-start | bytes 388
  9.0 5.7 %copy-start.2 = (bf16[4,5120]{1,0:T(4,128)(2,1)S(1)}, bf16[4,5120]{1,0:T(4,128)(2,1)}, u32[]{:S(2)}) copy-start(bf16[4,5120]{1,0:T(4,128)(2,1)} %pack.1) | copy-start | bytes 122884
  9.0 7.1 %copy-start.1 = (bf16[4,128,128]{2,1,0:T(8,128)(2,1)S(1)}, bf16[4,128,128]{2,1,0:T(8,128)(2,1)}, u32[]{:S(2)}) copy-start(bf16[4,128,128]{2,1,0:T(8,128)(2,1)} %weight_ref.3) | copy-start | bytes 393220
  14.5 1.7 %collective-permute-start.3 = (bf16[1168,128]{1,0:T(8,128)(2,1)S(1)}, bf16[1168,128]{1,0:T(8,128)(2,1)S(1)}, u32[]{:S(2)}, u32[]{:S(2)}) collective-permute-start(bf16[1168,128]{1,0:T(8,128)(2,1)S(1)} %prefill.1.near_ref), channel_id=1, source_target_pairs={{0,1},{1,0},{2,3},{3,2},{4,5},{5,4},{6,7},{7,6},{8,9},{9,8},{10,11... | collective-permute-start | bytes 897032 | tf_op jit(solution)/shard_map/ppermute | solution.py:234
  17.3 5.8 %collective-permute-start.4 = (bf16[4,4096]{1,0:T(4,128)(2,1)S(1)}, bf16[4,4096]{1,0:T(4,128)(2,1)S(1)}, u32[]{:S(2)}, u32[]{:S(2)}) collective-permute-start(bf16[4,4096]{1,0:T(4,128)(2,1)S(1)} %get-tuple-element.9), channel_id=1, source_target_pairs={{0,4},{4,8},{8,12},{12,0},{1,5},{5,9},{9,13},{13,1},{2,6},{6,10},{... | collective-permute-start | bytes 98312 | tf_op jit(solution)/shard_map/ppermute | solution.py:243
  19.8 5.1 %collective-permute-start.5 = (bf16[4,4096]{1,0:T(4,128)(2,1)S(1)}, bf16[4,4096]{1,0:T(4,128)(2,1)S(1)}, u32[]{:S(2)}, u32[]{:S(2)}) collective-permute-start(bf16[4,4096]{1,0:T(4,128)(2,1)S(1)} %get-tuple-element.10), channel_id=1, source_target_pairs={{0,8},{4,12},{8,0},{12,4},{1,9},{5,13},{9,1},{13,5},{2,10},{6,14},... | collective-permute-start | bytes 98312 | tf_op jit(solution)/shard_map/ppermute | solution.py:243
  20.7 4.3 %collective-permute-start.6 = (bf16[4,4096]{1,0:T(4,128)(2,1)S(1)}, bf16[4,4096]{1,0:T(4,128)(2,1)S(1)}, u32[]{:S(2)}, u32[]{:S(2)}) collective-permute-start(bf16[4,4096]{1,0:T(4,128)(2,1)S(1)} %get-tuple-element.11), channel_id=1, source_target_pairs={{0,12},{4,0},{8,4},{12,8},{1,13},{5,1},{9,5},{13,9},{2,14},{6,2},{... | collective-permute-start | bytes 98312 | tf_op jit(solution)/shard_map/ppermute | solution.py:243

commit v3 on v2

--- a/solution.py
+++ b/solution.py
@@ -151,13 +151,14 @@
     )(lengths, keys, values, weight)
 
 
-def decode_kernel(rows_ref, weight_ref, near_ref, far_ref, *out_refs):
+def decode_kernel(rows_ref, weight_ref, near_ref, far_ref, out_ref):
     heads, head_size, feats = weight_ref.shape
     count = rows_ref.shape[0]
     group = (rows_ref.shape[1] - 2 * heads * head_size) // (heads * head_size)
     keys_at = heads * group * head_size
     values_at = keys_at + heads * head_size
-    each = count // len(out_refs)
+    parts, each = out_ref.shape[:2]
+    home = lax.axis_index("sect")
     tile_at = heads * feats
     halves = (near_ref, far_ref)
     tiles = [ref[tile_at : tile_at + 16, :].astype(jnp.float32) for ref in halves]
@@ -198,9 +199,9 @@
         result = ((linear * back + num) / den).astype(jnp.bfloat16)
         for h in range(group):
             at = (g * group + h) * head_size
-            for k, out_ref in enumerate(out_refs):
+            for k in range(parts):
                 start = h * count + k * each
-                out_ref[:, at : at + head_size] = result[start : start + each]
+                out_ref[lax.rem(home - k + parts, parts), :, at : at + head_size] = result[start : start + each]
 
 
 def decode(rows, weight, near, far, parts):
@@ -211,8 +212,8 @@
     return pl.pallas_call(
         decode_kernel,
         in_specs=[vmem] * 4,
-        out_specs=[vmem] * parts,
-        out_shape=[jax.ShapeDtypeStruct((count // parts, width), jnp.bfloat16)] * parts,
+        out_specs=vmem,
+        out_shape=jax.ShapeDtypeStruct((parts, count // parts, width), jnp.bfloat16),
         compiler_params=pltpu.CompilerParams(vmem_limit_bytes=32 * 1024 * 1024),
         cost_estimate=pl.CostEstimate(
             flops=10 * count * width * feats, bytes_accessed=4 * count * width, transcendentals=2 * count * width
@@ -237,11 +238,10 @@
     count = queries.shape[0]
     first_row = (sect * lax.axis_size("sub") + sub) * count
     prompts = lax.dynamic_slice_in_dim(row_prompt, first_row, count, 0)
+    results = lax.all_to_all(results, "sect", 0, 0, tiled=True)
     out = jnp.zeros_like(queries)
-    for k, result in enumerate(results):
-        if k > 0:
-            result = lax.ppermute(result, "sect", [(i, (i - k) % sects) for i in range(sects)])
-        out = jnp.where((prompts == (sect + k) % sects)[:, None], result, out)
+    for k in range(sects):
+        out = jnp.where((prompts == k)[:, None], results[k], out)
     return out
 
 

time: 25.9 us -> 29.3 us (1.13)
  waiting for transfers between devices: 4.06 us -> 7.56 us
  starting transfers between devices: 11.1 us -> 10.2 us
  Pallas kernels: 8.01 us -> 8.65 us
    all_to_all x0 -> x1, waiting for transfers between devices: none -> 6.21 us  [body(): results = lax.all_to_all(results, 'sect', 0, 0, tiled=True)]
    ppermute x3 -> x0, starting transfers between devices: 4.97 us -> none  [body(): lax.ppermute(result, 'sect', [(i, (i - k) % sects) for i in range(sects)])]
    all_to_all x0 -> x1, starting transfers between devices: none -> 4.08 us  [body(): results = lax.all_to_all(results, 'sect', 0, 0, tiled=True)]
    ppermute x3 -> x0, waiting for transfers between devices: 2.72 us -> none  [body(): lax.ppermute(result, 'sect', [(i, (i - k) % sects) for i in range(sects)])]
    pallas_call x1, Pallas kernels: 1.14 us -> 1.79 us  [decode(): pl.pallas_call(decode_kernel, in_specs=[vmem] * 4, out_specs=vmem, out_sh...]
  transfers between devices with their start and end apart: 7 -> 5, of which waited for: 4 -> 2; matrix products, arithmetic and copies ran while one was open for 1% -> 1% of each run, Pallas kernels for 21% -> 19%
where the time goes in v3:
time: 29.3 us; the launch traced here: 29 us
  starting transfers between devices  10.2 us (35%)
  Pallas kernels  8.65 us (30%)
  waiting for transfers between devices  7.56 us (26%)
  local copies, waits for them, and re-layouts  0.91 us (3%)
  other arithmetic  0.9 us (3%)
  between operations  0.72 us (2%)
    all_to_all x1, waiting for transfers between devices, body(): results = lax.all_to_all(results, 'sect', 0, 0, tiled=True)  6.21 us
    ppermute x3, starting transfers between devices, body(): lax.ppermute(mine, 'sect', [(i, (i + k) % sects) for i in range(sects)])  6.06 us
    pallas_call x1, Pallas kernels, prefill(): pl.pallas_call(prefill_kernel, in_specs=[pl.BlockSpec(memory_space=pltpu....  5.48 us
    all_to_all x1, starting transfers between devices, body(): results = lax.all_to_all(results, 'sect', 0, 0, tiled=True)  4.08 us
    pallas_call x1, Pallas kernels, decode(): pl.pallas_call(decode_kernel, in_specs=[vmem] * 4, out_specs=vmem, out_sh...  1.79 us
    pallas_call x1, Pallas kernels, pack(): pl.pallas_call(pack_kernel, in_specs=[vmem] * 3, out_specs=vmem, out_shap...  1.39 us
    ppermute x1, waiting for transfers between devices, body(): far = lax.ppermute(near, 'sub', [(0, 1), (1, 0)])  1.35 us
    unnamed x8, local copies, waits for them, and re-layouts  0.91 us
  transfers between devices with their start and end apart: 5, of which 2 were waited for; matrix products, arithmetic and copies ran while one was open for 1% of the time, Pallas kernels for 19%

profile of v3, /device:TPU:0, one launch (start us, length us, event | category | flops | bytes accessed | tf_op | source)
XLA Modules:
  0.0 29.0 jit_solution(14023204804782755490)
XLA Ops:
  0.0 1.4 %pack.1 = bf16[4,5120]{1,0:T(4,128)(2,1)} custom-call(bf16[4,4096]{1,0:T(4,128)(2,1)} %queries_ref.1, bf16[4,512]{1,0:T(4,128)(2,1)} %keys_ref.2, bf16[4,512]{1,0:T(4,128)(2,1)} %values_ref.2), custom_call_target="tpu_custom_call" | custom-call | tf_op jit(solution)/shard_map/pack/pallas_call | solution.py:31
  1.4 5.0 %collective-permute-start.2 = (bf16[4,5120]{1,0:T(4,128)(2,1)}, bf16[4,5120]{1,0:T(4,128)(2,1)S(1)}, u32[]{:S(2)}, u32[]{:S(2)}) collective-permute-start(bf16[4,5120]{1,0:T(4,128)(2,1)} %pack.1), channel_id=1, source_target_pairs={{0,12},{4,0},{8,4},{12,8},{1,13},{5,1},{9,5},{13,9},{2,14},{6,2},{... | collective-permute-start | bytes 122888 | tf_op jit(solution)/shard_map/ppermute | solution.py:232
  6.4 0.0 collective-permute-start.1
  6.4 1.0 %collective-permute-start = (bf16[4,5120]{1,0:T(4,128)(2,1)}, bf16[4,5120]{1,0:T(4,128)(2,1)S(1)}, u32[]{:S(2)}, u32[]{:S(2)}) collective-permute-start(bf16[4,5120]{1,0:T(4,128)(2,1)} %pack.1), channel_id=1, source_target_pairs={{0,4},{4,8},{8,12},{12,0},{1,5},{5,9},{9,13},{13,1},{2,6},{6,10},{... | collective-permute-start | bytes 122888 | tf_op jit(solution)/shard_map/ppermute | solution.py:232
  8.1 0.0 copy-start
  8.1 0.9 %copy-done = bf16[4,128,128]{2,1,0:T(8,128)(2,1)S(1)} copy-done((bf16[4,128,128]{2,1,0:T(8,128)(2,1)S(1)}, bf16[4,128,128]{2,1,0:T(8,128)(2,1)}, u32[]{:S(2)}) %copy-start) | copy-done | bytes 131096
  9.0 0.0 copy-start.3
  9.0 0.0 copy-start.2
  9.0 0.0 copy-start.1
  9.0 5.5 %prefill.1.near_ref = bf16[1168,128]{1,0:T(8,128)(2,1)S(1)} custom-call(s32[1]{0:T(128)S(6)} %copy.9.lengths_ref, bf16[1,4096,512]{2,1,0:T(8,128)(2,1)} %keys_ref.3, bf16[1,4096,512]{2,1,0:T(8,128)(2,1)} %values_ref.3, bf16[4,128,128]{2,1,0:T(8,128)(2,1)S(1)} %copy-done), custom_call_target="tpu_custom_call" | custom-call | flops 1073741824 | bytes 8388608 | tf_op jit(solution)/shard_map/prefill/pallas_call | solution.py:130
  14.5 0.1 collective-permute-start.3
  14.6 0.0 copy-done.3
  14.6 0.1 broadcast_compare_fusion.3
  14.7 0.0 collective-permute-done.2
  14.7 0.0 collective-permute-done.1
  14.7 0.0 collective-permute-done
  14.7 0.0 copy-done.2
  14.7 0.1 pad_maximum_fusion.rows_ref
  14.8 1.3 %collective-permute-done.3.far_ref = bf16[1168,128]{1,0:T(8,128)(2,1)S(1)} collective-permute-done((bf16[1168,128]{1,0:T(8,128)(2,1)S(1)}, bf16[1168,128]{1,0:T(8,128)(2,1)S(1)}, u32[]{:S(2)}, u32[]{:S(2)}) %collective-permute-start.3) | collective-permute-done | bytes 299040 | tf_op jit(solution)/shard_map/ppermute | solution.py:235
  16.2 0.0 copy-done.1
  16.2 1.8 %decode.1 = bf16[4,4,4096]{2,1,0:T(4,128)(2,1)} custom-call(bf16[16,5120]{1,0:T(8,128)(2,1)S(1)} %pad_maximum_fusion.rows_ref, bf16[4,128,128]{2,1,0:T(8,128)(2,1)S(1)} %copy-done.1, bf16[1168,128]{1,0:T(8,128)(2,1)S(1)} %prefill.1.near_ref, bf16[1168,128]{1,0:T(8,128)(2,1)S(1)} %collective-permute-done.3.far_ref), custom_call_target="tpu_custom_call" | custom-call | flops 83886080 | bytes 262144 | tf_op jit(solution)/shard_map/decode/pallas_call | solution.py:212
  17.9 4.1 %all-to-all-start = ((bf16[4,4,4096]{2,1,0:T(4,128)(2,1)}), bf16[4,4,4096]{2,1,0:T(4,128)(2,1)S(1)}, u32[]{:S(2)}, u32[]{:S(2)}) async-start(bf16[4,4,4096]{2,1,0:T(4,128)(2,1)} %decode.1), calls=%async_computation | async-start | bytes 262144 | tf_op jit(solution)/shard_map/all_to_all | solution.py:241
  22.0 6.2 %all-to-all-done = bf16[4,4,4096]{2,1,0:T(4,128)(2,1)S(1)} async-done(((bf16[4,4,4096]{2,1,0:T(4,128)(2,1)}), bf16[4,4,4096]{2,1,0:T(4,128)(2,1)S(1)}, u32[]{:S(2)}, u32[]{:S(2)}) %all-to-all-start) | async-done | bytes 131104 | tf_op jit(solution)/shard_map/all_to_all | solution.py:241
  28.2 0.7 %fusion.3 = bf16[4,4096]{1,0:T(4,128)(2,1)} fusion(bf16[4,4,4096]{2,1,0:T(4,128)(2,1)S(1)} %all-to-all-done, pred[4]{0:T(512)(128)(4,1)S(1)} %get-tuple-element.9, pred[4]{0:T(512)(128)(4,1)S(1)} %get-tuple-element.8, pred[4]{0:T(512)(128)(4,1)S(1)} %get-tuple-element.7, pred[4]{0:T(512)(128)(4,1)S(1)} %get-tuple-element.5), kind=kLoop, calls=%fused_computation.5 | loop fusion | flops 65536 | bytes 163856 | tf_op jit(solution)/shard_map/jit(_where)/select_n | solution.py:244
  (1 shorter events, 0.0 us)
Async XLA Ops:
  1.4 13.3 %collective-permute-start.2 = (bf16[4,5120]{1,0:T(4,128)(2,1)}, bf16[4,5120]{1,0:T(4,128)(2,1)S(1)}, u32[]{:S(2)}, u32[]{:S(2)}) collective-permute-start(bf16[4,5120]{1,0:T(4,128)(2,1)} %pack.1), channel_id=1, source_target_pairs={{0,12},{4,0},{8,4},{12,8},{1,13},{5,1},{9,5},{13,9},{2,14},{6,2},{... | collective-permute-start | bytes 122888 | tf_op jit(solution)/shard_map/ppermute | solution.py:232
  6.4 8.2 %collective-permute-start.1 = (bf16[4,5120]{1,0:T(4,128)(2,1)}, bf16[4,5120]{1,0:T(4,128)(2,1)S(1)}, u32[]{:S(2)}, u32[]{:S(2)}) collective-permute-start(bf16[4,5120]{1,0:T(4,128)(2,1)} %pack.1), channel_id=1, source_target_pairs={{0,8},{4,12},{8,0},{12,4},{1,9},{5,13},{9,1},{13,5},{2,10},{6,14},... | collective-permute-start | bytes 122888 | tf_op jit(solution)/shard_map/ppermute | solution.py:232
  6.4 8.2 %collective-permute-start = (bf16[4,5120]{1,0:T(4,128)(2,1)}, bf16[4,5120]{1,0:T(4,128)(2,1)S(1)}, u32[]{:S(2)}, u32[]{:S(2)}) collective-permute-start(bf16[4,5120]{1,0:T(4,128)(2,1)} %pack.1), channel_id=1, source_target_pairs={{0,4},{4,8},{8,12},{12,0},{1,5},{5,9},{9,13},{13,1},{2,6},{6,10},{... | collective-permute-start | bytes 122888 | tf_op jit(solution)/shard_map/ppermute | solution.py:232
  8.1 0.9 %copy-start = (bf16[4,128,128]{2,1,0:T(8,128)(2,1)S(1)}, bf16[4,128,128]{2,1,0:T(8,128)(2,1)}, u32[]{:S(2)}) copy-start(bf16[4,128,128]{2,1,0:T(8,128)(2,1)} %weight_ref.3) | copy-start | bytes 393220
  9.0 5.6 %copy-start.3 = (s32[32]{0:T(128)S(1)}, s32[32]{0:T(128)}, u32[]{:S(2)}) copy-start(s32[32]{0:T(128)} %param.15) | copy-start | bytes 388
  9.0 5.7 %copy-start.2 = (bf16[4,5120]{1,0:T(4,128)(2,1)S(1)}, bf16[4,5120]{1,0:T(4,128)(2,1)}, u32[]{:S(2)}) copy-start(bf16[4,5120]{1,0:T(4,128)(2,1)} %pack.1) | copy-start | bytes 122884
  9.0 7.1 %copy-start.1 = (bf16[4,128,128]{2,1,0:T(8,128)(2,1)S(1)}, bf16[4,128,128]{2,1,0:T(8,128)(2,1)}, u32[]{:S(2)}) copy-start(bf16[4,128,128]{2,1,0:T(8,128)(2,1)} %weight_ref.3) | copy-start | bytes 393220
  14.5 1.7 %collective-permute-start.3 = (bf16[1168,128]{1,0:T(8,128)(2,1)S(1)}, bf16[1168,128]{1,0:T(8,128)(2,1)S(1)}, u32[]{:S(2)}, u32[]{:S(2)}) collective-permute-start(bf16[1168,128]{1,0:T(8,128)(2,1)S(1)} %prefill.1.near_ref), channel_id=1, source_target_pairs={{0,1},{1,0},{2,3},{3,2},{4,5},{5,4},{6,7},{7,6},{8,9},{9,8},{10,11... | collective-permute-start | bytes 897032 | tf_op jit(solution)/shard_map/ppermute | solution.py:235
  17.9 10.3 %all-to-all-start = ((bf16[4,4,4096]{2,1,0:T(4,128)(2,1)}), bf16[4,4,4096]{2,1,0:T(4,128)(2,1)S(1)}, u32[]{:S(2)}, u32[]{:S(2)}) async-start(bf16[4,4,4096]{2,1,0:T(4,128)(2,1)} %decode.1), calls=%async_computation | async-start | bytes 262144 | tf_op jit(solution)/shard_map/all_to_all | solution.py:241

commit v4 on v2

--- a/solution.py
+++ b/solution.py
@@ -226,22 +226,25 @@
 ):
     sub = lax.axis_index("sub")
     sect = lax.axis_index("sect")
+    up = [[(i, i + k) for i in range(sects - k)] for k in range(sects)]
+    down = [[(i + k, i) for i in range(sects - k)] for k in range(sects)]
     mine = pack(queries, new_keys, new_values)
-    blocks = [mine] + [
-        lax.ppermute(mine, "sect", [(i, (i + k) % sects) for i in range(sects)]) for k in range(1, sects)
-    ]
+    risen = {k: lax.ppermute(mine, "sect", up[k]) for k in range(sects - 1, 0, -1)}
     near = prefill(prompt_keys, prompt_values, feature_weight, lengths)
     far = lax.ppermute(near, "sub", [(0, 1), (1, 0)])
+    later, near = lax.optimization_barrier((mine, near))
+    sunk = {k: lax.ppermute(later, "sect", down[k]) for k in range(sects - 1, 0, -1)}
+    blocks = [mine] + [jnp.where(sect >= k, risen[k], sunk[sects - k]) for k in range(1, sects)]
     results = decode(jnp.concatenate(blocks, axis=0), feature_weight, near, far, sects)
 
     count = queries.shape[0]
     first_row = (sect * lax.axis_size("sub") + sub) * count
-    prompts = lax.dynamic_slice_in_dim(row_prompt, first_row, count, 0)
-    out = jnp.zeros_like(queries)
-    for k, result in enumerate(results):
-        if k > 0:
-            result = lax.ppermute(result, "sect", [(i, (i - k) % sects) for i in range(sects)])
-        out = jnp.where((prompts == (sect + k) % sects)[:, None], result, out)
+    prompts = lax.dynamic_slice_in_dim(row_prompt, first_row, count, 0)[:, None]
+    out = results[0]
+    for k in range(sects - 1, 0, -1):
+        out = jnp.where(prompts == sect + k, lax.ppermute(results[k], "sect", down[k]), out)
+    for k in range(sects - 1, 0, -1):
+        out = jnp.where(prompts == sect - k, lax.ppermute(results[sects - k], "sect", up[k]), out)
     return out
 
 

time: 25.9 us -> 50.3 us (1.94)
  starting transfers between devices: 11.1 us -> 26 us
  waiting for transfers between devices: 4.06 us -> 13 us
    ppermute x6 -> x12, starting transfers between devices: 11 us -> 25.9 us  [the longest x3 12.8 us: body(): lax.ppermute(mine, 'sect', up[k])]
    ppermute x6 -> x12, waiting for transfers between devices: 2.72 us -> 13 us  [the longest x3 6.81 us: body(): lax.ppermute(results[k], 'sect', down[k])]
    ppermute x1, waiting for transfers between devices: 1.34 us -> 0.01 us  [body(): far = lax.ppermute(near, 'sub', [(0, 1), (1, 0)])]
  transfers between devices with their start and end apart: 7 -> 13, of which waited for: 4 -> 4; matrix products, arithmetic and copies ran while one was open for 1% -> 1% of each run, Pallas kernels for 21% -> 11%
where the time goes in v4:
time: 50.3 us; the launch traced here: 49.9 us
  starting transfers between devices  26 us (52%)
  waiting for transfers between devices  13 us (26%)
  Pallas kernels  8.01 us (16%)
  other arithmetic  1.01 us (2%)
  between operations  0.92 us (2%)
  local copies, waits for them, and re-layouts  0.91 us (2%)
    ppermute x3, starting transfers between devices, body(): lax.ppermute(mine, 'sect', up[k])  12.8 us
    ppermute x3, waiting for transfers between devices, body(): lax.ppermute(results[k], 'sect', down[k])  6.81 us
    ppermute x3, waiting for transfers between devices, body(): lax.ppermute(later, 'sect', down[k])  6.07 us
    pallas_call x1, Pallas kernels, prefill(): pl.pallas_call(prefill_kernel, in_specs=[pl.BlockSpec(memory_space=pltpu....  5.48 us
    ppermute x3, starting transfers between devices, body(): lax.ppermute(results[sects - k], 'sect', up[k])  5.36 us
    ppermute x3, starting transfers between devices, body(): lax.ppermute(results[k], 'sect', down[k])  3.88 us
    ppermute x3, starting transfers between devices, body(): lax.ppermute(later, 'sect', down[k])  3.88 us
    pallas_call x1, Pallas kernels, pack(): pl.pallas_call(pack_kernel, in_specs=[vmem] * 3, out_specs=vmem, out_shap...  1.39 us
  transfers between devices with their start and end apart: 13, of which 4 were waited for; matrix products, arithmetic and copies ran while one was open for 1% of the time, Pallas kernels for 11%

profile of v4, /device:TPU:0, one launch (start us, length us, event | category | flops | bytes accessed | tf_op | source)
XLA Modules:
  0.0 49.9 jit_solution(15879064561101236053)
XLA Ops:
  0.0 1.4 %pack.1 = bf16[4,5120]{1,0:T(4,128)(2,1)} custom-call(bf16[4,4096]{1,0:T(4,128)(2,1)} %queries_ref.1, bf16[4,512]{1,0:T(4,128)(2,1)} %keys_ref.2, bf16[4,512]{1,0:T(4,128)(2,1)} %values_ref.2), custom_call_target="tpu_custom_call" | custom-call | tf_op jit(solution)/shard_map/pack/pallas_call | solution.py:31
  1.4 6.9 %collective-permute-start.4 = (bf16[4,5120]{1,0:T(4,128)(2,1)}, bf16[4,5120]{1,0:T(4,128)(2,1)S(1)}, u32[]{:S(2)}, u32[]{:S(2)}) collective-permute-start(bf16[4,5120]{1,0:T(4,128)(2,1)} %pack.1), channel_id=1, source_target_pairs={{0,12},{1,13},{2,14},{3,15},{16,28},{17,29},{18,30},{19,31}} | collective-permute-start | bytes 122888 | tf_op jit(solution)/shard_map/ppermute | solution.py:232
  9.0 0.0 copy-start
  9.0 0.9 %copy-done = bf16[4,128,128]{2,1,0:T(8,128)(2,1)S(1)} copy-done((bf16[4,128,128]{2,1,0:T(8,128)(2,1)S(1)}, bf16[4,128,128]{2,1,0:T(8,128)(2,1)}, u32[]{:S(2)}) %copy-start) | copy-done | bytes 131096
  9.9 0.0 copy-start.2
  9.9 0.0 copy-start.1
  9.9 0.0 copy-start.3
  9.9 5.5 %prefill.1.near_ref = bf16[1168,128]{1,0:T(8,128)(2,1)S(1)} custom-call(s32[1]{0:T(128)S(6)} %copy.9.lengths_ref, bf16[1,4096,512]{2,1,0:T(8,128)(2,1)} %keys_ref.3, bf16[1,4096,512]{2,1,0:T(8,128)(2,1)} %values_ref.3, bf16[4,128,128]{2,1,0:T(8,128)(2,1)S(1)} %copy-done), custom_call_target="tpu_custom_call" | custom-call | flops 1073741824 | bytes 8388608 | tf_op jit(solution)/shard_map/prefill/pallas_call | solution.py:130
  15.4 0.0 copy-done.2
  15.4 1.3 %collective-permute-start.5 = (bf16[4,5120]{1,0:T(4,128)(2,1)S(1)}, bf16[4,5120]{1,0:T(4,128)(2,1)S(1)}, u32[]{:S(2)}, u32[]{:S(2)}) collective-permute-start(bf16[4,5120]{1,0:T(4,128)(2,1)S(1)} %copy-done.2), channel_id=1, source_target_pairs={{4,0},{8,4},{12,8},{5,1},{9,5},{13,9},{6,2},{10,6},{14,10},{7,3},{... | collective-permute-start | bytes 122888 | tf_op jit(solution)/shard_map/ppermute | solution.py:236
  16.7 1.3 %collective-permute-start.2 = (bf16[4,5120]{1,0:T(4,128)(2,1)S(1)}, bf16[4,5120]{1,0:T(4,128)(2,1)S(1)}, u32[]{:S(2)}, u32[]{:S(2)}) collective-permute-start(bf16[4,5120]{1,0:T(4,128)(2,1)S(1)} %copy-done.2), channel_id=1, source_target_pairs={{0,8},{4,12},{1,9},{5,13},{2,10},{6,14},{3,11},{7,15},{16,24},{20,... | collective-permute-start | bytes 122888 | tf_op jit(solution)/shard_map/ppermute | solution.py:232
  18.0 1.3 %collective-permute-start.3 = (bf16[4,5120]{1,0:T(4,128)(2,1)S(1)}, bf16[4,5120]{1,0:T(4,128)(2,1)S(1)}, u32[]{:S(2)}, u32[]{:S(2)}) collective-permute-start(bf16[4,5120]{1,0:T(4,128)(2,1)S(1)} %copy-done.2), channel_id=1, source_target_pairs={{8,0},{12,4},{9,1},{13,5},{10,2},{14,6},{11,3},{15,7},{24,16},{28,... | collective-permute-start | bytes 122888 | tf_op jit(solution)/shard_map/ppermute | solution.py:236
  19.3 4.5 %collective-permute-start = (bf16[4,5120]{1,0:T(4,128)(2,1)S(1)}, bf16[4,5120]{1,0:T(4,128)(2,1)S(1)}, u32[]{:S(2)}, u32[]{:S(2)}) collective-permute-start(bf16[4,5120]{1,0:T(4,128)(2,1)S(1)} %copy-done.2), channel_id=1, source_target_pairs={{0,4},{4,8},{8,12},{1,5},{5,9},{9,13},{2,6},{6,10},{10,14},{3,7},{... | collective-permute-start | bytes 122888 | tf_op jit(solution)/shard_map/ppermute | solution.py:232
  23.9 0.0 collective-permute-done.4
  23.9 1.3 %collective-permute-start.1 = (bf16[4,5120]{1,0:T(4,128)(2,1)S(1)}, bf16[4,5120]{1,0:T(4,128)(2,1)S(1)}, u32[]{:S(2)}, u32[]{:S(2)}) collective-permute-start(bf16[4,5120]{1,0:T(4,128)(2,1)S(1)} %copy-done.2), channel_id=1, source_target_pairs={{12,0},{13,1},{14,2},{15,3},{28,16},{29,17},{30,18},{31,19}} | collective-permute-start | bytes 122888 | tf_op jit(solution)/shard_map/ppermute | solution.py:236
  25.2 0.0 collective-permute-done.5
  25.2 0.1 collective-permute-start.6
  25.3 0.0 collective-permute-done.2
  25.3 0.0 collective-permute-done.3
  25.4 0.2 collective-permute-done
  25.5 6.1 %collective-permute-done.1 = bf16[4,5120]{1,0:T(4,128)(2,1)S(1)} collective-permute-done((bf16[4,5120]{1,0:T(4,128)(2,1)S(1)}, bf16[4,5120]{1,0:T(4,128)(2,1)S(1)}, u32[]{:S(2)}, u32[]{:S(2)}) %collective-permute-start.1) | collective-permute-done | bytes 40992 | tf_op jit(solution)/shard_map/ppermute | solution.py:236
  31.6 0.1 pad_maximum_fusion.rows_ref
  31.7 0.0 collective-permute-done.6.far_ref
  31.7 0.0 copy-done.1
  31.7 1.1 %decode.1 = (bf16[4,4096]{1,0:T(4,128)(2,1)S(1)}, bf16[4,4096]{1,0:T(4,128)(2,1)S(1)}, bf16[4,4096]{1,0:T(4,128)(2,1)S(1)}, bf16[4,4096]{1,0:T(4,128)(2,1)S(1)}) custom-call(bf16[16,5120]{1,0:T(8,128)(2,1)S(1)} %pad_maximum_fusion.rows_ref, bf16[4,128,128]{2,1,0:T(8,128)(2,1)S(1)} %copy-done.1, bf16[1168,128]{1,0:T(8,128)(2,1)S(1)} %prefill.1.near_ref, ...), custom_call_target="tpu_custom_call" | custom-call | flops 83886080 | bytes 262144 | tf_op jit(solution)/shard_map/decode/pallas_call | solution.py:211
  32.9 1.3 %collective-permute-start.7 = (bf16[4,4096]{1,0:T(4,128)(2,1)S(1)}, bf16[4,4096]{1,0:T(4,128)(2,1)S(1)}, u32[]{:S(2)}, u32[]{:S(2)}) collective-permute-start(bf16[4,4096]{1,0:T(4,128)(2,1)S(1)} %get-tuple-element.13), channel_id=1, source_target_pairs={{0,4},{4,8},{8,12},{1,5},{5,9},{9,13},{2,6},{6,10},{10,14},{3,7},{... | collective-permute-start | bytes 98312 | tf_op jit(solution)/shard_map/ppermute | solution.py:247
  34.2 0.0 copy-done.3
  34.2 0.1 broadcast_compare_fusion.5
  34.3 1.6 %collective-permute-start.9 = (bf16[4,4096]{1,0:T(4,128)(2,1)S(1)}, bf16[4,4096]{1,0:T(4,128)(2,1)S(1)}, u32[]{:S(2)}, u32[]{:S(2)}) collective-permute-start(bf16[4,4096]{1,0:T(4,128)(2,1)S(1)} %get-tuple-element.15), channel_id=1, source_target_pairs={{0,12},{1,13},{2,14},{3,15},{16,28},{17,29},{18,30},{19,31}} | collective-permute-start | bytes 98312 | tf_op jit(solution)/shard_map/ppermute | solution.py:247
  35.9 1.3 %collective-permute-start.10 = (bf16[4,4096]{1,0:T(4,128)(2,1)S(1)}, bf16[4,4096]{1,0:T(4,128)(2,1)S(1)}, u32[]{:S(2)}, u32[]{:S(2)}) collective-permute-start(bf16[4,4096]{1,0:T(4,128)(2,1)S(1)} %get-tuple-element.15), channel_id=1, source_target_pairs={{4,0},{8,4},{12,8},{5,1},{9,5},{13,9},{6,2},{10,6},{14,10},{7,3},{... | collective-permute-start | bytes 98312 | tf_op jit(solution)/shard_map/ppermute | solution.py:245
  37.2 2.5 %collective-permute-start.8 = (bf16[4,4096]{1,0:T(4,128)(2,1)S(1)}, bf16[4,4096]{1,0:T(4,128)(2,1)S(1)}, u32[]{:S(2)}, u32[]{:S(2)}) collective-permute-start(bf16[4,4096]{1,0:T(4,128)(2,1)S(1)} %get-tuple-element.14), channel_id=1, source_target_pairs={{0,8},{4,12},{1,9},{5,13},{2,10},{6,14},{3,11},{7,15},{16,24},{20,... | collective-permute-start | bytes 98312 | tf_op jit(solution)/shard_map/ppermute | solution.py:247
  39.7 1.3 %collective-permute-start.11 = (bf16[4,4096]{1,0:T(4,128)(2,1)S(1)}, bf16[4,4096]{1,0:T(4,128)(2,1)S(1)}, u32[]{:S(2)}, u32[]{:S(2)}) collective-permute-start(bf16[4,4096]{1,0:T(4,128)(2,1)S(1)} %get-tuple-element.14), channel_id=1, source_target_pairs={{8,0},{12,4},{9,1},{13,5},{10,2},{14,6},{11,3},{15,7},{24,16},{28,... | collective-permute-start | bytes 98312 | tf_op jit(solution)/shard_map/ppermute | solution.py:245
  41.0 0.0 collective-permute-done.7
  41.0 1.3 %collective-permute-start.12 = (bf16[4,4096]{1,0:T(4,128)(2,1)S(1)}, bf16[4,4096]{1,0:T(4,128)(2,1)S(1)}, u32[]{:S(2)}, u32[]{:S(2)}) collective-permute-start(bf16[4,4096]{1,0:T(4,128)(2,1)S(1)} %get-tuple-element.13), channel_id=1, source_target_pairs={{12,0},{13,1},{14,2},{15,3},{28,16},{29,17},{30,18},{31,19}} | collective-permute-start | bytes 98312 | tf_op jit(solution)/shard_map/ppermute | solution.py:245
  42.3 0.0 collective-permute-done.8
  42.3 0.0 collective-permute-done.9
  42.3 0.0 collective-permute-done.10
  42.3 4.0 %collective-permute-done.11 = bf16[4,4096]{1,0:T(4,128)(2,1)S(1)} collective-permute-done((bf16[4,4096]{1,0:T(4,128)(2,1)S(1)}, bf16[4,4096]{1,0:T(4,128)(2,1)S(1)}, u32[]{:S(2)}, u32[]{:S(2)}) %collective-permute-start.11) | collective-permute-done | bytes 32800 | tf_op jit(solution)/shard_map/ppermute | solution.py:245
  46.4 2.8 %collective-permute-done.12 = bf16[4,4096]{1,0:T(4,128)(2,1)S(1)} collective-permute-done((bf16[4,4096]{1,0:T(4,128)(2,1)S(1)}, bf16[4,4096]{1,0:T(4,128)(2,1)S(1)}, u32[]{:S(2)}, u32[]{:S(2)}) %collective-permute-start.12) | collective-permute-done | bytes 32800 | tf_op jit(solution)/shard_map/ppermute | solution.py:245
  49.1 0.7 %select_select_fusion = bf16[4,4096]{1,0:T(4,128)(2,1)} fusion(bf16[4,4096]{1,0:T(4,128)(2,1)S(1)} %collective-permute-done.7, bf16[4,4096]{1,0:T(4,128)(2,1)S(1)} %collective-permute-done.8, bf16[4,4096]{1,0:T(4,128)(2,1)S(1)} %collective-permute-done.9, bf16[4,4096]{1,0:T(4,128)(2,1)S(1)} %collective-permute-done.10, ...), kind=kLoop, calls=%fused_computation.4 | loop fusion | flops 98304 | bytes 262168 | tf_op jit(solution)/shard_map/jit(_where)/select_n | solution.py:247
  (4 shorter events, 0.1 us)
Async XLA Ops:
  1.4 22.5 %collective-permute-start.4 = (bf16[4,5120]{1,0:T(4,128)(2,1)}, bf16[4,5120]{1,0:T(4,128)(2,1)S(1)}, u32[]{:S(2)}, u32[]{:S(2)}) collective-permute-start(bf16[4,5120]{1,0:T(4,128)(2,1)} %pack.1), channel_id=1, source_target_pairs={{0,12},{1,13},{2,14},{3,15},{16,28},{17,29},{18,30},{19,31}} | collective-permute-start | bytes 122888 | tf_op jit(solution)/shard_map/ppermute | solution.py:232
  9.0 0.9 %copy-start = (bf16[4,128,128]{2,1,0:T(8,128)(2,1)S(1)}, bf16[4,128,128]{2,1,0:T(8,128)(2,1)}, u32[]{:S(2)}) copy-start(bf16[4,128,128]{2,1,0:T(8,128)(2,1)} %weight_ref.3) | copy-start | bytes 393220
  9.9 5.5 %copy-start.2 = (bf16[4,5120]{1,0:T(4,128)(2,1)S(1)}, bf16[4,5120]{1,0:T(4,128)(2,1)}, u32[]{:S(2)}) copy-start(bf16[4,5120]{1,0:T(4,128)(2,1)} %pack.1) | copy-start | bytes 122884
  9.9 21.8 %copy-start.1 = (bf16[4,128,128]{2,1,0:T(8,128)(2,1)S(1)}, bf16[4,128,128]{2,1,0:T(8,128)(2,1)}, u32[]{:S(2)}) copy-start(bf16[4,128,128]{2,1,0:T(8,128)(2,1)} %weight_ref.3) | copy-start | bytes 393220
  9.9 24.3 %copy-start.3 = (s32[32]{0:T(128)S(1)}, s32[32]{0:T(128)}, u32[]{:S(2)}) copy-start(s32[32]{0:T(128)} %param.15) | copy-start | bytes 388
  15.4 9.8 %collective-permute-start.5 = (bf16[4,5120]{1,0:T(4,128)(2,1)S(1)}, bf16[4,5120]{1,0:T(4,128)(2,1)S(1)}, u32[]{:S(2)}, u32[]{:S(2)}) collective-permute-start(bf16[4,5120]{1,0:T(4,128)(2,1)S(1)} %copy-done.2), channel_id=1, source_target_pairs={{4,0},{8,4},{12,8},{5,1},{9,5},{13,9},{6,2},{10,6},{14,10},{7,3},{... | collective-permute-start | bytes 122888 | tf_op jit(solution)/shard_map/ppermute | solution.py:236
  16.7 8.6 %collective-permute-start.2 = (bf16[4,5120]{1,0:T(4,128)(2,1)S(1)}, bf16[4,5120]{1,0:T(4,128)(2,1)S(1)}, u32[]{:S(2)}, u32[]{:S(2)}) collective-permute-start(bf16[4,5120]{1,0:T(4,128)(2,1)S(1)} %copy-done.2), channel_id=1, source_target_pairs={{0,8},{4,12},{1,9},{5,13},{2,10},{6,14},{3,11},{7,15},{16,24},{20,... | collective-permute-start | bytes 122888 | tf_op jit(solution)/shard_map/ppermute | solution.py:232
  18.0 7.3 %collective-permute-start.3 = (bf16[4,5120]{1,0:T(4,128)(2,1)S(1)}, bf16[4,5120]{1,0:T(4,128)(2,1)S(1)}, u32[]{:S(2)}, u32[]{:S(2)}) collective-permute-start(bf16[4,5120]{1,0:T(4,128)(2,1)S(1)} %copy-done.2), channel_id=1, source_target_pairs={{8,0},{12,4},{9,1},{13,5},{10,2},{14,6},{11,3},{15,7},{24,16},{28,... | collective-permute-start | bytes 122888 | tf_op jit(solution)/shard_map/ppermute | solution.py:236
  19.3 6.2 %collective-permute-start = (bf16[4,5120]{1,0:T(4,128)(2,1)S(1)}, bf16[4,5120]{1,0:T(4,128)(2,1)S(1)}, u32[]{:S(2)}, u32[]{:S(2)}) collective-permute-start(bf16[4,5120]{1,0:T(4,128)(2,1)S(1)} %copy-done.2), channel_id=1, source_target_pairs={{0,4},{4,8},{8,12},{1,5},{5,9},{9,13},{2,6},{6,10},{10,14},{3,7},{... | collective-permute-start | bytes 122888 | tf_op jit(solution)/shard_map/ppermute | solution.py:232
  23.9 7.7 %collective-permute-start.1 = (bf16[4,5120]{1,0:T(4,128)(2,1)S(1)}, bf16[4,5120]{1,0:T(4,128)(2,1)S(1)}, u32[]{:S(2)}, u32[]{:S(2)}) collective-permute-start(bf16[4,5120]{1,0:T(4,128)(2,1)S(1)} %copy-done.2), channel_id=1, source_target_pairs={{12,0},{13,1},{14,2},{15,3},{28,16},{29,17},{30,18},{31,19}} | collective-permute-start | bytes 122888 | tf_op jit(solution)/shard_map/ppermute | solution.py:236
  25.2 6.5 %collective-permute-start.6 = (bf16[1168,128]{1,0:T(8,128)(2,1)S(1)}, bf16[1168,128]{1,0:T(8,128)(2,1)S(1)}, u32[]{:S(2)}, u32[]{:S(2)}) collective-permute-start(bf16[1168,128]{1,0:T(8,128)(2,1)S(1)} %prefill.1.near_ref), channel_id=1, source_target_pairs={{0,1},{1,0},{2,3},{3,2},{4,5},{5,4},{6,7},{7,6},{8,9},{9,8},{10,11... | collective-permute-start | bytes 897032 | tf_op jit(solution)/shard_map/ppermute | solution.py:234
  32.9 8.1 %collective-permute-start.7 = (bf16[4,4096]{1,0:T(4,128)(2,1)S(1)}, bf16[4,4096]{1,0:T(4,128)(2,1)S(1)}, u32[]{:S(2)}, u32[]{:S(2)}) collective-permute-start(bf16[4,4096]{1,0:T(4,128)(2,1)S(1)} %get-tuple-element.13), channel_id=1, source_target_pairs={{0,4},{4,8},{8,12},{1,5},{5,9},{9,13},{2,6},{6,10},{10,14},{3,7},{... | collective-permute-start | bytes 98312 | tf_op jit(solution)/shard_map/ppermute | solution.py:247
  34.3 8.0 %collective-permute-start.9 = (bf16[4,4096]{1,0:T(4,128)(2,1)S(1)}, bf16[4,4096]{1,0:T(4,128)(2,1)S(1)}, u32[]{:S(2)}, u32[]{:S(2)}) collective-permute-start(bf16[4,4096]{1,0:T(4,128)(2,1)S(1)} %get-tuple-element.15), channel_id=1, source_target_pairs={{0,12},{1,13},{2,14},{3,15},{16,28},{17,29},{18,30},{19,31}} | collective-permute-start | bytes 98312 | tf_op jit(solution)/shard_map/ppermute | solution.py:247
  35.9 6.4 %collective-permute-start.10 = (bf16[4,4096]{1,0:T(4,128)(2,1)S(1)}, bf16[4,4096]{1,0:T(4,128)(2,1)S(1)}, u32[]{:S(2)}, u32[]{:S(2)}) collective-permute-start(bf16[4,4096]{1,0:T(4,128)(2,1)S(1)} %get-tuple-element.15), channel_id=1, source_target_pairs={{4,0},{8,4},{12,8},{5,1},{9,5},{13,9},{6,2},{10,6},{14,10},{7,3},{... | collective-permute-start | bytes 98312 | tf_op jit(solution)/shard_map/ppermute | solution.py:245
  37.2 5.1 %collective-permute-start.8 = (bf16[4,4096]{1,0:T(4,128)(2,1)S(1)}, bf16[4,4096]{1,0:T(4,128)(2,1)S(1)}, u32[]{:S(2)}, u32[]{:S(2)}) collective-permute-start(bf16[4,4096]{1,0:T(4,128)(2,1)S(1)} %get-tuple-element.14), channel_id=1, source_target_pairs={{0,8},{4,12},{1,9},{5,13},{2,10},{6,14},{3,11},{7,15},{16,24},{20,... | collective-permute-start | bytes 98312 | tf_op jit(solution)/shard_map/ppermute | solution.py:247
  39.7 6.7 %collective-permute-start.11 = (bf16[4,4096]{1,0:T(4,128)(2,1)S(1)}, bf16[4,4096]{1,0:T(4,128)(2,1)S(1)}, u32[]{:S(2)}, u32[]{:S(2)}) collective-permute-start(bf16[4,4096]{1,0:T(4,128)(2,1)S(1)} %get-tuple-element.14), channel_id=1, source_target_pairs={{8,0},{12,4},{9,1},{13,5},{10,2},{14,6},{11,3},{15,7},{24,16},{28,... | collective-permute-start | bytes 98312 | tf_op jit(solution)/shard_map/ppermute | solution.py:245
  41.0 8.2 %collective-permute-start.12 = (bf16[4,4096]{1,0:T(4,128)(2,1)S(1)}, bf16[4,4096]{1,0:T(4,128)(2,1)S(1)}, u32[]{:S(2)}, u32[]{:S(2)}) collective-permute-start(bf16[4,4096]{1,0:T(4,128)(2,1)S(1)} %get-tuple-element.13), channel_id=1, source_target_pairs={{12,0},{13,1},{14,2},{15,3},{28,16},{29,17},{30,18},{31,19}} | collective-permute-start | bytes 98312 | tf_op jit(solution)/shard_map/ppermute | solution.py:245

commit v5 on v2

--- a/solution.py
+++ b/solution.py
@@ -18,32 +18,14 @@
     return jnp.maximum(proj, 0.0) + jnp.exp(jnp.minimum(proj, 0.0))
 
 
-def pack_kernel(queries_ref, keys_ref, values_ref, out_ref):
-    width, each = queries_ref.shape[1], keys_ref.shape[1]
-    out_ref[:, :width] = queries_ref[...]
-    out_ref[:, width : width + each] = keys_ref[...]
-    out_ref[:, width + each :] = values_ref[...]
-
-
-def pack(queries, new_keys, new_values):
-    vmem = pl.BlockSpec(memory_space=pltpu.VMEM)
-    width = queries.shape[1] + 2 * new_keys.shape[1]
-    return pl.pallas_call(
-        pack_kernel,
-        in_specs=[vmem] * 3,
-        out_specs=vmem,
-        out_shape=jax.ShapeDtypeStruct((queries.shape[0], width), jnp.bfloat16),
-        name="pack",
-    )(queries, new_keys, new_values)
-
-
 SLAB = WINDOW + 16
 MASK_ROW = 8
 
 
 def prefill_kernel(
-    lengths_ref, keys_ref, values_ref, weight_ref, out_ref,
-    keys_at, values_at, weight_at, wide_ref, state_ref, norm_ref, weight_sem, load_sem, slab_sem,
+    lengths_ref, keys_ref, values_ref, weight_ref, queries_ref, new_keys_ref, new_values_ref, out_ref, mine_ref,
+    keys_at, values_at, weight_at, wide_ref, state_ref, norm_ref,
+    weight_sem, load_sem, slab_sem, pack_sem,
 ):
     heads, head_size, feats = weight_ref.shape
     pairs = heads // 2
@@ -63,6 +45,13 @@
         for load in loads[-1]:
             load.start()
 
+    packs, at = [], 0
+    for i, ref in enumerate((queries_ref, new_keys_ref, new_values_ref)):
+        size = ref.shape[1]
+        packs.append(pltpu.make_async_copy(ref, mine_ref.at[:, at : at + size], pack_sem.at[i]))
+        packs[-1].start()
+        at += size
+
     state_ref[...] = jnp.zeros_like(state_ref)
     norm_ref[...] = jnp.zeros_like(norm_ref)
     wide_ref[...] = jnp.zeros_like(wide_ref)
@@ -118,20 +107,24 @@
     tile.append(jnp.where((slot >= begin) & (slot < begin + WINDOW), 1.0, 0.0))
     tile.append(jnp.zeros((15 - MASK_ROW, head_size), jnp.float32))
     out_ref[heads * feats : heads * feats + 16, :] = jnp.concatenate(tile, axis=0).astype(jnp.bfloat16)
-    for slab in slabs:
-        slab.wait()
-
-
-def prefill(keys, values, weight, lengths):
+    for copy in slabs + packs:
+        copy.wait()
+
+
+def prefill(keys, values, weight, lengths, queries, new_keys, new_values):
     heads, head_size, feats = weight.shape
     span, width = keys.shape[1:]
+    arrays = (keys, values, weight, queries, new_keys, new_values)
     hbm = pl.BlockSpec(memory_space=pltpu.MemorySpace.HBM)
     vmem = pl.BlockSpec(memory_space=pltpu.VMEM)
     return pl.pallas_call(
         prefill_kernel,
-        in_specs=[pl.BlockSpec(memory_space=pltpu.SMEM), hbm, hbm, hbm],
-        out_specs=vmem,
-        out_shape=jax.ShapeDtypeStruct((heads * feats + 16 + 2 * heads * SLAB, head_size), jnp.bfloat16),
+        in_specs=[pl.BlockSpec(memory_space=pltpu.SMEM)] + [hbm] * len(arrays),
+        out_specs=[vmem, vmem],
+        out_shape=[
+            jax.ShapeDtypeStruct((heads * feats + 16 + 2 * heads * SLAB, head_size), jnp.bfloat16),
+            jax.ShapeDtypeStruct((queries.shape[0], queries.shape[1] + 2 * width), jnp.bfloat16),
+        ],
         scratch_shapes=[
             pltpu.VMEM((span, width), jnp.bfloat16),
             pltpu.VMEM((span, width), jnp.bfloat16),
@@ -142,13 +135,14 @@
             pltpu.SemaphoreType.DMA,
             pltpu.SemaphoreType.DMA((2, span // BLOCK)),
             pltpu.SemaphoreType.DMA((2, heads)),
+            pltpu.SemaphoreType.DMA((3,)),
         ],
-        compiler_params=pltpu.CompilerParams(vmem_limit_bytes=52 * 1024 * 1024),
+        compiler_params=pltpu.CompilerParams(vmem_limit_bytes=40 * 1024 * 1024),
         cost_estimate=pl.CostEstimate(
             flops=4 * span * width * feats, bytes_accessed=4 * span * width, transcendentals=span * width
         ),
         name="prefill",
-    )(lengths, keys, values, weight)
+    )(lengths, *[pltpu.with_memory_space_constraint(x, pltpu.MemorySpace.HBM) for x in arrays])
 
 
 def decode_kernel(rows_ref, weight_ref, near_ref, far_ref, *out_refs):
@@ -226,12 +220,11 @@
 ):
     sub = lax.axis_index("sub")
     sect = lax.axis_index("sect")
-    mine = pack(queries, new_keys, new_values)
+    near, mine = prefill(prompt_keys, prompt_values, feature_weight, lengths, queries, new_keys, new_values)
+    far = lax.ppermute(near, "sub", [(0, 1), (1, 0)])
     blocks = [mine] + [
-        lax.ppermute(mine, "sect", [(i, (i + k) % sects) for i in range(sects)]) for k in range(1, sects)
+        lax.ppermute(mine, "sect", [((i + k) % sects, i) for i in range(sects)]) for k in range(1, sects)
     ]
-    near = prefill(prompt_keys, prompt_values, feature_weight, lengths)
-    far = lax.ppermute(near, "sub", [(0, 1), (1, 0)])
     results = decode(jnp.concatenate(blocks, axis=0), feature_weight, near, far, sects)
 
     count = queries.shape[0]
@@ -240,8 +233,8 @@
     out = jnp.zeros_like(queries)
     for k, result in enumerate(results):
         if k > 0:
-            result = lax.ppermute(result, "sect", [(i, (i - k) % sects) for i in range(sects)])
-        out = jnp.where((prompts == (sect + k) % sects)[:, None], result, out)
+            result = lax.ppermute(result, "sect", [(i, (i + k) % sects) for i in range(sects)])
+        out = jnp.where((prompts == (sect - k) % sects)[:, None], result, out)
     return out
 
 

time: 25.9 us -> 28.9 us (1.12)
  waiting for transfers between devices: 4.06 us -> 7.64 us
  local copies, waits for them, and re-layouts: 0.91 us -> 0.01 us
  Pallas kernels: 8.01 us -> 8.69 us
  starting transfers between devices: 11.1 us -> 10.8 us
    ppermute x6, waiting for transfers between devices: 2.72 us -> 7.64 us  [the longest x3 5.07 us: body(): lax.ppermute(result, 'sect', [(i, (i + k) % sects) for i in range(sects)])]
    pallas_call x1, Pallas kernels: 5.47 us -> 7.54 us  [prefill(): pl.pallas_call(prefill_kernel, in_specs=[pl.BlockSpec(memory_space=pltpu....]
    pallas_call x1 -> x0, Pallas kernels: 1.39 us -> none  [pack(): pl.pallas_call(pack_kernel, in_specs=[vmem] * 3, out_specs=vmem, out_shap...]
    ppermute x1, waiting for transfers between devices: 1.34 us -> 0.01 us  [body(): far = lax.ppermute(near, 'sub', [(0, 1), (1, 0)])]
    unnamed x8 -> x4, local copies, waits for them, and re-layouts: 0.91 us -> 0.01 us
  transfers between devices with their start and end apart: 7 -> 7, of which waited for: 4 -> 5; matrix products, arithmetic and copies ran while one was open for 1% -> 1% of each run, Pallas kernels for 21% -> 0%
where the time goes in v5:
time: 28.9 us; the launch traced here: 28.8 us
  starting transfers between devices  10.8 us (37%)
  Pallas kernels  8.69 us (30%)
  waiting for transfers between devices  7.64 us (26%)
  other arithmetic  0.89 us (3%)
  between operations  0.71 us (2%)
    pallas_call x1, Pallas kernels, prefill(): pl.pallas_call(prefill_kernel, in_specs=[pl.BlockSpec(memory_space=pltpu....  7.54 us
    ppermute x3, starting transfers between devices, body(): lax.ppermute(mine, 'sect', [((i + k) % sects, i) for i in range(sects)])  7.01 us
    ppermute x3, waiting for transfers between devices, body(): lax.ppermute(result, 'sect', [(i, (i + k) % sects) for i in range(sects)])  5.07 us
    ppermute x3, starting transfers between devices, body(): lax.ppermute(result, 'sect', [(i, (i + k) % sects) for i in range(sects)])  3.84 us
    ppermute x3, waiting for transfers between devices, body(): lax.ppermute(mine, 'sect', [((i + k) % sects, i) for i in range(sects)])  2.57 us
    pallas_call x1, Pallas kernels, decode(): pl.pallas_call(decode_kernel, in_specs=[vmem] * 4, out_specs=[vmem] * par...  1.15 us
    select_n x1, other arithmetic, body(): out = jnp.where((prompts == (sect - k) % sects)[:, None], result, out)  0.71 us
  transfers between devices with their start and end apart: 7, of which 5 were waited for; matrix products, arithmetic and copies ran while one was open for 1% of the time, Pallas kernels for 0%

profile of v5, /device:TPU:0, one launch (start us, length us, event | category | flops | bytes accessed | tf_op | source)
XLA Modules:
  0.0 28.8 jit_solution(3693638562262374257)
XLA Ops:
  0.7 0.0 copy-start.1
  0.7 0.0 copy-start
  0.7 7.5 %prefill.1 = (bf16[1168,128]{1,0:T(8,128)(2,1)S(1)}, bf16[4,5120]{1,0:T(4,128)(2,1)S(1)}) custom-call(s32[1]{0:T(128)S(6)} %copy.9.lengths_ref, bf16[1,4096,512]{2,1,0:T(8,128)(2,1)} %keys_ref.1, bf16[1,4096,512]{2,1,0:T(8,128)(2,1)} %values_ref.1, bf16[4,128,128]{2,1,0:T(8,128)(2,1)} %weight_ref.3, bf16[4,4096]{1,0:T(4,128)(2,1)} %queries_ref.1, ...), custom_call_target="tpu_custom_call" | custom-call | flops 1073741824 | bytes 8388608 | tf_op jit(solution)/shard_map/prefill/pallas_call | solution.py:120
  8.2 3.1 %collective-permute-start.2 = (bf16[4,5120]{1,0:T(4,128)(2,1)S(1)}, bf16[4,5120]{1,0:T(4,128)(2,1)S(1)}, u32[]{:S(2)}, u32[]{:S(2)}) collective-permute-start(bf16[4,5120]{1,0:T(4,128)(2,1)S(1)} %get-tuple-element.11), channel_id=1, source_target_pairs={{12,0},{0,4},{4,8},{8,12},{13,1},{1,5},{5,9},{9,13},{14,2},{2,6},{... | collective-permute-start | bytes 122888 | tf_op jit(solution)/shard_map/ppermute | solution.py:226
  11.3 2.6 %collective-permute-start.1 = (bf16[4,5120]{1,0:T(4,128)(2,1)S(1)}, bf16[4,5120]{1,0:T(4,128)(2,1)S(1)}, u32[]{:S(2)}, u32[]{:S(2)}) collective-permute-start(bf16[4,5120]{1,0:T(4,128)(2,1)S(1)} %get-tuple-element.11), channel_id=1, source_target_pairs={{8,0},{12,4},{0,8},{4,12},{9,1},{13,5},{1,9},{5,13},{10,2},{14,6},... | collective-permute-start | bytes 122888 | tf_op jit(solution)/shard_map/ppermute | solution.py:226
  13.9 1.3 %collective-permute-start = (bf16[4,5120]{1,0:T(4,128)(2,1)S(1)}, bf16[4,5120]{1,0:T(4,128)(2,1)S(1)}, u32[]{:S(2)}, u32[]{:S(2)}) collective-permute-start(bf16[4,5120]{1,0:T(4,128)(2,1)S(1)} %get-tuple-element.11), channel_id=1, source_target_pairs={{4,0},{8,4},{12,8},{0,12},{5,1},{9,5},{13,9},{1,13},{6,2},{10,6},{... | collective-permute-start | bytes 122888 | tf_op jit(solution)/shard_map/ppermute | solution.py:226
  15.2 0.0 collective-permute-start.3
  15.2 0.0 copy-done.1
  15.2 0.1 broadcast_compare_fusion.3
  15.3 0.0 collective-permute-done.2
  15.3 1.4 %collective-permute-done.1 = bf16[4,5120]{1,0:T(4,128)(2,1)S(1)} collective-permute-done((bf16[4,5120]{1,0:T(4,128)(2,1)S(1)}, bf16[4,5120]{1,0:T(4,128)(2,1)S(1)}, u32[]{:S(2)}, u32[]{:S(2)}) %collective-permute-start.1) | collective-permute-done | bytes 40992 | tf_op jit(solution)/shard_map/ppermute | solution.py:226
  16.7 1.2 %collective-permute-done = bf16[4,5120]{1,0:T(4,128)(2,1)S(1)} collective-permute-done((bf16[4,5120]{1,0:T(4,128)(2,1)S(1)}, bf16[4,5120]{1,0:T(4,128)(2,1)S(1)}, u32[]{:S(2)}, u32[]{:S(2)}) %collective-permute-start) | collective-permute-done | bytes 40992 | tf_op jit(solution)/shard_map/ppermute | solution.py:226
  17.9 0.1 pad_maximum_fusion.rows_ref
  18.0 0.0 collective-permute-done.3.far_ref
  18.0 0.0 copy-done
  18.0 1.1 %decode.1 = (bf16[4,4096]{1,0:T(4,128)(2,1)S(1)}, bf16[4,4096]{1,0:T(4,128)(2,1)S(1)}, bf16[4,4096]{1,0:T(4,128)(2,1)S(1)}, bf16[4,4096]{1,0:T(4,128)(2,1)S(1)}) custom-call(bf16[16,5120]{1,0:T(8,128)(2,1)S(1)} %pad_maximum_fusion.rows_ref, bf16[4,128,128]{2,1,0:T(8,128)(2,1)S(1)} %copy-done, bf16[1168,128]{1,0:T(8,128)(2,1)S(1)} %get-tuple-element.12.near_ref, ...), custom_call_target="tpu_custom_call" | custom-call | flops 83886080 | bytes 262144 | tf_op jit(solution)/shard_map/decode/pallas_call | solution.py:205
  19.2 3.2 %collective-permute-start.4 = (bf16[4,4096]{1,0:T(4,128)(2,1)S(1)}, bf16[4,4096]{1,0:T(4,128)(2,1)S(1)}, u32[]{:S(2)}, u32[]{:S(2)}) collective-permute-start(bf16[4,4096]{1,0:T(4,128)(2,1)S(1)} %get-tuple-element.13), channel_id=1, source_target_pairs={{0,12},{4,0},{8,4},{12,8},{1,13},{5,1},{9,5},{13,9},{2,14},{6,2},{... | collective-permute-start | bytes 98312 | tf_op jit(solution)/shard_map/ppermute | solution.py:236
  22.4 0.0 collective-permute-start.5
  22.4 0.6 %collective-permute-start.6 = (bf16[4,4096]{1,0:T(4,128)(2,1)S(1)}, bf16[4,4096]{1,0:T(4,128)(2,1)S(1)}, u32[]{:S(2)}, u32[]{:S(2)}) collective-permute-start(bf16[4,4096]{1,0:T(4,128)(2,1)S(1)} %get-tuple-element.15), channel_id=1, source_target_pairs={{0,4},{4,8},{8,12},{12,0},{1,5},{5,9},{9,13},{13,1},{2,6},{6,10},{... | collective-permute-start | bytes 98312 | tf_op jit(solution)/shard_map/ppermute | solution.py:236
  23.0 0.9 %collective-permute-done.4 = bf16[4,4096]{1,0:T(4,128)(2,1)S(1)} collective-permute-done((bf16[4,4096]{1,0:T(4,128)(2,1)S(1)}, bf16[4,4096]{1,0:T(4,128)(2,1)S(1)}, u32[]{:S(2)}, u32[]{:S(2)}) %collective-permute-start.4) | collective-permute-done | bytes 32800 | tf_op jit(solution)/shard_map/ppermute | solution.py:236
  24.0 3.2 %collective-permute-done.5 = bf16[4,4096]{1,0:T(4,128)(2,1)S(1)} collective-permute-done((bf16[4,4096]{1,0:T(4,128)(2,1)S(1)}, bf16[4,4096]{1,0:T(4,128)(2,1)S(1)}, u32[]{:S(2)}, u32[]{:S(2)}) %collective-permute-start.5) | collective-permute-done | bytes 32800 | tf_op jit(solution)/shard_map/ppermute | solution.py:236
  27.2 0.9 %collective-permute-done.6 = bf16[4,4096]{1,0:T(4,128)(2,1)S(1)} collective-permute-done((bf16[4,4096]{1,0:T(4,128)(2,1)S(1)}, bf16[4,4096]{1,0:T(4,128)(2,1)S(1)}, u32[]{:S(2)}, u32[]{:S(2)}) %collective-permute-start.6) | collective-permute-done | bytes 32800 | tf_op jit(solution)/shard_map/ppermute | solution.py:236
  28.1 0.7 %select_select_fusion = bf16[4,4096]{1,0:T(4,128)(2,1)} fusion(bf16[4,4096]{1,0:T(4,128)(2,1)S(1)} %collective-permute-done.4, bf16[4,4096]{1,0:T(4,128)(2,1)S(1)} %collective-permute-done.5, bf16[4,4096]{1,0:T(4,128)(2,1)S(1)} %collective-permute-done.6, bf16[4,4096]{1,0:T(4,128)(2,1)S(1)} %get-tuple-element.16, pred[4]{0:T(512)(128)(4,1)S(1)} %get-tuple-element.21, ...), kind=kLoop, calls=%fused_computation.1 | loop fusion | flops 65536 | bytes 163856 | tf_op jit(solution)/shard_map/jit(_where)/select_n | solution.py:237
  (1 shorter events, 0.0 us)
Async XLA Ops:
  0.7 14.6 %copy-start.1 = (s32[32]{0:T(128)S(1)}, s32[32]{0:T(128)}, u32[]{:S(2)}) copy-start(s32[32]{0:T(128)} %param.15) | copy-start | bytes 388
  0.7 17.3 %copy-start = (bf16[4,128,128]{2,1,0:T(8,128)(2,1)S(1)}, bf16[4,128,128]{2,1,0:T(8,128)(2,1)}, u32[]{:S(2)}) copy-start(bf16[4,128,128]{2,1,0:T(8,128)(2,1)} %weight_ref.3) | copy-start | bytes 393220
  8.2 7.1 %collective-permute-start.2 = (bf16[4,5120]{1,0:T(4,128)(2,1)S(1)}, bf16[4,5120]{1,0:T(4,128)(2,1)S(1)}, u32[]{:S(2)}, u32[]{:S(2)}) collective-permute-start(bf16[4,5120]{1,0:T(4,128)(2,1)S(1)} %get-tuple-element.11), channel_id=1, source_target_pairs={{12,0},{0,4},{4,8},{8,12},{13,1},{1,5},{5,9},{9,13},{14,2},{2,6},{... | collective-permute-start | bytes 122888 | tf_op jit(solution)/shard_map/ppermute | solution.py:226
  11.3 5.4 %collective-permute-start.1 = (bf16[4,5120]{1,0:T(4,128)(2,1)S(1)}, bf16[4,5120]{1,0:T(4,128)(2,1)S(1)}, u32[]{:S(2)}, u32[]{:S(2)}) collective-permute-start(bf16[4,5120]{1,0:T(4,128)(2,1)S(1)} %get-tuple-element.11), channel_id=1, source_target_pairs={{8,0},{12,4},{0,8},{4,12},{9,1},{13,5},{1,9},{5,13},{10,2},{14,6},... | collective-permute-start | bytes 122888 | tf_op jit(solution)/shard_map/ppermute | solution.py:226
  13.9 4.0 %collective-permute-start = (bf16[4,5120]{1,0:T(4,128)(2,1)S(1)}, bf16[4,5120]{1,0:T(4,128)(2,1)S(1)}, u32[]{:S(2)}, u32[]{:S(2)}) collective-permute-start(bf16[4,5120]{1,0:T(4,128)(2,1)S(1)} %get-tuple-element.11), channel_id=1, source_target_pairs={{4,0},{8,4},{12,8},{0,12},{5,1},{9,5},{13,9},{1,13},{6,2},{10,6},{... | collective-permute-start | bytes 122888 | tf_op jit(solution)/shard_map/ppermute | solution.py:226
  15.2 2.8 %collective-permute-start.3 = (bf16[1168,128]{1,0:T(8,128)(2,1)S(1)}, bf16[1168,128]{1,0:T(8,128)(2,1)S(1)}, u32[]{:S(2)}, u32[]{:S(2)}) collective-permute-start(bf16[1168,128]{1,0:T(8,128)(2,1)S(1)} %get-tuple-element.12.near_ref), channel_id=1, source_target_pairs={{0,1},{1,0},{2,3},{3,2},{4,5},{5,4},{6,7},{7,6},{8,9},{9,8},{10,11... | collective-permute-start | bytes 897032 | tf_op jit(solution)/shard_map/ppermute | solution.py:224
  19.2 4.8 %collective-permute-start.4 = (bf16[4,4096]{1,0:T(4,128)(2,1)S(1)}, bf16[4,4096]{1,0:T(4,128)(2,1)S(1)}, u32[]{:S(2)}, u32[]{:S(2)}) collective-permute-start(bf16[4,4096]{1,0:T(4,128)(2,1)S(1)} %get-tuple-element.13), channel_id=1, source_target_pairs={{0,12},{4,0},{8,4},{12,8},{1,13},{5,1},{9,5},{13,9},{2,14},{6,2},{... | collective-permute-start | bytes 98312 | tf_op jit(solution)/shard_map/ppermute | solution.py:236
  22.4 4.8 %collective-permute-start.5 = (bf16[4,4096]{1,0:T(4,128)(2,1)S(1)}, bf16[4,4096]{1,0:T(4,128)(2,1)S(1)}, u32[]{:S(2)}, u32[]{:S(2)}) collective-permute-start(bf16[4,4096]{1,0:T(4,128)(2,1)S(1)} %get-tuple-element.14), channel_id=1, source_target_pairs={{0,8},{4,12},{8,0},{12,4},{1,9},{5,13},{9,1},{13,5},{2,10},{6,14},... | collective-permute-start | bytes 98312 | tf_op jit(solution)/shard_map/ppermute | solution.py:236
  22.4 5.7 %collective-permute-start.6 = (bf16[4,4096]{1,0:T(4,128)(2,1)S(1)}, bf16[4,4096]{1,0:T(4,128)(2,1)S(1)}, u32[]{:S(2)}, u32[]{:S(2)}) collective-permute-start(bf16[4,4096]{1,0:T(4,128)(2,1)S(1)} %get-tuple-element.15), channel_id=1, source_target_pairs={{0,4},{4,8},{8,12},{12,0},{1,5},{5,9},{9,13},{13,1},{2,6},{6,10},{... | collective-permute-start | bytes 98312 | tf_op jit(solution)/shard_map/ppermute | solution.py:236

commit v6 on v2

--- a/solution.py
+++ b/solution.py
@@ -18,32 +18,14 @@
     return jnp.maximum(proj, 0.0) + jnp.exp(jnp.minimum(proj, 0.0))
 
 
-def pack_kernel(queries_ref, keys_ref, values_ref, out_ref):
-    width, each = queries_ref.shape[1], keys_ref.shape[1]
-    out_ref[:, :width] = queries_ref[...]
-    out_ref[:, width : width + each] = keys_ref[...]
-    out_ref[:, width + each :] = values_ref[...]
-
-
-def pack(queries, new_keys, new_values):
-    vmem = pl.BlockSpec(memory_space=pltpu.VMEM)
-    width = queries.shape[1] + 2 * new_keys.shape[1]
-    return pl.pallas_call(
-        pack_kernel,
-        in_specs=[vmem] * 3,
-        out_specs=vmem,
-        out_shape=jax.ShapeDtypeStruct((queries.shape[0], width), jnp.bfloat16),
-        name="pack",
-    )(queries, new_keys, new_values)
-
-
 SLAB = WINDOW + 16
 MASK_ROW = 8
 
 
 def prefill_kernel(
     lengths_ref, keys_ref, values_ref, weight_ref, out_ref,
-    keys_at, values_at, weight_at, wide_ref, state_ref, norm_ref, weight_sem, load_sem, slab_sem,
+    keys_at, values_at, weight_at, wide_ref, state_ref, norm_ref,
+    weight_sem, load_sem, slab_sem,
 ):
     heads, head_size, feats = weight_ref.shape
     pairs = heads // 2
@@ -125,11 +107,12 @@
 def prefill(keys, values, weight, lengths):
     heads, head_size, feats = weight.shape
     span, width = keys.shape[1:]
+    arrays = (keys, values, weight)
     hbm = pl.BlockSpec(memory_space=pltpu.MemorySpace.HBM)
     vmem = pl.BlockSpec(memory_space=pltpu.VMEM)
     return pl.pallas_call(
         prefill_kernel,
-        in_specs=[pl.BlockSpec(memory_space=pltpu.SMEM), hbm, hbm, hbm],
+        in_specs=[pl.BlockSpec(memory_space=pltpu.SMEM)] + [hbm] * len(arrays),
         out_specs=vmem,
         out_shape=jax.ShapeDtypeStruct((heads * feats + 16 + 2 * heads * SLAB, head_size), jnp.bfloat16),
         scratch_shapes=[
@@ -143,24 +126,24 @@
             pltpu.SemaphoreType.DMA((2, span // BLOCK)),
             pltpu.SemaphoreType.DMA((2, heads)),
         ],
-        compiler_params=pltpu.CompilerParams(vmem_limit_bytes=52 * 1024 * 1024),
+        compiler_params=pltpu.CompilerParams(vmem_limit_bytes=40 * 1024 * 1024),
         cost_estimate=pl.CostEstimate(
             flops=4 * span * width * feats, bytes_accessed=4 * span * width, transcendentals=span * width
         ),
         name="prefill",
-    )(lengths, keys, values, weight)
+    )(lengths, *[pltpu.with_memory_space_constraint(x, pltpu.MemorySpace.HBM) for x in arrays])
 
 
 def decode_kernel(rows_ref, weight_ref, near_ref, far_ref, *out_refs):
     heads, head_size, feats = weight_ref.shape
-    count = rows_ref.shape[0]
-    group = (rows_ref.shape[1] - 2 * heads * head_size) // (heads * head_size)
-    keys_at = heads * group * head_size
-    values_at = keys_at + heads * head_size
+    count, width = rows_ref.shape
+    group = width // (heads * head_size)
     each = count // len(out_refs)
     tile_at = heads * feats
     halves = (near_ref, far_ref)
     tiles = [ref[tile_at : tile_at + 16, :].astype(jnp.float32) for ref in halves]
+    lane = lax.broadcasted_iota(jnp.int32, (count, head_size), 1)
+    dens = jnp.zeros((count, head_size), jnp.float32)
     for g in range(heads):
         query = jnp.concatenate(
             [
@@ -172,14 +155,7 @@
         wide = query.astype(jnp.float32)
         phi = feature(jnp.dot(query, weight_ref[g], preferred_element_type=jnp.float32)).astype(jnp.bfloat16)
         scale = (TAU / head_size) * lax.rsqrt(jnp.mean(wide * wide, axis=-1, keepdims=True) + EPS)
-        own_key = rows_ref[:, keys_at + g * head_size : keys_at + (g + 1) * head_size].astype(jnp.float32)
-        own_value = rows_ref[:, values_at + g * head_size : values_at + (g + 1) * head_size].astype(jnp.float32)
-        own_key = own_key * lax.rsqrt(jnp.mean(own_key * own_key, axis=-1, keepdims=True) + EPS)
-        own_score = jnp.sum(wide * jnp.concatenate([own_key] * group, axis=0), axis=-1, keepdims=True) * scale
-        own_weight = jnp.exp(own_score)
-        num = own_weight.astype(jnp.bfloat16).astype(jnp.float32) * jnp.concatenate([own_value] * group, axis=0)
-        den = own_weight
-        linear = jnp.zeros_like(num)
+        num, den, linear = 0.0, 0.0, 0.0
         for ref, tile in zip(halves, tiles):
             linear += jnp.dot(phi, ref[g * feats : (g + 1) * feats, :], preferred_element_type=jnp.float32)
             at = tile_at + 16 + g * SLAB
@@ -195,24 +171,29 @@
         norm = (tiles[0] + tiles[1])[g : g + 1]
         back = 1.0 / (feats * feats)
         den += jnp.sum(phi.astype(jnp.float32) * norm, axis=-1, keepdims=True) * back
-        result = ((linear * back + num) / den).astype(jnp.bfloat16)
+        result = (linear * back + num).astype(jnp.bfloat16)
         for h in range(group):
-            at = (g * group + h) * head_size
+            head = g * group + h
+            dens = jnp.where(lane == head, den[h * count : (h + 1) * count], dens)
             for k, out_ref in enumerate(out_refs):
                 start = h * count + k * each
-                out_ref[:, at : at + head_size] = result[start : start + each]
+                out_ref[:, head * head_size : (head + 1) * head_size] = result[start : start + each]
+    high = dens.astype(jnp.bfloat16)
+    low = (dens - high.astype(jnp.float32)).astype(jnp.bfloat16)
+    for k, out_ref in enumerate(out_refs):
+        out_ref[:, width : width + head_size] = high[k * each : (k + 1) * each]
+        out_ref[:, width + head_size :] = low[k * each : (k + 1) * each]
 
 
 def decode(rows, weight, near, far, parts):
     heads, head_size, feats = weight.shape
-    count = rows.shape[0]
-    width = rows.shape[1] - 2 * heads * head_size
+    count, width = rows.shape
     vmem = pl.BlockSpec(memory_space=pltpu.VMEM)
     return pl.pallas_call(
         decode_kernel,
         in_specs=[vmem] * 4,
         out_specs=[vmem] * parts,
-        out_shape=[jax.ShapeDtypeStruct((count // parts, width), jnp.bfloat16)] * parts,
+        out_shape=[jax.ShapeDtypeStruct((count // parts, width + 2 * head_size), jnp.bfloat16)] * parts,
         compiler_params=pltpu.CompilerParams(vmem_limit_bytes=32 * 1024 * 1024),
         cost_estimate=pl.CostEstimate(
             flops=10 * count * width * feats, bytes_accessed=4 * count * width, transcendentals=2 * count * width
@@ -221,28 +202,94 @@
     )(rows, weight, near, far)
 
 
+def own_kernel(queries_ref, keys_ref, values_ref, _, num_ref, weight_ref):
+    count, width = queries_ref.shape
+    head_size = weight_ref.shape[1]
+    heads = keys_ref.shape[1] // head_size
+    group = width // (heads * head_size)
+    lane = lax.broadcasted_iota(jnp.int32, (count, head_size), 1)
+    kept = jnp.zeros((count, head_size), jnp.float32)
+    for g in range(heads):
+        cols = slice(g * head_size, (g + 1) * head_size)
+        key = keys_ref[:, cols].astype(jnp.float32)
+        value = values_ref[:, cols].astype(jnp.float32)
+        key = key * lax.rsqrt(jnp.mean(key * key, axis=-1, keepdims=True) + EPS)
+        for h in range(group):
+            head = g * group + h
+            span = slice(head * head_size, (head + 1) * head_size)
+            query = queries_ref[:, span].astype(jnp.float32)
+            scale = (TAU / head_size) * lax.rsqrt(jnp.mean(query * query, axis=-1, keepdims=True) + EPS)
+            weight = jnp.exp(jnp.sum(query * key, axis=-1, keepdims=True) * scale)
+            num_ref[:, span] = weight.astype(jnp.bfloat16).astype(jnp.float32) * value
+            kept = jnp.where(lane == head, weight, kept)
+    weight_ref[...] = kept
+
+
+def own(queries, new_keys, new_values, after, head_size):
+    vmem = pl.BlockSpec(memory_space=pltpu.VMEM)
+    count, width = queries.shape
+    return pl.pallas_call(
+        own_kernel,
+        in_specs=[vmem] * 3 + [pl.BlockSpec(memory_space=pl.ANY)],
+        out_specs=[vmem, vmem],
+        out_shape=[
+            jax.ShapeDtypeStruct((count, width), jnp.float32),
+            jax.ShapeDtypeStruct((count, head_size), jnp.float32),
+        ],
+        cost_estimate=pl.CostEstimate(
+            flops=8 * count * width, bytes_accessed=8 * count * width, transcendentals=count * width // head_size
+        ),
+        name="own",
+    )(queries, new_keys, new_values, after)
+
+
+def finish_kernel(prompts_ref, num_ref, weight_ref, *refs):
+    block_refs, out_ref = refs[:-1], refs[-1]
+    count, width = out_ref.shape
+    head_size = weight_ref.shape[1]
+    sects = len(block_refs)
+    sect = lax.axis_index("sect")
+    first = (sect * lax.axis_size("sub") + lax.axis_index("sub")) * count
+    rows = prompts_ref.shape[1]
+    row = first + lax.broadcasted_iota(jnp.int32, (count, rows), 0)
+    lane = lax.broadcasted_iota(jnp.int32, (count, rows), 1)
+    prompt = jnp.sum(jnp.where(lane == row, prompts_ref[...], 0), axis=1, keepdims=True)
+    chosen = block_refs[0][...].astype(jnp.float32)
+    for k in range(1, sects):
+        source = lax.rem(sect - k + sects, sects)
+        chosen = jnp.where(prompt == source, block_refs[k][...].astype(jnp.float32), chosen)
+    den = chosen[:, width : width + head_size] + chosen[:, width + head_size :] + weight_ref[...]
+    scale = 1.0 / den
+    for head in range(width // head_size):
+        span = slice(head * head_size, (head + 1) * head_size)
+        out_ref[:, span] = ((chosen[:, span] + num_ref[:, span]) * scale[:, head : head + 1]).astype(out_ref.dtype)
+
+
+def finish(row_prompt, num, weight, blocks):
+    vmem = pl.BlockSpec(memory_space=pltpu.VMEM)
+    return pl.pallas_call(
+        finish_kernel,
+        in_specs=[vmem] * (3 + len(blocks)),
+        out_specs=vmem,
+        out_shape=jax.ShapeDtypeStruct(num.shape, jnp.bfloat16),
+        name="finish",
+    )(row_prompt.reshape(1, -1), num, weight, *blocks)
+
+
 def body(
     sects, prompt_keys, prompt_values, lengths, feature_weight, queries, new_keys, new_values, row_prompt
 ):
-    sub = lax.axis_index("sub")
-    sect = lax.axis_index("sect")
-    mine = pack(queries, new_keys, new_values)
-    blocks = [mine] + [
-        lax.ppermute(mine, "sect", [(i, (i + k) % sects) for i in range(sects)]) for k in range(1, sects)
+    blocks = [queries] + [
+        lax.ppermute(queries, "sect", [((i + k) % sects, i) for i in range(sects)]) for k in range(1, sects)
     ]
     near = prefill(prompt_keys, prompt_values, feature_weight, lengths)
     far = lax.ppermute(near, "sub", [(0, 1), (1, 0)])
     results = decode(jnp.concatenate(blocks, axis=0), feature_weight, near, far, sects)
-
-    count = queries.shape[0]
-    first_row = (sect * lax.axis_size("sub") + sub) * count
-    prompts = lax.dynamic_slice_in_dim(row_prompt, first_row, count, 0)
-    out = jnp.zeros_like(queries)
-    for k, result in enumerate(results):
-        if k > 0:
-            result = lax.ppermute(result, "sect", [(i, (i - k) % sects) for i in range(sects)])
-        out = jnp.where((prompts == (sect + k) % sects)[:, None], result, out)
-    return out
+    num, weight = own(queries, new_keys, new_values, results[0], feature_weight.shape[1])
+    back = [results[0]] + [
+        lax.ppermute(results[k], "sect", [(i, (i + k) % sects) for i in range(sects)]) for k in range(1, sects)
+    ]
+    return finish(row_prompt, num, weight, back)
 
 
 def solution(mesh):

time: 25.9 us -> 27.3 us (1.054)
  Pallas kernels: 8.01 us -> 11.8 us
  waiting for transfers between devices: 4.06 us -> 2.4 us
  other arithmetic: 0.9 us -> 0.08 us
  local copies, waits for them, and re-layouts: 0.91 us -> 1.23 us
    pallas_call x1, Pallas kernels: 5.47 us -> 7.61 us  [prefill(): pl.pallas_call(prefill_kernel, in_specs=[pl.BlockSpec(memory_space=pltpu....]
    pallas_call x1 -> x2, Pallas kernels: 1.39 us -> 3.34 us  [the longest x1 1.73 us: finish(): pl.pallas_call(finish_kernel, in_specs=[vmem] * (3 + len(blocks)), out_sp...]
    ppermute x6, waiting for transfers between devices: 2.72 us -> 0.96 us  [the longest x3 0.95 us: body(): lax.ppermute(results[k], 'sect', [(i, (i + k) % sects) for i in range(sec...]
    select_n x1 -> x0, other arithmetic: 0.71 us -> none  [body(): out = jnp.where((prompts == (sect + k) % sects)[:, None], result, out)]
    unnamed x8 -> x12, local copies, waits for them, and re-layouts: 0.91 us -> 1.23 us
    pallas_call x1, Pallas kernels: 1.14 us -> 0.85 us  [decode(): pl.pallas_call(decode_kernel, in_specs=[vmem] * 4, out_specs=[vmem] * par...]
  transfers between devices with their start and end apart: 7 -> 7, of which waited for: 4 -> 3; matrix products, arithmetic and copies ran while one was open for 1% -> 0% of each run, Pallas kernels for 21% -> 34%
where the time goes in v6:
time: 27.3 us; the launch traced here: 27.1 us
  Pallas kernels  11.8 us (43%)
  starting transfers between devices  10.9 us (40%)
  waiting for transfers between devices  2.4 us (9%)
  local copies, waits for them, and re-layouts  1.23 us (5%)
  between operations  0.75 us (3%)
    pallas_call x1, Pallas kernels, prefill(): pl.pallas_call(prefill_kernel, in_specs=[pl.BlockSpec(memory_space=pltpu....  7.61 us
    ppermute x3, starting transfers between devices, body(): lax.ppermute(queries, 'sect', [((i + k) % sects, i) for i in range(sects)])  6.96 us
    ppermute x3, starting transfers between devices, body(): lax.ppermute(results[k], 'sect', [(i, (i + k) % sects) for i in range(sec...  3.83 us
    pallas_call x1, Pallas kernels, finish(): pl.pallas_call(finish_kernel, in_specs=[vmem] * (3 + len(blocks)), out_sp...  1.73 us
    pallas_call x1, Pallas kernels, own(): pl.pallas_call(own_kernel, in_specs=[vmem] * 3 + [pl.BlockSpec(memory_spa...  1.61 us
    ppermute x1, waiting for transfers between devices, body(): far = lax.ppermute(near, 'sub', [(0, 1), (1, 0)])  1.44 us
    unnamed x12, local copies, waits for them, and re-layouts  1.23 us
    ppermute x3, waiting for transfers between devices, body(): lax.ppermute(results[k], 'sect', [(i, (i + k) % sects) for i in range(sec...  0.95 us
  transfers between devices with their start and end apart: 7, of which 3 were waited for; matrix products, arithmetic and copies ran while one was open for 0% of the time, Pallas kernels for 34%

profile of v6, /device:TPU:0, one launch (start us, length us, event | category | flops | bytes accessed | tf_op | source)
XLA Modules:
  0.0 27.1 jit_solution(405398777290640071)
XLA Ops:
  0.0 3.0 %collective-permute-start.2 = (bf16[4,4096]{1,0:T(4,128)(2,1)}, bf16[4,4096]{1,0:T(4,128)(2,1)S(1)}, u32[]{:S(2)}, u32[]{:S(2)}) collective-permute-start(bf16[4,4096]{1,0:T(4,128)(2,1)} %queries_ref.1), channel_id=1, source_target_pairs={{12,0},{0,4},{4,8},{8,12},{13,1},{1,5},{5,9},{9,13},{14,2},{2,6},{... | collective-permute-start | bytes 98312 | tf_op jit(solution)/shard_map/ppermute | solution.py:283
  3.0 2.6 %collective-permute-start.1 = (bf16[4,4096]{1,0:T(4,128)(2,1)}, bf16[4,4096]{1,0:T(4,128)(2,1)S(1)}, u32[]{:S(2)}, u32[]{:S(2)}) collective-permute-start(bf16[4,4096]{1,0:T(4,128)(2,1)} %queries_ref.1), channel_id=1, source_target_pairs={{8,0},{12,4},{0,8},{4,12},{9,1},{13,5},{1,9},{5,13},{10,2},{14,6},... | collective-permute-start | bytes 98312 | tf_op jit(solution)/shard_map/ppermute | solution.py:283
  5.6 1.3 %collective-permute-start = (bf16[4,4096]{1,0:T(4,128)(2,1)}, bf16[4,4096]{1,0:T(4,128)(2,1)S(1)}, u32[]{:S(2)}, u32[]{:S(2)}) collective-permute-start(bf16[4,4096]{1,0:T(4,128)(2,1)} %queries_ref.1), channel_id=1, source_target_pairs={{4,0},{8,4},{12,8},{0,12},{5,1},{9,5},{13,9},{1,13},{6,2},{10,6},{... | collective-permute-start | bytes 98312 | tf_op jit(solution)/shard_map/ppermute | solution.py:283
  7.6 0.0 copy-start.2
  7.6 0.0 copy-start
  7.6 7.6 %prefill.1.near_ref = bf16[1168,128]{1,0:T(8,128)(2,1)S(1)} custom-call(s32[1]{0:T(128)S(6)} %copy.9.lengths_ref, bf16[1,4096,512]{2,1,0:T(8,128)(2,1)} %keys_ref.2, bf16[1,4096,512]{2,1,0:T(8,128)(2,1)} %values_ref.2, bf16[4,128,128]{2,1,0:T(8,128)(2,1)} %weight_ref.3), custom_call_target="tpu_custom_call" | custom-call | flops 1073741824 | bytes 8388608 | tf_op jit(solution)/shard_map/prefill/pallas_call | solution.py:113
  15.3 0.1 collective-permute-start.3
  15.3 0.0 collective-permute-done.2
  15.3 0.0 collective-permute-done.1
  15.4 0.0 collective-permute-done
  15.4 0.0 copy-done.2
  15.4 0.1 pad_maximum_fusion.rows_ref
  15.5 1.4 %collective-permute-done.3.far_ref = bf16[1168,128]{1,0:T(8,128)(2,1)S(1)} collective-permute-done((bf16[1168,128]{1,0:T(8,128)(2,1)S(1)}, bf16[1168,128]{1,0:T(8,128)(2,1)S(1)}, u32[]{:S(2)}, u32[]{:S(2)}) %collective-permute-start.3) | collective-permute-done | bytes 299040 | tf_op jit(solution)/shard_map/ppermute | solution.py:286
  16.9 0.0 copy-done
  16.9 0.8 %decode.1 = (bf16[4,4352]{1,0:T(4,128)(2,1)S(1)}, bf16[4,4352]{1,0:T(4,128)(2,1)S(1)}, bf16[4,4352]{1,0:T(4,128)(2,1)S(1)}, bf16[4,4352]{1,0:T(4,128)(2,1)S(1)}) custom-call(bf16[16,4096]{1,0:T(8,128)(2,1)S(1)} %pad_maximum_fusion.rows_ref, bf16[4,128,128]{2,1,0:T(8,128)(2,1)S(1)} %copy-done, bf16[1168,128]{1,0:T(8,128)(2,1)S(1)} %prefill.1.near_ref, ...), custom_call_target="tpu_custom_call" | custom-call | flops 83886080 | bytes 262144 | tf_op jit(solution)/shard_map/decode/pallas_call | solution.py:192
  17.8 0.0 copy-start.1
  17.8 0.6 %copy-done.1 = bf16[4,4352]{1,0:T(4,128)(2,1)} copy-done((bf16[4,4352]{1,0:T(4,128)(2,1)}, bf16[4,4352]{1,0:T(4,128)(2,1)S(1)}, u32[]{:S(2)}) %copy-start.1) | copy-done | bytes 34840
  18.4 0.7 %collective-permute-start.4 = (bf16[4,4352]{1,0:T(4,128)(2,1)S(1)}, bf16[4,4352]{1,0:T(4,128)(2,1)S(1)}, u32[]{:S(2)}, u32[]{:S(2)}) collective-permute-start(bf16[4,4352]{1,0:T(4,128)(2,1)S(1)} %get-tuple-element.14), channel_id=1, source_target_pairs={{0,4},{4,8},{8,12},{12,0},{1,5},{5,9},{9,13},{13,1},{2,6},{6,10},{... | collective-permute-start | bytes 104456 | tf_op jit(solution)/shard_map/ppermute | solution.py:290
  19.1 0.3 %collective-permute-start.5 = (bf16[4,4352]{1,0:T(4,128)(2,1)S(1)}, bf16[4,4352]{1,0:T(4,128)(2,1)S(1)}, u32[]{:S(2)}, u32[]{:S(2)}) collective-permute-start(bf16[4,4352]{1,0:T(4,128)(2,1)S(1)} %get-tuple-element.15), channel_id=1, source_target_pairs={{0,8},{4,12},{8,0},{12,4},{1,9},{5,13},{9,1},{13,5},{2,10},{6,14},... | collective-permute-start | bytes 104456 | tf_op jit(solution)/shard_map/ppermute | solution.py:290
  19.4 2.8 %collective-permute-start.6 = (bf16[4,4352]{1,0:T(4,128)(2,1)S(1)}, bf16[4,4352]{1,0:T(4,128)(2,1)S(1)}, u32[]{:S(2)}, u32[]{:S(2)}) collective-permute-start(bf16[4,4352]{1,0:T(4,128)(2,1)S(1)} %get-tuple-element.16), channel_id=1, source_target_pairs={{0,12},{4,0},{8,4},{12,8},{1,13},{5,1},{9,5},{13,9},{2,14},{6,2},{... | collective-permute-start | bytes 104456 | tf_op jit(solution)/shard_map/ppermute | solution.py:290
  22.2 1.6 %own.1 = (f32[4,4096]{1,0:T(4,128)}, f32[4,128]{1,0:T(4,128)}) custom-call(bf16[4,4096]{1,0:T(4,128)(2,1)} %queries_ref.1, bf16[4,512]{1,0:T(4,128)(2,1)} %keys_ref.3, bf16[4,512]{1,0:T(4,128)(2,1)} %values_ref.3, bf16[4,4352]{1,0:T(4,128)(2,1)} %copy-done.1), custom_call_target="tpu_custom_call" | custom-call | flops 131072 | bytes 131072 | tf_op jit(solution)/shard_map/own/pallas_call | solution.py:231
  23.8 0.6 %collective-permute-done.4.refs_1_ = bf16[4,4352]{1,0:T(4,128)(2,1)S(1)} collective-permute-done((bf16[4,4352]{1,0:T(4,128)(2,1)S(1)}, bf16[4,4352]{1,0:T(4,128)(2,1)S(1)}, u32[]{:S(2)}, u32[]{:S(2)}) %collective-permute-start.4) | collective-permute-done | bytes 34848 | tf_op jit(solution)/shard_map/ppermute | solution.py:290
  24.4 0.0 copy-start.3
  24.4 0.0 collective-permute-done.5.refs_2_
  24.4 0.0 copy-start.4
  24.4 0.4 %collective-permute-done.6.refs_3_ = bf16[4,4352]{1,0:T(4,128)(2,1)S(1)} collective-permute-done((bf16[4,4352]{1,0:T(4,128)(2,1)S(1)}, bf16[4,4352]{1,0:T(4,128)(2,1)S(1)}, u32[]{:S(2)}, u32[]{:S(2)}) %collective-permute-start.6) | collective-permute-done | bytes 34848 | tf_op jit(solution)/shard_map/ppermute | solution.py:290
  24.8 0.0 copy-start.5
  24.8 0.2 copy-done.3
  25.0 0.0 copy-done.4
  25.1 0.3 %copy-done.5 = bf16[4,4352]{1,0:T(4,128)(2,1)} copy-done((bf16[4,4352]{1,0:T(4,128)(2,1)}, bf16[4,4352]{1,0:T(4,128)(2,1)S(1)}, u32[]{:S(2)}) %copy-start.5) | copy-done | bytes 34840
  25.4 1.7 %finish.1 = bf16[4,4096]{1,0:T(4,128)(2,1)} custom-call(s32[1,32]{1,0:T(1,128)} %bitcast.1, f32[4,4096]{1,0:T(4,128)} %get-tuple-element.12.num_ref, f32[4,128]{1,0:T(4,128)} %get-tuple-element.13.weight_ref, bf16[4,4352]{1,0:T(4,128)(2,1)} %copy-done.1, bf16[4,4352]{1,0:T(4,128)(2,1)} %copy-done.3, bf16[4,4352]{1,0:T(4,128)(2,1)} %copy-done.4, ...), custom_call_target="tpu_custom_call" | custom-call | tf_op jit(solution)/shard_map/finish/pallas_call | solution.py:270
Async XLA Ops:
  0.0 15.3 %collective-permute-start.2 = (bf16[4,4096]{1,0:T(4,128)(2,1)}, bf16[4,4096]{1,0:T(4,128)(2,1)S(1)}, u32[]{:S(2)}, u32[]{:S(2)}) collective-permute-start(bf16[4,4096]{1,0:T(4,128)(2,1)} %queries_ref.1), channel_id=1, source_target_pairs={{12,0},{0,4},{4,8},{8,12},{13,1},{1,5},{5,9},{9,13},{14,2},{2,6},{... | collective-permute-start | bytes 98312 | tf_op jit(solution)/shard_map/ppermute | solution.py:283
  3.0 12.3 %collective-permute-start.1 = (bf16[4,4096]{1,0:T(4,128)(2,1)}, bf16[4,4096]{1,0:T(4,128)(2,1)S(1)}, u32[]{:S(2)}, u32[]{:S(2)}) collective-permute-start(bf16[4,4096]{1,0:T(4,128)(2,1)} %queries_ref.1), channel_id=1, source_target_pairs={{8,0},{12,4},{0,8},{4,12},{9,1},{13,5},{1,9},{5,13},{10,2},{14,6},... | collective-permute-start | bytes 98312 | tf_op jit(solution)/shard_map/ppermute | solution.py:283
  5.6 9.7 %collective-permute-start = (bf16[4,4096]{1,0:T(4,128)(2,1)}, bf16[4,4096]{1,0:T(4,128)(2,1)S(1)}, u32[]{:S(2)}, u32[]{:S(2)}) collective-permute-start(bf16[4,4096]{1,0:T(4,128)(2,1)} %queries_ref.1), channel_id=1, source_target_pairs={{4,0},{8,4},{12,8},{0,12},{5,1},{9,5},{13,9},{1,13},{6,2},{10,6},{... | collective-permute-start | bytes 98312 | tf_op jit(solution)/shard_map/ppermute | solution.py:283
  7.6 7.8 %copy-start.2 = (bf16[4,4096]{1,0:T(4,128)(2,1)S(1)}, bf16[4,4096]{1,0:T(4,128)(2,1)}, u32[]{:S(2)}) copy-start(bf16[4,4096]{1,0:T(4,128)(2,1)} %queries_ref.1) | copy-start | bytes 98308
  7.6 9.3 %copy-start = (bf16[4,128,128]{2,1,0:T(8,128)(2,1)S(1)}, bf16[4,128,128]{2,1,0:T(8,128)(2,1)}, u32[]{:S(2)}) copy-start(bf16[4,128,128]{2,1,0:T(8,128)(2,1)} %weight_ref.3) | copy-start | bytes 393220
  15.3 1.7 %collective-permute-start.3 = (bf16[1168,128]{1,0:T(8,128)(2,1)S(1)}, bf16[1168,128]{1,0:T(8,128)(2,1)S(1)}, u32[]{:S(2)}, u32[]{:S(2)}) collective-permute-start(bf16[1168,128]{1,0:T(8,128)(2,1)S(1)} %prefill.1.near_ref), channel_id=1, source_target_pairs={{0,1},{1,0},{2,3},{3,2},{4,5},{5,4},{6,7},{7,6},{8,9},{9,8},{10,11... | collective-permute-start | bytes 897032 | tf_op jit(solution)/shard_map/ppermute | solution.py:286
  17.8 0.6 %copy-start.1 = (bf16[4,4352]{1,0:T(4,128)(2,1)}, bf16[4,4352]{1,0:T(4,128)(2,1)S(1)}, u32[]{:S(2)}) copy-start(bf16[4,4352]{1,0:T(4,128)(2,1)S(1)} %get-tuple-element.11._.refs_0_) | copy-start | bytes 104452
  18.4 6.0 %collective-permute-start.4 = (bf16[4,4352]{1,0:T(4,128)(2,1)S(1)}, bf16[4,4352]{1,0:T(4,128)(2,1)S(1)}, u32[]{:S(2)}, u32[]{:S(2)}) collective-permute-start(bf16[4,4352]{1,0:T(4,128)(2,1)S(1)} %get-tuple-element.14), channel_id=1, source_target_pairs={{0,4},{4,8},{8,12},{12,0},{1,5},{5,9},{9,13},{13,1},{2,6},{6,10},{... | collective-permute-start | bytes 104456 | tf_op jit(solution)/shard_map/ppermute | solution.py:290
  19.1 5.4 %collective-permute-start.5 = (bf16[4,4352]{1,0:T(4,128)(2,1)S(1)}, bf16[4,4352]{1,0:T(4,128)(2,1)S(1)}, u32[]{:S(2)}, u32[]{:S(2)}) collective-permute-start(bf16[4,4352]{1,0:T(4,128)(2,1)S(1)} %get-tuple-element.15), channel_id=1, source_target_pairs={{0,8},{4,12},{8,0},{12,4},{1,9},{5,13},{9,1},{13,5},{2,10},{6,14},... | collective-permute-start | bytes 104456 | tf_op jit(solution)/shard_map/ppermute | solution.py:290
  19.4 5.4 %collective-permute-start.6 = (bf16[4,4352]{1,0:T(4,128)(2,1)S(1)}, bf16[4,4352]{1,0:T(4,128)(2,1)S(1)}, u32[]{:S(2)}, u32[]{:S(2)}) collective-permute-start(bf16[4,4352]{1,0:T(4,128)(2,1)S(1)} %get-tuple-element.16), channel_id=1, source_target_pairs={{0,12},{4,0},{8,4},{12,8},{1,13},{5,1},{9,5},{13,9},{2,14},{6,2},{... | collective-permute-start | bytes 104456 | tf_op jit(solution)/shard_map/ppermute | solution.py:290
  24.4 0.6 %copy-start.3 = (bf16[4,4352]{1,0:T(4,128)(2,1)}, bf16[4,4352]{1,0:T(4,128)(2,1)S(1)}, u32[]{:S(2)}) copy-start(bf16[4,4352]{1,0:T(4,128)(2,1)S(1)} %collective-permute-done.4.refs_1_) | copy-start | bytes 104452
  24.4 0.6 %copy-start.4 = (bf16[4,4352]{1,0:T(4,128)(2,1)}, bf16[4,4352]{1,0:T(4,128)(2,1)S(1)}, u32[]{:S(2)}) copy-start(bf16[4,4352]{1,0:T(4,128)(2,1)S(1)} %collective-permute-done.5.refs_2_) | copy-start | bytes 104452
  24.8 0.6 %copy-start.5 = (bf16[4,4352]{1,0:T(4,128)(2,1)}, bf16[4,4352]{1,0:T(4,128)(2,1)S(1)}, u32[]{:S(2)}) copy-start(bf16[4,4352]{1,0:T(4,128)(2,1)S(1)} %collective-permute-done.6.refs_3_) | copy-start | bytes 104452

commit v7 on v6

--- a/solution.py
+++ b/solution.py
@@ -11,6 +11,7 @@
 TAU = 10.0
 EPS = 1e-06
 BLOCK = 512
+AHEAD = 3
 NT = (((1,), (1,)), ((), ()))
 
 
@@ -42,9 +43,13 @@
                 pltpu.make_async_copy(values_ref.at[0, rows, :], values_at.at[rows, :], load_sem.at[1, c]),
             ]
         )
-        for load in loads[-1]:
-            load.start()
-
+
+    def fetch(c):
+        for priority, load in enumerate(loads[c]):
+            load.start(priority=priority)
+
+    for c in range(AHEAD):
+        fetch(c)
     state_ref[...] = jnp.zeros_like(state_ref)
     norm_ref[...] = jnp.zeros_like(norm_ref)
     wide_ref[...] = jnp.zeros_like(wide_ref)
@@ -74,6 +79,8 @@
         rows = slice(c * BLOCK, (c + 1) * BLOCK)
         for load in loads[c]:
             load.wait()
+        if c + AHEAD < chunks:
+            fetch(c + AHEAD)
         position = c * BLOCK + lax.broadcasted_iota(jnp.int32, (1, BLOCK), 1)
         live = position < begin
         for j in range(pairs):
@@ -230,12 +237,13 @@
     count, width = queries.shape
     return pl.pallas_call(
         own_kernel,
-        in_specs=[vmem] * 3 + [pl.BlockSpec(memory_space=pl.ANY)],
+        in_specs=[vmem] * 4,
         out_specs=[vmem, vmem],
         out_shape=[
             jax.ShapeDtypeStruct((count, width), jnp.float32),
             jax.ShapeDtypeStruct((count, head_size), jnp.float32),
         ],
+        compiler_params=pltpu.CompilerParams(vmem_limit_bytes=8 * 1024 * 1024),
         cost_estimate=pl.CostEstimate(
             flops=8 * count * width, bytes_accessed=8 * count * width, transcendentals=count * width // head_size
         ),
@@ -272,6 +280,7 @@
         in_specs=[vmem] * (3 + len(blocks)),
         out_specs=vmem,
         out_shape=jax.ShapeDtypeStruct(num.shape, jnp.bfloat16),
+        compiler_params=pltpu.CompilerParams(vmem_limit_bytes=8 * 1024 * 1024),
         name="finish",
     )(row_prompt.reshape(1, -1), num, weight, *blocks)
 

time: 27.3 us -> 23.4 us (0.86)
  Pallas kernels: 11.8 us -> 7.67 us
  waiting for transfers between devices: 2.4 us -> 3.79 us
  local copies, waits for them, and re-layouts: 1.23 us -> 0.02 us
    pallas_call x1, Pallas kernels: 7.61 us -> 5.75 us  [prefill(): pl.pallas_call(prefill_kernel, in_specs=[pl.BlockSpec(memory_space=pltpu....]
    pallas_call x1, Pallas kernels: 1.61 us -> 0.21 us  [own(): pl.pallas_call(own_kernel, in_specs=[vmem] * 4, out_specs=[vmem, vmem], o...]
    ppermute x3, waiting for transfers between devices: 0.95 us -> 2.34 us  [body(): lax.ppermute(results[k], 'sect', [(i, (i + k) % sects) for i in range(sec...]
    unnamed x12 -> x10, local copies, waits for them, and re-layouts: 1.23 us -> 0.02 us
    pallas_call x1, Pallas kernels: 1.73 us -> 0.86 us  [finish(): pl.pallas_call(finish_kernel, in_specs=[vmem] * (3 + len(blocks)), out_sp...]
  transfers between devices with their start and end apart: 7 -> 7, of which waited for: 3 -> 3; matrix products, arithmetic and copies ran while one was open for 0% -> 0% of each run, Pallas kernels for 34% -> 26%
where the time goes in v7:
time: 23.4 us; the launch traced here: 23.2 us
  starting transfers between devices  10.9 us (47%)
  Pallas kernels  7.67 us (33%)
  waiting for transfers between devices  3.79 us (16%)
  between operations  0.77 us (3%)
    ppermute x3, starting transfers between devices, body(): lax.ppermute(queries, 'sect', [((i + k) % sects, i) for i in range(sects)])  6.96 us
    pallas_call x1, Pallas kernels, prefill(): pl.pallas_call(prefill_kernel, in_specs=[pl.BlockSpec(memory_space=pltpu....  5.75 us
    ppermute x3, starting transfers between devices, body(): lax.ppermute(results[k], 'sect', [(i, (i + k) % sects) for i in range(sec...  3.88 us
    ppermute x3, waiting for transfers between devices, body(): lax.ppermute(results[k], 'sect', [(i, (i + k) % sects) for i in range(sec...  2.34 us
    ppermute x1, waiting for transfers between devices, body(): far = lax.ppermute(near, 'sub', [(0, 1), (1, 0)])  1.44 us
    pallas_call x1, Pallas kernels, finish(): pl.pallas_call(finish_kernel, in_specs=[vmem] * (3 + len(blocks)), out_sp...  0.86 us
    pallas_call x1, Pallas kernels, decode(): pl.pallas_call(decode_kernel, in_specs=[vmem] * 4, out_specs=[vmem] * par...  0.85 us
  transfers between devices with their start and end apart: 7, of which 3 were waited for; matrix products, arithmetic and copies ran while one was open for 0% of the time, Pallas kernels for 26%

profile of v7, /device:TPU:0, one launch (start us, length us, event | category | flops | bytes accessed | tf_op | source)
XLA Modules:
  0.0 23.2 jit_solution(14851947711941055251)
XLA Ops:
  0.0 3.0 %collective-permute-start.2 = (bf16[4,4096]{1,0:T(4,128)(2,1)}, bf16[4,4096]{1,0:T(4,128)(2,1)S(1)}, u32[]{:S(2)}, u32[]{:S(2)}) collective-permute-start(bf16[4,4096]{1,0:T(4,128)(2,1)} %queries_ref.1), channel_id=1, source_target_pairs={{12,0},{0,4},{4,8},{8,12},{13,1},{1,5},{5,9},{9,13},{14,2},{2,6},{... | collective-permute-start | bytes 98312 | tf_op jit(solution)/shard_map/ppermute | solution.py:292
  3.0 2.6 %collective-permute-start.1 = (bf16[4,4096]{1,0:T(4,128)(2,1)}, bf16[4,4096]{1,0:T(4,128)(2,1)S(1)}, u32[]{:S(2)}, u32[]{:S(2)}) collective-permute-start(bf16[4,4096]{1,0:T(4,128)(2,1)} %queries_ref.1), channel_id=1, source_target_pairs={{8,0},{12,4},{0,8},{4,12},{9,1},{13,5},{1,9},{5,13},{10,2},{14,6},... | collective-permute-start | bytes 98312 | tf_op jit(solution)/shard_map/ppermute | solution.py:292
  5.6 1.3 %collective-permute-start = (bf16[4,4096]{1,0:T(4,128)(2,1)}, bf16[4,4096]{1,0:T(4,128)(2,1)S(1)}, u32[]{:S(2)}, u32[]{:S(2)}) collective-permute-start(bf16[4,4096]{1,0:T(4,128)(2,1)} %queries_ref.1), channel_id=1, source_target_pairs={{4,0},{8,4},{12,8},{0,12},{5,1},{9,5},{13,9},{1,13},{6,2},{10,6},{... | collective-permute-start | bytes 98312 | tf_op jit(solution)/shard_map/ppermute | solution.py:292
  7.6 0.0 copy-start.1
  7.6 0.0 copy-start
  7.6 0.0 copy-start.2
  7.6 0.0 copy-start.3
  7.7 0.0 copy-start.4
  7.7 5.8 %prefill.1.near_ref = bf16[1168,128]{1,0:T(8,128)(2,1)S(1)} custom-call(s32[1]{0:T(128)S(6)} %copy.9.lengths_ref, bf16[1,4096,512]{2,1,0:T(8,128)(2,1)} %keys_ref.2, bf16[1,4096,512]{2,1,0:T(8,128)(2,1)} %values_ref.2, bf16[4,128,128]{2,1,0:T(8,128)(2,1)} %weight_ref.3), custom_call_target="tpu_custom_call" | custom-call | flops 1073741824 | bytes 8388608 | tf_op jit(solution)/shard_map/prefill/pallas_call | solution.py:120
  13.4 0.1 collective-permute-start.3
  13.5 0.0 collective-permute-done.2
  13.5 0.0 collective-permute-done.1
  13.5 0.0 collective-permute-done
  13.5 0.0 copy-done.1
  13.5 0.1 pad_maximum_fusion.rows_ref
  13.6 1.4 %collective-permute-done.3.far_ref = bf16[1168,128]{1,0:T(8,128)(2,1)S(1)} collective-permute-done((bf16[1168,128]{1,0:T(8,128)(2,1)S(1)}, bf16[1168,128]{1,0:T(8,128)(2,1)S(1)}, u32[]{:S(2)}, u32[]{:S(2)}) %collective-permute-start.3) | collective-permute-done | bytes 299040 | tf_op jit(solution)/shard_map/ppermute | solution.py:295
  15.1 0.0 copy-done
  15.1 0.8 %decode.1 = (bf16[4,4352]{1,0:T(4,128)(2,1)S(1)}, bf16[4,4352]{1,0:T(4,128)(2,1)S(1)}, bf16[4,4352]{1,0:T(4,128)(2,1)S(1)}, bf16[4,4352]{1,0:T(4,128)(2,1)S(1)}) custom-call(bf16[16,4096]{1,0:T(8,128)(2,1)S(1)} %pad_maximum_fusion.rows_ref, bf16[4,128,128]{2,1,0:T(8,128)(2,1)S(1)} %copy-done, bf16[1168,128]{1,0:T(8,128)(2,1)S(1)} %prefill.1.near_ref, ...), custom_call_target="tpu_custom_call" | custom-call | flops 83886080 | bytes 262144 | tf_op jit(solution)/shard_map/decode/pallas_call | solution.py:199
  15.9 0.7 %collective-permute-start.4 = (bf16[4,4352]{1,0:T(4,128)(2,1)S(1)}, bf16[4,4352]{1,0:T(4,128)(2,1)S(1)}, u32[]{:S(2)}, u32[]{:S(2)}) collective-permute-start(bf16[4,4352]{1,0:T(4,128)(2,1)S(1)} %get-tuple-element.14), channel_id=1, source_target_pairs={{0,4},{4,8},{8,12},{12,0},{1,5},{5,9},{9,13},{13,1},{2,6},{6,10},{... | collective-permute-start | bytes 104456 | tf_op jit(solution)/shard_map/ppermute | solution.py:299
  16.7 0.3 %collective-permute-start.5 = (bf16[4,4352]{1,0:T(4,128)(2,1)S(1)}, bf16[4,4352]{1,0:T(4,128)(2,1)S(1)}, u32[]{:S(2)}, u32[]{:S(2)}) collective-permute-start(bf16[4,4352]{1,0:T(4,128)(2,1)S(1)} %get-tuple-element.15), channel_id=1, source_target_pairs={{0,8},{4,12},{8,0},{12,4},{1,9},{5,13},{9,1},{13,5},{2,10},{6,14},... | collective-permute-start | bytes 104456 | tf_op jit(solution)/shard_map/ppermute | solution.py:299
  17.0 2.8 %collective-permute-start.6 = (bf16[4,4352]{1,0:T(4,128)(2,1)S(1)}, bf16[4,4352]{1,0:T(4,128)(2,1)S(1)}, u32[]{:S(2)}, u32[]{:S(2)}) collective-permute-start(bf16[4,4352]{1,0:T(4,128)(2,1)S(1)} %get-tuple-element.16), channel_id=1, source_target_pairs={{0,12},{4,0},{8,4},{12,8},{1,13},{5,1},{9,5},{13,9},{2,14},{6,2},{... | collective-permute-start | bytes 104456 | tf_op jit(solution)/shard_map/ppermute | solution.py:299
  19.8 0.0 copy-done.2
  19.8 0.0 copy-done.3
  19.8 0.2 own.1
  20.0 2.0 %collective-permute-done.4.refs_1_ = bf16[4,4352]{1,0:T(4,128)(2,1)S(1)} collective-permute-done((bf16[4,4352]{1,0:T(4,128)(2,1)S(1)}, bf16[4,4352]{1,0:T(4,128)(2,1)S(1)}, u32[]{:S(2)}, u32[]{:S(2)}) %collective-permute-start.4) | collective-permute-done | bytes 34848 | tf_op jit(solution)/shard_map/ppermute | solution.py:299
  22.0 0.0 collective-permute-done.5.refs_2_
  22.0 0.4 %collective-permute-done.6.refs_3_ = bf16[4,4352]{1,0:T(4,128)(2,1)S(1)} collective-permute-done((bf16[4,4352]{1,0:T(4,128)(2,1)S(1)}, bf16[4,4352]{1,0:T(4,128)(2,1)S(1)}, u32[]{:S(2)}, u32[]{:S(2)}) %collective-permute-start.6) | collective-permute-done | bytes 34848 | tf_op jit(solution)/shard_map/ppermute | solution.py:299
  22.4 0.0 copy-done.4
  22.4 0.9 %finish.1 = bf16[4,4096]{1,0:T(4,128)(2,1)} custom-call(s32[1,32]{1,0:T(1,128)S(1)} %bitcast.1, f32[4,4096]{1,0:T(4,128)S(1)} %get-tuple-element.12.num_ref, f32[4,128]{1,0:T(4,128)S(1)} %get-tuple-element.13.weight_ref, bf16[4,4352]{1,0:T(4,128)(2,1)S(1)} %get-tuple-element.11._.refs_0_, bf16[4,4352]{1,0:T(4,128)(2,1)S(1)} %collective-permute-done.4.refs_1_, ...), custom_call_target="tpu_custom_call" | custom-call | tf_op jit(solution)/shard_map/finish/pallas_call | solution.py:278
Async XLA Ops:
  0.0 13.5 %collective-permute-start.2 = (bf16[4,4096]{1,0:T(4,128)(2,1)}, bf16[4,4096]{1,0:T(4,128)(2,1)S(1)}, u32[]{:S(2)}, u32[]{:S(2)}) collective-permute-start(bf16[4,4096]{1,0:T(4,128)(2,1)} %queries_ref.1), channel_id=1, source_target_pairs={{12,0},{0,4},{4,8},{8,12},{13,1},{1,5},{5,9},{9,13},{14,2},{2,6},{... | collective-permute-start | bytes 98312 | tf_op jit(solution)/shard_map/ppermute | solution.py:292
  3.0 10.5 %collective-permute-start.1 = (bf16[4,4096]{1,0:T(4,128)(2,1)}, bf16[4,4096]{1,0:T(4,128)(2,1)S(1)}, u32[]{:S(2)}, u32[]{:S(2)}) collective-permute-start(bf16[4,4096]{1,0:T(4,128)(2,1)} %queries_ref.1), channel_id=1, source_target_pairs={{8,0},{12,4},{0,8},{4,12},{9,1},{13,5},{1,9},{5,13},{10,2},{14,6},... | collective-permute-start | bytes 98312 | tf_op jit(solution)/shard_map/ppermute | solution.py:292
  5.6 7.9 %collective-permute-start = (bf16[4,4096]{1,0:T(4,128)(2,1)}, bf16[4,4096]{1,0:T(4,128)(2,1)S(1)}, u32[]{:S(2)}, u32[]{:S(2)}) collective-permute-start(bf16[4,4096]{1,0:T(4,128)(2,1)} %queries_ref.1), channel_id=1, source_target_pairs={{4,0},{8,4},{12,8},{0,12},{5,1},{9,5},{13,9},{1,13},{6,2},{10,6},{... | collective-permute-start | bytes 98312 | tf_op jit(solution)/shard_map/ppermute | solution.py:292
  7.6 5.9 %copy-start.1 = (bf16[4,4096]{1,0:T(4,128)(2,1)S(1)}, bf16[4,4096]{1,0:T(4,128)(2,1)}, u32[]{:S(2)}) copy-start(bf16[4,4096]{1,0:T(4,128)(2,1)} %queries_ref.1) | copy-start | bytes 98308
  7.6 7.5 %copy-start = (bf16[4,128,128]{2,1,0:T(8,128)(2,1)S(1)}, bf16[4,128,128]{2,1,0:T(8,128)(2,1)}, u32[]{:S(2)}) copy-start(bf16[4,128,128]{2,1,0:T(8,128)(2,1)} %weight_ref.3) | copy-start | bytes 393220
  7.6 12.2 %copy-start.2 = (bf16[4,512]{1,0:T(4,128)(2,1)S(1)}, bf16[4,512]{1,0:T(4,128)(2,1)}, u32[]{:S(2)}) copy-start(bf16[4,512]{1,0:T(4,128)(2,1)} %keys_ref.3) | copy-start | bytes 12292
  7.6 12.2 %copy-start.3 = (bf16[4,512]{1,0:T(4,128)(2,1)S(1)}, bf16[4,512]{1,0:T(4,128)(2,1)}, u32[]{:S(2)}) copy-start(bf16[4,512]{1,0:T(4,128)(2,1)} %values_ref.3) | copy-start | bytes 12292
  7.7 14.7 %copy-start.4 = (s32[32]{0:T(128)S(1)}, s32[32]{0:T(128)}, u32[]{:S(2)}) copy-start(s32[32]{0:T(128)} %param.15) | copy-start | bytes 388
  13.4 1.7 %collective-permute-start.3 = (bf16[1168,128]{1,0:T(8,128)(2,1)S(1)}, bf16[1168,128]{1,0:T(8,128)(2,1)S(1)}, u32[]{:S(2)}, u32[]{:S(2)}) collective-permute-start(bf16[1168,128]{1,0:T(8,128)(2,1)S(1)} %prefill.1.near_ref), channel_id=1, source_target_pairs={{0,1},{1,0},{2,3},{3,2},{4,5},{5,4},{6,7},{7,6},{8,9},{9,8},{10,11... | collective-permute-start | bytes 897032 | tf_op jit(solution)/shard_map/ppermute | solution.py:295
  15.9 6.1 %collective-permute-start.4 = (bf16[4,4352]{1,0:T(4,128)(2,1)S(1)}, bf16[4,4352]{1,0:T(4,128)(2,1)S(1)}, u32[]{:S(2)}, u32[]{:S(2)}) collective-permute-start(bf16[4,4352]{1,0:T(4,128)(2,1)S(1)} %get-tuple-element.14), channel_id=1, source_target_pairs={{0,4},{4,8},{8,12},{12,0},{1,5},{5,9},{9,13},{13,1},{2,6},{6,10},{... | collective-permute-start | bytes 104456 | tf_op jit(solution)/shard_map/ppermute | solution.py:299
  16.7 5.4 %collective-permute-start.5 = (bf16[4,4352]{1,0:T(4,128)(2,1)S(1)}, bf16[4,4352]{1,0:T(4,128)(2,1)S(1)}, u32[]{:S(2)}, u32[]{:S(2)}) collective-permute-start(bf16[4,4352]{1,0:T(4,128)(2,1)S(1)} %get-tuple-element.15), channel_id=1, source_target_pairs={{0,8},{4,12},{8,0},{12,4},{1,9},{5,13},{9,1},{13,5},{2,10},{6,14},... | collective-permute-start | bytes 104456 | tf_op jit(solution)/shard_map/ppermute | solution.py:299
  17.0 5.4 %collective-permute-start.6 = (bf16[4,4352]{1,0:T(4,128)(2,1)S(1)}, bf16[4,4352]{1,0:T(4,128)(2,1)S(1)}, u32[]{:S(2)}, u32[]{:S(2)}) collective-permute-start(bf16[4,4352]{1,0:T(4,128)(2,1)S(1)} %get-tuple-element.16), channel_id=1, source_target_pairs={{0,12},{4,0},{8,4},{12,8},{1,13},{5,1},{9,5},{13,9},{2,14},{6,2},{... | collective-permute-start | bytes 104456 | tf_op jit(solution)/shard_map/ppermute | solution.py:299

commit v8 on v7

--- a/solution.py
+++ b/solution.py
@@ -13,6 +13,7 @@
 BLOCK = 512
 AHEAD = 3
 NT = (((1,), (1,)), ((), ()))
+TN = (((0,), (0,)), ((), ()))
 
 
 def feature(proj):
@@ -56,8 +57,7 @@
     get_weight.wait()
     for g in range(heads):
         half = g % 2
-        turned = weight_at[g].astype(jnp.float32).T.astype(jnp.bfloat16)
-        wide_ref[g // 2, half * feats : (half + 1) * feats, half * head_size : (half + 1) * head_size] = turned
+        wide_ref[g // 2, half * head_size : (half + 1) * head_size, half * feats : (half + 1) * feats] = weight_at[g]
 
     begin = lengths_ref[0] - WINDOW - lax.axis_index("sub") * span
     first = jnp.clip(begin, 0, span - SLAB)
@@ -81,27 +81,23 @@
             load.wait()
         if c + AHEAD < chunks:
             fetch(c + AHEAD)
-        position = c * BLOCK + lax.broadcasted_iota(jnp.int32, (1, BLOCK), 1)
+        position = c * BLOCK + lax.broadcasted_iota(jnp.int32, (BLOCK, 1), 0)
         live = position < begin
         for j in range(pairs):
             cols = slice(j * 2 * head_size, (j + 1) * 2 * head_size)
-            proj = lax.dot_general(wide_ref[j], keys_at[rows, cols], NT, preferred_element_type=jnp.float32)
+            proj = jnp.dot(keys_at[rows, cols], wide_ref[j], preferred_element_type=jnp.float32)
             mapped = jnp.where(live, feature(proj), 0.0)
-            total = norm_ref[j]
-            for k in range(BLOCK // 128):
-                total = total + mapped[:, k * 128 : (k + 1) * 128]
-            norm_ref[j] = total
-            state_ref[j] += jnp.dot(
-                mapped.astype(jnp.bfloat16), values_at[rows, cols], preferred_element_type=jnp.float32
+            norm_ref[j] += jnp.sum(mapped.reshape(BLOCK // 8, 8, 2 * feats), axis=0)
+            state_ref[j] += lax.dot_general(
+                values_at[rows, cols], mapped.astype(jnp.bfloat16), TN, preferred_element_type=jnp.float32
             )
 
     tile = []
     for g in range(heads):
         half = g % 2
-        part = state_ref[g // 2, half * feats : (half + 1) * feats, half * head_size : (half + 1) * head_size]
-        out_ref[g * feats : (g + 1) * feats, :] = part.astype(jnp.bfloat16)
-        sums = norm_ref[g // 2, half * feats : (half + 1) * feats, :]
-        tile.append(jnp.sum(sums.T, axis=0, keepdims=True))
+        part = state_ref[g // 2, half * head_size : (half + 1) * head_size, half * feats : (half + 1) * feats]
+        out_ref[g * head_size : (g + 1) * head_size, :] = part.astype(jnp.bfloat16)
+        tile.append(jnp.sum(norm_ref[g // 2, :, half * feats : (half + 1) * feats], axis=0, keepdims=True))
     slot = first + lax.broadcasted_iota(jnp.int32, (1, head_size), 1)
     tile.append(jnp.zeros((MASK_ROW - heads, head_size), jnp.float32))
     tile.append(jnp.where((slot >= begin) & (slot < begin + WINDOW), 1.0, 0.0))
@@ -126,9 +122,9 @@
             pltpu.VMEM((span, width), jnp.bfloat16),
             pltpu.VMEM((span, width), jnp.bfloat16),
             pltpu.VMEM(weight.shape, jnp.bfloat16),
-            pltpu.VMEM((heads // 2, 2 * feats, 2 * head_size), jnp.bfloat16),
-            pltpu.VMEM((heads // 2, 2 * feats, 2 * head_size), jnp.float32),
-            pltpu.VMEM((heads // 2, 2 * feats, 128), jnp.float32),
+            pltpu.VMEM((heads // 2, 2 * head_size, 2 * feats), jnp.bfloat16),
+            pltpu.VMEM((heads // 2, 2 * head_size, 2 * feats), jnp.float32),
+            pltpu.VMEM((heads // 2, 8, 2 * feats), jnp.float32),
             pltpu.SemaphoreType.DMA,
             pltpu.SemaphoreType.DMA((2, span // BLOCK)),
             pltpu.SemaphoreType.DMA((2, heads)),
@@ -164,7 +160,9 @@
         scale = (TAU / head_size) * lax.rsqrt(jnp.mean(wide * wide, axis=-1, keepdims=True) + EPS)
         num, den, linear = 0.0, 0.0, 0.0
         for ref, tile in zip(halves, tiles):
-            linear += jnp.dot(phi, ref[g * feats : (g + 1) * feats, :], preferred_element_type=jnp.float32)
+            linear += lax.dot_general(
+                phi, ref[g * head_size : (g + 1) * head_size, :], NT, preferred_element_type=jnp.float32
+            )
             at = tile_at + 16 + g * SLAB
             keys = ref[at : at + SLAB, :]
             at += heads * SLAB

time: 23.4 us -> 24 us (1.026)
  Pallas kernels: 7.67 us -> 8.3 us
    pallas_call x1, Pallas kernels: 5.75 us -> 6.28 us  [prefill(): pl.pallas_call(prefill_kernel, in_specs=[pl.BlockSpec(memory_space=pltpu....]
  transfers between devices with their start and end apart: 7 -> 7, of which waited for: 3 -> 3; matrix products, arithmetic and copies ran while one was open for 0% -> 0% of each run, Pallas kernels for 26% -> 27%
where the time goes in v8:
time: 24 us; the launch traced here: 23.9 us
  starting transfers between devices  10.9 us (45%)
  Pallas kernels  8.3 us (35%)
  waiting for transfers between devices  3.79 us (16%)
  between operations  0.77 us (3%)
    ppermute x3, starting transfers between devices, body(): lax.ppermute(queries, 'sect', [((i + k) % sects, i) for i in range(sects)])  6.96 us
    pallas_call x1, Pallas kernels, prefill(): pl.pallas_call(prefill_kernel, in_specs=[pl.BlockSpec(memory_space=pltpu....  6.28 us
    ppermute x3, starting transfers between devices, body(): lax.ppermute(results[k], 'sect', [(i, (i + k) % sects) for i in range(sec...  3.88 us
    ppermute x3, waiting for transfers between devices, body(): lax.ppermute(results[k], 'sect', [(i, (i + k) % sects) for i in range(sec...  2.34 us
    ppermute x1, waiting for transfers between devices, body(): far = lax.ppermute(near, 'sub', [(0, 1), (1, 0)])  1.44 us
    pallas_call x1, Pallas kernels, decode(): pl.pallas_call(decode_kernel, in_specs=[vmem] * 4, out_specs=[vmem] * par...  0.94 us
    pallas_call x1, Pallas kernels, finish(): pl.pallas_call(finish_kernel, in_specs=[vmem] * (3 + len(blocks)), out_sp...  0.86 us
  transfers between devices with their start and end apart: 7, of which 3 were waited for; matrix products, arithmetic and copies ran while one was open for 0% of the time, Pallas kernels for 27%

profile of v8, /device:TPU:0, one launch (start us, length us, event | category | flops | bytes accessed | tf_op | source)
XLA Modules:
  0.0 23.9 jit_solution(7305411854893099319)
XLA Ops:
  0.0 3.0 %collective-permute-start.2 = (bf16[4,4096]{1,0:T(4,128)(2,1)}, bf16[4,4096]{1,0:T(4,128)(2,1)S(1)}, u32[]{:S(2)}, u32[]{:S(2)}) collective-permute-start(bf16[4,4096]{1,0:T(4,128)(2,1)} %queries_ref.1), channel_id=1, source_target_pairs={{12,0},{0,4},{4,8},{8,12},{13,1},{1,5},{5,9},{9,13},{14,2},{2,6},{... | collective-permute-start | bytes 98312 | tf_op jit(solution)/shard_map/ppermute | solution.py:290
  3.0 2.6 %collective-permute-start.1 = (bf16[4,4096]{1,0:T(4,128)(2,1)}, bf16[4,4096]{1,0:T(4,128)(2,1)S(1)}, u32[]{:S(2)}, u32[]{:S(2)}) collective-permute-start(bf16[4,4096]{1,0:T(4,128)(2,1)} %queries_ref.1), channel_id=1, source_target_pairs={{8,0},{12,4},{0,8},{4,12},{9,1},{13,5},{1,9},{5,13},{10,2},{14,6},... | collective-permute-start | bytes 98312 | tf_op jit(solution)/shard_map/ppermute | solution.py:290
  5.6 1.3 %collective-permute-start = (bf16[4,4096]{1,0:T(4,128)(2,1)}, bf16[4,4096]{1,0:T(4,128)(2,1)S(1)}, u32[]{:S(2)}, u32[]{:S(2)}) collective-permute-start(bf16[4,4096]{1,0:T(4,128)(2,1)} %queries_ref.1), channel_id=1, source_target_pairs={{4,0},{8,4},{12,8},{0,12},{5,1},{9,5},{13,9},{1,13},{6,2},{10,6},{... | collective-permute-start | bytes 98312 | tf_op jit(solution)/shard_map/ppermute | solution.py:290
  7.6 0.0 copy-start.1
  7.6 0.0 copy-start
  7.6 0.0 copy-start.2
  7.6 0.0 copy-start.3
  7.7 0.0 copy-start.4
  7.7 6.3 %prefill.1.near_ref = bf16[1168,128]{1,0:T(8,128)(2,1)S(1)} custom-call(s32[1]{0:T(128)S(6)} %copy.9.lengths_ref, bf16[1,4096,512]{2,1,0:T(8,128)(2,1)} %keys_ref.2, bf16[1,4096,512]{2,1,0:T(8,128)(2,1)} %values_ref.2, bf16[4,128,128]{2,1,0:T(8,128)(2,1)} %weight_ref.3), custom_call_target="tpu_custom_call" | custom-call | flops 1073741824 | bytes 8388608 | tf_op jit(solution)/shard_map/prefill/pallas_call | solution.py:116
  13.9 0.1 collective-permute-start.3
  14.0 0.0 collective-permute-done.2
  14.0 0.0 collective-permute-done.1
  14.0 0.0 collective-permute-done
  14.1 0.0 copy-done.1
  14.1 0.1 pad_maximum_fusion.rows_ref
  14.2 1.4 %collective-permute-done.3.far_ref = bf16[1168,128]{1,0:T(8,128)(2,1)S(1)} collective-permute-done((bf16[1168,128]{1,0:T(8,128)(2,1)S(1)}, bf16[1168,128]{1,0:T(8,128)(2,1)S(1)}, u32[]{:S(2)}, u32[]{:S(2)}) %collective-permute-start.3) | collective-permute-done | bytes 299040 | tf_op jit(solution)/shard_map/ppermute | solution.py:293
  15.6 0.0 copy-done
  15.6 0.9 %decode.1 = (bf16[4,4352]{1,0:T(4,128)(2,1)S(1)}, bf16[4,4352]{1,0:T(4,128)(2,1)S(1)}, bf16[4,4352]{1,0:T(4,128)(2,1)S(1)}, bf16[4,4352]{1,0:T(4,128)(2,1)S(1)}) custom-call(bf16[16,4096]{1,0:T(8,128)(2,1)S(1)} %pad_maximum_fusion.rows_ref, bf16[4,128,128]{2,1,0:T(8,128)(2,1)S(1)} %copy-done, bf16[1168,128]{1,0:T(8,128)(2,1)S(1)} %prefill.1.near_ref, ...), custom_call_target="tpu_custom_call" | custom-call | flops 83886080 | bytes 262144 | tf_op jit(solution)/shard_map/decode/pallas_call | solution.py:197
  16.6 0.7 %collective-permute-start.4 = (bf16[4,4352]{1,0:T(4,128)(2,1)S(1)}, bf16[4,4352]{1,0:T(4,128)(2,1)S(1)}, u32[]{:S(2)}, u32[]{:S(2)}) collective-permute-start(bf16[4,4352]{1,0:T(4,128)(2,1)S(1)} %get-tuple-element.14), channel_id=1, source_target_pairs={{0,4},{4,8},{8,12},{12,0},{1,5},{5,9},{9,13},{13,1},{2,6},{6,10},{... | collective-permute-start | bytes 104456 | tf_op jit(solution)/shard_map/ppermute | solution.py:297
  17.3 0.3 %collective-permute-start.5 = (bf16[4,4352]{1,0:T(4,128)(2,1)S(1)}, bf16[4,4352]{1,0:T(4,128)(2,1)S(1)}, u32[]{:S(2)}, u32[]{:S(2)}) collective-permute-start(bf16[4,4352]{1,0:T(4,128)(2,1)S(1)} %get-tuple-element.15), channel_id=1, source_target_pairs={{0,8},{4,12},{8,0},{12,4},{1,9},{5,13},{9,1},{13,5},{2,10},{6,14},... | collective-permute-start | bytes 104456 | tf_op jit(solution)/shard_map/ppermute | solution.py:297
  17.6 2.8 %collective-permute-start.6 = (bf16[4,4352]{1,0:T(4,128)(2,1)S(1)}, bf16[4,4352]{1,0:T(4,128)(2,1)S(1)}, u32[]{:S(2)}, u32[]{:S(2)}) collective-permute-start(bf16[4,4352]{1,0:T(4,128)(2,1)S(1)} %get-tuple-element.16), channel_id=1, source_target_pairs={{0,12},{4,0},{8,4},{12,8},{1,13},{5,1},{9,5},{13,9},{2,14},{6,2},{... | collective-permute-start | bytes 104456 | tf_op jit(solution)/shard_map/ppermute | solution.py:297
  20.4 0.0 copy-done.2
  20.4 0.0 copy-done.3
  20.4 0.2 own.1
  20.7 2.0 %collective-permute-done.4.refs_1_ = bf16[4,4352]{1,0:T(4,128)(2,1)S(1)} collective-permute-done((bf16[4,4352]{1,0:T(4,128)(2,1)S(1)}, bf16[4,4352]{1,0:T(4,128)(2,1)S(1)}, u32[]{:S(2)}, u32[]{:S(2)}) %collective-permute-start.4) | collective-permute-done | bytes 34848 | tf_op jit(solution)/shard_map/ppermute | solution.py:297
  22.6 0.0 collective-permute-done.5.refs_2_
  22.6 0.4 %collective-permute-done.6.refs_3_ = bf16[4,4352]{1,0:T(4,128)(2,1)S(1)} collective-permute-done((bf16[4,4352]{1,0:T(4,128)(2,1)S(1)}, bf16[4,4352]{1,0:T(4,128)(2,1)S(1)}, u32[]{:S(2)}, u32[]{:S(2)}) %collective-permute-start.6) | collective-permute-done | bytes 34848 | tf_op jit(solution)/shard_map/ppermute | solution.py:297
  23.0 0.0 copy-done.4
  23.0 0.9 %finish.1 = bf16[4,4096]{1,0:T(4,128)(2,1)} custom-call(s32[1,32]{1,0:T(1,128)S(1)} %bitcast.1, f32[4,4096]{1,0:T(4,128)S(1)} %get-tuple-element.12.num_ref, f32[4,128]{1,0:T(4,128)S(1)} %get-tuple-element.13.weight_ref, bf16[4,4352]{1,0:T(4,128)(2,1)S(1)} %get-tuple-element.11._.refs_0_, bf16[4,4352]{1,0:T(4,128)(2,1)S(1)} %collective-permute-done.4.refs_1_, ...), custom_call_target="tpu_custom_call" | custom-call | tf_op jit(solution)/shard_map/finish/pallas_call | solution.py:276
Async XLA Ops:
  0.0 14.0 %collective-permute-start.2 = (bf16[4,4096]{1,0:T(4,128)(2,1)}, bf16[4,4096]{1,0:T(4,128)(2,1)S(1)}, u32[]{:S(2)}, u32[]{:S(2)}) collective-permute-start(bf16[4,4096]{1,0:T(4,128)(2,1)} %queries_ref.1), channel_id=1, source_target_pairs={{12,0},{0,4},{4,8},{8,12},{13,1},{1,5},{5,9},{9,13},{14,2},{2,6},{... | collective-permute-start | bytes 98312 | tf_op jit(solution)/shard_map/ppermute | solution.py:290
  3.0 11.0 %collective-permute-start.1 = (bf16[4,4096]{1,0:T(4,128)(2,1)}, bf16[4,4096]{1,0:T(4,128)(2,1)S(1)}, u32[]{:S(2)}, u32[]{:S(2)}) collective-permute-start(bf16[4,4096]{1,0:T(4,128)(2,1)} %queries_ref.1), channel_id=1, source_target_pairs={{8,0},{12,4},{0,8},{4,12},{9,1},{13,5},{1,9},{5,13},{10,2},{14,6},... | collective-permute-start | bytes 98312 | tf_op jit(solution)/shard_map/ppermute | solution.py:290
  5.6 8.4 %collective-permute-start = (bf16[4,4096]{1,0:T(4,128)(2,1)}, bf16[4,4096]{1,0:T(4,128)(2,1)S(1)}, u32[]{:S(2)}, u32[]{:S(2)}) collective-permute-start(bf16[4,4096]{1,0:T(4,128)(2,1)} %queries_ref.1), channel_id=1, source_target_pairs={{4,0},{8,4},{12,8},{0,12},{5,1},{9,5},{13,9},{1,13},{6,2},{10,6},{... | collective-permute-start | bytes 98312 | tf_op jit(solution)/shard_map/ppermute | solution.py:290
  7.6 6.4 %copy-start.1 = (bf16[4,4096]{1,0:T(4,128)(2,1)S(1)}, bf16[4,4096]{1,0:T(4,128)(2,1)}, u32[]{:S(2)}) copy-start(bf16[4,4096]{1,0:T(4,128)(2,1)} %queries_ref.1) | copy-start | bytes 98308
  7.6 8.0 %copy-start = (bf16[4,128,128]{2,1,0:T(8,128)(2,1)S(1)}, bf16[4,128,128]{2,1,0:T(8,128)(2,1)}, u32[]{:S(2)}) copy-start(bf16[4,128,128]{2,1,0:T(8,128)(2,1)} %weight_ref.3) | copy-start | bytes 393220
  7.6 12.8 %copy-start.2 = (bf16[4,512]{1,0:T(4,128)(2,1)S(1)}, bf16[4,512]{1,0:T(4,128)(2,1)}, u32[]{:S(2)}) copy-start(bf16[4,512]{1,0:T(4,128)(2,1)} %keys_ref.3) | copy-start | bytes 12292
  7.6 12.8 %copy-start.3 = (bf16[4,512]{1,0:T(4,128)(2,1)S(1)}, bf16[4,512]{1,0:T(4,128)(2,1)}, u32[]{:S(2)}) copy-start(bf16[4,512]{1,0:T(4,128)(2,1)} %values_ref.3) | copy-start | bytes 12292
  7.7 15.3 %copy-start.4 = (s32[32]{0:T(128)S(1)}, s32[32]{0:T(128)}, u32[]{:S(2)}) copy-start(s32[32]{0:T(128)} %param.15) | copy-start | bytes 388
  13.9 1.7 %collective-permute-start.3 = (bf16[1168,128]{1,0:T(8,128)(2,1)S(1)}, bf16[1168,128]{1,0:T(8,128)(2,1)S(1)}, u32[]{:S(2)}, u32[]{:S(2)}) collective-permute-start(bf16[1168,128]{1,0:T(8,128)(2,1)S(1)} %prefill.1.near_ref), channel_id=1, source_target_pairs={{0,1},{1,0},{2,3},{3,2},{4,5},{5,4},{6,7},{7,6},{8,9},{9,8},{10,11... | collective-permute-start | bytes 897032 | tf_op jit(solution)/shard_map/ppermute | solution.py:293
  16.6 6.1 %collective-permute-start.4 = (bf16[4,4352]{1,0:T(4,128)(2,1)S(1)}, bf16[4,4352]{1,0:T(4,128)(2,1)S(1)}, u32[]{:S(2)}, u32[]{:S(2)}) collective-permute-start(bf16[4,4352]{1,0:T(4,128)(2,1)S(1)} %get-tuple-element.14), channel_id=1, source_target_pairs={{0,4},{4,8},{8,12},{12,0},{1,5},{5,9},{9,13},{13,1},{2,6},{6,10},{... | collective-permute-start | bytes 104456 | tf_op jit(solution)/shard_map/ppermute | solution.py:297
  17.3 5.4 %collective-permute-start.5 = (bf16[4,4352]{1,0:T(4,128)(2,1)S(1)}, bf16[4,4352]{1,0:T(4,128)(2,1)S(1)}, u32[]{:S(2)}, u32[]{:S(2)}) collective-permute-start(bf16[4,4352]{1,0:T(4,128)(2,1)S(1)} %get-tuple-element.15), channel_id=1, source_target_pairs={{0,8},{4,12},{8,0},{12,4},{1,9},{5,13},{9,1},{13,5},{2,10},{6,14},... | collective-permute-start | bytes 104456 | tf_op jit(solution)/shard_map/ppermute | solution.py:297
  17.6 5.4 %collective-permute-start.6 = (bf16[4,4352]{1,0:T(4,128)(2,1)S(1)}, bf16[4,4352]{1,0:T(4,128)(2,1)S(1)}, u32[]{:S(2)}, u32[]{:S(2)}) collective-permute-start(bf16[4,4352]{1,0:T(4,128)(2,1)S(1)} %get-tuple-element.16), channel_id=1, source_target_pairs={{0,12},{4,0},{8,4},{12,8},{1,13},{5,1},{9,5},{13,9},{2,14},{6,2},{... | collective-permute-start | bytes 104456 | tf_op jit(solution)/shard_map/ppermute | solution.py:297

commit v9 on v7

--- a/solution.py
+++ b/solution.py
@@ -25,7 +25,7 @@
 
 def prefill_kernel(
     lengths_ref, keys_ref, values_ref, weight_ref, out_ref,
-    keys_at, values_at, weight_at, wide_ref, state_ref, norm_ref,
+    keys_at, values_at, weight_at, wide_ref, proj_ref, state_ref, norm_ref,
     weight_sem, load_sem, slab_sem,
 ):
     heads, head_size, feats = weight_ref.shape
@@ -75,25 +75,40 @@
             )
             slabs[-1].start()
 
-    for c in range(chunks):
-        rows = slice(c * BLOCK, (c + 1) * BLOCK)
+    def project(c):
         for load in loads[c]:
             load.wait()
         if c + AHEAD < chunks:
             fetch(c + AHEAD)
+        for j in range(pairs):
+            proj = lax.dot_general(
+                wide_ref[j],
+                keys_at[c * BLOCK : (c + 1) * BLOCK, j * 2 * head_size : (j + 1) * 2 * head_size],
+                NT,
+                preferred_element_type=jnp.float32,
+            )
+            proj_ref[c % 2, j] = proj.astype(jnp.bfloat16)
+
+    def collect(c):
         position = c * BLOCK + lax.broadcasted_iota(jnp.int32, (1, BLOCK), 1)
-        live = position < begin
+        live = jnp.where(position < begin, 1.0, 0.0).astype(jnp.bfloat16)
         for j in range(pairs):
-            cols = slice(j * 2 * head_size, (j + 1) * 2 * head_size)
-            proj = lax.dot_general(wide_ref[j], keys_at[rows, cols], NT, preferred_element_type=jnp.float32)
-            mapped = jnp.where(live, feature(proj), 0.0)
-            total = norm_ref[j]
-            for k in range(BLOCK // 128):
-                total = total + mapped[:, k * 128 : (k + 1) * 128]
-            norm_ref[j] = total
+            mapped = feature(proj_ref[c % 2, j]) * live
+            some = [mapped[:, k * 128 : (k + 1) * 128] for k in range(BLOCK // 128)]
+            while len(some) > 1:
+                some = [x + y for x, y in zip(some[::2], some[1::2])]
+            norm_ref[j] += some[0].astype(jnp.float32)
             state_ref[j] += jnp.dot(
-                mapped.astype(jnp.bfloat16), values_at[rows, cols], preferred_element_type=jnp.float32
+                mapped,
+                values_at[c * BLOCK : (c + 1) * BLOCK, j * 2 * head_size : (j + 1) * 2 * head_size],
+                preferred_element_type=jnp.float32,
             )
+
+    project(0)
+    for c in range(chunks):
+        if c + 1 < chunks:
+            project(c + 1)
+        collect(c)
 
     tile = []
     for g in range(heads):
@@ -127,6 +142,7 @@
             pltpu.VMEM((span, width), jnp.bfloat16),
             pltpu.VMEM(weight.shape, jnp.bfloat16),
             pltpu.VMEM((heads // 2, 2 * feats, 2 * head_size), jnp.bfloat16),
+            pltpu.VMEM((2, heads // 2, 2 * feats, BLOCK), jnp.bfloat16),
             pltpu.VMEM((heads // 2, 2 * feats, 2 * head_size), jnp.float32),
             pltpu.VMEM((heads // 2, 2 * feats, 128), jnp.float32),
             pltpu.SemaphoreType.DMA,

time: 23.4 us -> 23.2 us (level)
  transfers between devices with their start and end apart: 7 -> 7, of which waited for: 3 -> 3; matrix products, arithmetic and copies ran while one was open for 0% -> 0% of each run, Pallas kernels for 26% -> 25%
where the time goes in v9:
time: 23.2 us; the launch traced here: 23 us
  starting transfers between devices  10.9 us (47%)
  Pallas kernels  7.47 us (32%)
  waiting for transfers between devices  3.79 us (16%)
  between operations  0.77 us (3%)
    ppermute x3, starting transfers between devices, body(): lax.ppermute(queries, 'sect', [((i + k) % sects, i) for i in range(sects)])  6.96 us
    pallas_call x1, Pallas kernels, prefill(): pl.pallas_call(prefill_kernel, in_specs=[pl.BlockSpec(memory_space=pltpu....  5.55 us
    ppermute x3, starting transfers between devices, body(): lax.ppermute(results[k], 'sect', [(i, (i + k) % sects) for i in range(sec...  3.88 us
    ppermute x3, waiting for transfers between devices, body(): lax.ppermute(results[k], 'sect', [(i, (i + k) % sects) for i in range(sec...  2.34 us
    ppermute x1, waiting for transfers between devices, body(): far = lax.ppermute(near, 'sub', [(0, 1), (1, 0)])  1.44 us
    pallas_call x1, Pallas kernels, finish(): pl.pallas_call(finish_kernel, in_specs=[vmem] * (3 + len(blocks)), out_sp...  0.86 us
    pallas_call x1, Pallas kernels, decode(): pl.pallas_call(decode_kernel, in_specs=[vmem] * 4, out_specs=[vmem] * par...  0.85 us
  transfers between devices with their start and end apart: 7, of which 3 were waited for; matrix products, arithmetic and copies ran while one was open for 0% of the time, Pallas kernels for 25%

profile of v9, /device:TPU:0, one launch (start us, length us, event | category | flops | bytes accessed | tf_op | source)
XLA Modules:
  0.0 23.0 jit_solution(2628431350566999982)
XLA Ops:
  0.0 3.0 %collective-permute-start.2 = (bf16[4,4096]{1,0:T(4,128)(2,1)}, bf16[4,4096]{1,0:T(4,128)(2,1)S(1)}, u32[]{:S(2)}, u32[]{:S(2)}) collective-permute-start(bf16[4,4096]{1,0:T(4,128)(2,1)} %queries_ref.1), channel_id=1, source_target_pairs={{12,0},{0,4},{4,8},{8,12},{13,1},{1,5},{5,9},{9,13},{14,2},{2,6},{... | collective-permute-start | bytes 98312 | tf_op jit(solution)/shard_map/ppermute | solution.py:308
  3.0 2.6 %collective-permute-start.1 = (bf16[4,4096]{1,0:T(4,128)(2,1)}, bf16[4,4096]{1,0:T(4,128)(2,1)S(1)}, u32[]{:S(2)}, u32[]{:S(2)}) collective-permute-start(bf16[4,4096]{1,0:T(4,128)(2,1)} %queries_ref.1), channel_id=1, source_target_pairs={{8,0},{12,4},{0,8},{4,12},{9,1},{13,5},{1,9},{5,13},{10,2},{14,6},... | collective-permute-start | bytes 98312 | tf_op jit(solution)/shard_map/ppermute | solution.py:308
  5.6 1.3 %collective-permute-start = (bf16[4,4096]{1,0:T(4,128)(2,1)}, bf16[4,4096]{1,0:T(4,128)(2,1)S(1)}, u32[]{:S(2)}, u32[]{:S(2)}) collective-permute-start(bf16[4,4096]{1,0:T(4,128)(2,1)} %queries_ref.1), channel_id=1, source_target_pairs={{4,0},{8,4},{12,8},{0,12},{5,1},{9,5},{13,9},{1,13},{6,2},{10,6},{... | collective-permute-start | bytes 98312 | tf_op jit(solution)/shard_map/ppermute | solution.py:308
  7.6 0.0 copy-start.1
  7.6 0.0 copy-start
  7.6 0.0 copy-start.2
  7.6 0.0 copy-start.3
  7.7 0.0 copy-start.4
  7.7 5.5 %prefill.1.near_ref = bf16[1168,128]{1,0:T(8,128)(2,1)S(1)} custom-call(s32[1]{0:T(128)S(6)} %copy.9.lengths_ref, bf16[1,4096,512]{2,1,0:T(8,128)(2,1)} %keys_ref.2, bf16[1,4096,512]{2,1,0:T(8,128)(2,1)} %values_ref.2, bf16[4,128,128]{2,1,0:T(8,128)(2,1)} %weight_ref.3), custom_call_target="tpu_custom_call" | custom-call | flops 1073741824 | bytes 8388608 | tf_op jit(solution)/shard_map/prefill/pallas_call | solution.py:135
  13.2 0.1 collective-permute-start.3
  13.3 0.0 collective-permute-done.2
  13.3 0.0 collective-permute-done.1
  13.3 0.0 collective-permute-done
  13.3 0.0 copy-done.1
  13.3 0.1 pad_maximum_fusion.rows_ref
  13.4 1.4 %collective-permute-done.3.far_ref = bf16[1168,128]{1,0:T(8,128)(2,1)S(1)} collective-permute-done((bf16[1168,128]{1,0:T(8,128)(2,1)S(1)}, bf16[1168,128]{1,0:T(8,128)(2,1)S(1)}, u32[]{:S(2)}, u32[]{:S(2)}) %collective-permute-start.3) | collective-permute-done | bytes 299040 | tf_op jit(solution)/shard_map/ppermute | solution.py:311
  14.9 0.0 copy-done
  14.9 0.8 %decode.1 = (bf16[4,4352]{1,0:T(4,128)(2,1)S(1)}, bf16[4,4352]{1,0:T(4,128)(2,1)S(1)}, bf16[4,4352]{1,0:T(4,128)(2,1)S(1)}, bf16[4,4352]{1,0:T(4,128)(2,1)S(1)}) custom-call(bf16[16,4096]{1,0:T(8,128)(2,1)S(1)} %pad_maximum_fusion.rows_ref, bf16[4,128,128]{2,1,0:T(8,128)(2,1)S(1)} %copy-done, bf16[1168,128]{1,0:T(8,128)(2,1)S(1)} %prefill.1.near_ref, ...), custom_call_target="tpu_custom_call" | custom-call | flops 83886080 | bytes 262144 | tf_op jit(solution)/shard_map/decode/pallas_call | solution.py:215
  15.7 0.7 %collective-permute-start.4 = (bf16[4,4352]{1,0:T(4,128)(2,1)S(1)}, bf16[4,4352]{1,0:T(4,128)(2,1)S(1)}, u32[]{:S(2)}, u32[]{:S(2)}) collective-permute-start(bf16[4,4352]{1,0:T(4,128)(2,1)S(1)} %get-tuple-element.14), channel_id=1, source_target_pairs={{0,4},{4,8},{8,12},{12,0},{1,5},{5,9},{9,13},{13,1},{2,6},{6,10},{... | collective-permute-start | bytes 104456 | tf_op jit(solution)/shard_map/ppermute | solution.py:315
  16.5 0.3 %collective-permute-start.5 = (bf16[4,4352]{1,0:T(4,128)(2,1)S(1)}, bf16[4,4352]{1,0:T(4,128)(2,1)S(1)}, u32[]{:S(2)}, u32[]{:S(2)}) collective-permute-start(bf16[4,4352]{1,0:T(4,128)(2,1)S(1)} %get-tuple-element.15), channel_id=1, source_target_pairs={{0,8},{4,12},{8,0},{12,4},{1,9},{5,13},{9,1},{13,5},{2,10},{6,14},... | collective-permute-start | bytes 104456 | tf_op jit(solution)/shard_map/ppermute | solution.py:315
  16.8 2.8 %collective-permute-start.6 = (bf16[4,4352]{1,0:T(4,128)(2,1)S(1)}, bf16[4,4352]{1,0:T(4,128)(2,1)S(1)}, u32[]{:S(2)}, u32[]{:S(2)}) collective-permute-start(bf16[4,4352]{1,0:T(4,128)(2,1)S(1)} %get-tuple-element.16), channel_id=1, source_target_pairs={{0,12},{4,0},{8,4},{12,8},{1,13},{5,1},{9,5},{13,9},{2,14},{6,2},{... | collective-permute-start | bytes 104456 | tf_op jit(solution)/shard_map/ppermute | solution.py:315
  19.6 0.0 copy-done.2
  19.6 0.0 copy-done.3
  19.6 0.2 own.1
  19.8 2.0 %collective-permute-done.4.refs_1_ = bf16[4,4352]{1,0:T(4,128)(2,1)S(1)} collective-permute-done((bf16[4,4352]{1,0:T(4,128)(2,1)S(1)}, bf16[4,4352]{1,0:T(4,128)(2,1)S(1)}, u32[]{:S(2)}, u32[]{:S(2)}) %collective-permute-start.4) | collective-permute-done | bytes 34848 | tf_op jit(solution)/shard_map/ppermute | solution.py:315
  21.8 0.0 collective-permute-done.5.refs_2_
  21.8 0.4 %collective-permute-done.6.refs_3_ = bf16[4,4352]{1,0:T(4,128)(2,1)S(1)} collective-permute-done((bf16[4,4352]{1,0:T(4,128)(2,1)S(1)}, bf16[4,4352]{1,0:T(4,128)(2,1)S(1)}, u32[]{:S(2)}, u32[]{:S(2)}) %collective-permute-start.6) | collective-permute-done | bytes 34848 | tf_op jit(solution)/shard_map/ppermute | solution.py:315
  22.2 0.0 copy-done.4
  22.2 0.9 %finish.1 = bf16[4,4096]{1,0:T(4,128)(2,1)} custom-call(s32[1,32]{1,0:T(1,128)S(1)} %bitcast.1, f32[4,4096]{1,0:T(4,128)S(1)} %get-tuple-element.12.num_ref, f32[4,128]{1,0:T(4,128)S(1)} %get-tuple-element.13.weight_ref, bf16[4,4352]{1,0:T(4,128)(2,1)S(1)} %get-tuple-element.11._.refs_0_, bf16[4,4352]{1,0:T(4,128)(2,1)S(1)} %collective-permute-done.4.refs_1_, ...), custom_call_target="tpu_custom_call" | custom-call | tf_op jit(solution)/shard_map/finish/pallas_call | solution.py:294
Async XLA Ops:
  0.0 13.3 %collective-permute-start.2 = (bf16[4,4096]{1,0:T(4,128)(2,1)}, bf16[4,4096]{1,0:T(4,128)(2,1)S(1)}, u32[]{:S(2)}, u32[]{:S(2)}) collective-permute-start(bf16[4,4096]{1,0:T(4,128)(2,1)} %queries_ref.1), channel_id=1, source_target_pairs={{12,0},{0,4},{4,8},{8,12},{13,1},{1,5},{5,9},{9,13},{14,2},{2,6},{... | collective-permute-start | bytes 98312 | tf_op jit(solution)/shard_map/ppermute | solution.py:308
  3.0 10.3 %collective-permute-start.1 = (bf16[4,4096]{1,0:T(4,128)(2,1)}, bf16[4,4096]{1,0:T(4,128)(2,1)S(1)}, u32[]{:S(2)}, u32[]{:S(2)}) collective-permute-start(bf16[4,4096]{1,0:T(4,128)(2,1)} %queries_ref.1), channel_id=1, source_target_pairs={{8,0},{12,4},{0,8},{4,12},{9,1},{13,5},{1,9},{5,13},{10,2},{14,6},... | collective-permute-start | bytes 98312 | tf_op jit(solution)/shard_map/ppermute | solution.py:308
  5.6 7.7 %collective-permute-start = (bf16[4,4096]{1,0:T(4,128)(2,1)}, bf16[4,4096]{1,0:T(4,128)(2,1)S(1)}, u32[]{:S(2)}, u32[]{:S(2)}) collective-permute-start(bf16[4,4096]{1,0:T(4,128)(2,1)} %queries_ref.1), channel_id=1, source_target_pairs={{4,0},{8,4},{12,8},{0,12},{5,1},{9,5},{13,9},{1,13},{6,2},{10,6},{... | collective-permute-start | bytes 98312 | tf_op jit(solution)/shard_map/ppermute | solution.py:308
  7.6 5.7 %copy-start.1 = (bf16[4,4096]{1,0:T(4,128)(2,1)S(1)}, bf16[4,4096]{1,0:T(4,128)(2,1)}, u32[]{:S(2)}) copy-start(bf16[4,4096]{1,0:T(4,128)(2,1)} %queries_ref.1) | copy-start | bytes 98308
  7.6 7.3 %copy-start = (bf16[4,128,128]{2,1,0:T(8,128)(2,1)S(1)}, bf16[4,128,128]{2,1,0:T(8,128)(2,1)}, u32[]{:S(2)}) copy-start(bf16[4,128,128]{2,1,0:T(8,128)(2,1)} %weight_ref.3) | copy-start | bytes 393220
  7.6 12.0 %copy-start.2 = (bf16[4,512]{1,0:T(4,128)(2,1)S(1)}, bf16[4,512]{1,0:T(4,128)(2,1)}, u32[]{:S(2)}) copy-start(bf16[4,512]{1,0:T(4,128)(2,1)} %keys_ref.3) | copy-start | bytes 12292
  7.6 12.0 %copy-start.3 = (bf16[4,512]{1,0:T(4,128)(2,1)S(1)}, bf16[4,512]{1,0:T(4,128)(2,1)}, u32[]{:S(2)}) copy-start(bf16[4,512]{1,0:T(4,128)(2,1)} %values_ref.3) | copy-start | bytes 12292
  7.7 14.5 %copy-start.4 = (s32[32]{0:T(128)S(1)}, s32[32]{0:T(128)}, u32[]{:S(2)}) copy-start(s32[32]{0:T(128)} %param.15) | copy-start | bytes 388
  13.2 1.7 %collective-permute-start.3 = (bf16[1168,128]{1,0:T(8,128)(2,1)S(1)}, bf16[1168,128]{1,0:T(8,128)(2,1)S(1)}, u32[]{:S(2)}, u32[]{:S(2)}) collective-permute-start(bf16[1168,128]{1,0:T(8,128)(2,1)S(1)} %prefill.1.near_ref), channel_id=1, source_target_pairs={{0,1},{1,0},{2,3},{3,2},{4,5},{5,4},{6,7},{7,6},{8,9},{9,8},{10,11... | collective-permute-start | bytes 897032 | tf_op jit(solution)/shard_map/ppermute | solution.py:311
  15.7 6.1 %collective-permute-start.4 = (bf16[4,4352]{1,0:T(4,128)(2,1)S(1)}, bf16[4,4352]{1,0:T(4,128)(2,1)S(1)}, u32[]{:S(2)}, u32[]{:S(2)}) collective-permute-start(bf16[4,4352]{1,0:T(4,128)(2,1)S(1)} %get-tuple-element.14), channel_id=1, source_target_pairs={{0,4},{4,8},{8,12},{12,0},{1,5},{5,9},{9,13},{13,1},{2,6},{6,10},{... | collective-permute-start | bytes 104456 | tf_op jit(solution)/shard_map/ppermute | solution.py:315
  16.5 5.3 %collective-permute-start.5 = (bf16[4,4352]{1,0:T(4,128)(2,1)S(1)}, bf16[4,4352]{1,0:T(4,128)(2,1)S(1)}, u32[]{:S(2)}, u32[]{:S(2)}) collective-permute-start(bf16[4,4352]{1,0:T(4,128)(2,1)S(1)} %get-tuple-element.15), channel_id=1, source_target_pairs={{0,8},{4,12},{8,0},{12,4},{1,9},{5,13},{9,1},{13,5},{2,10},{6,14},... | collective-permute-start | bytes 104456 | tf_op jit(solution)/shard_map/ppermute | solution.py:315
  16.8 5.4 %collective-permute-start.6 = (bf16[4,4352]{1,0:T(4,128)(2,1)S(1)}, bf16[4,4352]{1,0:T(4,128)(2,1)S(1)}, u32[]{:S(2)}, u32[]{:S(2)}) collective-permute-start(bf16[4,4352]{1,0:T(4,128)(2,1)S(1)} %get-tuple-element.16), channel_id=1, source_target_pairs={{0,12},{4,0},{8,4},{12,8},{1,13},{5,1},{9,5},{13,9},{2,14},{6,2},{... | collective-permute-start | bytes 104456 | tf_op jit(solution)/shard_map/ppermute | solution.py:315

commit v10 on v9

--- a/solution.py
+++ b/solution.py
@@ -10,8 +10,8 @@
 WINDOW = 64
 TAU = 10.0
 EPS = 1e-06
-BLOCK = 512
-AHEAD = 3
+BLOCK = 1024
+AHEAD = 2
 NT = (((1,), (1,)), ((), ()))
 
 
@@ -31,12 +31,13 @@
     heads, head_size, feats = weight_ref.shape
     pairs = heads // 2
     span = keys_ref.shape[1]
-    chunks = span // BLOCK
+    cuts = [0, BLOCK // 4] + list(range(BLOCK, span + 1, BLOCK))
+    chunks = len(cuts) - 1
     get_weight = pltpu.make_async_copy(weight_ref, weight_at, weight_sem)
     get_weight.start()
     loads = []
     for c in range(chunks):
-        rows = pl.ds(c * BLOCK, BLOCK)
+        rows = pl.ds(cuts[c], cuts[c + 1] - cuts[c])
         loads.append(
             [
                 pltpu.make_async_copy(keys_ref.at[0, rows, :], keys_at.at[rows, :], load_sem.at[0, c]),
@@ -50,8 +51,6 @@
 
     for c in range(AHEAD):
         fetch(c)
-    state_ref[...] = jnp.zeros_like(state_ref)
-    norm_ref[...] = jnp.zeros_like(norm_ref)
     wide_ref[...] = jnp.zeros_like(wide_ref)
     get_weight.wait()
     for g in range(heads):
@@ -83,26 +82,29 @@
         for j in range(pairs):
             proj = lax.dot_general(
                 wide_ref[j],
-                keys_at[c * BLOCK : (c + 1) * BLOCK, j * 2 * head_size : (j + 1) * 2 * head_size],
+                keys_at[cuts[c] : cuts[c + 1], j * 2 * head_size : (j + 1) * 2 * head_size],
                 NT,
                 preferred_element_type=jnp.float32,
             )
-            proj_ref[c % 2, j] = proj.astype(jnp.bfloat16)
+            proj_ref[c % 2, j, :, : cuts[c + 1] - cuts[c]] = proj.astype(jnp.bfloat16)
 
     def collect(c):
-        position = c * BLOCK + lax.broadcasted_iota(jnp.int32, (1, BLOCK), 1)
+        size = cuts[c + 1] - cuts[c]
+        position = cuts[c] + lax.broadcasted_iota(jnp.int32, (1, size), 1)
         live = jnp.where(position < begin, 1.0, 0.0).astype(jnp.bfloat16)
         for j in range(pairs):
-            mapped = feature(proj_ref[c % 2, j]) * live
-            some = [mapped[:, k * 128 : (k + 1) * 128] for k in range(BLOCK // 128)]
+            mapped = feature(proj_ref[c % 2, j, :, :size]) * live
+            some = [mapped[:, k * 128 : (k + 1) * 128] for k in range(size // 128)]
             while len(some) > 1:
-                some = [x + y for x, y in zip(some[::2], some[1::2])]
-            norm_ref[j] += some[0].astype(jnp.float32)
-            state_ref[j] += jnp.dot(
+                some = [x + y for x, y in zip(some[::2], some[1::2])] + some[len(some) // 2 * 2 :]
+            total = some[0].astype(jnp.float32)
+            part = jnp.dot(
                 mapped,
-                values_at[c * BLOCK : (c + 1) * BLOCK, j * 2 * head_size : (j + 1) * 2 * head_size],
+                values_at[cuts[c] : cuts[c + 1], j * 2 * head_size : (j + 1) * 2 * head_size],
                 preferred_element_type=jnp.float32,
             )
+            norm_ref[j] = total if c == 0 else norm_ref[j] + total
+            state_ref[j] = part if c == 0 else state_ref[j] + part
 
     project(0)
     for c in range(chunks):
@@ -146,7 +148,7 @@
             pltpu.VMEM((heads // 2, 2 * feats, 2 * head_size), jnp.float32),
             pltpu.VMEM((heads // 2, 2 * feats, 128), jnp.float32),
             pltpu.SemaphoreType.DMA,
-            pltpu.SemaphoreType.DMA((2, span // BLOCK)),
+            pltpu.SemaphoreType.DMA((2, span // BLOCK + 1)),
             pltpu.SemaphoreType.DMA((2, heads)),
         ],
         compiler_params=pltpu.CompilerParams(vmem_limit_bytes=40 * 1024 * 1024),

time: 23.2 us -> 24.3 us (1.047)
  Pallas kernels: 7.47 us -> 8.51 us
    pallas_call x1, Pallas kernels: 5.55 us -> 6.59 us  [prefill(): pl.pallas_call(prefill_kernel, in_specs=[pl.BlockSpec(memory_space=pltpu....]
  transfers between devices with their start and end apart: 7 -> 7, of which waited for: 3 -> 3; matrix products, arithmetic and copies ran while one was open for 0% -> 0% of each run, Pallas kernels for 25% -> 28%
where the time goes in v10:
time: 24.3 us; the launch traced here: 24.1 us
  starting transfers between devices  10.9 us (45%)
  Pallas kernels  8.51 us (35%)
  waiting for transfers between devices  3.79 us (16%)
  between operations  0.77 us (3%)
    ppermute x3, starting transfers between devices, body(): lax.ppermute(queries, 'sect', [((i + k) % sects, i) for i in range(sects)])  6.96 us
    pallas_call x1, Pallas kernels, prefill(): pl.pallas_call(prefill_kernel, in_specs=[pl.BlockSpec(memory_space=pltpu....  6.59 us
    ppermute x3, starting transfers between devices, body(): lax.ppermute(results[k], 'sect', [(i, (i + k) % sects) for i in range(sec...  3.88 us
    ppermute x3, waiting for transfers between devices, body(): lax.ppermute(results[k], 'sect', [(i, (i + k) % sects) for i in range(sec...  2.33 us
    ppermute x1, waiting for transfers between devices, body(): far = lax.ppermute(near, 'sub', [(0, 1), (1, 0)])  1.44 us
    pallas_call x1, Pallas kernels, finish(): pl.pallas_call(finish_kernel, in_specs=[vmem] * (3 + len(blocks)), out_sp...  0.86 us
    pallas_call x1, Pallas kernels, decode(): pl.pallas_call(decode_kernel, in_specs=[vmem] * 4, out_specs=[vmem] * par...  0.85 us
  transfers between devices with their start and end apart: 7, of which 3 were waited for; matrix products, arithmetic and copies ran while one was open for 0% of the time, Pallas kernels for 28%

profile of v10, /device:TPU:0, one launch (start us, length us, event | category | flops | bytes accessed | tf_op | source)
XLA Modules:
  0.0 24.1 jit_solution(1168749306446288257)
XLA Ops:
  0.0 3.0 %collective-permute-start.2 = (bf16[4,4096]{1,0:T(4,128)(2,1)}, bf16[4,4096]{1,0:T(4,128)(2,1)S(1)}, u32[]{:S(2)}, u32[]{:S(2)}) collective-permute-start(bf16[4,4096]{1,0:T(4,128)(2,1)} %queries_ref.1), channel_id=1, source_target_pairs={{12,0},{0,4},{4,8},{8,12},{13,1},{1,5},{5,9},{9,13},{14,2},{2,6},{... | collective-permute-start | bytes 98312 | tf_op jit(solution)/shard_map/ppermute | solution.py:310
  3.0 2.6 %collective-permute-start.1 = (bf16[4,4096]{1,0:T(4,128)(2,1)}, bf16[4,4096]{1,0:T(4,128)(2,1)S(1)}, u32[]{:S(2)}, u32[]{:S(2)}) collective-permute-start(bf16[4,4096]{1,0:T(4,128)(2,1)} %queries_ref.1), channel_id=1, source_target_pairs={{8,0},{12,4},{0,8},{4,12},{9,1},{13,5},{1,9},{5,13},{10,2},{14,6},... | collective-permute-start | bytes 98312 | tf_op jit(solution)/shard_map/ppermute | solution.py:310
  5.6 1.3 %collective-permute-start = (bf16[4,4096]{1,0:T(4,128)(2,1)}, bf16[4,4096]{1,0:T(4,128)(2,1)S(1)}, u32[]{:S(2)}, u32[]{:S(2)}) collective-permute-start(bf16[4,4096]{1,0:T(4,128)(2,1)} %queries_ref.1), channel_id=1, source_target_pairs={{4,0},{8,4},{12,8},{0,12},{5,1},{9,5},{13,9},{1,13},{6,2},{10,6},{... | collective-permute-start | bytes 98312 | tf_op jit(solution)/shard_map/ppermute | solution.py:310
  7.6 0.0 copy-start.1
  7.6 0.0 copy-start
  7.6 0.0 copy-start.2
  7.6 0.0 copy-start.3
  7.7 0.0 copy-start.4
  7.7 6.6 %prefill.1.near_ref = bf16[1168,128]{1,0:T(8,128)(2,1)S(1)} custom-call(s32[1]{0:T(128)S(6)} %copy.9.lengths_ref, bf16[1,4096,512]{2,1,0:T(8,128)(2,1)} %keys_ref.2, bf16[1,4096,512]{2,1,0:T(8,128)(2,1)} %values_ref.2, bf16[4,128,128]{2,1,0:T(8,128)(2,1)} %weight_ref.3), custom_call_target="tpu_custom_call" | custom-call | flops 1073741824 | bytes 8388608 | tf_op jit(solution)/shard_map/prefill/pallas_call | solution.py:137
  14.3 0.1 collective-permute-start.3
  14.3 0.0 collective-permute-done.2
  14.4 0.0 collective-permute-done.1
  14.4 0.0 collective-permute-done
  14.4 0.0 copy-done.1
  14.4 0.1 pad_maximum_fusion.rows_ref
  14.5 1.4 %collective-permute-done.3.far_ref = bf16[1168,128]{1,0:T(8,128)(2,1)S(1)} collective-permute-done((bf16[1168,128]{1,0:T(8,128)(2,1)S(1)}, bf16[1168,128]{1,0:T(8,128)(2,1)S(1)}, u32[]{:S(2)}, u32[]{:S(2)}) %collective-permute-start.3) | collective-permute-done | bytes 299040 | tf_op jit(solution)/shard_map/ppermute | solution.py:313
  15.9 0.0 copy-done
  15.9 0.8 %decode.1 = (bf16[4,4352]{1,0:T(4,128)(2,1)S(1)}, bf16[4,4352]{1,0:T(4,128)(2,1)S(1)}, bf16[4,4352]{1,0:T(4,128)(2,1)S(1)}, bf16[4,4352]{1,0:T(4,128)(2,1)S(1)}) custom-call(bf16[16,4096]{1,0:T(8,128)(2,1)S(1)} %pad_maximum_fusion.rows_ref, bf16[4,128,128]{2,1,0:T(8,128)(2,1)S(1)} %copy-done, bf16[1168,128]{1,0:T(8,128)(2,1)S(1)} %prefill.1.near_ref, ...), custom_call_target="tpu_custom_call" | custom-call | flops 83886080 | bytes 262144 | tf_op jit(solution)/shard_map/decode/pallas_call | solution.py:217
  16.8 0.7 %collective-permute-start.4 = (bf16[4,4352]{1,0:T(4,128)(2,1)S(1)}, bf16[4,4352]{1,0:T(4,128)(2,1)S(1)}, u32[]{:S(2)}, u32[]{:S(2)}) collective-permute-start(bf16[4,4352]{1,0:T(4,128)(2,1)S(1)} %get-tuple-element.14), channel_id=1, source_target_pairs={{0,4},{4,8},{8,12},{12,0},{1,5},{5,9},{9,13},{13,1},{2,6},{6,10},{... | collective-permute-start | bytes 104456 | tf_op jit(solution)/shard_map/ppermute | solution.py:317
  17.5 0.3 %collective-permute-start.5 = (bf16[4,4352]{1,0:T(4,128)(2,1)S(1)}, bf16[4,4352]{1,0:T(4,128)(2,1)S(1)}, u32[]{:S(2)}, u32[]{:S(2)}) collective-permute-start(bf16[4,4352]{1,0:T(4,128)(2,1)S(1)} %get-tuple-element.15), channel_id=1, source_target_pairs={{0,8},{4,12},{8,0},{12,4},{1,9},{5,13},{9,1},{13,5},{2,10},{6,14},... | collective-permute-start | bytes 104456 | tf_op jit(solution)/shard_map/ppermute | solution.py:317
  17.8 2.8 %collective-permute-start.6 = (bf16[4,4352]{1,0:T(4,128)(2,1)S(1)}, bf16[4,4352]{1,0:T(4,128)(2,1)S(1)}, u32[]{:S(2)}, u32[]{:S(2)}) collective-permute-start(bf16[4,4352]{1,0:T(4,128)(2,1)S(1)} %get-tuple-element.16), channel_id=1, source_target_pairs={{0,12},{4,0},{8,4},{12,8},{1,13},{5,1},{9,5},{13,9},{2,14},{6,2},{... | collective-permute-start | bytes 104456 | tf_op jit(solution)/shard_map/ppermute | solution.py:317
  20.7 0.0 copy-done.2
  20.7 0.0 copy-done.3
  20.7 0.2 own.1
  20.9 2.0 %collective-permute-done.4.refs_1_ = bf16[4,4352]{1,0:T(4,128)(2,1)S(1)} collective-permute-done((bf16[4,4352]{1,0:T(4,128)(2,1)S(1)}, bf16[4,4352]{1,0:T(4,128)(2,1)S(1)}, u32[]{:S(2)}, u32[]{:S(2)}) %collective-permute-start.4) | collective-permute-done | bytes 34848 | tf_op jit(solution)/shard_map/ppermute | solution.py:317
  22.9 0.0 collective-permute-done.5.refs_2_
  22.9 0.4 %collective-permute-done.6.refs_3_ = bf16[4,4352]{1,0:T(4,128)(2,1)S(1)} collective-permute-done((bf16[4,4352]{1,0:T(4,128)(2,1)S(1)}, bf16[4,4352]{1,0:T(4,128)(2,1)S(1)}, u32[]{:S(2)}, u32[]{:S(2)}) %collective-permute-start.6) | collective-permute-done | bytes 34848 | tf_op jit(solution)/shard_map/ppermute | solution.py:317
  23.2 0.0 copy-done.4
  23.2 0.9 %finish.1 = bf16[4,4096]{1,0:T(4,128)(2,1)} custom-call(s32[1,32]{1,0:T(1,128)S(1)} %bitcast.1, f32[4,4096]{1,0:T(4,128)S(1)} %get-tuple-element.12.num_ref, f32[4,128]{1,0:T(4,128)S(1)} %get-tuple-element.13.weight_ref, bf16[4,4352]{1,0:T(4,128)(2,1)S(1)} %get-tuple-element.11._.refs_0_, bf16[4,4352]{1,0:T(4,128)(2,1)S(1)} %collective-permute-done.4.refs_1_, ...), custom_call_target="tpu_custom_call" | custom-call | tf_op jit(solution)/shard_map/finish/pallas_call | solution.py:296
Async XLA Ops:
  0.0 14.3 %collective-permute-start.2 = (bf16[4,4096]{1,0:T(4,128)(2,1)}, bf16[4,4096]{1,0:T(4,128)(2,1)S(1)}, u32[]{:S(2)}, u32[]{:S(2)}) collective-permute-start(bf16[4,4096]{1,0:T(4,128)(2,1)} %queries_ref.1), channel_id=1, source_target_pairs={{12,0},{0,4},{4,8},{8,12},{13,1},{1,5},{5,9},{9,13},{14,2},{2,6},{... | collective-permute-start | bytes 98312 | tf_op jit(solution)/shard_map/ppermute | solution.py:310
  3.0 11.3 %collective-permute-start.1 = (bf16[4,4096]{1,0:T(4,128)(2,1)}, bf16[4,4096]{1,0:T(4,128)(2,1)S(1)}, u32[]{:S(2)}, u32[]{:S(2)}) collective-permute-start(bf16[4,4096]{1,0:T(4,128)(2,1)} %queries_ref.1), channel_id=1, source_target_pairs={{8,0},{12,4},{0,8},{4,12},{9,1},{13,5},{1,9},{5,13},{10,2},{14,6},... | collective-permute-start | bytes 98312 | tf_op jit(solution)/shard_map/ppermute | solution.py:310
  5.6 8.8 %collective-permute-start = (bf16[4,4096]{1,0:T(4,128)(2,1)}, bf16[4,4096]{1,0:T(4,128)(2,1)S(1)}, u32[]{:S(2)}, u32[]{:S(2)}) collective-permute-start(bf16[4,4096]{1,0:T(4,128)(2,1)} %queries_ref.1), channel_id=1, source_target_pairs={{4,0},{8,4},{12,8},{0,12},{5,1},{9,5},{13,9},{1,13},{6,2},{10,6},{... | collective-permute-start | bytes 98312 | tf_op jit(solution)/shard_map/ppermute | solution.py:310
  7.6 6.8 %copy-start.1 = (bf16[4,4096]{1,0:T(4,128)(2,1)S(1)}, bf16[4,4096]{1,0:T(4,128)(2,1)}, u32[]{:S(2)}) copy-start(bf16[4,4096]{1,0:T(4,128)(2,1)} %queries_ref.1) | copy-start | bytes 98308
  7.6 8.3 %copy-start = (bf16[4,128,128]{2,1,0:T(8,128)(2,1)S(1)}, bf16[4,128,128]{2,1,0:T(8,128)(2,1)}, u32[]{:S(2)}) copy-start(bf16[4,128,128]{2,1,0:T(8,128)(2,1)} %weight_ref.3) | copy-start | bytes 393220
  7.6 13.0 %copy-start.2 = (bf16[4,512]{1,0:T(4,128)(2,1)S(1)}, bf16[4,512]{1,0:T(4,128)(2,1)}, u32[]{:S(2)}) copy-start(bf16[4,512]{1,0:T(4,128)(2,1)} %keys_ref.3) | copy-start | bytes 12292
  7.6 13.0 %copy-start.3 = (bf16[4,512]{1,0:T(4,128)(2,1)S(1)}, bf16[4,512]{1,0:T(4,128)(2,1)}, u32[]{:S(2)}) copy-start(bf16[4,512]{1,0:T(4,128)(2,1)} %values_ref.3) | copy-start | bytes 12292
  7.7 15.6 %copy-start.4 = (s32[32]{0:T(128)S(1)}, s32[32]{0:T(128)}, u32[]{:S(2)}) copy-start(s32[32]{0:T(128)} %param.15) | copy-start | bytes 388
  14.3 1.7 %collective-permute-start.3 = (bf16[1168,128]{1,0:T(8,128)(2,1)S(1)}, bf16[1168,128]{1,0:T(8,128)(2,1)S(1)}, u32[]{:S(2)}, u32[]{:S(2)}) collective-permute-start(bf16[1168,128]{1,0:T(8,128)(2,1)S(1)} %prefill.1.near_ref), channel_id=1, source_target_pairs={{0,1},{1,0},{2,3},{3,2},{4,5},{5,4},{6,7},{7,6},{8,9},{9,8},{10,11... | collective-permute-start | bytes 897032 | tf_op jit(solution)/shard_map/ppermute | solution.py:313
  16.8 6.1 %collective-permute-start.4 = (bf16[4,4352]{1,0:T(4,128)(2,1)S(1)}, bf16[4,4352]{1,0:T(4,128)(2,1)S(1)}, u32[]{:S(2)}, u32[]{:S(2)}) collective-permute-start(bf16[4,4352]{1,0:T(4,128)(2,1)S(1)} %get-tuple-element.14), channel_id=1, source_target_pairs={{0,4},{4,8},{8,12},{12,0},{1,5},{5,9},{9,13},{13,1},{2,6},{6,10},{... | collective-permute-start | bytes 104456 | tf_op jit(solution)/shard_map/ppermute | solution.py:317
  17.5 5.3 %collective-permute-start.5 = (bf16[4,4352]{1,0:T(4,128)(2,1)S(1)}, bf16[4,4352]{1,0:T(4,128)(2,1)S(1)}, u32[]{:S(2)}, u32[]{:S(2)}) collective-permute-start(bf16[4,4352]{1,0:T(4,128)(2,1)S(1)} %get-tuple-element.15), channel_id=1, source_target_pairs={{0,8},{4,12},{8,0},{12,4},{1,9},{5,13},{9,1},{13,5},{2,10},{6,14},... | collective-permute-start | bytes 104456 | tf_op jit(solution)/shard_map/ppermute | solution.py:317
  17.8 5.4 %collective-permute-start.6 = (bf16[4,4352]{1,0:T(4,128)(2,1)S(1)}, bf16[4,4352]{1,0:T(4,128)(2,1)S(1)}, u32[]{:S(2)}, u32[]{:S(2)}) collective-permute-start(bf16[4,4352]{1,0:T(4,128)(2,1)S(1)} %get-tuple-element.16), channel_id=1, source_target_pairs={{0,12},{4,0},{8,4},{12,8},{1,13},{5,1},{9,5},{13,9},{2,14},{6,2},{... | collective-permute-start | bytes 104456 | tf_op jit(solution)/shard_map/ppermute | solution.py:317

commit v11 on v10

--- a/solution.py
+++ b/solution.py
@@ -10,8 +10,8 @@
 WINDOW = 64
 TAU = 10.0
 EPS = 1e-06
-BLOCK = 1024
-AHEAD = 2
+BLOCK = 256
+AHEAD = 8
 NT = (((1,), (1,)), ((), ()))
 
 
@@ -31,7 +31,7 @@
     heads, head_size, feats = weight_ref.shape
     pairs = heads // 2
     span = keys_ref.shape[1]
-    cuts = [0, BLOCK // 4] + list(range(BLOCK, span + 1, BLOCK))
+    cuts = list(range(0, span + 1, BLOCK))
     chunks = len(cuts) - 1
     get_weight = pltpu.make_async_copy(weight_ref, weight_at, weight_sem)
     get_weight.start()

time: 24.3 us -> 24.4 us (level)
  transfers between devices with their start and end apart: 7 -> 7, of which waited for: 3 -> 3; matrix products, arithmetic and copies ran while one was open for 0% -> 0% of each run, Pallas kernels for 28% -> 29%
where the time goes in v11:
time: 24.4 us; the launch traced here: 24.2 us
  starting transfers between devices  10.9 us (45%)
  Pallas kernels  8.64 us (35%)
  waiting for transfers between devices  3.79 us (16%)
  between operations  0.77 us (3%)
    ppermute x3, starting transfers between devices, body(): lax.ppermute(queries, 'sect', [((i + k) % sects, i) for i in range(sects)])  6.96 us
    pallas_call x1, Pallas kernels, prefill(): pl.pallas_call(prefill_kernel, in_specs=[pl.BlockSpec(memory_space=pltpu....  6.72 us
    ppermute x3, starting transfers between devices, body(): lax.ppermute(results[k], 'sect', [(i, (i + k) % sects) for i in range(sec...  3.88 us
    ppermute x3, waiting for transfers between devices, body(): lax.ppermute(results[k], 'sect', [(i, (i + k) % sects) for i in range(sec...  2.34 us
    ppermute x1, waiting for transfers between devices, body(): far = lax.ppermute(near, 'sub', [(0, 1), (1, 0)])  1.44 us
    pallas_call x1, Pallas kernels, finish(): pl.pallas_call(finish_kernel, in_specs=[vmem] * (3 + len(blocks)), out_sp...  0.86 us
    pallas_call x1, Pallas kernels, decode(): pl.pallas_call(decode_kernel, in_specs=[vmem] * 4, out_specs=[vmem] * par...  0.85 us
  transfers between devices with their start and end apart: 7, of which 3 were waited for; matrix products, arithmetic and copies ran while one was open for 0% of the time, Pallas kernels for 29%

profile of v11, /device:TPU:0, one launch (start us, length us, event | category | flops | bytes accessed | tf_op | source)
XLA Modules:
  0.0 24.2 jit_solution(7651776939087032793)
XLA Ops:
  0.0 3.0 %collective-permute-start.2 = (bf16[4,4096]{1,0:T(4,128)(2,1)}, bf16[4,4096]{1,0:T(4,128)(2,1)S(1)}, u32[]{:S(2)}, u32[]{:S(2)}) collective-permute-start(bf16[4,4096]{1,0:T(4,128)(2,1)} %queries_ref.1), channel_id=1, source_target_pairs={{12,0},{0,4},{4,8},{8,12},{13,1},{1,5},{5,9},{9,13},{14,2},{2,6},{... | collective-permute-start | bytes 98312 | tf_op jit(solution)/shard_map/ppermute | solution.py:310
  3.0 2.6 %collective-permute-start.1 = (bf16[4,4096]{1,0:T(4,128)(2,1)}, bf16[4,4096]{1,0:T(4,128)(2,1)S(1)}, u32[]{:S(2)}, u32[]{:S(2)}) collective-permute-start(bf16[4,4096]{1,0:T(4,128)(2,1)} %queries_ref.1), channel_id=1, source_target_pairs={{8,0},{12,4},{0,8},{4,12},{9,1},{13,5},{1,9},{5,13},{10,2},{14,6},... | collective-permute-start | bytes 98312 | tf_op jit(solution)/shard_map/ppermute | solution.py:310
  5.6 1.3 %collective-permute-start = (bf16[4,4096]{1,0:T(4,128)(2,1)}, bf16[4,4096]{1,0:T(4,128)(2,1)S(1)}, u32[]{:S(2)}, u32[]{:S(2)}) collective-permute-start(bf16[4,4096]{1,0:T(4,128)(2,1)} %queries_ref.1), channel_id=1, source_target_pairs={{4,0},{8,4},{12,8},{0,12},{5,1},{9,5},{13,9},{1,13},{6,2},{10,6},{... | collective-permute-start | bytes 98312 | tf_op jit(solution)/shard_map/ppermute | solution.py:310
  7.6 0.0 copy-start.1
  7.6 0.0 copy-start
  7.6 0.0 copy-start.2
  7.6 0.0 copy-start.3
  7.7 0.0 copy-start.4
  7.7 6.7 %prefill.1.near_ref = bf16[1168,128]{1,0:T(8,128)(2,1)S(1)} custom-call(s32[1]{0:T(128)S(6)} %copy.9.lengths_ref, bf16[1,4096,512]{2,1,0:T(8,128)(2,1)} %keys_ref.2, bf16[1,4096,512]{2,1,0:T(8,128)(2,1)} %values_ref.2, bf16[4,128,128]{2,1,0:T(8,128)(2,1)} %weight_ref.3), custom_call_target="tpu_custom_call" | custom-call | flops 1073741824 | bytes 8388608 | tf_op jit(solution)/shard_map/prefill/pallas_call | solution.py:137
  14.4 0.1 collective-permute-start.3
  14.5 0.0 collective-permute-done.2
  14.5 0.0 collective-permute-done.1
  14.5 0.0 collective-permute-done
  14.5 0.0 copy-done.1
  14.5 0.1 pad_maximum_fusion.rows_ref
  14.6 1.4 %collective-permute-done.3.far_ref = bf16[1168,128]{1,0:T(8,128)(2,1)S(1)} collective-permute-done((bf16[1168,128]{1,0:T(8,128)(2,1)S(1)}, bf16[1168,128]{1,0:T(8,128)(2,1)S(1)}, u32[]{:S(2)}, u32[]{:S(2)}) %collective-permute-start.3) | collective-permute-done | bytes 299040 | tf_op jit(solution)/shard_map/ppermute | solution.py:313
  16.0 0.0 copy-done
  16.1 0.8 %decode.1 = (bf16[4,4352]{1,0:T(4,128)(2,1)S(1)}, bf16[4,4352]{1,0:T(4,128)(2,1)S(1)}, bf16[4,4352]{1,0:T(4,128)(2,1)S(1)}, bf16[4,4352]{1,0:T(4,128)(2,1)S(1)}) custom-call(bf16[16,4096]{1,0:T(8,128)(2,1)S(1)} %pad_maximum_fusion.rows_ref, bf16[4,128,128]{2,1,0:T(8,128)(2,1)S(1)} %copy-done, bf16[1168,128]{1,0:T(8,128)(2,1)S(1)} %prefill.1.near_ref, ...), custom_call_target="tpu_custom_call" | custom-call | flops 83886080 | bytes 262144 | tf_op jit(solution)/shard_map/decode/pallas_call | solution.py:217
  16.9 0.7 %collective-permute-start.4 = (bf16[4,4352]{1,0:T(4,128)(2,1)S(1)}, bf16[4,4352]{1,0:T(4,128)(2,1)S(1)}, u32[]{:S(2)}, u32[]{:S(2)}) collective-permute-start(bf16[4,4352]{1,0:T(4,128)(2,1)S(1)} %get-tuple-element.14), channel_id=1, source_target_pairs={{0,4},{4,8},{8,12},{12,0},{1,5},{5,9},{9,13},{13,1},{2,6},{6,10},{... | collective-permute-start | bytes 104456 | tf_op jit(solution)/shard_map/ppermute | solution.py:317
  17.6 0.3 %collective-permute-start.5 = (bf16[4,4352]{1,0:T(4,128)(2,1)S(1)}, bf16[4,4352]{1,0:T(4,128)(2,1)S(1)}, u32[]{:S(2)}, u32[]{:S(2)}) collective-permute-start(bf16[4,4352]{1,0:T(4,128)(2,1)S(1)} %get-tuple-element.15), channel_id=1, source_target_pairs={{0,8},{4,12},{8,0},{12,4},{1,9},{5,13},{9,1},{13,5},{2,10},{6,14},... | collective-permute-start | bytes 104456 | tf_op jit(solution)/shard_map/ppermute | solution.py:317
  18.0 2.8 %collective-permute-start.6 = (bf16[4,4352]{1,0:T(4,128)(2,1)S(1)}, bf16[4,4352]{1,0:T(4,128)(2,1)S(1)}, u32[]{:S(2)}, u32[]{:S(2)}) collective-permute-start(bf16[4,4352]{1,0:T(4,128)(2,1)S(1)} %get-tuple-element.16), channel_id=1, source_target_pairs={{0,12},{4,0},{8,4},{12,8},{1,13},{5,1},{9,5},{13,9},{2,14},{6,2},{... | collective-permute-start | bytes 104456 | tf_op jit(solution)/shard_map/ppermute | solution.py:317
  20.8 0.0 copy-done.2
  20.8 0.0 copy-done.3
  20.8 0.2 own.1
  21.0 2.0 %collective-permute-done.4.refs_1_ = bf16[4,4352]{1,0:T(4,128)(2,1)S(1)} collective-permute-done((bf16[4,4352]{1,0:T(4,128)(2,1)S(1)}, bf16[4,4352]{1,0:T(4,128)(2,1)S(1)}, u32[]{:S(2)}, u32[]{:S(2)}) %collective-permute-start.4) | collective-permute-done | bytes 34848 | tf_op jit(solution)/shard_map/ppermute | solution.py:317
  23.0 0.0 collective-permute-done.5.refs_2_
  23.0 0.4 %collective-permute-done.6.refs_3_ = bf16[4,4352]{1,0:T(4,128)(2,1)S(1)} collective-permute-done((bf16[4,4352]{1,0:T(4,128)(2,1)S(1)}, bf16[4,4352]{1,0:T(4,128)(2,1)S(1)}, u32[]{:S(2)}, u32[]{:S(2)}) %collective-permute-start.6) | collective-permute-done | bytes 34848 | tf_op jit(solution)/shard_map/ppermute | solution.py:317
  23.4 0.0 copy-done.4
  23.4 0.9 %finish.1 = bf16[4,4096]{1,0:T(4,128)(2,1)} custom-call(s32[1,32]{1,0:T(1,128)S(1)} %bitcast.1, f32[4,4096]{1,0:T(4,128)S(1)} %get-tuple-element.12.num_ref, f32[4,128]{1,0:T(4,128)S(1)} %get-tuple-element.13.weight_ref, bf16[4,4352]{1,0:T(4,128)(2,1)S(1)} %get-tuple-element.11._.refs_0_, bf16[4,4352]{1,0:T(4,128)(2,1)S(1)} %collective-permute-done.4.refs_1_, ...), custom_call_target="tpu_custom_call" | custom-call | tf_op jit(solution)/shard_map/finish/pallas_call | solution.py:296
Async XLA Ops:
  0.0 14.5 %collective-permute-start.2 = (bf16[4,4096]{1,0:T(4,128)(2,1)}, bf16[4,4096]{1,0:T(4,128)(2,1)S(1)}, u32[]{:S(2)}, u32[]{:S(2)}) collective-permute-start(bf16[4,4096]{1,0:T(4,128)(2,1)} %queries_ref.1), channel_id=1, source_target_pairs={{12,0},{0,4},{4,8},{8,12},{13,1},{1,5},{5,9},{9,13},{14,2},{2,6},{... | collective-permute-start | bytes 98312 | tf_op jit(solution)/shard_map/ppermute | solution.py:310
  3.0 11.5 %collective-permute-start.1 = (bf16[4,4096]{1,0:T(4,128)(2,1)}, bf16[4,4096]{1,0:T(4,128)(2,1)S(1)}, u32[]{:S(2)}, u32[]{:S(2)}) collective-permute-start(bf16[4,4096]{1,0:T(4,128)(2,1)} %queries_ref.1), channel_id=1, source_target_pairs={{8,0},{12,4},{0,8},{4,12},{9,1},{13,5},{1,9},{5,13},{10,2},{14,6},... | collective-permute-start | bytes 98312 | tf_op jit(solution)/shard_map/ppermute | solution.py:310
  5.6 8.9 %collective-permute-start = (bf16[4,4096]{1,0:T(4,128)(2,1)}, bf16[4,4096]{1,0:T(4,128)(2,1)S(1)}, u32[]{:S(2)}, u32[]{:S(2)}) collective-permute-start(bf16[4,4096]{1,0:T(4,128)(2,1)} %queries_ref.1), channel_id=1, source_target_pairs={{4,0},{8,4},{12,8},{0,12},{5,1},{9,5},{13,9},{1,13},{6,2},{10,6},{... | collective-permute-start | bytes 98312 | tf_op jit(solution)/shard_map/ppermute | solution.py:310
  7.6 6.9 %copy-start.1 = (bf16[4,4096]{1,0:T(4,128)(2,1)S(1)}, bf16[4,4096]{1,0:T(4,128)(2,1)}, u32[]{:S(2)}) copy-start(bf16[4,4096]{1,0:T(4,128)(2,1)} %queries_ref.1) | copy-start | bytes 98308
  7.6 8.4 %copy-start = (bf16[4,128,128]{2,1,0:T(8,128)(2,1)S(1)}, bf16[4,128,128]{2,1,0:T(8,128)(2,1)}, u32[]{:S(2)}) copy-start(bf16[4,128,128]{2,1,0:T(8,128)(2,1)} %weight_ref.3) | copy-start | bytes 393220
  7.6 13.2 %copy-start.2 = (bf16[4,512]{1,0:T(4,128)(2,1)S(1)}, bf16[4,512]{1,0:T(4,128)(2,1)}, u32[]{:S(2)}) copy-start(bf16[4,512]{1,0:T(4,128)(2,1)} %keys_ref.3) | copy-start | bytes 12292
  7.6 13.1 %copy-start.3 = (bf16[4,512]{1,0:T(4,128)(2,1)S(1)}, bf16[4,512]{1,0:T(4,128)(2,1)}, u32[]{:S(2)}) copy-start(bf16[4,512]{1,0:T(4,128)(2,1)} %values_ref.3) | copy-start | bytes 12292
  7.7 15.7 %copy-start.4 = (s32[32]{0:T(128)S(1)}, s32[32]{0:T(128)}, u32[]{:S(2)}) copy-start(s32[32]{0:T(128)} %param.15) | copy-start | bytes 388
  14.4 1.7 %collective-permute-start.3 = (bf16[1168,128]{1,0:T(8,128)(2,1)S(1)}, bf16[1168,128]{1,0:T(8,128)(2,1)S(1)}, u32[]{:S(2)}, u32[]{:S(2)}) collective-permute-start(bf16[1168,128]{1,0:T(8,128)(2,1)S(1)} %prefill.1.near_ref), channel_id=1, source_target_pairs={{0,1},{1,0},{2,3},{3,2},{4,5},{5,4},{6,7},{7,6},{8,9},{9,8},{10,11... | collective-permute-start | bytes 897032 | tf_op jit(solution)/shard_map/ppermute | solution.py:313
  16.9 6.1 %collective-permute-start.4 = (bf16[4,4352]{1,0:T(4,128)(2,1)S(1)}, bf16[4,4352]{1,0:T(4,128)(2,1)S(1)}, u32[]{:S(2)}, u32[]{:S(2)}) collective-permute-start(bf16[4,4352]{1,0:T(4,128)(2,1)S(1)} %get-tuple-element.14), channel_id=1, source_target_pairs={{0,4},{4,8},{8,12},{12,0},{1,5},{5,9},{9,13},{13,1},{2,6},{6,10},{... | collective-permute-start | bytes 104456 | tf_op jit(solution)/shard_map/ppermute | solution.py:317
  17.6 5.4 %collective-permute-start.5 = (bf16[4,4352]{1,0:T(4,128)(2,1)S(1)}, bf16[4,4352]{1,0:T(4,128)(2,1)S(1)}, u32[]{:S(2)}, u32[]{:S(2)}) collective-permute-start(bf16[4,4352]{1,0:T(4,128)(2,1)S(1)} %get-tuple-element.15), channel_id=1, source_target_pairs={{0,8},{4,12},{8,0},{12,4},{1,9},{5,13},{9,1},{13,5},{2,10},{6,14},... | collective-permute-start | bytes 104456 | tf_op jit(solution)/shard_map/ppermute | solution.py:317
  18.0 5.4 %collective-permute-start.6 = (bf16[4,4352]{1,0:T(4,128)(2,1)S(1)}, bf16[4,4352]{1,0:T(4,128)(2,1)S(1)}, u32[]{:S(2)}, u32[]{:S(2)}) collective-permute-start(bf16[4,4352]{1,0:T(4,128)(2,1)S(1)} %get-tuple-element.16), channel_id=1, source_target_pairs={{0,12},{4,0},{8,4},{12,8},{1,13},{5,1},{9,5},{13,9},{2,14},{6,2},{... | collective-permute-start | bytes 104456 | tf_op jit(solution)/shard_map/ppermute | solution.py:317

commit v12 on v9

--- a/solution.py
+++ b/solution.py
@@ -11,7 +11,7 @@
 TAU = 10.0
 EPS = 1e-06
 BLOCK = 512
-AHEAD = 3
+AHEAD = 2
 NT = (((1,), (1,)), ((), ()))
 
 
@@ -21,6 +21,18 @@
 
 SLAB = WINDOW + 16
 MASK_ROW = 8
+
+
+def paired(sects):
+    return sects & (sects - 1) == 0
+
+
+def partner(sect, k, sects):
+    return sect ^ k if paired(sects) else (sect + k) % sects
+
+
+def home_order(sects):
+    return list(range(2, sects)) + [1]
 
 
 def prefill_kernel(
@@ -34,22 +46,19 @@
     chunks = span // BLOCK
     get_weight = pltpu.make_async_copy(weight_ref, weight_at, weight_sem)
     get_weight.start()
-    loads = []
-    for c in range(chunks):
-        rows = pl.ds(c * BLOCK, BLOCK)
-        loads.append(
-            [
-                pltpu.make_async_copy(keys_ref.at[0, rows, :], keys_at.at[rows, :], load_sem.at[0, c]),
-                pltpu.make_async_copy(values_ref.at[0, rows, :], values_at.at[rows, :], load_sem.at[1, c]),
-            ]
-        )
-
-    def fetch(c):
-        for priority, load in enumerate(loads[c]):
-            load.start(priority=priority)
-
+    loads = [
+        [
+            pltpu.make_async_copy(
+                source.at[0, pl.ds(c * BLOCK, BLOCK), :], place.at[pl.ds(c * BLOCK, BLOCK), :], load_sem.at[i, c]
+            )
+            for c in range(chunks)
+        ]
+        for i, (source, place) in enumerate(((keys_ref, keys_at), (values_ref, values_at)))
+    ]
     for c in range(AHEAD):
-        fetch(c)
+        for load in loads:
+            load[c].start()
+
     state_ref[...] = jnp.zeros_like(state_ref)
     norm_ref[...] = jnp.zeros_like(norm_ref)
     wide_ref[...] = jnp.zeros_like(wide_ref)
@@ -75,11 +84,13 @@
             )
             slabs[-1].start()
 
+    def arrive(i, c):
+        loads[i][c].wait()
+        if c + AHEAD < chunks:
+            loads[i][c + AHEAD].start()
+
     def project(c):
-        for load in loads[c]:
-            load.wait()
-        if c + AHEAD < chunks:
-            fetch(c + AHEAD)
+        arrive(0, c)
         for j in range(pairs):
             proj = lax.dot_general(
                 wide_ref[j],
@@ -90,6 +101,7 @@
             proj_ref[c % 2, j] = proj.astype(jnp.bfloat16)
 
     def collect(c):
+        arrive(1, c)
         position = c * BLOCK + lax.broadcasted_iota(jnp.int32, (1, BLOCK), 1)
         live = jnp.where(position < begin, 1.0, 0.0).astype(jnp.bfloat16)
         for j in range(pairs):
@@ -279,9 +291,9 @@
     lane = lax.broadcasted_iota(jnp.int32, (count, rows), 1)
     prompt = jnp.sum(jnp.where(lane == row, prompts_ref[...], 0), axis=1, keepdims=True)
     chosen = block_refs[0][...].astype(jnp.float32)
-    for k in range(1, sects):
-        source = lax.rem(sect - k + sects, sects)
-        chosen = jnp.where(prompt == source, block_refs[k][...].astype(jnp.float32), chosen)
+    for k, ref in zip(home_order(sects), block_refs[1:]):
+        source = partner(sect, k if paired(sects) else sects - k, sects)
+        chosen = jnp.where(prompt == source, ref[...].astype(jnp.float32), chosen)
     den = chosen[:, width : width + head_size] + chosen[:, width + head_size :] + weight_ref[...]
     scale = 1.0 / den
     for head in range(width // head_size):
@@ -304,17 +316,17 @@
 def body(
     sects, prompt_keys, prompt_values, lengths, feature_weight, queries, new_keys, new_values, row_prompt
 ):
-    blocks = [queries] + [
-        lax.ppermute(queries, "sect", [((i + k) % sects, i) for i in range(sects)]) for k in range(1, sects)
-    ]
+    asked = {k: lax.ppermute(queries, "sect", [(partner(i, k, sects), i) for i in range(sects)]) for k in range(1, sects)}
     near = prefill(prompt_keys, prompt_values, feature_weight, lengths)
     far = lax.ppermute(near, "sub", [(0, 1), (1, 0)])
-    results = decode(jnp.concatenate(blocks, axis=0), feature_weight, near, far, sects)
+    blocks = [asked[k] for k in range(sects - 1, 0, -1)] + [queries]
+    results = decode(jnp.concatenate(blocks, axis=0), feature_weight, near, far, sects)[::-1]
     num, weight = own(queries, new_keys, new_values, results[0], feature_weight.shape[1])
-    back = [results[0]] + [
-        lax.ppermute(results[k], "sect", [(i, (i + k) % sects) for i in range(sects)]) for k in range(1, sects)
+    back = [
+        lax.ppermute(results[k], "sect", [(i, partner(i, k, sects)) for i in range(sects)])
+        for k in home_order(sects)
     ]
-    return finish(row_prompt, num, weight, back)
+    return finish(row_prompt, num, weight, [results[0]] + back)
 
 
 def solution(mesh):

time: 23.2 us -> 25 us (1.078)
  Pallas kernels: 7.47 us -> 8.94 us
  waiting for transfers between devices: 3.79 us -> 4.85 us
  starting transfers between devices: 10.9 us -> 10.1 us
    pallas_call x1, Pallas kernels: 5.55 us -> 7.02 us  [prefill(): pl.pallas_call(prefill_kernel, in_specs=[pl.BlockSpec(memory_space=pltpu....]
    ppermute x6, waiting for transfers between devices: 2.34 us -> 3.41 us  [the longest x3 3.4 us: body(): lax.ppermute(results[k], 'sect', [(i, partner(i, k, sects)) for i in rang...]
    ppermute x6, starting transfers between devices: 10.8 us -> 10.1 us  [the longest x3 5.62 us: body(): lax.ppermute(queries, 'sect', [(partner(i, k, sects), i) for i in range(s...]
  transfers between devices with their start and end apart: 7 -> 7, of which waited for: 3 -> 4; matrix products, arithmetic and copies ran while one was open for 0% -> 0% of each run, Pallas kernels for 25% -> 29%
where the time goes in v12:
time: 25 us; the launch traced here: 24.8 us
  starting transfers between devices  10.1 us (40%)
  Pallas kernels  8.94 us (36%)
  waiting for transfers between devices  4.85 us (19%)
  between operations  0.77 us (3%)
    pallas_call x1, Pallas kernels, prefill(): pl.pallas_call(prefill_kernel, in_specs=[pl.BlockSpec(memory_space=pltpu....  7.02 us
    ppermute x3, starting transfers between devices, body(): lax.ppermute(queries, 'sect', [(partner(i, k, sects), i) for i in range(s...  5.62 us
    ppermute x3, starting transfers between devices, body(): lax.ppermute(results[k], 'sect', [(i, partner(i, k, sects)) for i in rang...  4.46 us
    ppermute x3, waiting for transfers between devices, body(): lax.ppermute(results[k], 'sect', [(i, partner(i, k, sects)) for i in rang...  3.4 us
    ppermute x1, waiting for transfers between devices, body(): far = lax.ppermute(near, 'sub', [(0, 1), (1, 0)])  1.44 us
    pallas_call x1, Pallas kernels, finish(): pl.pallas_call(finish_kernel, in_specs=[vmem] * (3 + len(blocks)), out_sp...  0.86 us
    pallas_call x1, Pallas kernels, decode(): pl.pallas_call(decode_kernel, in_specs=[vmem] * 4, out_specs=[vmem] * par...  0.85 us
  transfers between devices with their start and end apart: 7, of which 4 were waited for; matrix products, arithmetic and copies ran while one was open for 0% of the time, Pallas kernels for 29%

profile of v12, /device:TPU:0, one launch (start us, length us, event | category | flops | bytes accessed | tf_op | source)
XLA Modules:
  0.0 24.8 jit_solution(7479469358956046552)
XLA Ops:
  0.0 3.0 %collective-permute-start.2 = (bf16[4,4096]{1,0:T(4,128)(2,1)}, bf16[4,4096]{1,0:T(4,128)(2,1)S(1)}, u32[]{:S(2)}, u32[]{:S(2)}) collective-permute-start(bf16[4,4096]{1,0:T(4,128)(2,1)} %queries_ref.1), channel_id=1, source_target_pairs={{4,0},{0,4},{12,8},{8,12},{5,1},{1,5},{13,9},{9,13},{6,2},{2,6},{1... | collective-permute-start | bytes 98312 | tf_op jit(solution)/shard_map/ppermute | solution.py:319
  3.0 2.6 %collective-permute-start.1 = (bf16[4,4096]{1,0:T(4,128)(2,1)}, bf16[4,4096]{1,0:T(4,128)(2,1)S(1)}, u32[]{:S(2)}, u32[]{:S(2)}) collective-permute-start(bf16[4,4096]{1,0:T(4,128)(2,1)} %queries_ref.1), channel_id=1, source_target_pairs={{8,0},{12,4},{0,8},{4,12},{9,1},{13,5},{1,9},{5,13},{10,2},{14,6},... | collective-permute-start | bytes 98312 | tf_op jit(solution)/shard_map/ppermute | solution.py:319
  5.6 0.0 collective-permute-start
  6.3 0.0 copy-start.1
  6.3 0.0 copy-start
  6.3 0.0 copy-start.2
  6.3 0.0 copy-start.3
  6.3 0.0 copy-start.4
  6.3 7.0 %prefill.1.near_ref = bf16[1168,128]{1,0:T(8,128)(2,1)S(1)} custom-call(s32[1]{0:T(128)S(6)} %copy.9.lengths_ref, bf16[1,4096,512]{2,1,0:T(8,128)(2,1)} %keys_ref.2, bf16[1,4096,512]{2,1,0:T(8,128)(2,1)} %values_ref.2, bf16[4,128,128]{2,1,0:T(8,128)(2,1)} %weight_ref.3), custom_call_target="tpu_custom_call" | custom-call | flops 1073741824 | bytes 8388608 | tf_op jit(solution)/shard_map/prefill/pallas_call | solution.py:147
  13.3 0.1 collective-permute-start.3
  13.4 0.0 collective-permute-done.2
  13.4 0.0 collective-permute-done.1
  13.4 0.0 collective-permute-done
  13.5 0.0 copy-done.1
  13.5 0.1 pad_maximum_fusion.rows_ref
  13.6 1.4 %collective-permute-done.3.far_ref = bf16[1168,128]{1,0:T(8,128)(2,1)S(1)} collective-permute-done((bf16[1168,128]{1,0:T(8,128)(2,1)S(1)}, bf16[1168,128]{1,0:T(8,128)(2,1)S(1)}, u32[]{:S(2)}, u32[]{:S(2)}) %collective-permute-start.3) | collective-permute-done | bytes 299040 | tf_op jit(solution)/shard_map/ppermute | solution.py:321
  15.0 0.0 copy-done
  15.0 0.8 %decode.1 = (bf16[4,4352]{1,0:T(4,128)(2,1)S(1)}, bf16[4,4352]{1,0:T(4,128)(2,1)S(1)}, bf16[4,4352]{1,0:T(4,128)(2,1)S(1)}, bf16[4,4352]{1,0:T(4,128)(2,1)S(1)}) custom-call(bf16[16,4096]{1,0:T(8,128)(2,1)S(1)} %pad_maximum_fusion.rows_ref, bf16[4,128,128]{2,1,0:T(8,128)(2,1)S(1)} %copy-done, bf16[1168,128]{1,0:T(8,128)(2,1)S(1)} %prefill.1.near_ref, ...), custom_call_target="tpu_custom_call" | custom-call | flops 83886080 | bytes 262144 | tf_op jit(solution)/shard_map/decode/pallas_call | solution.py:227
  15.9 2.0 %collective-permute-start.4 = (bf16[4,4352]{1,0:T(4,128)(2,1)S(1)}, bf16[4,4352]{1,0:T(4,128)(2,1)S(1)}, u32[]{:S(2)}, u32[]{:S(2)}) collective-permute-start(bf16[4,4352]{1,0:T(4,128)(2,1)S(1)} %get-tuple-element.14), channel_id=1, source_target_pairs={{0,8},{4,12},{8,0},{12,4},{1,9},{5,13},{9,1},{13,5},{2,10},{6,14},... | collective-permute-start | bytes 104456 | tf_op jit(solution)/shard_map/ppermute | solution.py:326
  17.8 2.0 %collective-permute-start.5 = (bf16[4,4352]{1,0:T(4,128)(2,1)S(1)}, bf16[4,4352]{1,0:T(4,128)(2,1)S(1)}, u32[]{:S(2)}, u32[]{:S(2)}) collective-permute-start(bf16[4,4352]{1,0:T(4,128)(2,1)S(1)} %get-tuple-element.15), channel_id=1, source_target_pairs={{0,12},{4,8},{8,4},{12,0},{1,13},{5,9},{9,5},{13,1},{2,14},{6,10},... | collective-permute-start | bytes 104456 | tf_op jit(solution)/shard_map/ppermute | solution.py:326
  19.8 0.5 %collective-permute-start.6 = (bf16[4,4352]{1,0:T(4,128)(2,1)S(1)}, bf16[4,4352]{1,0:T(4,128)(2,1)S(1)}, u32[]{:S(2)}, u32[]{:S(2)}) collective-permute-start(bf16[4,4352]{1,0:T(4,128)(2,1)S(1)} %get-tuple-element.16), channel_id=1, source_target_pairs={{0,4},{4,0},{8,12},{12,8},{1,5},{5,1},{9,13},{13,9},{2,6},{6,2},{1... | collective-permute-start | bytes 104456 | tf_op jit(solution)/shard_map/ppermute | solution.py:326
  20.3 0.0 copy-done.2
  20.3 0.0 copy-done.3
  20.3 0.2 own.1
  20.5 0.2 collective-permute-done.4.refs_1_
  20.8 3.0 %collective-permute-done.5.refs_2_ = bf16[4,4352]{1,0:T(4,128)(2,1)S(1)} collective-permute-done((bf16[4,4352]{1,0:T(4,128)(2,1)S(1)}, bf16[4,4352]{1,0:T(4,128)(2,1)S(1)}, u32[]{:S(2)}, u32[]{:S(2)}) %collective-permute-start.5) | collective-permute-done | bytes 34848 | tf_op jit(solution)/shard_map/ppermute | solution.py:326
  23.7 0.2 collective-permute-done.6.refs_3_
  23.9 0.0 copy-done.4
  23.9 0.9 %finish.1 = bf16[4,4096]{1,0:T(4,128)(2,1)} custom-call(s32[1,32]{1,0:T(1,128)S(1)} %bitcast.1, f32[4,4096]{1,0:T(4,128)S(1)} %get-tuple-element.12.num_ref, f32[4,128]{1,0:T(4,128)S(1)} %get-tuple-element.13.weight_ref, bf16[4,4352]{1,0:T(4,128)(2,1)S(1)} %get-tuple-element.11._.refs_0_, bf16[4,4352]{1,0:T(4,128)(2,1)S(1)} %collective-permute-done.4.refs_1_, ...), custom_call_target="tpu_custom_call" | custom-call | tf_op jit(solution)/shard_map/finish/pallas_call | solution.py:306
Async XLA Ops:
  0.0 13.4 %collective-permute-start.2 = (bf16[4,4096]{1,0:T(4,128)(2,1)}, bf16[4,4096]{1,0:T(4,128)(2,1)S(1)}, u32[]{:S(2)}, u32[]{:S(2)}) collective-permute-start(bf16[4,4096]{1,0:T(4,128)(2,1)} %queries_ref.1), channel_id=1, source_target_pairs={{4,0},{0,4},{12,8},{8,12},{5,1},{1,5},{13,9},{9,13},{6,2},{2,6},{1... | collective-permute-start | bytes 98312 | tf_op jit(solution)/shard_map/ppermute | solution.py:319
  3.0 10.4 %collective-permute-start.1 = (bf16[4,4096]{1,0:T(4,128)(2,1)}, bf16[4,4096]{1,0:T(4,128)(2,1)S(1)}, u32[]{:S(2)}, u32[]{:S(2)}) collective-permute-start(bf16[4,4096]{1,0:T(4,128)(2,1)} %queries_ref.1), channel_id=1, source_target_pairs={{8,0},{12,4},{0,8},{4,12},{9,1},{13,5},{1,9},{5,13},{10,2},{14,6},... | collective-permute-start | bytes 98312 | tf_op jit(solution)/shard_map/ppermute | solution.py:319
  5.6 7.8 %collective-permute-start = (bf16[4,4096]{1,0:T(4,128)(2,1)}, bf16[4,4096]{1,0:T(4,128)(2,1)S(1)}, u32[]{:S(2)}, u32[]{:S(2)}) collective-permute-start(bf16[4,4096]{1,0:T(4,128)(2,1)} %queries_ref.1), channel_id=1, source_target_pairs={{12,0},{8,4},{4,8},{0,12},{13,1},{9,5},{5,9},{1,13},{14,2},{10,6},... | collective-permute-start | bytes 98312 | tf_op jit(solution)/shard_map/ppermute | solution.py:319
  6.3 7.2 %copy-start.1 = (bf16[4,4096]{1,0:T(4,128)(2,1)S(1)}, bf16[4,4096]{1,0:T(4,128)(2,1)}, u32[]{:S(2)}) copy-start(bf16[4,4096]{1,0:T(4,128)(2,1)} %queries_ref.1) | copy-start | bytes 98308
  6.3 8.7 %copy-start = (bf16[4,128,128]{2,1,0:T(8,128)(2,1)S(1)}, bf16[4,128,128]{2,1,0:T(8,128)(2,1)}, u32[]{:S(2)}) copy-start(bf16[4,128,128]{2,1,0:T(8,128)(2,1)} %weight_ref.3) | copy-start | bytes 393220
  6.3 14.0 %copy-start.2 = (bf16[4,512]{1,0:T(4,128)(2,1)S(1)}, bf16[4,512]{1,0:T(4,128)(2,1)}, u32[]{:S(2)}) copy-start(bf16[4,512]{1,0:T(4,128)(2,1)} %keys_ref.3) | copy-start | bytes 12292
  6.3 14.0 %copy-start.3 = (bf16[4,512]{1,0:T(4,128)(2,1)S(1)}, bf16[4,512]{1,0:T(4,128)(2,1)}, u32[]{:S(2)}) copy-start(bf16[4,512]{1,0:T(4,128)(2,1)} %values_ref.3) | copy-start | bytes 12292
  6.3 17.6 %copy-start.4 = (s32[32]{0:T(128)S(1)}, s32[32]{0:T(128)}, u32[]{:S(2)}) copy-start(s32[32]{0:T(128)} %param.15) | copy-start | bytes 388
  13.3 1.7 %collective-permute-start.3 = (bf16[1168,128]{1,0:T(8,128)(2,1)S(1)}, bf16[1168,128]{1,0:T(8,128)(2,1)S(1)}, u32[]{:S(2)}, u32[]{:S(2)}) collective-permute-start(bf16[1168,128]{1,0:T(8,128)(2,1)S(1)} %prefill.1.near_ref), channel_id=1, source_target_pairs={{0,1},{1,0},{2,3},{3,2},{4,5},{5,4},{6,7},{7,6},{8,9},{9,8},{10,11... | collective-permute-start | bytes 897032 | tf_op jit(solution)/shard_map/ppermute | solution.py:321
  15.9 4.9 %collective-permute-start.4 = (bf16[4,4352]{1,0:T(4,128)(2,1)S(1)}, bf16[4,4352]{1,0:T(4,128)(2,1)S(1)}, u32[]{:S(2)}, u32[]{:S(2)}) collective-permute-start(bf16[4,4352]{1,0:T(4,128)(2,1)S(1)} %get-tuple-element.14), channel_id=1, source_target_pairs={{0,8},{4,12},{8,0},{12,4},{1,9},{5,13},{9,1},{13,5},{2,10},{6,14},... | collective-permute-start | bytes 104456 | tf_op jit(solution)/shard_map/ppermute | solution.py:326
  17.8 5.9 %collective-permute-start.5 = (bf16[4,4352]{1,0:T(4,128)(2,1)S(1)}, bf16[4,4352]{1,0:T(4,128)(2,1)S(1)}, u32[]{:S(2)}, u32[]{:S(2)}) collective-permute-start(bf16[4,4352]{1,0:T(4,128)(2,1)S(1)} %get-tuple-element.15), channel_id=1, source_target_pairs={{0,12},{4,8},{8,4},{12,0},{1,13},{5,9},{9,5},{13,1},{2,14},{6,10},... | collective-permute-start | bytes 104456 | tf_op jit(solution)/shard_map/ppermute | solution.py:326
  19.8 4.1 %collective-permute-start.6 = (bf16[4,4352]{1,0:T(4,128)(2,1)S(1)}, bf16[4,4352]{1,0:T(4,128)(2,1)S(1)}, u32[]{:S(2)}, u32[]{:S(2)}) collective-permute-start(bf16[4,4352]{1,0:T(4,128)(2,1)S(1)} %get-tuple-element.16), channel_id=1, source_target_pairs={{0,4},{4,0},{8,12},{12,8},{1,5},{5,1},{9,13},{13,9},{2,6},{6,2},{1... | collective-permute-start | bytes 104456 | tf_op jit(solution)/shard_map/ppermute | solution.py:326

commit v13 on v9

--- a/solution.py
+++ b/solution.py
@@ -25,7 +25,7 @@
 
 def prefill_kernel(
     lengths_ref, keys_ref, values_ref, weight_ref, out_ref,
-    keys_at, values_at, weight_at, wide_ref, proj_ref, state_ref, norm_ref,
+    keys_at, values_at, weight_at, wide_ref, proj_ref, mapped_ref, state_ref, norm_ref,
     weight_sem, load_sem, slab_sem,
 ):
     heads, head_size, feats = weight_ref.shape
@@ -89,7 +89,7 @@
             )
             proj_ref[c % 2, j] = proj.astype(jnp.bfloat16)
 
-    def collect(c):
+    def featurize(c):
         position = c * BLOCK + lax.broadcasted_iota(jnp.int32, (1, BLOCK), 1)
         live = jnp.where(position < begin, 1.0, 0.0).astype(jnp.bfloat16)
         for j in range(pairs):
@@ -98,17 +98,23 @@
             while len(some) > 1:
                 some = [x + y for x, y in zip(some[::2], some[1::2])]
             norm_ref[j] += some[0].astype(jnp.float32)
+            mapped_ref[c % 2, j] = mapped
+
+    def collect(c):
+        for j in range(pairs):
             state_ref[j] += jnp.dot(
-                mapped,
+                mapped_ref[c % 2, j],
                 values_at[c * BLOCK : (c + 1) * BLOCK, j * 2 * head_size : (j + 1) * 2 * head_size],
                 preferred_element_type=jnp.float32,
             )
 
-    project(0)
-    for c in range(chunks):
-        if c + 1 < chunks:
-            project(c + 1)
-        collect(c)
+    for step in range(chunks + 2):
+        if step < chunks:
+            project(step)
+        if 0 <= step - 1 < chunks:
+            featurize(step - 1)
+        if step >= 2:
+            collect(step - 2)
 
     tile = []
     for g in range(heads):
@@ -142,6 +148,7 @@
             pltpu.VMEM((span, width), jnp.bfloat16),
             pltpu.VMEM(weight.shape, jnp.bfloat16),
             pltpu.VMEM((heads // 2, 2 * feats, 2 * head_size), jnp.bfloat16),
+            pltpu.VMEM((2, heads // 2, 2 * feats, BLOCK), jnp.bfloat16),
             pltpu.VMEM((2, heads // 2, 2 * feats, BLOCK), jnp.bfloat16),
             pltpu.VMEM((heads // 2, 2 * feats, 2 * head_size), jnp.float32),
             pltpu.VMEM((heads // 2, 2 * feats, 128), jnp.float32),

time: 23.2 us -> 23.9 us (1.030)
  Pallas kernels: 7.47 us -> 8.13 us
    pallas_call x1, Pallas kernels: 5.55 us -> 6.21 us  [prefill(): pl.pallas_call(prefill_kernel, in_specs=[pl.BlockSpec(memory_space=pltpu....]
  transfers between devices with their start and end apart: 7 -> 7, of which waited for: 3 -> 3; matrix products, arithmetic and copies ran while one was open for 0% -> 0% of each run, Pallas kernels for 25% -> 27%
where the time goes in v13:
time: 23.9 us; the launch traced here: 23.7 us
  starting transfers between devices  10.9 us (46%)
  Pallas kernels  8.13 us (34%)
  waiting for transfers between devices  3.79 us (16%)
  between operations  0.77 us (3%)
    ppermute x3, starting transfers between devices, body(): lax.ppermute(queries, 'sect', [((i + k) % sects, i) for i in range(sects)])  6.96 us
    pallas_call x1, Pallas kernels, prefill(): pl.pallas_call(prefill_kernel, in_specs=[pl.BlockSpec(memory_space=pltpu....  6.21 us
    ppermute x3, starting transfers between devices, body(): lax.ppermute(results[k], 'sect', [(i, (i + k) % sects) for i in range(sec...  3.88 us
    ppermute x3, waiting for transfers between devices, body(): lax.ppermute(results[k], 'sect', [(i, (i + k) % sects) for i in range(sec...  2.34 us
    ppermute x1, waiting for transfers between devices, body(): far = lax.ppermute(near, 'sub', [(0, 1), (1, 0)])  1.44 us
    pallas_call x1, Pallas kernels, finish(): pl.pallas_call(finish_kernel, in_specs=[vmem] * (3 + len(blocks)), out_sp...  0.86 us
    pallas_call x1, Pallas kernels, decode(): pl.pallas_call(decode_kernel, in_specs=[vmem] * 4, out_specs=[vmem] * par...  0.85 us
  transfers between devices with their start and end apart: 7, of which 3 were waited for; matrix products, arithmetic and copies ran while one was open for 0% of the time, Pallas kernels for 27%

profile of v13, /device:TPU:0, one launch (start us, length us, event | category | flops | bytes accessed | tf_op | source)
XLA Modules:
  0.0 23.7 jit_solution(18329136638423810112)
XLA Ops:
  0.0 3.0 %collective-permute-start.2 = (bf16[4,4096]{1,0:T(4,128)(2,1)}, bf16[4,4096]{1,0:T(4,128)(2,1)S(1)}, u32[]{:S(2)}, u32[]{:S(2)}) collective-permute-start(bf16[4,4096]{1,0:T(4,128)(2,1)} %queries_ref.1), channel_id=1, source_target_pairs={{12,0},{0,4},{4,8},{8,12},{13,1},{1,5},{5,9},{9,13},{14,2},{2,6},{... | collective-permute-start | bytes 98312 | tf_op jit(solution)/shard_map/ppermute | solution.py:315
  3.0 2.6 %collective-permute-start.1 = (bf16[4,4096]{1,0:T(4,128)(2,1)}, bf16[4,4096]{1,0:T(4,128)(2,1)S(1)}, u32[]{:S(2)}, u32[]{:S(2)}) collective-permute-start(bf16[4,4096]{1,0:T(4,128)(2,1)} %queries_ref.1), channel_id=1, source_target_pairs={{8,0},{12,4},{0,8},{4,12},{9,1},{13,5},{1,9},{5,13},{10,2},{14,6},... | collective-permute-start | bytes 98312 | tf_op jit(solution)/shard_map/ppermute | solution.py:315
  5.6 1.3 %collective-permute-start = (bf16[4,4096]{1,0:T(4,128)(2,1)}, bf16[4,4096]{1,0:T(4,128)(2,1)S(1)}, u32[]{:S(2)}, u32[]{:S(2)}) collective-permute-start(bf16[4,4096]{1,0:T(4,128)(2,1)} %queries_ref.1), channel_id=1, source_target_pairs={{4,0},{8,4},{12,8},{0,12},{5,1},{9,5},{13,9},{1,13},{6,2},{10,6},{... | collective-permute-start | bytes 98312 | tf_op jit(solution)/shard_map/ppermute | solution.py:315
  7.6 0.0 copy-start.1
  7.6 0.0 copy-start
  7.6 0.0 copy-start.2
  7.6 0.0 copy-start.3
  7.7 0.0 copy-start.4
  7.7 6.2 %prefill.1.near_ref = bf16[1168,128]{1,0:T(8,128)(2,1)S(1)} custom-call(s32[1]{0:T(128)S(6)} %copy.9.lengths_ref, bf16[1,4096,512]{2,1,0:T(8,128)(2,1)} %keys_ref.2, bf16[1,4096,512]{2,1,0:T(8,128)(2,1)} %values_ref.2, bf16[4,128,128]{2,1,0:T(8,128)(2,1)} %weight_ref.3), custom_call_target="tpu_custom_call" | custom-call | flops 1073741824 | bytes 8388608 | tf_op jit(solution)/shard_map/prefill/pallas_call | solution.py:141
  13.9 0.1 collective-permute-start.3
  14.0 0.0 collective-permute-done.2
  14.0 0.0 collective-permute-done.1
  14.0 0.0 collective-permute-done
  14.0 0.0 copy-done.1
  14.0 0.1 pad_maximum_fusion.rows_ref
  14.1 1.4 %collective-permute-done.3.far_ref = bf16[1168,128]{1,0:T(8,128)(2,1)S(1)} collective-permute-done((bf16[1168,128]{1,0:T(8,128)(2,1)S(1)}, bf16[1168,128]{1,0:T(8,128)(2,1)S(1)}, u32[]{:S(2)}, u32[]{:S(2)}) %collective-permute-start.3) | collective-permute-done | bytes 299040 | tf_op jit(solution)/shard_map/ppermute | solution.py:318
  15.5 0.0 copy-done
  15.5 0.8 %decode.1 = (bf16[4,4352]{1,0:T(4,128)(2,1)S(1)}, bf16[4,4352]{1,0:T(4,128)(2,1)S(1)}, bf16[4,4352]{1,0:T(4,128)(2,1)S(1)}, bf16[4,4352]{1,0:T(4,128)(2,1)S(1)}) custom-call(bf16[16,4096]{1,0:T(8,128)(2,1)S(1)} %pad_maximum_fusion.rows_ref, bf16[4,128,128]{2,1,0:T(8,128)(2,1)S(1)} %copy-done, bf16[1168,128]{1,0:T(8,128)(2,1)S(1)} %prefill.1.near_ref, ...), custom_call_target="tpu_custom_call" | custom-call | flops 83886080 | bytes 262144 | tf_op jit(solution)/shard_map/decode/pallas_call | solution.py:222
  16.4 0.7 %collective-permute-start.4 = (bf16[4,4352]{1,0:T(4,128)(2,1)S(1)}, bf16[4,4352]{1,0:T(4,128)(2,1)S(1)}, u32[]{:S(2)}, u32[]{:S(2)}) collective-permute-start(bf16[4,4352]{1,0:T(4,128)(2,1)S(1)} %get-tuple-element.14), channel_id=1, source_target_pairs={{0,4},{4,8},{8,12},{12,0},{1,5},{5,9},{9,13},{13,1},{2,6},{6,10},{... | collective-permute-start | bytes 104456 | tf_op jit(solution)/shard_map/ppermute | solution.py:322
  17.1 0.3 %collective-permute-start.5 = (bf16[4,4352]{1,0:T(4,128)(2,1)S(1)}, bf16[4,4352]{1,0:T(4,128)(2,1)S(1)}, u32[]{:S(2)}, u32[]{:S(2)}) collective-permute-start(bf16[4,4352]{1,0:T(4,128)(2,1)S(1)} %get-tuple-element.15), channel_id=1, source_target_pairs={{0,8},{4,12},{8,0},{12,4},{1,9},{5,13},{9,1},{13,5},{2,10},{6,14},... | collective-permute-start | bytes 104456 | tf_op jit(solution)/shard_map/ppermute | solution.py:322
  17.5 2.8 %collective-permute-start.6 = (bf16[4,4352]{1,0:T(4,128)(2,1)S(1)}, bf16[4,4352]{1,0:T(4,128)(2,1)S(1)}, u32[]{:S(2)}, u32[]{:S(2)}) collective-permute-start(bf16[4,4352]{1,0:T(4,128)(2,1)S(1)} %get-tuple-element.16), channel_id=1, source_target_pairs={{0,12},{4,0},{8,4},{12,8},{1,13},{5,1},{9,5},{13,9},{2,14},{6,2},{... | collective-permute-start | bytes 104456 | tf_op jit(solution)/shard_map/ppermute | solution.py:322
  20.3 0.0 copy-done.2
  20.3 0.0 copy-done.3
  20.3 0.2 own.1
  20.5 2.0 %collective-permute-done.4.refs_1_ = bf16[4,4352]{1,0:T(4,128)(2,1)S(1)} collective-permute-done((bf16[4,4352]{1,0:T(4,128)(2,1)S(1)}, bf16[4,4352]{1,0:T(4,128)(2,1)S(1)}, u32[]{:S(2)}, u32[]{:S(2)}) %collective-permute-start.4) | collective-permute-done | bytes 34848 | tf_op jit(solution)/shard_map/ppermute | solution.py:322
  22.5 0.0 collective-permute-done.5.refs_2_
  22.5 0.4 %collective-permute-done.6.refs_3_ = bf16[4,4352]{1,0:T(4,128)(2,1)S(1)} collective-permute-done((bf16[4,4352]{1,0:T(4,128)(2,1)S(1)}, bf16[4,4352]{1,0:T(4,128)(2,1)S(1)}, u32[]{:S(2)}, u32[]{:S(2)}) %collective-permute-start.6) | collective-permute-done | bytes 34848 | tf_op jit(solution)/shard_map/ppermute | solution.py:322
  22.8 0.0 copy-done.4
  22.8 0.9 %finish.1 = bf16[4,4096]{1,0:T(4,128)(2,1)} custom-call(s32[1,32]{1,0:T(1,128)S(1)} %bitcast.1, f32[4,4096]{1,0:T(4,128)S(1)} %get-tuple-element.12.num_ref, f32[4,128]{1,0:T(4,128)S(1)} %get-tuple-element.13.weight_ref, bf16[4,4352]{1,0:T(4,128)(2,1)S(1)} %get-tuple-element.11._.refs_0_, bf16[4,4352]{1,0:T(4,128)(2,1)S(1)} %collective-permute-done.4.refs_1_, ...), custom_call_target="tpu_custom_call" | custom-call | tf_op jit(solution)/shard_map/finish/pallas_call | solution.py:301
Async XLA Ops:
  0.0 14.0 %collective-permute-start.2 = (bf16[4,4096]{1,0:T(4,128)(2,1)}, bf16[4,4096]{1,0:T(4,128)(2,1)S(1)}, u32[]{:S(2)}, u32[]{:S(2)}) collective-permute-start(bf16[4,4096]{1,0:T(4,128)(2,1)} %queries_ref.1), channel_id=1, source_target_pairs={{12,0},{0,4},{4,8},{8,12},{13,1},{1,5},{5,9},{9,13},{14,2},{2,6},{... | collective-permute-start | bytes 98312 | tf_op jit(solution)/shard_map/ppermute | solution.py:315
  3.0 10.9 %collective-permute-start.1 = (bf16[4,4096]{1,0:T(4,128)(2,1)}, bf16[4,4096]{1,0:T(4,128)(2,1)S(1)}, u32[]{:S(2)}, u32[]{:S(2)}) collective-permute-start(bf16[4,4096]{1,0:T(4,128)(2,1)} %queries_ref.1), channel_id=1, source_target_pairs={{8,0},{12,4},{0,8},{4,12},{9,1},{13,5},{1,9},{5,13},{10,2},{14,6},... | collective-permute-start | bytes 98312 | tf_op jit(solution)/shard_map/ppermute | solution.py:315
  5.6 8.4 %collective-permute-start = (bf16[4,4096]{1,0:T(4,128)(2,1)}, bf16[4,4096]{1,0:T(4,128)(2,1)S(1)}, u32[]{:S(2)}, u32[]{:S(2)}) collective-permute-start(bf16[4,4096]{1,0:T(4,128)(2,1)} %queries_ref.1), channel_id=1, source_target_pairs={{4,0},{8,4},{12,8},{0,12},{5,1},{9,5},{13,9},{1,13},{6,2},{10,6},{... | collective-permute-start | bytes 98312 | tf_op jit(solution)/shard_map/ppermute | solution.py:315
  7.6 6.4 %copy-start.1 = (bf16[4,4096]{1,0:T(4,128)(2,1)S(1)}, bf16[4,4096]{1,0:T(4,128)(2,1)}, u32[]{:S(2)}) copy-start(bf16[4,4096]{1,0:T(4,128)(2,1)} %queries_ref.1) | copy-start | bytes 98308
  7.6 7.9 %copy-start = (bf16[4,128,128]{2,1,0:T(8,128)(2,1)S(1)}, bf16[4,128,128]{2,1,0:T(8,128)(2,1)}, u32[]{:S(2)}) copy-start(bf16[4,128,128]{2,1,0:T(8,128)(2,1)} %weight_ref.3) | copy-start | bytes 393220
  7.6 12.6 %copy-start.2 = (bf16[4,512]{1,0:T(4,128)(2,1)S(1)}, bf16[4,512]{1,0:T(4,128)(2,1)}, u32[]{:S(2)}) copy-start(bf16[4,512]{1,0:T(4,128)(2,1)} %keys_ref.3) | copy-start | bytes 12292
  7.6 12.6 %copy-start.3 = (bf16[4,512]{1,0:T(4,128)(2,1)S(1)}, bf16[4,512]{1,0:T(4,128)(2,1)}, u32[]{:S(2)}) copy-start(bf16[4,512]{1,0:T(4,128)(2,1)} %values_ref.3) | copy-start | bytes 12292
  7.7 15.2 %copy-start.4 = (s32[32]{0:T(128)S(1)}, s32[32]{0:T(128)}, u32[]{:S(2)}) copy-start(s32[32]{0:T(128)} %param.15) | copy-start | bytes 388
  13.9 1.7 %collective-permute-start.3 = (bf16[1168,128]{1,0:T(8,128)(2,1)S(1)}, bf16[1168,128]{1,0:T(8,128)(2,1)S(1)}, u32[]{:S(2)}, u32[]{:S(2)}) collective-permute-start(bf16[1168,128]{1,0:T(8,128)(2,1)S(1)} %prefill.1.near_ref), channel_id=1, source_target_pairs={{0,1},{1,0},{2,3},{3,2},{4,5},{5,4},{6,7},{7,6},{8,9},{9,8},{10,11... | collective-permute-start | bytes 897032 | tf_op jit(solution)/shard_map/ppermute | solution.py:318
  16.4 6.1 %collective-permute-start.4 = (bf16[4,4352]{1,0:T(4,128)(2,1)S(1)}, bf16[4,4352]{1,0:T(4,128)(2,1)S(1)}, u32[]{:S(2)}, u32[]{:S(2)}) collective-permute-start(bf16[4,4352]{1,0:T(4,128)(2,1)S(1)} %get-tuple-element.14), channel_id=1, source_target_pairs={{0,4},{4,8},{8,12},{12,0},{1,5},{5,9},{9,13},{13,1},{2,6},{6,10},{... | collective-permute-start | bytes 104456 | tf_op jit(solution)/shard_map/ppermute | solution.py:322
  17.1 5.3 %collective-permute-start.5 = (bf16[4,4352]{1,0:T(4,128)(2,1)S(1)}, bf16[4,4352]{1,0:T(4,128)(2,1)S(1)}, u32[]{:S(2)}, u32[]{:S(2)}) collective-permute-start(bf16[4,4352]{1,0:T(4,128)(2,1)S(1)} %get-tuple-element.15), channel_id=1, source_target_pairs={{0,8},{4,12},{8,0},{12,4},{1,9},{5,13},{9,1},{13,5},{2,10},{6,14},... | collective-permute-start | bytes 104456 | tf_op jit(solution)/shard_map/ppermute | solution.py:322
  17.5 5.4 %collective-permute-start.6 = (bf16[4,4352]{1,0:T(4,128)(2,1)S(1)}, bf16[4,4352]{1,0:T(4,128)(2,1)S(1)}, u32[]{:S(2)}, u32[]{:S(2)}) collective-permute-start(bf16[4,4352]{1,0:T(4,128)(2,1)S(1)} %get-tuple-element.16), channel_id=1, source_target_pairs={{0,12},{4,0},{8,4},{12,8},{1,13},{5,1},{9,5},{13,9},{2,14},{6,2},{... | collective-permute-start | bytes 104456 | tf_op jit(solution)/shard_map/ppermute | solution.py:322

commit v14 on v9

--- a/solution.py
+++ b/solution.py
@@ -25,31 +25,16 @@
 
 def prefill_kernel(
     lengths_ref, keys_ref, values_ref, weight_ref, out_ref,
-    keys_at, values_at, weight_at, wide_ref, proj_ref, state_ref, norm_ref,
-    weight_sem, load_sem, slab_sem,
+    weight_at, wide_ref, proj_ref, state_ref, norm_ref,
+    weight_sem, slab_sem,
 ):
     heads, head_size, feats = weight_ref.shape
     pairs = heads // 2
     span = keys_ref.shape[1]
+    keys_at, values_at = keys_ref.at[0], values_ref.at[0]
     chunks = span // BLOCK
     get_weight = pltpu.make_async_copy(weight_ref, weight_at, weight_sem)
     get_weight.start()
-    loads = []
-    for c in range(chunks):
-        rows = pl.ds(c * BLOCK, BLOCK)
-        loads.append(
-            [
-                pltpu.make_async_copy(keys_ref.at[0, rows, :], keys_at.at[rows, :], load_sem.at[0, c]),
-                pltpu.make_async_copy(values_ref.at[0, rows, :], values_at.at[rows, :], load_sem.at[1, c]),
-            ]
-        )
-
-    def fetch(c):
-        for priority, load in enumerate(loads[c]):
-            load.start(priority=priority)
-
-    for c in range(AHEAD):
-        fetch(c)
     state_ref[...] = jnp.zeros_like(state_ref)
     norm_ref[...] = jnp.zeros_like(norm_ref)
     wide_ref[...] = jnp.zeros_like(wide_ref)
@@ -76,10 +61,6 @@
             slabs[-1].start()
 
     def project(c):
-        for load in loads[c]:
-            load.wait()
-        if c + AHEAD < chunks:
-            fetch(c + AHEAD)
         for j in range(pairs):
             proj = lax.dot_general(
                 wide_ref[j],
@@ -129,32 +110,33 @@
 def prefill(keys, values, weight, lengths):
     heads, head_size, feats = weight.shape
     span, width = keys.shape[1:]
-    arrays = (keys, values, weight)
     hbm = pl.BlockSpec(memory_space=pltpu.MemorySpace.HBM)
     vmem = pl.BlockSpec(memory_space=pltpu.VMEM)
     return pl.pallas_call(
         prefill_kernel,
-        in_specs=[pl.BlockSpec(memory_space=pltpu.SMEM)] + [hbm] * len(arrays),
+        in_specs=[pl.BlockSpec(memory_space=pltpu.SMEM), vmem, vmem, hbm],
         out_specs=vmem,
         out_shape=jax.ShapeDtypeStruct((heads * feats + 16 + 2 * heads * SLAB, head_size), jnp.bfloat16),
         scratch_shapes=[
-            pltpu.VMEM((span, width), jnp.bfloat16),
-            pltpu.VMEM((span, width), jnp.bfloat16),
             pltpu.VMEM(weight.shape, jnp.bfloat16),
             pltpu.VMEM((heads // 2, 2 * feats, 2 * head_size), jnp.bfloat16),
             pltpu.VMEM((2, heads // 2, 2 * feats, BLOCK), jnp.bfloat16),
             pltpu.VMEM((heads // 2, 2 * feats, 2 * head_size), jnp.float32),
             pltpu.VMEM((heads // 2, 2 * feats, 128), jnp.float32),
             pltpu.SemaphoreType.DMA,
-            pltpu.SemaphoreType.DMA((2, span // BLOCK)),
             pltpu.SemaphoreType.DMA((2, heads)),
         ],
-        compiler_params=pltpu.CompilerParams(vmem_limit_bytes=40 * 1024 * 1024),
+        compiler_params=pltpu.CompilerParams(vmem_limit_bytes=16 * 1024 * 1024),
         cost_estimate=pl.CostEstimate(
             flops=4 * span * width * feats, bytes_accessed=4 * span * width, transcendentals=span * width
         ),
         name="prefill",
-    )(lengths, *[pltpu.with_memory_space_constraint(x, pltpu.MemorySpace.HBM) for x in arrays])
+    )(
+        lengths,
+        pltpu.with_memory_space_constraint(keys, pltpu.MemorySpace.VMEM),
+        pltpu.with_memory_space_constraint(values, pltpu.MemorySpace.VMEM),
+        pltpu.with_memory_space_constraint(weight, pltpu.MemorySpace.HBM),
+    )
 
 
 def decode_kernel(rows_ref, weight_ref, near_ref, far_ref, *out_refs):
@@ -304,9 +286,13 @@
 def body(
     sects, prompt_keys, prompt_values, lengths, feature_weight, queries, new_keys, new_values, row_prompt
 ):
-    blocks = [queries] + [
-        lax.ppermute(queries, "sect", [((i + k) % sects, i) for i in range(sects)]) for k in range(1, sects)
+    asked = [
+        lax.ppermute(queries, "sect", [((i + k) % sects, i) for i in range(sects)]) for k in range(sects - 1, 0, -1)
     ]
+    blocks = [queries] + asked[::-1]
+    stay = [(0, 0), (1, 1)]
+    prompt_keys = lax.ppermute(prompt_keys, "sub", stay)
+    prompt_values = lax.ppermute(prompt_values, "sub", stay)
     near = prefill(prompt_keys, prompt_values, feature_weight, lengths)
     far = lax.ppermute(near, "sub", [(0, 1), (1, 0)])
     results = decode(jnp.concatenate(blocks, axis=0), feature_weight, near, far, sects)

time: 23.2 us -> 26.4 us (1.14)
  starting transfers between devices: 10.9 us -> 15.5 us
  Pallas kernels: 7.47 us -> 5.86 us
    ppermute x0 -> x2, starting transfers between devices: none -> 4.38 us  [the longest x1 2.19 us: body(): prompt_keys = lax.ppermute(prompt_keys, 'sub', stay)]
    pallas_call x1, Pallas kernels: 5.55 us -> 3.94 us  [prefill(): pl.pallas_call(prefill_kernel, in_specs=[pl.BlockSpec(memory_space=pltpu....]
    ppermute x3, starting transfers between devices: 3.88 us -> 4.97 us  [body(): lax.ppermute(results[k], 'sect', [(i, (i + k) % sects) for i in range(sec...]
    ppermute x3, starting transfers between devices: 6.96 us -> 6.06 us  [body(): lax.ppermute(queries, 'sect', [((i + k) % sects, i) for i in range(sects)])]
  transfers between devices with their start and end apart: 7 -> 9, of which waited for: 3 -> 5; matrix products, arithmetic and copies ran while one was open for 0% -> 0% of each run, Pallas kernels for 25% -> 16%
where the time goes in v14:
time: 26.4 us; the launch traced here: 26.2 us
  starting transfers between devices  15.5 us (59%)
  Pallas kernels  5.86 us (22%)
  waiting for transfers between devices  4.02 us (15%)
  between operations  0.77 us (3%)
    ppermute x3, starting transfers between devices, body(): lax.ppermute(queries, 'sect', [((i + k) % sects, i) for i in range(sects)])  6.06 us
    ppermute x3, starting transfers between devices, body(): lax.ppermute(results[k], 'sect', [(i, (i + k) % sects) for i in range(sec...  4.97 us
    pallas_call x1, Pallas kernels, prefill(): pl.pallas_call(prefill_kernel, in_specs=[pl.BlockSpec(memory_space=pltpu....  3.94 us
    ppermute x3, waiting for transfers between devices, body(): lax.ppermute(results[k], 'sect', [(i, (i + k) % sects) for i in range(sec...  2.54 us
    ppermute x1, starting transfers between devices, body(): prompt_keys = lax.ppermute(prompt_keys, 'sub', stay)  2.19 us
    ppermute x1, starting transfers between devices, body(): prompt_values = lax.ppermute(prompt_values, 'sub', stay)  2.19 us
    ppermute x1, waiting for transfers between devices, body(): far = lax.ppermute(near, 'sub', [(0, 1), (1, 0)])  1.33 us
    pallas_call x1, Pallas kernels, finish(): pl.pallas_call(finish_kernel, in_specs=[vmem] * (3 + len(blocks)), out_sp...  0.86 us
  transfers between devices with their start and end apart: 9, of which 5 were waited for; matrix products, arithmetic and copies ran while one was open for 0% of the time, Pallas kernels for 16%

profile of v14, /device:TPU:0, one launch (start us, length us, event | category | flops | bytes accessed | tf_op | source)
XLA Modules:
  0.0 26.2 jit_solution(3471689194327769168)
XLA Ops:
  0.0 2.2 %collective-permute-start.3 = (bf16[1,4096,512]{2,1,0:T(8,128)(2,1)}, bf16[1,4096,512]{2,1,0:T(8,128)(2,1)S(1)}, u32[]{:S(2)}, u32[]{:S(2)}) collective-permute-start(bf16[1,4096,512]{2,1,0:T(8,128)(2,1)} %param.8), channel_id=1, source_target_pairs={{0,0},{1,1},{2,2},{3,3},{4,4},{5,5},{6,6},{7,7},{8,8},{9,9},{10,10... | collective-permute-start | bytes 12582920 | tf_op jit(solution)/shard_map/ppermute | solution.py:294
  2.2 2.2 %collective-permute-start.4 = (bf16[1,4096,512]{2,1,0:T(8,128)(2,1)}, bf16[1,4096,512]{2,1,0:T(8,128)(2,1)S(1)}, u32[]{:S(2)}, u32[]{:S(2)}) collective-permute-start(bf16[1,4096,512]{2,1,0:T(8,128)(2,1)} %param.9), channel_id=1, source_target_pairs={{0,0},{1,1},{2,2},{3,3},{4,4},{5,5},{6,6},{7,7},{8,8},{9,9},{10,10... | collective-permute-start | bytes 12582920 | tf_op jit(solution)/shard_map/ppermute | solution.py:295
  4.4 5.0 %collective-permute-start = (bf16[4,4096]{1,0:T(4,128)(2,1)}, bf16[4,4096]{1,0:T(4,128)(2,1)S(1)}, u32[]{:S(2)}, u32[]{:S(2)}) collective-permute-start(bf16[4,4096]{1,0:T(4,128)(2,1)} %queries_ref.1), channel_id=1, source_target_pairs={{4,0},{8,4},{12,8},{0,12},{5,1},{9,5},{13,9},{1,13},{6,2},{10,6},{... | collective-permute-start | bytes 98312 | tf_op jit(solution)/shard_map/ppermute | solution.py:290
  9.4 0.0 collective-permute-start.1
  9.4 1.0 %collective-permute-start.2 = (bf16[4,4096]{1,0:T(4,128)(2,1)}, bf16[4,4096]{1,0:T(4,128)(2,1)S(1)}, u32[]{:S(2)}, u32[]{:S(2)}) collective-permute-start(bf16[4,4096]{1,0:T(4,128)(2,1)} %queries_ref.1), channel_id=1, source_target_pairs={{12,0},{0,4},{4,8},{8,12},{13,1},{1,5},{5,9},{9,13},{14,2},{2,6},{... | collective-permute-start | bytes 98312 | tf_op jit(solution)/shard_map/ppermute | solution.py:290
  11.1 0.0 copy-start.1
  11.1 0.0 copy-start
  11.1 0.0 copy-start.2
  11.1 0.0 copy-start.3
  11.1 0.0 copy-start.4
  11.1 0.0 collective-permute-done.3.keys_ref
  11.2 0.0 collective-permute-done.4.values_ref
  11.2 3.9 %prefill.1.near_ref = bf16[1168,128]{1,0:T(8,128)(2,1)S(1)} custom-call(s32[1]{0:T(128)S(6)} %copy.9.lengths_ref, bf16[1,4096,512]{2,1,0:T(8,128)(2,1)S(1)} %collective-permute-done.3.keys_ref, bf16[1,4096,512]{2,1,0:T(8,128)(2,1)S(1)} %collective-permute-done.4.values_ref, bf16[4,128,128]{2,1,0:T(8,128)(2,1)} %weight_ref.3), custom_call_target="tpu_custom_call" | custom-call | flops 1073741824 | bytes 8388608 | tf_op jit(solution)/shard_map/prefill/pallas_call | solution.py:115
  15.1 0.1 collective-permute-start.5
  15.2 0.0 collective-permute-done
  15.2 0.0 collective-permute-done.1
  15.2 0.1 collective-permute-done.2
  15.4 0.0 copy-done.1
  15.4 0.1 pad_maximum_fusion.rows_ref
  15.4 1.3 %collective-permute-done.5.far_ref = bf16[1168,128]{1,0:T(8,128)(2,1)S(1)} collective-permute-done((bf16[1168,128]{1,0:T(8,128)(2,1)S(1)}, bf16[1168,128]{1,0:T(8,128)(2,1)S(1)}, u32[]{:S(2)}, u32[]{:S(2)}) %collective-permute-start.5) | collective-permute-done | bytes 299040 | tf_op jit(solution)/shard_map/ppermute | solution.py:297
  16.8 0.0 copy-done
  16.8 0.8 %decode.1 = (bf16[4,4352]{1,0:T(4,128)(2,1)S(1)}, bf16[4,4352]{1,0:T(4,128)(2,1)S(1)}, bf16[4,4352]{1,0:T(4,128)(2,1)S(1)}, bf16[4,4352]{1,0:T(4,128)(2,1)S(1)}) custom-call(bf16[16,4096]{1,0:T(8,128)(2,1)S(1)} %pad_maximum_fusion.rows_ref, bf16[4,128,128]{2,1,0:T(8,128)(2,1)S(1)} %copy-done, bf16[1168,128]{1,0:T(8,128)(2,1)S(1)} %prefill.1.near_ref, ...), custom_call_target="tpu_custom_call" | custom-call | flops 83886080 | bytes 262144 | tf_op jit(solution)/shard_map/decode/pallas_call | solution.py:197
  17.6 2.5 %collective-permute-start.6 = (bf16[4,4352]{1,0:T(4,128)(2,1)S(1)}, bf16[4,4352]{1,0:T(4,128)(2,1)S(1)}, u32[]{:S(2)}, u32[]{:S(2)}) collective-permute-start(bf16[4,4352]{1,0:T(4,128)(2,1)S(1)} %get-tuple-element.14), channel_id=1, source_target_pairs={{0,4},{4,8},{8,12},{12,0},{1,5},{5,9},{9,13},{13,1},{2,6},{6,10},{... | collective-permute-start | bytes 104456 | tf_op jit(solution)/shard_map/ppermute | solution.py:301
  20.2 0.9 %collective-permute-start.7 = (bf16[4,4352]{1,0:T(4,128)(2,1)S(1)}, bf16[4,4352]{1,0:T(4,128)(2,1)S(1)}, u32[]{:S(2)}, u32[]{:S(2)}) collective-permute-start(bf16[4,4352]{1,0:T(4,128)(2,1)S(1)} %get-tuple-element.15), channel_id=1, source_target_pairs={{0,8},{4,12},{8,0},{12,4},{1,9},{5,13},{9,1},{13,5},{2,10},{6,14},... | collective-permute-start | bytes 104456 | tf_op jit(solution)/shard_map/ppermute | solution.py:301
  21.1 1.5 %collective-permute-start.8 = (bf16[4,4352]{1,0:T(4,128)(2,1)S(1)}, bf16[4,4352]{1,0:T(4,128)(2,1)S(1)}, u32[]{:S(2)}, u32[]{:S(2)}) collective-permute-start(bf16[4,4352]{1,0:T(4,128)(2,1)S(1)} %get-tuple-element.16), channel_id=1, source_target_pairs={{0,12},{4,0},{8,4},{12,8},{1,13},{5,1},{9,5},{13,9},{2,14},{6,2},{... | collective-permute-start | bytes 104456 | tf_op jit(solution)/shard_map/ppermute | solution.py:301
  22.6 0.0 copy-done.2
  22.6 0.0 copy-done.3
  22.6 0.2 own.1
  22.8 0.7 %collective-permute-done.6.refs_1_ = bf16[4,4352]{1,0:T(4,128)(2,1)S(1)} collective-permute-done((bf16[4,4352]{1,0:T(4,128)(2,1)S(1)}, bf16[4,4352]{1,0:T(4,128)(2,1)S(1)}, u32[]{:S(2)}, u32[]{:S(2)}) %collective-permute-start.6) | collective-permute-done | bytes 34848 | tf_op jit(solution)/shard_map/ppermute | solution.py:301
  23.5 1.8 %collective-permute-done.7.refs_2_ = bf16[4,4352]{1,0:T(4,128)(2,1)S(1)} collective-permute-done((bf16[4,4352]{1,0:T(4,128)(2,1)S(1)}, bf16[4,4352]{1,0:T(4,128)(2,1)S(1)}, u32[]{:S(2)}, u32[]{:S(2)}) %collective-permute-start.7) | collective-permute-done | bytes 34848 | tf_op jit(solution)/shard_map/ppermute | solution.py:301
  25.3 0.1 collective-permute-done.8.refs_3_
  25.4 0.0 copy-done.4
  25.4 0.9 %finish.1 = bf16[4,4096]{1,0:T(4,128)(2,1)} custom-call(s32[1,32]{1,0:T(1,128)S(1)} %bitcast.1, f32[4,4096]{1,0:T(4,128)S(1)} %get-tuple-element.12.num_ref, f32[4,128]{1,0:T(4,128)S(1)} %get-tuple-element.13.weight_ref, bf16[4,4352]{1,0:T(4,128)(2,1)S(1)} %get-tuple-element.11._.refs_0_, bf16[4,4352]{1,0:T(4,128)(2,1)S(1)} %collective-permute-done.6.refs_1_, ...), custom_call_target="tpu_custom_call" | custom-call | tf_op jit(solution)/shard_map/finish/pallas_call | solution.py:276
Async XLA Ops:
  0.0 11.1 %collective-permute-start.3 = (bf16[1,4096,512]{2,1,0:T(8,128)(2,1)}, bf16[1,4096,512]{2,1,0:T(8,128)(2,1)S(1)}, u32[]{:S(2)}, u32[]{:S(2)}) collective-permute-start(bf16[1,4096,512]{2,1,0:T(8,128)(2,1)} %param.8), channel_id=1, source_target_pairs={{0,0},{1,1},{2,2},{3,3},{4,4},{5,5},{6,6},{7,7},{8,8},{9,9},{10,10... | collective-permute-start | bytes 12582920 | tf_op jit(solution)/shard_map/ppermute | solution.py:294
  2.2 9.0 %collective-permute-start.4 = (bf16[1,4096,512]{2,1,0:T(8,128)(2,1)}, bf16[1,4096,512]{2,1,0:T(8,128)(2,1)S(1)}, u32[]{:S(2)}, u32[]{:S(2)}) collective-permute-start(bf16[1,4096,512]{2,1,0:T(8,128)(2,1)} %param.9), channel_id=1, source_target_pairs={{0,0},{1,1},{2,2},{3,3},{4,4},{5,5},{6,6},{7,7},{8,8},{9,9},{10,10... | collective-permute-start | bytes 12582920 | tf_op jit(solution)/shard_map/ppermute | solution.py:295
  4.4 10.8 %collective-permute-start = (bf16[4,4096]{1,0:T(4,128)(2,1)}, bf16[4,4096]{1,0:T(4,128)(2,1)S(1)}, u32[]{:S(2)}, u32[]{:S(2)}) collective-permute-start(bf16[4,4096]{1,0:T(4,128)(2,1)} %queries_ref.1), channel_id=1, source_target_pairs={{4,0},{8,4},{12,8},{0,12},{5,1},{9,5},{13,9},{1,13},{6,2},{10,6},{... | collective-permute-start | bytes 98312 | tf_op jit(solution)/shard_map/ppermute | solution.py:290
  9.4 5.8 %collective-permute-start.1 = (bf16[4,4096]{1,0:T(4,128)(2,1)}, bf16[4,4096]{1,0:T(4,128)(2,1)S(1)}, u32[]{:S(2)}, u32[]{:S(2)}) collective-permute-start(bf16[4,4096]{1,0:T(4,128)(2,1)} %queries_ref.1), channel_id=1, source_target_pairs={{8,0},{12,4},{0,8},{4,12},{9,1},{13,5},{1,9},{5,13},{10,2},{14,6},... | collective-permute-start | bytes 98312 | tf_op jit(solution)/shard_map/ppermute | solution.py:290
  9.4 5.9 %collective-permute-start.2 = (bf16[4,4096]{1,0:T(4,128)(2,1)}, bf16[4,4096]{1,0:T(4,128)(2,1)S(1)}, u32[]{:S(2)}, u32[]{:S(2)}) collective-permute-start(bf16[4,4096]{1,0:T(4,128)(2,1)} %queries_ref.1), channel_id=1, source_target_pairs={{12,0},{0,4},{4,8},{8,12},{13,1},{1,5},{5,9},{9,13},{14,2},{2,6},{... | collective-permute-start | bytes 98312 | tf_op jit(solution)/shard_map/ppermute | solution.py:290
  11.1 4.3 %copy-start.1 = (bf16[4,4096]{1,0:T(4,128)(2,1)S(1)}, bf16[4,4096]{1,0:T(4,128)(2,1)}, u32[]{:S(2)}) copy-start(bf16[4,4096]{1,0:T(4,128)(2,1)} %queries_ref.1) | copy-start | bytes 98308
  11.1 5.7 %copy-start = (bf16[4,128,128]{2,1,0:T(8,128)(2,1)S(1)}, bf16[4,128,128]{2,1,0:T(8,128)(2,1)}, u32[]{:S(2)}) copy-start(bf16[4,128,128]{2,1,0:T(8,128)(2,1)} %weight_ref.3) | copy-start | bytes 393220
  11.1 11.5 %copy-start.2 = (bf16[4,512]{1,0:T(4,128)(2,1)S(1)}, bf16[4,512]{1,0:T(4,128)(2,1)}, u32[]{:S(2)}) copy-start(bf16[4,512]{1,0:T(4,128)(2,1)} %keys_ref.1) | copy-start | bytes 12292
  11.1 11.5 %copy-start.3 = (bf16[4,512]{1,0:T(4,128)(2,1)S(1)}, bf16[4,512]{1,0:T(4,128)(2,1)}, u32[]{:S(2)}) copy-start(bf16[4,512]{1,0:T(4,128)(2,1)} %values_ref.1) | copy-start | bytes 12292
  11.1 14.2 %copy-start.4 = (s32[32]{0:T(128)S(1)}, s32[32]{0:T(128)}, u32[]{:S(2)}) copy-start(s32[32]{0:T(128)} %param.15) | copy-start | bytes 388
  15.1 1.7 %collective-permute-start.5 = (bf16[1168,128]{1,0:T(8,128)(2,1)S(1)}, bf16[1168,128]{1,0:T(8,128)(2,1)S(1)}, u32[]{:S(2)}, u32[]{:S(2)}) collective-permute-start(bf16[1168,128]{1,0:T(8,128)(2,1)S(1)} %prefill.1.near_ref), channel_id=1, source_target_pairs={{0,1},{1,0},{2,3},{3,2},{4,5},{5,4},{6,7},{7,6},{8,9},{9,8},{10,11... | collective-permute-start | bytes 897032 | tf_op jit(solution)/shard_map/ppermute | solution.py:297
  17.6 5.9 %collective-permute-start.6 = (bf16[4,4352]{1,0:T(4,128)(2,1)S(1)}, bf16[4,4352]{1,0:T(4,128)(2,1)S(1)}, u32[]{:S(2)}, u32[]{:S(2)}) collective-permute-start(bf16[4,4352]{1,0:T(4,128)(2,1)S(1)} %get-tuple-element.14), channel_id=1, source_target_pairs={{0,4},{4,8},{8,12},{12,0},{1,5},{5,9},{9,13},{13,1},{2,6},{6,10},{... | collective-permute-start | bytes 104456 | tf_op jit(solution)/shard_map/ppermute | solution.py:301
  20.2 5.1 %collective-permute-start.7 = (bf16[4,4352]{1,0:T(4,128)(2,1)S(1)}, bf16[4,4352]{1,0:T(4,128)(2,1)S(1)}, u32[]{:S(2)}, u32[]{:S(2)}) collective-permute-start(bf16[4,4352]{1,0:T(4,128)(2,1)S(1)} %get-tuple-element.15), channel_id=1, source_target_pairs={{0,8},{4,12},{8,0},{12,4},{1,9},{5,13},{9,1},{13,5},{2,10},{6,14},... | collective-permute-start | bytes 104456 | tf_op jit(solution)/shard_map/ppermute | solution.py:301
  21.1 4.3 %collective-permute-start.8 = (bf16[4,4352]{1,0:T(4,128)(2,1)S(1)}, bf16[4,4352]{1,0:T(4,128)(2,1)S(1)}, u32[]{:S(2)}, u32[]{:S(2)}) collective-permute-start(bf16[4,4352]{1,0:T(4,128)(2,1)S(1)} %get-tuple-element.16), channel_id=1, source_target_pairs={{0,12},{4,0},{8,4},{12,8},{1,13},{5,1},{9,5},{13,9},{2,14},{6,2},{... | collective-permute-start | bytes 104456 | tf_op jit(solution)/shard_map/ppermute | solution.py:301

commit v15 on v2

--- a/solution.py
+++ b/solution.py
@@ -18,23 +18,30 @@
     return jnp.maximum(proj, 0.0) + jnp.exp(jnp.minimum(proj, 0.0))
 
 
-def pack_kernel(queries_ref, keys_ref, values_ref, out_ref):
-    width, each = queries_ref.shape[1], keys_ref.shape[1]
-    out_ref[:, :width] = queries_ref[...]
-    out_ref[:, width : width + each] = keys_ref[...]
-    out_ref[:, width + each :] = values_ref[...]
+def pack_kernel(queries_ref, keys_ref, values_ref, out_ref, sems):
+    copies, at = [], 0
+    for i, ref in enumerate((queries_ref, keys_ref, values_ref)):
+        size = ref.shape[1]
+        copies.append(pltpu.make_async_copy(ref, out_ref.at[:, at : at + size], sems.at[i]))
+        copies[-1].start()
+        at += size
+    for copy in copies:
+        copy.wait()
 
 
 def pack(queries, new_keys, new_values):
-    vmem = pl.BlockSpec(memory_space=pltpu.VMEM)
     width = queries.shape[1] + 2 * new_keys.shape[1]
+    arrays = [pltpu.with_memory_space_constraint(x, pltpu.MemorySpace.HBM) for x in (queries, new_keys, new_values)]
     return pl.pallas_call(
         pack_kernel,
-        in_specs=[vmem] * 3,
-        out_specs=vmem,
+        in_specs=[pl.BlockSpec(memory_space=pltpu.MemorySpace.HBM)] * 3,
+        out_specs=pl.BlockSpec(memory_space=pltpu.VMEM),
         out_shape=jax.ShapeDtypeStruct((queries.shape[0], width), jnp.bfloat16),
+        scratch_shapes=[pltpu.SemaphoreType.DMA((3,))],
+        compiler_params=pltpu.CompilerParams(vmem_limit_bytes=8 * 1024 * 1024),
+        cost_estimate=pl.CostEstimate(flops=10**10, bytes_accessed=2**25, transcendentals=0),
         name="pack",
-    )(queries, new_keys, new_values)
+    )(*arrays)
 
 
 SLAB = WINDOW + 16
@@ -43,33 +50,20 @@
 
 def prefill_kernel(
     lengths_ref, keys_ref, values_ref, weight_ref, out_ref,
-    keys_at, values_at, weight_at, wide_ref, state_ref, norm_ref, weight_sem, load_sem, slab_sem,
+    wide_ref, proj_ref, state_ref, norm_ref,
+    slab_sem,
 ):
     heads, head_size, feats = weight_ref.shape
     pairs = heads // 2
     span = keys_ref.shape[1]
+    keys_at, values_at = keys_ref.at[0], values_ref.at[0]
     chunks = span // BLOCK
-    get_weight = pltpu.make_async_copy(weight_ref, weight_at, weight_sem)
-    get_weight.start()
-    loads = []
-    for c in range(chunks):
-        rows = pl.ds(c * BLOCK, BLOCK)
-        loads.append(
-            [
-                pltpu.make_async_copy(keys_ref.at[0, rows, :], keys_at.at[rows, :], load_sem.at[0, c]),
-                pltpu.make_async_copy(values_ref.at[0, rows, :], values_at.at[rows, :], load_sem.at[1, c]),
-            ]
-        )
-        for load in loads[-1]:
-            load.start()
-
     state_ref[...] = jnp.zeros_like(state_ref)
     norm_ref[...] = jnp.zeros_like(norm_ref)
     wide_ref[...] = jnp.zeros_like(wide_ref)
-    get_weight.wait()
     for g in range(heads):
         half = g % 2
-        turned = weight_at[g].astype(jnp.float32).T.astype(jnp.bfloat16)
+        turned = weight_ref[g].astype(jnp.float32).T.astype(jnp.bfloat16)
         wide_ref[g // 2, half * feats : (half + 1) * feats, half * head_size : (half + 1) * head_size] = turned
 
     begin = lengths_ref[0] - WINDOW - lax.axis_index("sub") * span
@@ -88,23 +82,36 @@
             )
             slabs[-1].start()
 
+    def project(c):
+        for j in range(pairs):
+            proj = lax.dot_general(
+                wide_ref[j],
+                keys_at[c * BLOCK : (c + 1) * BLOCK, j * 2 * head_size : (j + 1) * 2 * head_size],
+                NT,
+                preferred_element_type=jnp.float32,
+            )
+            proj_ref[c % 2, j] = proj.astype(jnp.bfloat16)
+
+    def collect(c):
+        position = c * BLOCK + lax.broadcasted_iota(jnp.int32, (1, BLOCK), 1)
+        live = jnp.where(position < begin, 1.0, 0.0).astype(jnp.bfloat16)
+        for j in range(pairs):
+            mapped = feature(proj_ref[c % 2, j]) * live
+            some = [mapped[:, k * 128 : (k + 1) * 128] for k in range(BLOCK // 128)]
+            while len(some) > 1:
+                some = [x + y for x, y in zip(some[::2], some[1::2])]
+            norm_ref[j] += some[0].astype(jnp.float32)
+            state_ref[j] += jnp.dot(
+                mapped,
+                values_at[c * BLOCK : (c + 1) * BLOCK, j * 2 * head_size : (j + 1) * 2 * head_size],
+                preferred_element_type=jnp.float32,
+            )
+
+    project(0)
     for c in range(chunks):
-        rows = slice(c * BLOCK, (c + 1) * BLOCK)
-        for load in loads[c]:
-            load.wait()
-        position = c * BLOCK + lax.broadcasted_iota(jnp.int32, (1, BLOCK), 1)
-        live = position < begin
-        for j in range(pairs):
-            cols = slice(j * 2 * head_size, (j + 1) * 2 * head_size)
-            proj = lax.dot_general(wide_ref[j], keys_at[rows, cols], NT, preferred_element_type=jnp.float32)
-            mapped = jnp.where(live, feature(proj), 0.0)
-            total = norm_ref[j]
-            for k in range(BLOCK // 128):
-                total = total + mapped[:, k * 128 : (k + 1) * 128]
-            norm_ref[j] = total
-            state_ref[j] += jnp.dot(
-                mapped.astype(jnp.bfloat16), values_at[rows, cols], preferred_element_type=jnp.float32
-            )
+        if c + 1 < chunks:
+            project(c + 1)
+        collect(c)
 
     tile = []
     for g in range(heads):
@@ -125,30 +132,30 @@
 def prefill(keys, values, weight, lengths):
     heads, head_size, feats = weight.shape
     span, width = keys.shape[1:]
-    hbm = pl.BlockSpec(memory_space=pltpu.MemorySpace.HBM)
     vmem = pl.BlockSpec(memory_space=pltpu.VMEM)
     return pl.pallas_call(
         prefill_kernel,
-        in_specs=[pl.BlockSpec(memory_space=pltpu.SMEM), hbm, hbm, hbm],
+        in_specs=[pl.BlockSpec(memory_space=pltpu.SMEM), vmem, vmem, vmem],
         out_specs=vmem,
         out_shape=jax.ShapeDtypeStruct((heads * feats + 16 + 2 * heads * SLAB, head_size), jnp.bfloat16),
         scratch_shapes=[
-            pltpu.VMEM((span, width), jnp.bfloat16),
-            pltpu.VMEM((span, width), jnp.bfloat16),
-            pltpu.VMEM(weight.shape, jnp.bfloat16),
             pltpu.VMEM((heads // 2, 2 * feats, 2 * head_size), jnp.bfloat16),
+            pltpu.VMEM((2, heads // 2, 2 * feats, BLOCK), jnp.bfloat16),
             pltpu.VMEM((heads // 2, 2 * feats, 2 * head_size), jnp.float32),
             pltpu.VMEM((heads // 2, 2 * feats, 128), jnp.float32),
-            pltpu.SemaphoreType.DMA,
-            pltpu.SemaphoreType.DMA((2, span // BLOCK)),
             pltpu.SemaphoreType.DMA((2, heads)),
         ],
-        compiler_params=pltpu.CompilerParams(vmem_limit_bytes=52 * 1024 * 1024),
+        compiler_params=pltpu.CompilerParams(vmem_limit_bytes=16 * 1024 * 1024),
         cost_estimate=pl.CostEstimate(
             flops=4 * span * width * feats, bytes_accessed=4 * span * width, transcendentals=span * width
         ),
         name="prefill",
-    )(lengths, keys, values, weight)
+    )(
+        lengths,
+        pltpu.with_memory_space_constraint(keys, pltpu.MemorySpace.VMEM),
+        pltpu.with_memory_space_constraint(values, pltpu.MemorySpace.VMEM),
+        pltpu.with_memory_space_constraint(weight, pltpu.MemorySpace.VMEM),
+    )
 
 
 def decode_kernel(rows_ref, weight_ref, near_ref, far_ref, *out_refs):
@@ -228,7 +235,7 @@
     sect = lax.axis_index("sect")
     mine = pack(queries, new_keys, new_values)
     blocks = [mine] + [
-        lax.ppermute(mine, "sect", [(i, (i + k) % sects) for i in range(sects)]) for k in range(1, sects)
+        lax.ppermute(mine, "sect", [((i + k) % sects, i) for i in range(sects)]) for k in range(1, sects)
     ]
     near = prefill(prompt_keys, prompt_values, feature_weight, lengths)
     far = lax.ppermute(near, "sub", [(0, 1), (1, 0)])
@@ -237,11 +244,10 @@
     count = queries.shape[0]
     first_row = (sect * lax.axis_size("sub") + sub) * count
     prompts = lax.dynamic_slice_in_dim(row_prompt, first_row, count, 0)
-    out = jnp.zeros_like(queries)
-    for k, result in enumerate(results):
-        if k > 0:
-            result = lax.ppermute(result, "sect", [(i, (i - k) % sects) for i in range(sects)])
-        out = jnp.where((prompts == (sect + k) % sects)[:, None], result, out)
+    out = results[0]
+    for k in range(1, sects):
+        result = lax.ppermute(results[k], "sect", [(i, (i + k) % sects) for i in range(sects)])
+        out = jnp.where((prompts == (sect - k) % sects)[:, None], result, out)
     return out
 
 

time: 25.9 us -> 23.2 us (0.90)
  Pallas kernels: 8.01 us -> 4.96 us
  waiting for transfers between devices: 4.06 us -> 6.94 us
  starting transfers between devices: 11.1 us -> 9.36 us
  local copies, waits for them, and re-layouts: 0.91 us -> 0.02 us
    ppermute x6, waiting for transfers between devices: 2.72 us -> 5.56 us  [the longest x3 5.55 us: body(): lax.ppermute(results[k], 'sect', [(i, (i + k) % sects) for i in range(sec...]
    pallas_call x1, Pallas kernels: 5.47 us -> 2.88 us  [prefill(): pl.pallas_call(prefill_kernel, in_specs=[pl.BlockSpec(memory_space=pltpu....]
    ppermute x6, starting transfers between devices: 11 us -> 9.29 us  [the longest x3 7.02 us: body(): lax.ppermute(mine, 'sect', [((i + k) % sects, i) for i in range(sects)])]
    unnamed x8, local copies, waits for them, and re-layouts: 0.91 us -> 0.02 us
    pallas_call x1, Pallas kernels: 1.39 us -> 0.94 us  [pack(): pl.pallas_call(pack_kernel, in_specs=[pl.BlockSpec(memory_space=pltpu.Mem...]
  transfers between devices with their start and end apart: 7 -> 7, of which waited for: 4 -> 4; matrix products, arithmetic and copies ran while one was open for 1% -> 1% of each run, Pallas kernels for 21% -> 13%
where the time goes in v15:
time: 23.2 us; the launch traced here: 23 us
  starting transfers between devices  9.36 us (40%)
  waiting for transfers between devices  6.94 us (30%)
  Pallas kernels  4.96 us (21%)
  other arithmetic  0.89 us (4%)
  between operations  0.81 us (3%)
    ppermute x3, starting transfers between devices, body(): lax.ppermute(mine, 'sect', [((i + k) % sects, i) for i in range(sects)])  7.02 us
    ppermute x3, waiting for transfers between devices, body(): lax.ppermute(results[k], 'sect', [(i, (i + k) % sects) for i in range(sec...  5.55 us
    pallas_call x1, Pallas kernels, prefill(): pl.pallas_call(prefill_kernel, in_specs=[pl.BlockSpec(memory_space=pltpu....  2.88 us
    ppermute x3, starting transfers between devices, body(): lax.ppermute(results[k], 'sect', [(i, (i + k) % sects) for i in range(sec...  2.27 us
    ppermute x1, waiting for transfers between devices, body(): far = lax.ppermute(near, 'sub', [(0, 1), (1, 0)])  1.38 us
    pallas_call x1, Pallas kernels, decode(): pl.pallas_call(decode_kernel, in_specs=[vmem] * 4, out_specs=[vmem] * par...  1.14 us
    pallas_call x1, Pallas kernels, pack(): pl.pallas_call(pack_kernel, in_specs=[pl.BlockSpec(memory_space=pltpu.Mem...  0.94 us
    select_n x1, other arithmetic, body(): out = jnp.where((prompts == (sect - k) % sects)[:, None], result, out)  0.71 us
  transfers between devices with their start and end apart: 7, of which 4 were waited for; matrix products, arithmetic and copies ran while one was open for 1% of the time, Pallas kernels for 13%

profile of v15, /device:TPU:0, one launch (start us, length us, event | category | flops | bytes accessed | tf_op | source)
XLA Modules:
  0.0 23.0 jit_solution(5342437631610560461)
XLA Ops:
  0.0 0.0 copy-start.2
  0.0 0.0 copy-start
  0.0 0.0 copy-start.1
  0.0 0.9 %pack.1 = bf16[4,5120]{1,0:T(4,128)(2,1)S(1)} custom-call(bf16[4,4096]{1,0:T(4,128)(2,1)} %queries_ref.1, bf16[4,512]{1,0:T(4,128)(2,1)} %keys_ref.2, bf16[4,512]{1,0:T(4,128)(2,1)} %values_ref.2), custom_call_target="tpu_custom_call" | custom-call | flops 10000000000 | bytes 33554432 | tf_op jit(solution)/shard_map/pack/pallas_call | solution.py:35
  1.0 3.1 %collective-permute-start.2 = (bf16[4,5120]{1,0:T(4,128)(2,1)S(1)}, bf16[4,5120]{1,0:T(4,128)(2,1)S(1)}, u32[]{:S(2)}, u32[]{:S(2)}) collective-permute-start(bf16[4,5120]{1,0:T(4,128)(2,1)S(1)} %pack.1), channel_id=1, source_target_pairs={{12,0},{0,4},{4,8},{8,12},{13,1},{1,5},{5,9},{9,13},{14,2},{2,6},{... | collective-permute-start | bytes 122888 | tf_op jit(solution)/shard_map/ppermute | solution.py:238
  4.0 2.6 %collective-permute-start.1 = (bf16[4,5120]{1,0:T(4,128)(2,1)S(1)}, bf16[4,5120]{1,0:T(4,128)(2,1)S(1)}, u32[]{:S(2)}, u32[]{:S(2)}) collective-permute-start(bf16[4,5120]{1,0:T(4,128)(2,1)S(1)} %pack.1), channel_id=1, source_target_pairs={{8,0},{12,4},{0,8},{4,12},{9,1},{13,5},{1,9},{5,13},{10,2},{14,6},... | collective-permute-start | bytes 122888 | tf_op jit(solution)/shard_map/ppermute | solution.py:238
  6.6 1.3 %collective-permute-start = (bf16[4,5120]{1,0:T(4,128)(2,1)S(1)}, bf16[4,5120]{1,0:T(4,128)(2,1)S(1)}, u32[]{:S(2)}, u32[]{:S(2)}) collective-permute-start(bf16[4,5120]{1,0:T(4,128)(2,1)S(1)} %pack.1), channel_id=1, source_target_pairs={{4,0},{8,4},{12,8},{0,12},{5,1},{9,5},{13,9},{1,13},{6,2},{10,6},{... | collective-permute-start | bytes 122888 | tf_op jit(solution)/shard_map/ppermute | solution.py:238
  8.6 0.0 copy-done.2
  8.6 0.0 copy-done
  8.6 0.0 copy-done.1
  8.7 0.0 copy-start.3
  8.7 2.9 %prefill.1.near_ref = bf16[1168,128]{1,0:T(8,128)(2,1)S(1)} custom-call(s32[1]{0:T(128)S(6)} %copy.9.lengths_ref, bf16[1,4096,512]{2,1,0:T(8,128)(2,1)S(1)} %copy-done, bf16[1,4096,512]{2,1,0:T(8,128)(2,1)S(1)} %copy-done.1, bf16[4,128,128]{2,1,0:T(8,128)(2,1)S(1)} %copy-done.2), custom_call_target="tpu_custom_call" | custom-call | flops 1073741824 | bytes 8388608 | tf_op jit(solution)/shard_map/prefill/pallas_call | solution.py:136
  11.6 0.1 collective-permute-start.3
  11.7 0.0 collective-permute-done.2
  11.7 0.0 collective-permute-done.1
  11.7 0.0 collective-permute-done
  11.7 0.1 pad_maximum_fusion.rows_ref
  11.8 1.4 %collective-permute-done.3.far_ref = bf16[1168,128]{1,0:T(8,128)(2,1)S(1)} collective-permute-done((bf16[1168,128]{1,0:T(8,128)(2,1)S(1)}, bf16[1168,128]{1,0:T(8,128)(2,1)S(1)}, u32[]{:S(2)}, u32[]{:S(2)}) %collective-permute-start.3) | collective-permute-done | bytes 299040 | tf_op jit(solution)/shard_map/ppermute | solution.py:241
  13.2 1.1 %decode.1 = (bf16[4,4096]{1,0:T(4,128)(2,1)S(1)}, bf16[4,4096]{1,0:T(4,128)(2,1)S(1)}, bf16[4,4096]{1,0:T(4,128)(2,1)S(1)}, bf16[4,4096]{1,0:T(4,128)(2,1)S(1)}) custom-call(bf16[16,5120]{1,0:T(8,128)(2,1)S(1)} %pad_maximum_fusion.rows_ref, bf16[4,128,128]{2,1,0:T(8,128)(2,1)S(1)} %copy-done.2, bf16[1168,128]{1,0:T(8,128)(2,1)S(1)} %prefill.1.near_ref, ...), custom_call_target="tpu_custom_call" | custom-call | flops 83886080 | bytes 262144 | tf_op jit(solution)/shard_map/decode/pallas_call | solution.py:218
  14.4 0.7 %collective-permute-start.4 = (bf16[4,4096]{1,0:T(4,128)(2,1)S(1)}, bf16[4,4096]{1,0:T(4,128)(2,1)S(1)}, u32[]{:S(2)}, u32[]{:S(2)}) collective-permute-start(bf16[4,4096]{1,0:T(4,128)(2,1)S(1)} %get-tuple-element.9), channel_id=1, source_target_pairs={{0,12},{4,0},{8,4},{12,8},{1,13},{5,1},{9,5},{13,9},{2,14},{6,2},{... | collective-permute-start | bytes 98312 | tf_op jit(solution)/shard_map/ppermute | solution.py:249
  15.1 1.5 %collective-permute-start.5 = (bf16[4,4096]{1,0:T(4,128)(2,1)S(1)}, bf16[4,4096]{1,0:T(4,128)(2,1)S(1)}, u32[]{:S(2)}, u32[]{:S(2)}) collective-permute-start(bf16[4,4096]{1,0:T(4,128)(2,1)S(1)} %get-tuple-element.10), channel_id=1, source_target_pairs={{0,8},{4,12},{8,0},{12,4},{1,9},{5,13},{9,1},{13,5},{2,10},{6,14},... | collective-permute-start | bytes 98312 | tf_op jit(solution)/shard_map/ppermute | solution.py:249
  16.6 0.1 collective-permute-start.6
  16.6 0.0 copy-done.3
  16.6 0.1 broadcast_compare_fusion.2
  16.7 1.7 %collective-permute-done.4 = bf16[4,4096]{1,0:T(4,128)(2,1)S(1)} collective-permute-done((bf16[4,4096]{1,0:T(4,128)(2,1)S(1)}, bf16[4,4096]{1,0:T(4,128)(2,1)S(1)}, u32[]{:S(2)}, u32[]{:S(2)}) %collective-permute-start.4) | collective-permute-done | bytes 32800 | tf_op jit(solution)/shard_map/ppermute | solution.py:249
  18.4 1.5 %collective-permute-done.5 = bf16[4,4096]{1,0:T(4,128)(2,1)S(1)} collective-permute-done((bf16[4,4096]{1,0:T(4,128)(2,1)S(1)}, bf16[4,4096]{1,0:T(4,128)(2,1)S(1)}, u32[]{:S(2)}, u32[]{:S(2)}) %collective-permute-start.5) | collective-permute-done | bytes 32800 | tf_op jit(solution)/shard_map/ppermute | solution.py:249
  19.9 2.3 %collective-permute-done.6 = bf16[4,4096]{1,0:T(4,128)(2,1)S(1)} collective-permute-done((bf16[4,4096]{1,0:T(4,128)(2,1)S(1)}, bf16[4,4096]{1,0:T(4,128)(2,1)S(1)}, u32[]{:S(2)}, u32[]{:S(2)}) %collective-permute-start.6) | collective-permute-done | bytes 32800 | tf_op jit(solution)/shard_map/ppermute | solution.py:249
  22.3 0.7 %select_select_fusion = bf16[4,4096]{1,0:T(4,128)(2,1)} fusion(bf16[4,4096]{1,0:T(4,128)(2,1)S(1)} %collective-permute-done.4, bf16[4,4096]{1,0:T(4,128)(2,1)S(1)} %collective-permute-done.5, bf16[4,4096]{1,0:T(4,128)(2,1)S(1)} %collective-permute-done.6, bf16[4,4096]{1,0:T(4,128)(2,1)S(1)} %get-tuple-element.12, pred[4]{0:T(512)(128)(4,1)S(1)} %get-tuple-element.15, ...), kind=kLoop, calls=%fused_computation.1 | loop fusion | flops 49152 | bytes 163852 | tf_op jit(solution)/shard_map/jit(_where)/select_n | solution.py:250
Async XLA Ops:
  0.0 8.6 %copy-start.2 = (bf16[4,128,128]{2,1,0:T(8,128)(2,1)S(1)}, bf16[4,128,128]{2,1,0:T(8,128)(2,1)}, u32[]{:S(2)}) copy-start(bf16[4,128,128]{2,1,0:T(8,128)(2,1)} %weight_ref.3) | copy-start | bytes 393220
  0.0 8.6 %copy-start = (bf16[1,4096,512]{2,1,0:T(8,128)(2,1)S(1)}, bf16[1,4096,512]{2,1,0:T(8,128)(2,1)}, u32[]{:S(2)}) copy-start(bf16[1,4096,512]{2,1,0:T(8,128)(2,1)} %keys_ref.3) | copy-start | bytes 12582916
  0.0 8.6 %copy-start.1 = (bf16[1,4096,512]{2,1,0:T(8,128)(2,1)S(1)}, bf16[1,4096,512]{2,1,0:T(8,128)(2,1)}, u32[]{:S(2)}) copy-start(bf16[1,4096,512]{2,1,0:T(8,128)(2,1)} %values_ref.3) | copy-start | bytes 12582916
  1.0 10.7 %collective-permute-start.2 = (bf16[4,5120]{1,0:T(4,128)(2,1)S(1)}, bf16[4,5120]{1,0:T(4,128)(2,1)S(1)}, u32[]{:S(2)}, u32[]{:S(2)}) collective-permute-start(bf16[4,5120]{1,0:T(4,128)(2,1)S(1)} %pack.1), channel_id=1, source_target_pairs={{12,0},{0,4},{4,8},{8,12},{13,1},{1,5},{5,9},{9,13},{14,2},{2,6},{... | collective-permute-start | bytes 122888 | tf_op jit(solution)/shard_map/ppermute | solution.py:238
  4.0 7.7 %collective-permute-start.1 = (bf16[4,5120]{1,0:T(4,128)(2,1)S(1)}, bf16[4,5120]{1,0:T(4,128)(2,1)S(1)}, u32[]{:S(2)}, u32[]{:S(2)}) collective-permute-start(bf16[4,5120]{1,0:T(4,128)(2,1)S(1)} %pack.1), channel_id=1, source_target_pairs={{8,0},{12,4},{0,8},{4,12},{9,1},{13,5},{1,9},{5,13},{10,2},{14,6},... | collective-permute-start | bytes 122888 | tf_op jit(solution)/shard_map/ppermute | solution.py:238
  6.6 5.1 %collective-permute-start = (bf16[4,5120]{1,0:T(4,128)(2,1)S(1)}, bf16[4,5120]{1,0:T(4,128)(2,1)S(1)}, u32[]{:S(2)}, u32[]{:S(2)}) collective-permute-start(bf16[4,5120]{1,0:T(4,128)(2,1)S(1)} %pack.1), channel_id=1, source_target_pairs={{4,0},{8,4},{12,8},{0,12},{5,1},{9,5},{13,9},{1,13},{6,2},{10,6},{... | collective-permute-start | bytes 122888 | tf_op jit(solution)/shard_map/ppermute | solution.py:238
  8.7 8.0 %copy-start.3 = (s32[32]{0:T(128)S(1)}, s32[32]{0:T(128)}, u32[]{:S(2)}) copy-start(s32[32]{0:T(128)} %param.15) | copy-start | bytes 388
  11.6 1.7 %collective-permute-start.3 = (bf16[1168,128]{1,0:T(8,128)(2,1)S(1)}, bf16[1168,128]{1,0:T(8,128)(2,1)S(1)}, u32[]{:S(2)}, u32[]{:S(2)}) collective-permute-start(bf16[1168,128]{1,0:T(8,128)(2,1)S(1)} %prefill.1.near_ref), channel_id=1, source_target_pairs={{0,1},{1,0},{2,3},{3,2},{4,5},{5,4},{6,7},{7,6},{8,9},{9,8},{10,11... | collective-permute-start | bytes 897032 | tf_op jit(solution)/shard_map/ppermute | solution.py:241
  14.4 4.1 %collective-permute-start.4 = (bf16[4,4096]{1,0:T(4,128)(2,1)S(1)}, bf16[4,4096]{1,0:T(4,128)(2,1)S(1)}, u32[]{:S(2)}, u32[]{:S(2)}) collective-permute-start(bf16[4,4096]{1,0:T(4,128)(2,1)S(1)} %get-tuple-element.9), channel_id=1, source_target_pairs={{0,12},{4,0},{8,4},{12,8},{1,13},{5,1},{9,5},{13,9},{2,14},{6,2},{... | collective-permute-start | bytes 98312 | tf_op jit(solution)/shard_map/ppermute | solution.py:249
  15.1 4.8 %collective-permute-start.5 = (bf16[4,4096]{1,0:T(4,128)(2,1)S(1)}, bf16[4,4096]{1,0:T(4,128)(2,1)S(1)}, u32[]{:S(2)}, u32[]{:S(2)}) collective-permute-start(bf16[4,4096]{1,0:T(4,128)(2,1)S(1)} %get-tuple-element.10), channel_id=1, source_target_pairs={{0,8},{4,12},{8,0},{12,4},{1,9},{5,13},{9,1},{13,5},{2,10},{6,14},... | collective-permute-start | bytes 98312 | tf_op jit(solution)/shard_map/ppermute | solution.py:249
  16.6 5.7 %collective-permute-start.6 = (bf16[4,4096]{1,0:T(4,128)(2,1)S(1)}, bf16[4,4096]{1,0:T(4,128)(2,1)S(1)}, u32[]{:S(2)}, u32[]{:S(2)}) collective-permute-start(bf16[4,4096]{1,0:T(4,128)(2,1)S(1)} %get-tuple-element.11), channel_id=1, source_target_pairs={{0,4},{4,8},{8,12},{12,0},{1,5},{5,9},{9,13},{13,1},{2,6},{6,10},{... | collective-permute-start | bytes 98312 | tf_op jit(solution)/shard_map/ppermute | solution.py:249

commit v16 on v15

--- a/solution.py
+++ b/solution.py
@@ -245,7 +245,7 @@
     first_row = (sect * lax.axis_size("sub") + sub) * count
     prompts = lax.dynamic_slice_in_dim(row_prompt, first_row, count, 0)
     out = results[0]
-    for k in range(1, sects):
+    for k in range(sects - 1, 0, -1):
         result = lax.ppermute(results[k], "sect", [(i, (i + k) % sects) for i in range(sects)])
         out = jnp.where((prompts == (sect - k) % sects)[:, None], result, out)
     return out

time: 23.2 us -> 21.6 us (0.931)
  waiting for transfers between devices: 6.94 us -> 3.76 us
  starting transfers between devices: 9.36 us -> 11 us
    ppermute x3, waiting for transfers between devices: 5.55 us -> 2.38 us  [body(): lax.ppermute(results[k], 'sect', [(i, (i + k) % sects) for i in range(sec...]
    ppermute x3, starting transfers between devices: 2.27 us -> 3.88 us  [body(): lax.ppermute(results[k], 'sect', [(i, (i + k) % sects) for i in range(sec...]
  transfers between devices with their start and end apart: 7 -> 7, of which waited for: 4 -> 3; matrix products, arithmetic and copies ran while one was open for 1% -> 1% of each run, Pallas kernels for 13% -> 13%
where the time goes in v16:
time: 21.6 us; the launch traced here: 21.4 us
  starting transfers between devices  11 us (51%)
  Pallas kernels  4.96 us (23%)
  waiting for transfers between devices  3.76 us (17%)
  other arithmetic  0.89 us (4%)
  between operations  0.81 us (4%)
    ppermute x3, starting transfers between devices, body(): lax.ppermute(mine, 'sect', [((i + k) % sects, i) for i in range(sects)])  7.02 us
    ppermute x3, starting transfers between devices, body(): lax.ppermute(results[k], 'sect', [(i, (i + k) % sects) for i in range(sec...  3.88 us
    pallas_call x1, Pallas kernels, prefill(): pl.pallas_call(prefill_kernel, in_specs=[pl.BlockSpec(memory_space=pltpu....  2.88 us
    ppermute x3, waiting for transfers between devices, body(): lax.ppermute(results[k], 'sect', [(i, (i + k) % sects) for i in range(sec...  2.38 us
    ppermute x1, waiting for transfers between devices, body(): far = lax.ppermute(near, 'sub', [(0, 1), (1, 0)])  1.38 us
    pallas_call x1, Pallas kernels, decode(): pl.pallas_call(decode_kernel, in_specs=[vmem] * 4, out_specs=[vmem] * par...  1.14 us
    pallas_call x1, Pallas kernels, pack(): pl.pallas_call(pack_kernel, in_specs=[pl.BlockSpec(memory_space=pltpu.Mem...  0.94 us
    select_n x1, other arithmetic, body(): out = jnp.where((prompts == (sect - k) % sects)[:, None], result, out)  0.71 us
  transfers between devices with their start and end apart: 7, of which 3 were waited for; matrix products, arithmetic and copies ran while one was open for 1% of the time, Pallas kernels for 13%

profile of v16, /device:TPU:0, one launch (start us, length us, event | category | flops | bytes accessed | tf_op | source)
XLA Modules:
  0.0 21.4 jit_solution(16000857837274713536)
XLA Ops:
  0.0 0.0 copy-start.2
  0.0 0.0 copy-start
  0.0 0.0 copy-start.1
  0.0 0.9 %pack.1 = bf16[4,5120]{1,0:T(4,128)(2,1)S(1)} custom-call(bf16[4,4096]{1,0:T(4,128)(2,1)} %queries_ref.1, bf16[4,512]{1,0:T(4,128)(2,1)} %keys_ref.2, bf16[4,512]{1,0:T(4,128)(2,1)} %values_ref.2), custom_call_target="tpu_custom_call" | custom-call | flops 10000000000 | bytes 33554432 | tf_op jit(solution)/shard_map/pack/pallas_call | solution.py:35
  1.0 3.1 %collective-permute-start.2 = (bf16[4,5120]{1,0:T(4,128)(2,1)S(1)}, bf16[4,5120]{1,0:T(4,128)(2,1)S(1)}, u32[]{:S(2)}, u32[]{:S(2)}) collective-permute-start(bf16[4,5120]{1,0:T(4,128)(2,1)S(1)} %pack.1), channel_id=1, source_target_pairs={{12,0},{0,4},{4,8},{8,12},{13,1},{1,5},{5,9},{9,13},{14,2},{2,6},{... | collective-permute-start | bytes 122888 | tf_op jit(solution)/shard_map/ppermute | solution.py:238
  4.0 2.6 %collective-permute-start.1 = (bf16[4,5120]{1,0:T(4,128)(2,1)S(1)}, bf16[4,5120]{1,0:T(4,128)(2,1)S(1)}, u32[]{:S(2)}, u32[]{:S(2)}) collective-permute-start(bf16[4,5120]{1,0:T(4,128)(2,1)S(1)} %pack.1), channel_id=1, source_target_pairs={{8,0},{12,4},{0,8},{4,12},{9,1},{13,5},{1,9},{5,13},{10,2},{14,6},... | collective-permute-start | bytes 122888 | tf_op jit(solution)/shard_map/ppermute | solution.py:238
  6.6 1.3 %collective-permute-start = (bf16[4,5120]{1,0:T(4,128)(2,1)S(1)}, bf16[4,5120]{1,0:T(4,128)(2,1)S(1)}, u32[]{:S(2)}, u32[]{:S(2)}) collective-permute-start(bf16[4,5120]{1,0:T(4,128)(2,1)S(1)} %pack.1), channel_id=1, source_target_pairs={{4,0},{8,4},{12,8},{0,12},{5,1},{9,5},{13,9},{1,13},{6,2},{10,6},{... | collective-permute-start | bytes 122888 | tf_op jit(solution)/shard_map/ppermute | solution.py:238
  8.6 0.0 copy-done.2
  8.6 0.0 copy-done
  8.6 0.0 copy-done.1
  8.7 0.0 copy-start.3
  8.7 2.9 %prefill.1.near_ref = bf16[1168,128]{1,0:T(8,128)(2,1)S(1)} custom-call(s32[1]{0:T(128)S(6)} %copy.9.lengths_ref, bf16[1,4096,512]{2,1,0:T(8,128)(2,1)S(1)} %copy-done, bf16[1,4096,512]{2,1,0:T(8,128)(2,1)S(1)} %copy-done.1, bf16[4,128,128]{2,1,0:T(8,128)(2,1)S(1)} %copy-done.2), custom_call_target="tpu_custom_call" | custom-call | flops 1073741824 | bytes 8388608 | tf_op jit(solution)/shard_map/prefill/pallas_call | solution.py:136
  11.6 0.1 collective-permute-start.3
  11.7 0.0 collective-permute-done.2
  11.7 0.0 collective-permute-done.1
  11.7 0.0 collective-permute-done
  11.7 0.1 pad_maximum_fusion.rows_ref
  11.8 1.4 %collective-permute-done.3.far_ref = bf16[1168,128]{1,0:T(8,128)(2,1)S(1)} collective-permute-done((bf16[1168,128]{1,0:T(8,128)(2,1)S(1)}, bf16[1168,128]{1,0:T(8,128)(2,1)S(1)}, u32[]{:S(2)}, u32[]{:S(2)}) %collective-permute-start.3) | collective-permute-done | bytes 299040 | tf_op jit(solution)/shard_map/ppermute | solution.py:241
  13.2 1.1 %decode.1 = (bf16[4,4096]{1,0:T(4,128)(2,1)S(1)}, bf16[4,4096]{1,0:T(4,128)(2,1)S(1)}, bf16[4,4096]{1,0:T(4,128)(2,1)S(1)}, bf16[4,4096]{1,0:T(4,128)(2,1)S(1)}) custom-call(bf16[16,5120]{1,0:T(8,128)(2,1)S(1)} %pad_maximum_fusion.rows_ref, bf16[4,128,128]{2,1,0:T(8,128)(2,1)S(1)} %copy-done.2, bf16[1168,128]{1,0:T(8,128)(2,1)S(1)} %prefill.1.near_ref, ...), custom_call_target="tpu_custom_call" | custom-call | flops 83886080 | bytes 262144 | tf_op jit(solution)/shard_map/decode/pallas_call | solution.py:218
  14.4 0.7 %collective-permute-start.4 = (bf16[4,4096]{1,0:T(4,128)(2,1)S(1)}, bf16[4,4096]{1,0:T(4,128)(2,1)S(1)}, u32[]{:S(2)}, u32[]{:S(2)}) collective-permute-start(bf16[4,4096]{1,0:T(4,128)(2,1)S(1)} %get-tuple-element.9), channel_id=1, source_target_pairs={{0,4},{4,8},{8,12},{12,0},{1,5},{5,9},{9,13},{13,1},{2,6},{6,10},{... | collective-permute-start | bytes 98312 | tf_op jit(solution)/shard_map/ppermute | solution.py:249
  15.1 0.6 %collective-permute-start.5 = (bf16[4,4096]{1,0:T(4,128)(2,1)S(1)}, bf16[4,4096]{1,0:T(4,128)(2,1)S(1)}, u32[]{:S(2)}, u32[]{:S(2)}) collective-permute-start(bf16[4,4096]{1,0:T(4,128)(2,1)S(1)} %get-tuple-element.10), channel_id=1, source_target_pairs={{0,8},{4,12},{8,0},{12,4},{1,9},{5,13},{9,1},{13,5},{2,10},{6,14},... | collective-permute-start | bytes 98312 | tf_op jit(solution)/shard_map/ppermute | solution.py:249
  15.7 2.6 %collective-permute-start.6 = (bf16[4,4096]{1,0:T(4,128)(2,1)S(1)}, bf16[4,4096]{1,0:T(4,128)(2,1)S(1)}, u32[]{:S(2)}, u32[]{:S(2)}) collective-permute-start(bf16[4,4096]{1,0:T(4,128)(2,1)S(1)} %get-tuple-element.11), channel_id=1, source_target_pairs={{0,12},{4,0},{8,4},{12,8},{1,13},{5,1},{9,5},{13,9},{2,14},{6,2},{... | collective-permute-start | bytes 98312 | tf_op jit(solution)/shard_map/ppermute | solution.py:249
  18.2 0.0 copy-done.3
  18.2 0.1 broadcast_compare_fusion.2
  18.3 2.0 %collective-permute-done.4 = bf16[4,4096]{1,0:T(4,128)(2,1)S(1)} collective-permute-done((bf16[4,4096]{1,0:T(4,128)(2,1)S(1)}, bf16[4,4096]{1,0:T(4,128)(2,1)S(1)}, u32[]{:S(2)}, u32[]{:S(2)}) %collective-permute-start.4) | collective-permute-done | bytes 32800 | tf_op jit(solution)/shard_map/ppermute | solution.py:249
  20.3 0.0 collective-permute-done.5
  20.4 0.3 %collective-permute-done.6 = bf16[4,4096]{1,0:T(4,128)(2,1)S(1)} collective-permute-done((bf16[4,4096]{1,0:T(4,128)(2,1)S(1)}, bf16[4,4096]{1,0:T(4,128)(2,1)S(1)}, u32[]{:S(2)}, u32[]{:S(2)}) %collective-permute-start.6) | collective-permute-done | bytes 32800 | tf_op jit(solution)/shard_map/ppermute | solution.py:249
  20.7 0.7 %select_select_fusion = bf16[4,4096]{1,0:T(4,128)(2,1)} fusion(bf16[4,4096]{1,0:T(4,128)(2,1)S(1)} %collective-permute-done.4, bf16[4,4096]{1,0:T(4,128)(2,1)S(1)} %collective-permute-done.5, bf16[4,4096]{1,0:T(4,128)(2,1)S(1)} %collective-permute-done.6, bf16[4,4096]{1,0:T(4,128)(2,1)S(1)} %get-tuple-element.12, pred[4]{0:T(512)(128)(4,1)S(1)} %get-tuple-element.15, ...), kind=kLoop, calls=%fused_computation.1 | loop fusion | flops 49152 | bytes 163852 | tf_op jit(solution)/shard_map/jit(_where)/select_n | solution.py:250
Async XLA Ops:
  0.0 8.6 %copy-start.2 = (bf16[4,128,128]{2,1,0:T(8,128)(2,1)S(1)}, bf16[4,128,128]{2,1,0:T(8,128)(2,1)}, u32[]{:S(2)}) copy-start(bf16[4,128,128]{2,1,0:T(8,128)(2,1)} %weight_ref.3) | copy-start | bytes 393220
  0.0 8.6 %copy-start = (bf16[1,4096,512]{2,1,0:T(8,128)(2,1)S(1)}, bf16[1,4096,512]{2,1,0:T(8,128)(2,1)}, u32[]{:S(2)}) copy-start(bf16[1,4096,512]{2,1,0:T(8,128)(2,1)} %keys_ref.3) | copy-start | bytes 12582916
  0.0 8.6 %copy-start.1 = (bf16[1,4096,512]{2,1,0:T(8,128)(2,1)S(1)}, bf16[1,4096,512]{2,1,0:T(8,128)(2,1)}, u32[]{:S(2)}) copy-start(bf16[1,4096,512]{2,1,0:T(8,128)(2,1)} %values_ref.3) | copy-start | bytes 12582916
  1.0 10.7 %collective-permute-start.2 = (bf16[4,5120]{1,0:T(4,128)(2,1)S(1)}, bf16[4,5120]{1,0:T(4,128)(2,1)S(1)}, u32[]{:S(2)}, u32[]{:S(2)}) collective-permute-start(bf16[4,5120]{1,0:T(4,128)(2,1)S(1)} %pack.1), channel_id=1, source_target_pairs={{12,0},{0,4},{4,8},{8,12},{13,1},{1,5},{5,9},{9,13},{14,2},{2,6},{... | collective-permute-start | bytes 122888 | tf_op jit(solution)/shard_map/ppermute | solution.py:238
  4.0 7.7 %collective-permute-start.1 = (bf16[4,5120]{1,0:T(4,128)(2,1)S(1)}, bf16[4,5120]{1,0:T(4,128)(2,1)S(1)}, u32[]{:S(2)}, u32[]{:S(2)}) collective-permute-start(bf16[4,5120]{1,0:T(4,128)(2,1)S(1)} %pack.1), channel_id=1, source_target_pairs={{8,0},{12,4},{0,8},{4,12},{9,1},{13,5},{1,9},{5,13},{10,2},{14,6},... | collective-permute-start | bytes 122888 | tf_op jit(solution)/shard_map/ppermute | solution.py:238
  6.6 5.1 %collective-permute-start = (bf16[4,5120]{1,0:T(4,128)(2,1)S(1)}, bf16[4,5120]{1,0:T(4,128)(2,1)S(1)}, u32[]{:S(2)}, u32[]{:S(2)}) collective-permute-start(bf16[4,5120]{1,0:T(4,128)(2,1)S(1)} %pack.1), channel_id=1, source_target_pairs={{4,0},{8,4},{12,8},{0,12},{5,1},{9,5},{13,9},{1,13},{6,2},{10,6},{... | collective-permute-start | bytes 122888 | tf_op jit(solution)/shard_map/ppermute | solution.py:238
  8.7 9.6 %copy-start.3 = (s32[32]{0:T(128)S(1)}, s32[32]{0:T(128)}, u32[]{:S(2)}) copy-start(s32[32]{0:T(128)} %param.15) | copy-start | bytes 388
  11.6 1.7 %collective-permute-start.3 = (bf16[1168,128]{1,0:T(8,128)(2,1)S(1)}, bf16[1168,128]{1,0:T(8,128)(2,1)S(1)}, u32[]{:S(2)}, u32[]{:S(2)}) collective-permute-start(bf16[1168,128]{1,0:T(8,128)(2,1)S(1)} %prefill.1.near_ref), channel_id=1, source_target_pairs={{0,1},{1,0},{2,3},{3,2},{4,5},{5,4},{6,7},{7,6},{8,9},{9,8},{10,11... | collective-permute-start | bytes 897032 | tf_op jit(solution)/shard_map/ppermute | solution.py:241
  14.4 6.0 %collective-permute-start.4 = (bf16[4,4096]{1,0:T(4,128)(2,1)S(1)}, bf16[4,4096]{1,0:T(4,128)(2,1)S(1)}, u32[]{:S(2)}, u32[]{:S(2)}) collective-permute-start(bf16[4,4096]{1,0:T(4,128)(2,1)S(1)} %get-tuple-element.9), channel_id=1, source_target_pairs={{0,4},{4,8},{8,12},{12,0},{1,5},{5,9},{9,13},{13,1},{2,6},{6,10},{... | collective-permute-start | bytes 98312 | tf_op jit(solution)/shard_map/ppermute | solution.py:249
  15.1 5.3 %collective-permute-start.5 = (bf16[4,4096]{1,0:T(4,128)(2,1)S(1)}, bf16[4,4096]{1,0:T(4,128)(2,1)S(1)}, u32[]{:S(2)}, u32[]{:S(2)}) collective-permute-start(bf16[4,4096]{1,0:T(4,128)(2,1)S(1)} %get-tuple-element.10), channel_id=1, source_target_pairs={{0,8},{4,12},{8,0},{12,4},{1,9},{5,13},{9,1},{13,5},{2,10},{6,14},... | collective-permute-start | bytes 98312 | tf_op jit(solution)/shard_map/ppermute | solution.py:249
  15.7 5.0 %collective-permute-start.6 = (bf16[4,4096]{1,0:T(4,128)(2,1)S(1)}, bf16[4,4096]{1,0:T(4,128)(2,1)S(1)}, u32[]{:S(2)}, u32[]{:S(2)}) collective-permute-start(bf16[4,4096]{1,0:T(4,128)(2,1)S(1)} %get-tuple-element.11), channel_id=1, source_target_pairs={{0,12},{4,0},{8,4},{12,8},{1,13},{5,1},{9,5},{13,9},{2,14},{6,2},{... | collective-permute-start | bytes 98312 | tf_op jit(solution)/shard_map/ppermute | solution.py:249

commit v17 on v16

--- a/solution.py
+++ b/solution.py
@@ -158,16 +158,31 @@
     )
 
 
-def decode_kernel(rows_ref, weight_ref, near_ref, far_ref, *out_refs):
+def share(query, phi, scale, ref, g, heads):
+    head_size = query.shape[1]
+    feats = phi.shape[1]
+    tile_at = heads * feats
+    tile = ref[tile_at : tile_at + 16, :].astype(jnp.float32)
+    linear = jnp.dot(phi, ref[g * feats : (g + 1) * feats, :], preferred_element_type=jnp.float32)
+    at = tile_at + 16 + g * SLAB
+    keys = ref[at : at + SLAB, :]
+    at += heads * SLAB
+    values = ref[at : at + SLAB, :]
+    keys_wide = keys.astype(jnp.float32)
+    key_scale = lax.rsqrt(jnp.mean((keys_wide * keys_wide).T, axis=0, keepdims=True) + EPS)
+    score = lax.dot_general(query, keys, NT, preferred_element_type=jnp.float32) * scale * key_scale
+    weights = jnp.exp(score) * tile[MASK_ROW : MASK_ROW + 1, :SLAB]
+    back = 1.0 / (feats * feats)
+    num = linear * back + jnp.dot(weights.astype(jnp.bfloat16), values, preferred_element_type=jnp.float32)
+    den = jnp.sum(weights, axis=-1, keepdims=True)
+    return num, den + jnp.sum(phi.astype(jnp.float32) * tile[g : g + 1], axis=-1, keepdims=True) * back
+
+
+def begin_kernel(rows_ref, weight_ref, near_ref, query_ref, phi_ref, num_ref, den_ref, scale_ref):
     heads, head_size, feats = weight_ref.shape
-    count = rows_ref.shape[0]
     group = (rows_ref.shape[1] - 2 * heads * head_size) // (heads * head_size)
     keys_at = heads * group * head_size
     values_at = keys_at + heads * head_size
-    each = count // len(out_refs)
-    tile_at = heads * feats
-    halves = (near_ref, far_ref)
-    tiles = [ref[tile_at : tile_at + 16, :].astype(jnp.float32) for ref in halves]
     for g in range(heads):
         query = jnp.concatenate(
             [
@@ -184,25 +199,23 @@
         own_key = own_key * lax.rsqrt(jnp.mean(own_key * own_key, axis=-1, keepdims=True) + EPS)
         own_score = jnp.sum(wide * jnp.concatenate([own_key] * group, axis=0), axis=-1, keepdims=True) * scale
         own_weight = jnp.exp(own_score)
-        num = own_weight.astype(jnp.bfloat16).astype(jnp.float32) * jnp.concatenate([own_value] * group, axis=0)
-        den = own_weight
-        linear = jnp.zeros_like(num)
-        for ref, tile in zip(halves, tiles):
-            linear += jnp.dot(phi, ref[g * feats : (g + 1) * feats, :], preferred_element_type=jnp.float32)
-            at = tile_at + 16 + g * SLAB
-            keys = ref[at : at + SLAB, :]
-            at += heads * SLAB
-            values = ref[at : at + SLAB, :]
-            keys_wide = keys.astype(jnp.float32)
-            key_scale = lax.rsqrt(jnp.mean((keys_wide * keys_wide).T, axis=0, keepdims=True) + EPS)
-            score = lax.dot_general(query, keys, NT, preferred_element_type=jnp.float32) * scale * key_scale
-            weights = jnp.exp(score) * tile[MASK_ROW : MASK_ROW + 1, :SLAB]
-            num += jnp.dot(weights.astype(jnp.bfloat16), values, preferred_element_type=jnp.float32)
-            den += jnp.sum(weights, axis=-1, keepdims=True)
-        norm = (tiles[0] + tiles[1])[g : g + 1]
-        back = 1.0 / (feats * feats)
-        den += jnp.sum(phi.astype(jnp.float32) * norm, axis=-1, keepdims=True) * back
-        result = ((linear * back + num) / den).astype(jnp.bfloat16)
+        num, den = share(query, phi, scale, near_ref, g, heads)
+        num += own_weight.astype(jnp.bfloat16).astype(jnp.float32) * jnp.concatenate([own_value] * group, axis=0)
+        query_ref[g] = query
+        phi_ref[g] = phi
+        num_ref[g] = num
+        den_ref[g] = jnp.broadcast_to(den + own_weight, num.shape)
+        scale_ref[g] = jnp.broadcast_to(scale, num.shape)
+
+
+def end_kernel(query_ref, phi_ref, num_ref, den_ref, scale_ref, far_ref, *out_refs):
+    heads, asked, head_size = query_ref.shape
+    each, width = out_refs[0].shape
+    group = width // (heads * head_size)
+    count = asked // group
+    for g in range(heads):
+        num, den = share(query_ref[g], phi_ref[g], scale_ref[g][:, :1], far_ref, g, heads)
+        result = ((num_ref[g] + num) / (den_ref[g] + den)).astype(jnp.bfloat16)
         for h in range(group):
             at = (g * group + h) * head_size
             for k, out_ref in enumerate(out_refs):
@@ -210,22 +223,38 @@
                 out_ref[:, at : at + head_size] = result[start : start + each]
 
 
-def decode(rows, weight, near, far, parts):
+def begin(rows, weight, near):
     heads, head_size, feats = weight.shape
     count = rows.shape[0]
-    width = rows.shape[1] - 2 * heads * head_size
+    group = (rows.shape[1] - 2 * heads * head_size) // (heads * head_size)
+    shape = (heads, group * count, head_size)
     vmem = pl.BlockSpec(memory_space=pltpu.VMEM)
     return pl.pallas_call(
-        decode_kernel,
-        in_specs=[vmem] * 4,
-        out_specs=[vmem] * parts,
-        out_shape=[jax.ShapeDtypeStruct((count // parts, width), jnp.bfloat16)] * parts,
+        begin_kernel,
+        in_specs=[vmem] * 3,
+        out_specs=[vmem] * 5,
+        out_shape=[jax.ShapeDtypeStruct(shape, jnp.bfloat16)] * 2 + [jax.ShapeDtypeStruct(shape, jnp.float32)] * 3,
         compiler_params=pltpu.CompilerParams(vmem_limit_bytes=32 * 1024 * 1024),
         cost_estimate=pl.CostEstimate(
-            flops=10 * count * width * feats, bytes_accessed=4 * count * width, transcendentals=2 * count * width
+            flops=6 * count * rows.shape[1] * feats, bytes_accessed=4 * rows.size, transcendentals=2 * rows.size
         ),
-        name="decode",
-    )(rows, weight, near, far)
+        name="begin",
+    )(rows, weight, near)
+
+
+def end(started, far, count, width, parts):
+    vmem = pl.BlockSpec(memory_space=pltpu.VMEM)
+    return pl.pallas_call(
+        end_kernel,
+        in_specs=[vmem] * 6,
+        out_specs=[vmem] * parts,
+        out_shape=[jax.ShapeDtypeStruct((count, width), jnp.bfloat16)] * parts,
+        compiler_params=pltpu.CompilerParams(vmem_limit_bytes=32 * 1024 * 1024),
+        cost_estimate=pl.CostEstimate(
+            flops=4 * started[0].size * 128, bytes_accessed=4 * started[0].size, transcendentals=started[0].size
+        ),
+        name="end",
+    )(*started, far)
 
 
 def body(
@@ -239,7 +268,8 @@
     ]
     near = prefill(prompt_keys, prompt_values, feature_weight, lengths)
     far = lax.ppermute(near, "sub", [(0, 1), (1, 0)])
-    results = decode(jnp.concatenate(blocks, axis=0), feature_weight, near, far, sects)
+    started = begin(jnp.concatenate(blocks, axis=0), feature_weight, near)
+    results = end(started, far, *queries.shape, sects)
 
     count = queries.shape[0]
     first_row = (sect * lax.axis_size("sub") + sub) * count

time: 21.6 us -> 21.2 us (0.981)
  waiting for transfers between devices: 3.76 us -> 2.9 us
  Pallas kernels: 4.96 us -> 5.43 us
    ppermute x1, waiting for transfers between devices: 1.38 us -> 0.52 us  [body(): far = lax.ppermute(near, 'sub', [(0, 1), (1, 0)])]
    pallas_call x1 -> x2, Pallas kernels: 1.14 us -> 1.61 us  [the longest x1 0.86 us: begin(): pl.pallas_call(begin_kernel, in_specs=[vmem] * 3, out_specs=[vmem] * 5, o...]
  transfers between devices with their start and end apart: 7 -> 7, of which waited for: 3 -> 3; matrix products, arithmetic and copies ran while one was open for 1% -> 1% of each run, Pallas kernels for 13% -> 18%
where the time goes in v17:
time: 21.2 us; the launch traced here: 21 us
  starting transfers between devices  11 us (52%)
  Pallas kernels  5.43 us (26%)
  waiting for transfers between devices  2.9 us (14%)
  other arithmetic  0.89 us (4%)
  between operations  0.81 us (4%)
    ppermute x3, starting transfers between devices, body(): lax.ppermute(mine, 'sect', [((i + k) % sects, i) for i in range(sects)])  7.02 us
    ppermute x3, starting transfers between devices, body(): lax.ppermute(results[k], 'sect', [(i, (i + k) % sects) for i in range(sec...  3.88 us
    pallas_call x1, Pallas kernels, prefill(): pl.pallas_call(prefill_kernel, in_specs=[pl.BlockSpec(memory_space=pltpu....  2.88 us
    ppermute x3, waiting for transfers between devices, body(): lax.ppermute(results[k], 'sect', [(i, (i + k) % sects) for i in range(sec...  2.37 us
    pallas_call x1, Pallas kernels, pack(): pl.pallas_call(pack_kernel, in_specs=[pl.BlockSpec(memory_space=pltpu.Mem...  0.94 us
    pallas_call x1, Pallas kernels, begin(): pl.pallas_call(begin_kernel, in_specs=[vmem] * 3, out_specs=[vmem] * 5, o...  0.86 us
    pallas_call x1, Pallas kernels, end(): pl.pallas_call(end_kernel, in_specs=[vmem] * 6, out_specs=[vmem] * parts,...  0.75 us
    select_n x1, other arithmetic, body(): out = jnp.where((prompts == (sect - k) % sects)[:, None], result, out)  0.71 us
  transfers between devices with their start and end apart: 7, of which 3 were waited for; matrix products, arithmetic and copies ran while one was open for 1% of the time, Pallas kernels for 18%

profile of v17, /device:TPU:0, one launch (start us, length us, event | category | flops | bytes accessed | tf_op | source)
XLA Modules:
  0.0 21.0 jit_solution(3129678043198454718)
XLA Ops:
  0.0 0.0 copy-start.2
  0.0 0.0 copy-start
  0.0 0.0 copy-start.1
  0.0 0.9 %pack.1 = bf16[4,5120]{1,0:T(4,128)(2,1)S(1)} custom-call(bf16[4,4096]{1,0:T(4,128)(2,1)} %queries_ref.1, bf16[4,512]{1,0:T(4,128)(2,1)} %keys_ref.2, bf16[4,512]{1,0:T(4,128)(2,1)} %values_ref.2), custom_call_target="tpu_custom_call" | custom-call | flops 10000000000 | bytes 33554432 | tf_op jit(solution)/shard_map/pack/pallas_call | solution.py:35
  1.0 3.1 %collective-permute-start.2 = (bf16[4,5120]{1,0:T(4,128)(2,1)S(1)}, bf16[4,5120]{1,0:T(4,128)(2,1)S(1)}, u32[]{:S(2)}, u32[]{:S(2)}) collective-permute-start(bf16[4,5120]{1,0:T(4,128)(2,1)S(1)} %pack.1), channel_id=1, source_target_pairs={{12,0},{0,4},{4,8},{8,12},{13,1},{1,5},{5,9},{9,13},{14,2},{2,6},{... | collective-permute-start | bytes 122888 | tf_op jit(solution)/shard_map/ppermute | solution.py:267
  4.0 2.6 %collective-permute-start.1 = (bf16[4,5120]{1,0:T(4,128)(2,1)S(1)}, bf16[4,5120]{1,0:T(4,128)(2,1)S(1)}, u32[]{:S(2)}, u32[]{:S(2)}) collective-permute-start(bf16[4,5120]{1,0:T(4,128)(2,1)S(1)} %pack.1), channel_id=1, source_target_pairs={{8,0},{12,4},{0,8},{4,12},{9,1},{13,5},{1,9},{5,13},{10,2},{14,6},... | collective-permute-start | bytes 122888 | tf_op jit(solution)/shard_map/ppermute | solution.py:267
  6.6 1.3 %collective-permute-start = (bf16[4,5120]{1,0:T(4,128)(2,1)S(1)}, bf16[4,5120]{1,0:T(4,128)(2,1)S(1)}, u32[]{:S(2)}, u32[]{:S(2)}) collective-permute-start(bf16[4,5120]{1,0:T(4,128)(2,1)S(1)} %pack.1), channel_id=1, source_target_pairs={{4,0},{8,4},{12,8},{0,12},{5,1},{9,5},{13,9},{1,13},{6,2},{10,6},{... | collective-permute-start | bytes 122888 | tf_op jit(solution)/shard_map/ppermute | solution.py:267
  8.6 0.0 copy-done.2
  8.6 0.0 copy-done
  8.6 0.0 copy-done.1
  8.7 0.0 copy-start.3
  8.7 2.9 %prefill.1.near_ref = bf16[1168,128]{1,0:T(8,128)(2,1)S(1)} custom-call(s32[1]{0:T(128)S(6)} %copy.9.lengths_ref, bf16[1,4096,512]{2,1,0:T(8,128)(2,1)S(1)} %copy-done, bf16[1,4096,512]{2,1,0:T(8,128)(2,1)S(1)} %copy-done.1, bf16[4,128,128]{2,1,0:T(8,128)(2,1)S(1)} %copy-done.2), custom_call_target="tpu_custom_call" | custom-call | flops 1073741824 | bytes 8388608 | tf_op jit(solution)/shard_map/prefill/pallas_call | solution.py:136
  11.6 0.1 collective-permute-start.3
  11.7 0.0 collective-permute-done.2
  11.7 0.0 collective-permute-done.1
  11.7 0.0 collective-permute-done
  11.7 0.1 pad_maximum_fusion.rows_ref
  11.8 0.9 %begin.1 = (bf16[4,128,128]{2,1,0:T(8,128)(2,1)S(1)}, bf16[4,128,128]{2,1,0:T(8,128)(2,1)S(1)}, f32[4,128,128]{2,1,0:T(8,128)S(1)}, f32[4,128,128]{2,1,0:T(8,128)S(1)}, f32[4,128,128]{2,1,0:T(8,128)S(1)}) custom-call(bf16[16,5120]{1,0:T(8,128)(2,1)S(1)} %pad_maximum_fusion.rows_ref, bf16[4,128,128]{2,1,0:T(8,128)(2,1)S(1)} %copy-done.2, ...), custom_call_target="tpu_custom_call" | custom-call | flops 62914560 | bytes 327680 | tf_op jit(solution)/shard_map/begin/pallas_call | solution.py:232
  12.7 0.5 %collective-permute-done.3.far_ref = bf16[1168,128]{1,0:T(8,128)(2,1)S(1)} collective-permute-done((bf16[1168,128]{1,0:T(8,128)(2,1)S(1)}, bf16[1168,128]{1,0:T(8,128)(2,1)S(1)}, u32[]{:S(2)}, u32[]{:S(2)}) %collective-permute-start.3) | collective-permute-done | bytes 299040 | tf_op jit(solution)/shard_map/ppermute | solution.py:270
  13.2 0.7 %end.1 = (bf16[4,4096]{1,0:T(4,128)(2,1)S(1)}, bf16[4,4096]{1,0:T(4,128)(2,1)S(1)}, bf16[4,4096]{1,0:T(4,128)(2,1)S(1)}, bf16[4,4096]{1,0:T(4,128)(2,1)S(1)}) custom-call(bf16[4,128,128]{2,1,0:T(8,128)(2,1)S(1)} %get-tuple-element.14.query_ref, bf16[4,128,128]{2,1,0:T(8,128)(2,1)S(1)} %get-tuple-element.15.phi_ref, ...), custom_call_target="tpu_custom_call" | custom-call | flops 33554432 | bytes 262144 | tf_op jit(solution)/shard_map/end/pallas_call | solution.py:247
  14.0 0.7 %collective-permute-start.4 = (bf16[4,4096]{1,0:T(4,128)(2,1)S(1)}, bf16[4,4096]{1,0:T(4,128)(2,1)S(1)}, u32[]{:S(2)}, u32[]{:S(2)}) collective-permute-start(bf16[4,4096]{1,0:T(4,128)(2,1)S(1)} %get-tuple-element.19), channel_id=1, source_target_pairs={{0,4},{4,8},{8,12},{12,0},{1,5},{5,9},{9,13},{13,1},{2,6},{6,10},{... | collective-permute-start | bytes 98312 | tf_op jit(solution)/shard_map/ppermute | solution.py:279
  14.7 1.4 %collective-permute-start.5 = (bf16[4,4096]{1,0:T(4,128)(2,1)S(1)}, bf16[4,4096]{1,0:T(4,128)(2,1)S(1)}, u32[]{:S(2)}, u32[]{:S(2)}) collective-permute-start(bf16[4,4096]{1,0:T(4,128)(2,1)S(1)} %get-tuple-element.20), channel_id=1, source_target_pairs={{0,8},{4,12},{8,0},{12,4},{1,9},{5,13},{9,1},{13,5},{2,10},{6,14},... | collective-permute-start | bytes 98312 | tf_op jit(solution)/shard_map/ppermute | solution.py:279
  16.1 1.7 %collective-permute-start.6 = (bf16[4,4096]{1,0:T(4,128)(2,1)S(1)}, bf16[4,4096]{1,0:T(4,128)(2,1)S(1)}, u32[]{:S(2)}, u32[]{:S(2)}) collective-permute-start(bf16[4,4096]{1,0:T(4,128)(2,1)S(1)} %get-tuple-element.21), channel_id=1, source_target_pairs={{0,12},{4,0},{8,4},{12,8},{1,13},{5,1},{9,5},{13,9},{2,14},{6,2},{... | collective-permute-start | bytes 98312 | tf_op jit(solution)/shard_map/ppermute | solution.py:279
  17.8 0.0 copy-done.3
  17.9 0.1 broadcast_compare_fusion.2
  17.9 2.0 %collective-permute-done.4 = bf16[4,4096]{1,0:T(4,128)(2,1)S(1)} collective-permute-done((bf16[4,4096]{1,0:T(4,128)(2,1)S(1)}, bf16[4,4096]{1,0:T(4,128)(2,1)S(1)}, u32[]{:S(2)}, u32[]{:S(2)}) %collective-permute-start.4) | collective-permute-done | bytes 32800 | tf_op jit(solution)/shard_map/ppermute | solution.py:279
  19.9 0.0 collective-permute-done.5
  20.0 0.3 %collective-permute-done.6 = bf16[4,4096]{1,0:T(4,128)(2,1)S(1)} collective-permute-done((bf16[4,4096]{1,0:T(4,128)(2,1)S(1)}, bf16[4,4096]{1,0:T(4,128)(2,1)S(1)}, u32[]{:S(2)}, u32[]{:S(2)}) %collective-permute-start.6) | collective-permute-done | bytes 32800 | tf_op jit(solution)/shard_map/ppermute | solution.py:279
  20.3 0.7 %select_select_fusion = bf16[4,4096]{1,0:T(4,128)(2,1)} fusion(bf16[4,4096]{1,0:T(4,128)(2,1)S(1)} %collective-permute-done.4, bf16[4,4096]{1,0:T(4,128)(2,1)S(1)} %collective-permute-done.5, bf16[4,4096]{1,0:T(4,128)(2,1)S(1)} %collective-permute-done.6, bf16[4,4096]{1,0:T(4,128)(2,1)S(1)} %get-tuple-element.22, pred[4]{0:T(512)(128)(4,1)S(1)} %get-tuple-element.25, ...), kind=kLoop, calls=%fused_computation.1 | loop fusion | flops 49152 | bytes 163852 | tf_op jit(solution)/shard_map/jit(_where)/select_n | solution.py:280
Async XLA Ops:
  0.0 8.6 %copy-start.2 = (bf16[4,128,128]{2,1,0:T(8,128)(2,1)S(1)}, bf16[4,128,128]{2,1,0:T(8,128)(2,1)}, u32[]{:S(2)}) copy-start(bf16[4,128,128]{2,1,0:T(8,128)(2,1)} %weight_ref.3) | copy-start | bytes 393220
  0.0 8.6 %copy-start = (bf16[1,4096,512]{2,1,0:T(8,128)(2,1)S(1)}, bf16[1,4096,512]{2,1,0:T(8,128)(2,1)}, u32[]{:S(2)}) copy-start(bf16[1,4096,512]{2,1,0:T(8,128)(2,1)} %keys_ref.3) | copy-start | bytes 12582916
  0.0 8.6 %copy-start.1 = (bf16[1,4096,512]{2,1,0:T(8,128)(2,1)S(1)}, bf16[1,4096,512]{2,1,0:T(8,128)(2,1)}, u32[]{:S(2)}) copy-start(bf16[1,4096,512]{2,1,0:T(8,128)(2,1)} %values_ref.3) | copy-start | bytes 12582916
  1.0 10.7 %collective-permute-start.2 = (bf16[4,5120]{1,0:T(4,128)(2,1)S(1)}, bf16[4,5120]{1,0:T(4,128)(2,1)S(1)}, u32[]{:S(2)}, u32[]{:S(2)}) collective-permute-start(bf16[4,5120]{1,0:T(4,128)(2,1)S(1)} %pack.1), channel_id=1, source_target_pairs={{12,0},{0,4},{4,8},{8,12},{13,1},{1,5},{5,9},{9,13},{14,2},{2,6},{... | collective-permute-start | bytes 122888 | tf_op jit(solution)/shard_map/ppermute | solution.py:267
  4.0 7.7 %collective-permute-start.1 = (bf16[4,5120]{1,0:T(4,128)(2,1)S(1)}, bf16[4,5120]{1,0:T(4,128)(2,1)S(1)}, u32[]{:S(2)}, u32[]{:S(2)}) collective-permute-start(bf16[4,5120]{1,0:T(4,128)(2,1)S(1)} %pack.1), channel_id=1, source_target_pairs={{8,0},{12,4},{0,8},{4,12},{9,1},{13,5},{1,9},{5,13},{10,2},{14,6},... | collective-permute-start | bytes 122888 | tf_op jit(solution)/shard_map/ppermute | solution.py:267
  6.6 5.1 %collective-permute-start = (bf16[4,5120]{1,0:T(4,128)(2,1)S(1)}, bf16[4,5120]{1,0:T(4,128)(2,1)S(1)}, u32[]{:S(2)}, u32[]{:S(2)}) collective-permute-start(bf16[4,5120]{1,0:T(4,128)(2,1)S(1)} %pack.1), channel_id=1, source_target_pairs={{4,0},{8,4},{12,8},{0,12},{5,1},{9,5},{13,9},{1,13},{6,2},{10,6},{... | collective-permute-start | bytes 122888 | tf_op jit(solution)/shard_map/ppermute | solution.py:267
  8.7 9.2 %copy-start.3 = (s32[32]{0:T(128)S(1)}, s32[32]{0:T(128)}, u32[]{:S(2)}) copy-start(s32[32]{0:T(128)} %param.15) | copy-start | bytes 388
  11.6 1.7 %collective-permute-start.3 = (bf16[1168,128]{1,0:T(8,128)(2,1)S(1)}, bf16[1168,128]{1,0:T(8,128)(2,1)S(1)}, u32[]{:S(2)}, u32[]{:S(2)}) collective-permute-start(bf16[1168,128]{1,0:T(8,128)(2,1)S(1)} %prefill.1.near_ref), channel_id=1, source_target_pairs={{0,1},{1,0},{2,3},{3,2},{4,5},{5,4},{6,7},{7,6},{8,9},{9,8},{10,11... | collective-permute-start | bytes 897032 | tf_op jit(solution)/shard_map/ppermute | solution.py:270
  14.0 6.0 %collective-permute-start.4 = (bf16[4,4096]{1,0:T(4,128)(2,1)S(1)}, bf16[4,4096]{1,0:T(4,128)(2,1)S(1)}, u32[]{:S(2)}, u32[]{:S(2)}) collective-permute-start(bf16[4,4096]{1,0:T(4,128)(2,1)S(1)} %get-tuple-element.19), channel_id=1, source_target_pairs={{0,4},{4,8},{8,12},{12,0},{1,5},{5,9},{9,13},{13,1},{2,6},{6,10},{... | collective-permute-start | bytes 98312 | tf_op jit(solution)/shard_map/ppermute | solution.py:279
  14.7 5.3 %collective-permute-start.5 = (bf16[4,4096]{1,0:T(4,128)(2,1)S(1)}, bf16[4,4096]{1,0:T(4,128)(2,1)S(1)}, u32[]{:S(2)}, u32[]{:S(2)}) collective-permute-start(bf16[4,4096]{1,0:T(4,128)(2,1)S(1)} %get-tuple-element.20), channel_id=1, source_target_pairs={{0,8},{4,12},{8,0},{12,4},{1,9},{5,13},{9,1},{13,5},{2,10},{6,14},... | collective-permute-start | bytes 98312 | tf_op jit(solution)/shard_map/ppermute | solution.py:279
  16.1 4.2 %collective-permute-start.6 = (bf16[4,4096]{1,0:T(4,128)(2,1)S(1)}, bf16[4,4096]{1,0:T(4,128)(2,1)S(1)}, u32[]{:S(2)}, u32[]{:S(2)}) collective-permute-start(bf16[4,4096]{1,0:T(4,128)(2,1)S(1)} %get-tuple-element.21), channel_id=1, source_target_pairs={{0,12},{4,0},{8,4},{12,8},{1,13},{5,1},{9,5},{13,9},{2,14},{6,2},{... | collective-permute-start | bytes 98312 | tf_op jit(solution)/shard_map/ppermute | solution.py:279

commit v18 on v17

--- a/solution.py
+++ b/solution.py
@@ -262,14 +262,15 @@
 ):
     sub = lax.axis_index("sub")
     sect = lax.axis_index("sect")
+    shifts = list(range(1, sects))
+    shifts[:2] = shifts[:2][::-1]
     mine = pack(queries, new_keys, new_values)
-    blocks = [mine] + [
-        lax.ppermute(mine, "sect", [((i + k) % sects, i) for i in range(sects)]) for k in range(1, sects)
-    ]
+    blocks = [mine] + [lax.ppermute(mine, "sect", [((i + k) % sects, i) for i in range(sects)]) for k in shifts]
     near = prefill(prompt_keys, prompt_values, feature_weight, lengths)
     far = lax.ppermute(near, "sub", [(0, 1), (1, 0)])
     started = begin(jnp.concatenate(blocks, axis=0), feature_weight, near)
     results = end(started, far, *queries.shape, sects)
+    results = dict(zip([0] + shifts, results))
 
     count = queries.shape[0]
     first_row = (sect * lax.axis_size("sub") + sub) * count

time: 21.2 us -> 21.1 us (level)
  waiting for transfers between devices: 2.9 us -> 2.63 us
    ppermute x3, starting transfers between devices: 3.88 us -> 4.96 us  [body(): lax.ppermute(results[k], 'sect', [(i, (i + k) % sects) for i in range(sec...]
    ppermute x3, starting transfers between devices: 7.02 us -> 6.12 us  [body(): lax.ppermute(mine, 'sect', [((i + k) % sects, i) for i in range(sects)])]
    ppermute x3, waiting for transfers between devices: 2.37 us -> 2.1 us  [body(): lax.ppermute(results[k], 'sect', [(i, (i + k) % sects) for i in range(sec...]
  transfers between devices with their start and end apart: 7 -> 7, of which waited for: 3 -> 4; matrix products, arithmetic and copies ran while one was open for 1% -> 1% of each run, Pallas kernels for 18% -> 18%
where the time goes in v18:
time: 21.1 us; the launch traced here: 20.9 us
  starting transfers between devices  11.2 us (53%)
  Pallas kernels  5.43 us (26%)
  waiting for transfers between devices  2.63 us (12%)
  other arithmetic  0.89 us (4%)
  between operations  0.8 us (4%)
    ppermute x3, starting transfers between devices, body(): lax.ppermute(mine, 'sect', [((i + k) % sects, i) for i in range(sects)])  6.12 us
    ppermute x3, starting transfers between devices, body(): lax.ppermute(results[k], 'sect', [(i, (i + k) % sects) for i in range(sec...  4.96 us
    pallas_call x1, Pallas kernels, prefill(): pl.pallas_call(prefill_kernel, in_specs=[pl.BlockSpec(memory_space=pltpu....  2.89 us
    ppermute x3, waiting for transfers between devices, body(): lax.ppermute(results[k], 'sect', [(i, (i + k) % sects) for i in range(sec...  2.1 us
    pallas_call x1, Pallas kernels, pack(): pl.pallas_call(pack_kernel, in_specs=[pl.BlockSpec(memory_space=pltpu.Mem...  0.94 us
    pallas_call x1, Pallas kernels, begin(): pl.pallas_call(begin_kernel, in_specs=[vmem] * 3, out_specs=[vmem] * 5, o...  0.86 us
    pallas_call x1, Pallas kernels, end(): pl.pallas_call(end_kernel, in_specs=[vmem] * 6, out_specs=[vmem] * parts,...  0.74 us
    select_n x1, other arithmetic, body(): out = jnp.where((prompts == (sect - k) % sects)[:, None], result, out)  0.71 us
  transfers between devices with their start and end apart: 7, of which 4 were waited for; matrix products, arithmetic and copies ran while one was open for 1% of the time, Pallas kernels for 18%

profile of v18, /device:TPU:0, one launch (start us, length us, event | category | flops | bytes accessed | tf_op | source)
XLA Modules:
  0.0 20.9 jit_solution(1752895302659984745)
XLA Ops:
  0.0 0.0 copy-start.2
  0.0 0.0 copy-start
  0.0 0.0 copy-start.1
  0.0 0.9 %pack.1 = bf16[4,5120]{1,0:T(4,128)(2,1)S(1)} custom-call(bf16[4,4096]{1,0:T(4,128)(2,1)} %queries_ref.1, bf16[4,512]{1,0:T(4,128)(2,1)} %keys_ref.2, bf16[4,512]{1,0:T(4,128)(2,1)} %values_ref.2), custom_call_target="tpu_custom_call" | custom-call | flops 10000000000 | bytes 33554432 | tf_op jit(solution)/shard_map/pack/pallas_call | solution.py:35
  1.0 3.1 %collective-permute-start.2 = (bf16[4,5120]{1,0:T(4,128)(2,1)S(1)}, bf16[4,5120]{1,0:T(4,128)(2,1)S(1)}, u32[]{:S(2)}, u32[]{:S(2)}) collective-permute-start(bf16[4,5120]{1,0:T(4,128)(2,1)S(1)} %pack.1), channel_id=1, source_target_pairs={{12,0},{0,4},{4,8},{8,12},{13,1},{1,5},{5,9},{9,13},{14,2},{2,6},{... | collective-permute-start | bytes 122888 | tf_op jit(solution)/shard_map/ppermute | solution.py:268
  4.0 2.1 %collective-permute-start.1 = (bf16[4,5120]{1,0:T(4,128)(2,1)S(1)}, bf16[4,5120]{1,0:T(4,128)(2,1)S(1)}, u32[]{:S(2)}, u32[]{:S(2)}) collective-permute-start(bf16[4,5120]{1,0:T(4,128)(2,1)S(1)} %pack.1), channel_id=1, source_target_pairs={{4,0},{8,4},{12,8},{0,12},{5,1},{9,5},{13,9},{1,13},{6,2},{10,6},{... | collective-permute-start | bytes 122888 | tf_op jit(solution)/shard_map/ppermute | solution.py:268
  6.1 0.9 %collective-permute-start = (bf16[4,5120]{1,0:T(4,128)(2,1)S(1)}, bf16[4,5120]{1,0:T(4,128)(2,1)S(1)}, u32[]{:S(2)}, u32[]{:S(2)}) collective-permute-start(bf16[4,5120]{1,0:T(4,128)(2,1)S(1)} %pack.1), channel_id=1, source_target_pairs={{8,0},{12,4},{0,8},{4,12},{9,1},{13,5},{1,9},{5,13},{10,2},{14,6},... | collective-permute-start | bytes 122888 | tf_op jit(solution)/shard_map/ppermute | solution.py:268
  7.7 0.0 copy-done.2
  7.7 0.0 copy-done
  7.7 0.0 copy-done.1
  7.8 0.0 copy-start.3
  7.8 2.9 %prefill.1.near_ref = bf16[1168,128]{1,0:T(8,128)(2,1)S(1)} custom-call(s32[1]{0:T(128)S(6)} %copy.9.lengths_ref, bf16[1,4096,512]{2,1,0:T(8,128)(2,1)S(1)} %copy-done, bf16[1,4096,512]{2,1,0:T(8,128)(2,1)S(1)} %copy-done.1, bf16[4,128,128]{2,1,0:T(8,128)(2,1)S(1)} %copy-done.2), custom_call_target="tpu_custom_call" | custom-call | flops 1073741824 | bytes 8388608 | tf_op jit(solution)/shard_map/prefill/pallas_call | solution.py:136
  10.7 0.1 collective-permute-start.3
  10.8 0.0 collective-permute-done.2
  10.8 0.0 collective-permute-done.1
  10.8 0.2 collective-permute-done
  11.0 0.1 pad_maximum_fusion.rows_ref
  11.1 0.9 %begin.1 = (bf16[4,128,128]{2,1,0:T(8,128)(2,1)S(1)}, bf16[4,128,128]{2,1,0:T(8,128)(2,1)S(1)}, f32[4,128,128]{2,1,0:T(8,128)S(1)}, f32[4,128,128]{2,1,0:T(8,128)S(1)}, f32[4,128,128]{2,1,0:T(8,128)S(1)}) custom-call(bf16[16,5120]{1,0:T(8,128)(2,1)S(1)} %pad_maximum_fusion.rows_ref, bf16[4,128,128]{2,1,0:T(8,128)(2,1)S(1)} %copy-done.2, ...), custom_call_target="tpu_custom_call" | custom-call | flops 62914560 | bytes 327680 | tf_op jit(solution)/shard_map/begin/pallas_call | solution.py:232
  12.0 0.3 %collective-permute-done.3.far_ref = bf16[1168,128]{1,0:T(8,128)(2,1)S(1)} collective-permute-done((bf16[1168,128]{1,0:T(8,128)(2,1)S(1)}, bf16[1168,128]{1,0:T(8,128)(2,1)S(1)}, u32[]{:S(2)}, u32[]{:S(2)}) %collective-permute-start.3) | collective-permute-done | bytes 299040 | tf_op jit(solution)/shard_map/ppermute | solution.py:270
  12.3 0.7 %end.1 = (bf16[4,4096]{1,0:T(4,128)(2,1)S(1)}, bf16[4,4096]{1,0:T(4,128)(2,1)S(1)}, bf16[4,4096]{1,0:T(4,128)(2,1)S(1)}, bf16[4,4096]{1,0:T(4,128)(2,1)S(1)}) custom-call(bf16[4,128,128]{2,1,0:T(8,128)(2,1)S(1)} %get-tuple-element.14.query_ref, bf16[4,128,128]{2,1,0:T(8,128)(2,1)S(1)} %get-tuple-element.15.phi_ref, ...), custom_call_target="tpu_custom_call" | custom-call | flops 33554432 | bytes 262144 | tf_op jit(solution)/shard_map/end/pallas_call | solution.py:247
  13.1 1.6 %collective-permute-start.4 = (bf16[4,4096]{1,0:T(4,128)(2,1)S(1)}, bf16[4,4096]{1,0:T(4,128)(2,1)S(1)}, u32[]{:S(2)}, u32[]{:S(2)}) collective-permute-start(bf16[4,4096]{1,0:T(4,128)(2,1)S(1)} %get-tuple-element.19), channel_id=1, source_target_pairs={{0,4},{4,8},{8,12},{12,0},{1,5},{5,9},{9,13},{13,1},{2,6},{6,10},{... | collective-permute-start | bytes 98312 | tf_op jit(solution)/shard_map/ppermute | solution.py:280
  14.7 1.0 %collective-permute-start.5 = (bf16[4,4096]{1,0:T(4,128)(2,1)S(1)}, bf16[4,4096]{1,0:T(4,128)(2,1)S(1)}, u32[]{:S(2)}, u32[]{:S(2)}) collective-permute-start(bf16[4,4096]{1,0:T(4,128)(2,1)S(1)} %get-tuple-element.20), channel_id=1, source_target_pairs={{0,8},{4,12},{8,0},{12,4},{1,9},{5,13},{9,1},{13,5},{2,10},{6,14},... | collective-permute-start | bytes 98312 | tf_op jit(solution)/shard_map/ppermute | solution.py:280
  15.7 2.4 %collective-permute-start.6 = (bf16[4,4096]{1,0:T(4,128)(2,1)S(1)}, bf16[4,4096]{1,0:T(4,128)(2,1)S(1)}, u32[]{:S(2)}, u32[]{:S(2)}) collective-permute-start(bf16[4,4096]{1,0:T(4,128)(2,1)S(1)} %get-tuple-element.21), channel_id=1, source_target_pairs={{0,12},{4,0},{8,4},{12,8},{1,13},{5,1},{9,5},{13,9},{2,14},{6,2},{... | collective-permute-start | bytes 98312 | tf_op jit(solution)/shard_map/ppermute | solution.py:280
  18.0 0.0 copy-done.3
  18.0 0.1 broadcast_compare_fusion.2
  18.1 1.0 %collective-permute-done.4 = bf16[4,4096]{1,0:T(4,128)(2,1)S(1)} collective-permute-done((bf16[4,4096]{1,0:T(4,128)(2,1)S(1)}, bf16[4,4096]{1,0:T(4,128)(2,1)S(1)}, u32[]{:S(2)}, u32[]{:S(2)}) %collective-permute-start.4) | collective-permute-done | bytes 32800 | tf_op jit(solution)/shard_map/ppermute | solution.py:280
  19.2 1.1 %collective-permute-done.5 = bf16[4,4096]{1,0:T(4,128)(2,1)S(1)} collective-permute-done((bf16[4,4096]{1,0:T(4,128)(2,1)S(1)}, bf16[4,4096]{1,0:T(4,128)(2,1)S(1)}, u32[]{:S(2)}, u32[]{:S(2)}) %collective-permute-start.5) | collective-permute-done | bytes 32800 | tf_op jit(solution)/shard_map/ppermute | solution.py:280
  20.2 0.0 collective-permute-done.6
  20.2 0.7 %select_select_fusion = bf16[4,4096]{1,0:T(4,128)(2,1)} fusion(bf16[4,4096]{1,0:T(4,128)(2,1)S(1)} %collective-permute-done.4, bf16[4,4096]{1,0:T(4,128)(2,1)S(1)} %collective-permute-done.5, bf16[4,4096]{1,0:T(4,128)(2,1)S(1)} %collective-permute-done.6, bf16[4,4096]{1,0:T(4,128)(2,1)S(1)} %get-tuple-element.22, pred[4]{0:T(512)(128)(4,1)S(1)} %get-tuple-element.25, ...), kind=kLoop, calls=%fused_computation.1 | loop fusion | flops 49152 | bytes 163852 | tf_op jit(solution)/shard_map/jit(_where)/select_n | solution.py:281
Async XLA Ops:
  0.0 7.7 %copy-start.2 = (bf16[4,128,128]{2,1,0:T(8,128)(2,1)S(1)}, bf16[4,128,128]{2,1,0:T(8,128)(2,1)}, u32[]{:S(2)}) copy-start(bf16[4,128,128]{2,1,0:T(8,128)(2,1)} %weight_ref.3) | copy-start | bytes 393220
  0.0 7.7 %copy-start = (bf16[1,4096,512]{2,1,0:T(8,128)(2,1)S(1)}, bf16[1,4096,512]{2,1,0:T(8,128)(2,1)}, u32[]{:S(2)}) copy-start(bf16[1,4096,512]{2,1,0:T(8,128)(2,1)} %keys_ref.3) | copy-start | bytes 12582916
  0.0 7.7 %copy-start.1 = (bf16[1,4096,512]{2,1,0:T(8,128)(2,1)S(1)}, bf16[1,4096,512]{2,1,0:T(8,128)(2,1)}, u32[]{:S(2)}) copy-start(bf16[1,4096,512]{2,1,0:T(8,128)(2,1)} %values_ref.3) | copy-start | bytes 12582916
  1.0 9.8 %collective-permute-start.2 = (bf16[4,5120]{1,0:T(4,128)(2,1)S(1)}, bf16[4,5120]{1,0:T(4,128)(2,1)S(1)}, u32[]{:S(2)}, u32[]{:S(2)}) collective-permute-start(bf16[4,5120]{1,0:T(4,128)(2,1)S(1)} %pack.1), channel_id=1, source_target_pairs={{12,0},{0,4},{4,8},{8,12},{13,1},{1,5},{5,9},{9,13},{14,2},{2,6},{... | collective-permute-start | bytes 122888 | tf_op jit(solution)/shard_map/ppermute | solution.py:268
  4.0 6.8 %collective-permute-start.1 = (bf16[4,5120]{1,0:T(4,128)(2,1)S(1)}, bf16[4,5120]{1,0:T(4,128)(2,1)S(1)}, u32[]{:S(2)}, u32[]{:S(2)}) collective-permute-start(bf16[4,5120]{1,0:T(4,128)(2,1)S(1)} %pack.1), channel_id=1, source_target_pairs={{4,0},{8,4},{12,8},{0,12},{5,1},{9,5},{13,9},{1,13},{6,2},{10,6},{... | collective-permute-start | bytes 122888 | tf_op jit(solution)/shard_map/ppermute | solution.py:268
  6.1 4.9 %collective-permute-start = (bf16[4,5120]{1,0:T(4,128)(2,1)S(1)}, bf16[4,5120]{1,0:T(4,128)(2,1)S(1)}, u32[]{:S(2)}, u32[]{:S(2)}) collective-permute-start(bf16[4,5120]{1,0:T(4,128)(2,1)S(1)} %pack.1), channel_id=1, source_target_pairs={{8,0},{12,4},{0,8},{4,12},{9,1},{13,5},{1,9},{5,13},{10,2},{14,6},... | collective-permute-start | bytes 122888 | tf_op jit(solution)/shard_map/ppermute | solution.py:268
  7.8 10.3 %copy-start.3 = (s32[32]{0:T(128)S(1)}, s32[32]{0:T(128)}, u32[]{:S(2)}) copy-start(s32[32]{0:T(128)} %param.15) | copy-start | bytes 388
  10.7 1.7 %collective-permute-start.3 = (bf16[1168,128]{1,0:T(8,128)(2,1)S(1)}, bf16[1168,128]{1,0:T(8,128)(2,1)S(1)}, u32[]{:S(2)}, u32[]{:S(2)}) collective-permute-start(bf16[1168,128]{1,0:T(8,128)(2,1)S(1)} %prefill.1.near_ref), channel_id=1, source_target_pairs={{0,1},{1,0},{2,3},{3,2},{4,5},{5,4},{6,7},{7,6},{8,9},{9,8},{10,11... | collective-permute-start | bytes 897032 | tf_op jit(solution)/shard_map/ppermute | solution.py:270
  13.1 6.1 %collective-permute-start.4 = (bf16[4,4096]{1,0:T(4,128)(2,1)S(1)}, bf16[4,4096]{1,0:T(4,128)(2,1)S(1)}, u32[]{:S(2)}, u32[]{:S(2)}) collective-permute-start(bf16[4,4096]{1,0:T(4,128)(2,1)S(1)} %get-tuple-element.19), channel_id=1, source_target_pairs={{0,4},{4,8},{8,12},{12,0},{1,5},{5,9},{9,13},{13,1},{2,6},{6,10},{... | collective-permute-start | bytes 98312 | tf_op jit(solution)/shard_map/ppermute | solution.py:280
  14.7 5.5 %collective-permute-start.5 = (bf16[4,4096]{1,0:T(4,128)(2,1)S(1)}, bf16[4,4096]{1,0:T(4,128)(2,1)S(1)}, u32[]{:S(2)}, u32[]{:S(2)}) collective-permute-start(bf16[4,4096]{1,0:T(4,128)(2,1)S(1)} %get-tuple-element.20), channel_id=1, source_target_pairs={{0,8},{4,12},{8,0},{12,4},{1,9},{5,13},{9,1},{13,5},{2,10},{6,14},... | collective-permute-start | bytes 98312 | tf_op jit(solution)/shard_map/ppermute | solution.py:280
  15.7 4.5 %collective-permute-start.6 = (bf16[4,4096]{1,0:T(4,128)(2,1)S(1)}, bf16[4,4096]{1,0:T(4,128)(2,1)S(1)}, u32[]{:S(2)}, u32[]{:S(2)}) collective-permute-start(bf16[4,4096]{1,0:T(4,128)(2,1)S(1)} %get-tuple-element.21), channel_id=1, source_target_pairs={{0,12},{4,0},{8,4},{12,8},{1,13},{5,1},{9,5},{13,9},{2,14},{6,2},{... | collective-permute-start | bytes 98312 | tf_op jit(solution)/shard_map/ppermute | solution.py:280

commit v19 on v18

--- a/solution.py
+++ b/solution.py
@@ -10,7 +10,7 @@
 WINDOW = 64
 TAU = 10.0
 EPS = 1e-06
-BLOCK = 512
+BLOCK = 1024
 NT = (((1,), (1,)), ((), ()))
 
 

time: 21.1 us -> 21.2 us (level)
  no operation moved by 1% of the time
where the time goes in v19:
time: 21.2 us; the launch traced here: 21.1 us
  starting transfers between devices  11.1 us (52%)
  Pallas kernels  5.57 us (26%)
  waiting for transfers between devices  2.64 us (12%)
  other arithmetic  0.89 us (4%)
  between operations  0.8 us (4%)
    ppermute x3, starting transfers between devices, body(): lax.ppermute(mine, 'sect', [((i + k) % sects, i) for i in range(sects)])  6.12 us
    ppermute x3, starting transfers between devices, body(): lax.ppermute(results[k], 'sect', [(i, (i + k) % sects) for i in range(sec...  4.95 us
    pallas_call x1, Pallas kernels, prefill(): pl.pallas_call(prefill_kernel, in_specs=[pl.BlockSpec(memory_space=pltpu....  3.03 us
    ppermute x3, waiting for transfers between devices, body(): lax.ppermute(results[k], 'sect', [(i, (i + k) % sects) for i in range(sec...  2.1 us
    pallas_call x1, Pallas kernels, pack(): pl.pallas_call(pack_kernel, in_specs=[pl.BlockSpec(memory_space=pltpu.Mem...  0.94 us
    pallas_call x1, Pallas kernels, begin(): pl.pallas_call(begin_kernel, in_specs=[vmem] * 3, out_specs=[vmem] * 5, o...  0.86 us
    pallas_call x1, Pallas kernels, end(): pl.pallas_call(end_kernel, in_specs=[vmem] * 6, out_specs=[vmem] * parts,...  0.74 us
    select_n x1, other arithmetic, body(): out = jnp.where((prompts == (sect - k) % sects)[:, None], result, out)  0.71 us
  transfers between devices with their start and end apart: 7, of which 4 were waited for; matrix products, arithmetic and copies ran while one was open for 1% of the time, Pallas kernels for 18%

profile of v19, /device:TPU:0, one launch (start us, length us, event | category | flops | bytes accessed | tf_op | source)
XLA Modules:
  0.0 21.1 jit_solution(17016579373546533366)
XLA Ops:
  0.0 0.0 copy-start.2
  0.0 0.0 copy-start
  0.0 0.0 copy-start.1
  0.0 0.9 %pack.1 = bf16[4,5120]{1,0:T(4,128)(2,1)S(1)} custom-call(bf16[4,4096]{1,0:T(4,128)(2,1)} %queries_ref.1, bf16[4,512]{1,0:T(4,128)(2,1)} %keys_ref.2, bf16[4,512]{1,0:T(4,128)(2,1)} %values_ref.2), custom_call_target="tpu_custom_call" | custom-call | flops 10000000000 | bytes 33554432 | tf_op jit(solution)/shard_map/pack/pallas_call | solution.py:35
  1.0 3.1 %collective-permute-start.2 = (bf16[4,5120]{1,0:T(4,128)(2,1)S(1)}, bf16[4,5120]{1,0:T(4,128)(2,1)S(1)}, u32[]{:S(2)}, u32[]{:S(2)}) collective-permute-start(bf16[4,5120]{1,0:T(4,128)(2,1)S(1)} %pack.1), channel_id=1, source_target_pairs={{12,0},{0,4},{4,8},{8,12},{13,1},{1,5},{5,9},{9,13},{14,2},{2,6},{... | collective-permute-start | bytes 122888 | tf_op jit(solution)/shard_map/ppermute | solution.py:268
  4.0 2.1 %collective-permute-start.1 = (bf16[4,5120]{1,0:T(4,128)(2,1)S(1)}, bf16[4,5120]{1,0:T(4,128)(2,1)S(1)}, u32[]{:S(2)}, u32[]{:S(2)}) collective-permute-start(bf16[4,5120]{1,0:T(4,128)(2,1)S(1)} %pack.1), channel_id=1, source_target_pairs={{4,0},{8,4},{12,8},{0,12},{5,1},{9,5},{13,9},{1,13},{6,2},{10,6},{... | collective-permute-start | bytes 122888 | tf_op jit(solution)/shard_map/ppermute | solution.py:268
  6.1 0.9 %collective-permute-start = (bf16[4,5120]{1,0:T(4,128)(2,1)S(1)}, bf16[4,5120]{1,0:T(4,128)(2,1)S(1)}, u32[]{:S(2)}, u32[]{:S(2)}) collective-permute-start(bf16[4,5120]{1,0:T(4,128)(2,1)S(1)} %pack.1), channel_id=1, source_target_pairs={{8,0},{12,4},{0,8},{4,12},{9,1},{13,5},{1,9},{5,13},{10,2},{14,6},... | collective-permute-start | bytes 122888 | tf_op jit(solution)/shard_map/ppermute | solution.py:268
  7.7 0.0 copy-done.2
  7.7 0.0 copy-done
  7.7 0.0 copy-done.1
  7.8 0.0 copy-start.3
  7.8 3.0 %prefill.1.near_ref = bf16[1168,128]{1,0:T(8,128)(2,1)S(1)} custom-call(s32[1]{0:T(128)S(6)} %copy.9.lengths_ref, bf16[1,4096,512]{2,1,0:T(8,128)(2,1)S(1)} %copy-done, bf16[1,4096,512]{2,1,0:T(8,128)(2,1)S(1)} %copy-done.1, bf16[4,128,128]{2,1,0:T(8,128)(2,1)S(1)} %copy-done.2), custom_call_target="tpu_custom_call" | custom-call | flops 1073741824 | bytes 8388608 | tf_op jit(solution)/shard_map/prefill/pallas_call | solution.py:136
  10.8 0.1 collective-permute-start.3
  10.9 0.0 collective-permute-done.2
  10.9 0.0 collective-permute-done.1
  11.0 0.1 collective-permute-done
  11.0 0.1 pad_maximum_fusion.rows_ref
  11.1 0.9 %begin.1 = (bf16[4,128,128]{2,1,0:T(8,128)(2,1)S(1)}, bf16[4,128,128]{2,1,0:T(8,128)(2,1)S(1)}, f32[4,128,128]{2,1,0:T(8,128)S(1)}, f32[4,128,128]{2,1,0:T(8,128)S(1)}, f32[4,128,128]{2,1,0:T(8,128)S(1)}) custom-call(bf16[16,5120]{1,0:T(8,128)(2,1)S(1)} %pad_maximum_fusion.rows_ref, bf16[4,128,128]{2,1,0:T(8,128)(2,1)S(1)} %copy-done.2, ...), custom_call_target="tpu_custom_call" | custom-call | flops 62914560 | bytes 327680 | tf_op jit(solution)/shard_map/begin/pallas_call | solution.py:232
  12.0 0.5 %collective-permute-done.3.far_ref = bf16[1168,128]{1,0:T(8,128)(2,1)S(1)} collective-permute-done((bf16[1168,128]{1,0:T(8,128)(2,1)S(1)}, bf16[1168,128]{1,0:T(8,128)(2,1)S(1)}, u32[]{:S(2)}, u32[]{:S(2)}) %collective-permute-start.3) | collective-permute-done | bytes 299040 | tf_op jit(solution)/shard_map/ppermute | solution.py:270
  12.5 0.7 %end.1 = (bf16[4,4096]{1,0:T(4,128)(2,1)S(1)}, bf16[4,4096]{1,0:T(4,128)(2,1)S(1)}, bf16[4,4096]{1,0:T(4,128)(2,1)S(1)}, bf16[4,4096]{1,0:T(4,128)(2,1)S(1)}) custom-call(bf16[4,128,128]{2,1,0:T(8,128)(2,1)S(1)} %get-tuple-element.14.query_ref, bf16[4,128,128]{2,1,0:T(8,128)(2,1)S(1)} %get-tuple-element.15.phi_ref, ...), custom_call_target="tpu_custom_call" | custom-call | flops 33554432 | bytes 262144 | tf_op jit(solution)/shard_map/end/pallas_call | solution.py:247
  13.2 1.6 %collective-permute-start.4 = (bf16[4,4096]{1,0:T(4,128)(2,1)S(1)}, bf16[4,4096]{1,0:T(4,128)(2,1)S(1)}, u32[]{:S(2)}, u32[]{:S(2)}) collective-permute-start(bf16[4,4096]{1,0:T(4,128)(2,1)S(1)} %get-tuple-element.19), channel_id=1, source_target_pairs={{0,4},{4,8},{8,12},{12,0},{1,5},{5,9},{9,13},{13,1},{2,6},{6,10},{... | collective-permute-start | bytes 98312 | tf_op jit(solution)/shard_map/ppermute | solution.py:280
  14.8 0.8 %collective-permute-start.5 = (bf16[4,4096]{1,0:T(4,128)(2,1)S(1)}, bf16[4,4096]{1,0:T(4,128)(2,1)S(1)}, u32[]{:S(2)}, u32[]{:S(2)}) collective-permute-start(bf16[4,4096]{1,0:T(4,128)(2,1)S(1)} %get-tuple-element.20), channel_id=1, source_target_pairs={{0,8},{4,12},{8,0},{12,4},{1,9},{5,13},{9,1},{13,5},{2,10},{6,14},... | collective-permute-start | bytes 98312 | tf_op jit(solution)/shard_map/ppermute | solution.py:280
  15.7 2.5 %collective-permute-start.6 = (bf16[4,4096]{1,0:T(4,128)(2,1)S(1)}, bf16[4,4096]{1,0:T(4,128)(2,1)S(1)}, u32[]{:S(2)}, u32[]{:S(2)}) collective-permute-start(bf16[4,4096]{1,0:T(4,128)(2,1)S(1)} %get-tuple-element.21), channel_id=1, source_target_pairs={{0,12},{4,0},{8,4},{12,8},{1,13},{5,1},{9,5},{13,9},{2,14},{6,2},{... | collective-permute-start | bytes 98312 | tf_op jit(solution)/shard_map/ppermute | solution.py:280
  18.2 0.0 copy-done.3
  18.2 0.1 broadcast_compare_fusion.2
  18.2 1.0 %collective-permute-done.4 = bf16[4,4096]{1,0:T(4,128)(2,1)S(1)} collective-permute-done((bf16[4,4096]{1,0:T(4,128)(2,1)S(1)}, bf16[4,4096]{1,0:T(4,128)(2,1)S(1)}, u32[]{:S(2)}, u32[]{:S(2)}) %collective-permute-start.4) | collective-permute-done | bytes 32800 | tf_op jit(solution)/shard_map/ppermute | solution.py:280
  19.3 1.1 %collective-permute-done.5 = bf16[4,4096]{1,0:T(4,128)(2,1)S(1)} collective-permute-done((bf16[4,4096]{1,0:T(4,128)(2,1)S(1)}, bf16[4,4096]{1,0:T(4,128)(2,1)S(1)}, u32[]{:S(2)}, u32[]{:S(2)}) %collective-permute-start.5) | collective-permute-done | bytes 32800 | tf_op jit(solution)/shard_map/ppermute | solution.py:280
  20.3 0.0 collective-permute-done.6
  20.3 0.7 %select_select_fusion = bf16[4,4096]{1,0:T(4,128)(2,1)} fusion(bf16[4,4096]{1,0:T(4,128)(2,1)S(1)} %collective-permute-done.4, bf16[4,4096]{1,0:T(4,128)(2,1)S(1)} %collective-permute-done.5, bf16[4,4096]{1,0:T(4,128)(2,1)S(1)} %collective-permute-done.6, bf16[4,4096]{1,0:T(4,128)(2,1)S(1)} %get-tuple-element.22, pred[4]{0:T(512)(128)(4,1)S(1)} %get-tuple-element.25, ...), kind=kLoop, calls=%fused_computation.1 | loop fusion | flops 49152 | bytes 163852 | tf_op jit(solution)/shard_map/jit(_where)/select_n | solution.py:281
Async XLA Ops:
  0.0 7.7 %copy-start.2 = (bf16[4,128,128]{2,1,0:T(8,128)(2,1)S(1)}, bf16[4,128,128]{2,1,0:T(8,128)(2,1)}, u32[]{:S(2)}) copy-start(bf16[4,128,128]{2,1,0:T(8,128)(2,1)} %weight_ref.3) | copy-start | bytes 393220
  0.0 7.7 %copy-start = (bf16[1,4096,512]{2,1,0:T(8,128)(2,1)S(1)}, bf16[1,4096,512]{2,1,0:T(8,128)(2,1)}, u32[]{:S(2)}) copy-start(bf16[1,4096,512]{2,1,0:T(8,128)(2,1)} %keys_ref.3) | copy-start | bytes 12582916
  0.0 7.7 %copy-start.1 = (bf16[1,4096,512]{2,1,0:T(8,128)(2,1)S(1)}, bf16[1,4096,512]{2,1,0:T(8,128)(2,1)}, u32[]{:S(2)}) copy-start(bf16[1,4096,512]{2,1,0:T(8,128)(2,1)} %values_ref.3) | copy-start | bytes 12582916
  1.0 10.0 %collective-permute-start.2 = (bf16[4,5120]{1,0:T(4,128)(2,1)S(1)}, bf16[4,5120]{1,0:T(4,128)(2,1)S(1)}, u32[]{:S(2)}, u32[]{:S(2)}) collective-permute-start(bf16[4,5120]{1,0:T(4,128)(2,1)S(1)} %pack.1), channel_id=1, source_target_pairs={{12,0},{0,4},{4,8},{8,12},{13,1},{1,5},{5,9},{9,13},{14,2},{2,6},{... | collective-permute-start | bytes 122888 | tf_op jit(solution)/shard_map/ppermute | solution.py:268
  4.0 6.9 %collective-permute-start.1 = (bf16[4,5120]{1,0:T(4,128)(2,1)S(1)}, bf16[4,5120]{1,0:T(4,128)(2,1)S(1)}, u32[]{:S(2)}, u32[]{:S(2)}) collective-permute-start(bf16[4,5120]{1,0:T(4,128)(2,1)S(1)} %pack.1), channel_id=1, source_target_pairs={{4,0},{8,4},{12,8},{0,12},{5,1},{9,5},{13,9},{1,13},{6,2},{10,6},{... | collective-permute-start | bytes 122888 | tf_op jit(solution)/shard_map/ppermute | solution.py:268
  6.1 4.9 %collective-permute-start = (bf16[4,5120]{1,0:T(4,128)(2,1)S(1)}, bf16[4,5120]{1,0:T(4,128)(2,1)S(1)}, u32[]{:S(2)}, u32[]{:S(2)}) collective-permute-start(bf16[4,5120]{1,0:T(4,128)(2,1)S(1)} %pack.1), channel_id=1, source_target_pairs={{8,0},{12,4},{0,8},{4,12},{9,1},{13,5},{1,9},{5,13},{10,2},{14,6},... | collective-permute-start | bytes 122888 | tf_op jit(solution)/shard_map/ppermute | solution.py:268
  7.8 10.4 %copy-start.3 = (s32[32]{0:T(128)S(1)}, s32[32]{0:T(128)}, u32[]{:S(2)}) copy-start(s32[32]{0:T(128)} %param.15) | copy-start | bytes 388
  10.8 1.7 %collective-permute-start.3 = (bf16[1168,128]{1,0:T(8,128)(2,1)S(1)}, bf16[1168,128]{1,0:T(8,128)(2,1)S(1)}, u32[]{:S(2)}, u32[]{:S(2)}) collective-permute-start(bf16[1168,128]{1,0:T(8,128)(2,1)S(1)} %prefill.1.near_ref), channel_id=1, source_target_pairs={{0,1},{1,0},{2,3},{3,2},{4,5},{5,4},{6,7},{7,6},{8,9},{9,8},{10,11... | collective-permute-start | bytes 897032 | tf_op jit(solution)/shard_map/ppermute | solution.py:270
  13.2 6.1 %collective-permute-start.4 = (bf16[4,4096]{1,0:T(4,128)(2,1)S(1)}, bf16[4,4096]{1,0:T(4,128)(2,1)S(1)}, u32[]{:S(2)}, u32[]{:S(2)}) collective-permute-start(bf16[4,4096]{1,0:T(4,128)(2,1)S(1)} %get-tuple-element.19), channel_id=1, source_target_pairs={{0,4},{4,8},{8,12},{12,0},{1,5},{5,9},{9,13},{13,1},{2,6},{6,10},{... | collective-permute-start | bytes 98312 | tf_op jit(solution)/shard_map/ppermute | solution.py:280
  14.8 5.5 %collective-permute-start.5 = (bf16[4,4096]{1,0:T(4,128)(2,1)S(1)}, bf16[4,4096]{1,0:T(4,128)(2,1)S(1)}, u32[]{:S(2)}, u32[]{:S(2)}) collective-permute-start(bf16[4,4096]{1,0:T(4,128)(2,1)S(1)} %get-tuple-element.20), channel_id=1, source_target_pairs={{0,8},{4,12},{8,0},{12,4},{1,9},{5,13},{9,1},{13,5},{2,10},{6,14},... | collective-permute-start | bytes 98312 | tf_op jit(solution)/shard_map/ppermute | solution.py:280
  15.7 4.7 %collective-permute-start.6 = (bf16[4,4096]{1,0:T(4,128)(2,1)S(1)}, bf16[4,4096]{1,0:T(4,128)(2,1)S(1)}, u32[]{:S(2)}, u32[]{:S(2)}) collective-permute-start(bf16[4,4096]{1,0:T(4,128)(2,1)S(1)} %get-tuple-element.21), channel_id=1, source_target_pairs={{0,12},{4,0},{8,4},{12,8},{1,13},{5,1},{9,5},{13,9},{2,14},{6,2},{... | collective-permute-start | bytes 98312 | tf_op jit(solution)/shard_map/ppermute | solution.py:280

commit v20 on v19

--- a/solution.py
+++ b/solution.py
@@ -10,7 +10,7 @@
 WINDOW = 64
 TAU = 10.0
 EPS = 1e-06
-BLOCK = 1024
+BLOCK = 256
 NT = (((1,), (1,)), ((), ()))
 
 

time: 21.2 us -> 21 us (level)
  Pallas kernels: 5.57 us -> 5.32 us
    ppermute x3, waiting for transfers between devices: 0.07 us -> 0.33 us  [body(): lax.ppermute(mine, 'sect', [((i + k) % sects, i) for i in range(sects)])]
    ppermute x1, waiting for transfers between devices: 0.47 us -> 0.21 us  [body(): far = lax.ppermute(near, 'sub', [(0, 1), (1, 0)])]
    pallas_call x1, Pallas kernels: 3.03 us -> 2.77 us  [prefill(): pl.pallas_call(prefill_kernel, in_specs=[pl.BlockSpec(memory_space=pltpu....]
  transfers between devices with their start and end apart: 7 -> 7, of which waited for: 4 -> 4; matrix products, arithmetic and copies ran while one was open for 1% -> 1% of each run, Pallas kernels for 18% -> 17%
where the time goes in v20:
time: 21 us; the launch traced here: 20.8 us
  starting transfers between devices  11.1 us (53%)
  Pallas kernels  5.32 us (25%)
  waiting for transfers between devices  2.63 us (13%)
  other arithmetic  0.89 us (4%)
  between operations  0.8 us (4%)
    ppermute x3, starting transfers between devices, body(): lax.ppermute(mine, 'sect', [((i + k) % sects, i) for i in range(sects)])  6.12 us
    ppermute x3, starting transfers between devices, body(): lax.ppermute(results[k], 'sect', [(i, (i + k) % sects) for i in range(sec...  4.95 us
    pallas_call x1, Pallas kernels, prefill(): pl.pallas_call(prefill_kernel, in_specs=[pl.BlockSpec(memory_space=pltpu....  2.77 us
    ppermute x3, waiting for transfers between devices, body(): lax.ppermute(results[k], 'sect', [(i, (i + k) % sects) for i in range(sec...  2.1 us
    pallas_call x1, Pallas kernels, pack(): pl.pallas_call(pack_kernel, in_specs=[pl.BlockSpec(memory_space=pltpu.Mem...  0.94 us
    pallas_call x1, Pallas kernels, begin(): pl.pallas_call(begin_kernel, in_specs=[vmem] * 3, out_specs=[vmem] * 5, o...  0.86 us
    pallas_call x1, Pallas kernels, end(): pl.pallas_call(end_kernel, in_specs=[vmem] * 6, out_specs=[vmem] * parts,...  0.75 us
    select_n x1, other arithmetic, body(): out = jnp.where((prompts == (sect - k) % sects)[:, None], result, out)  0.71 us
  transfers between devices with their start and end apart: 7, of which 4 were waited for; matrix products, arithmetic and copies ran while one was open for 1% of the time, Pallas kernels for 17%

profile of v20, /device:TPU:0, one launch (start us, length us, event | category | flops | bytes accessed | tf_op | source)
XLA Modules:
  0.0 20.8 jit_solution(15448188652855112710)
XLA Ops:
  0.0 0.0 copy-start.2
  0.0 0.0 copy-start
  0.0 0.0 copy-start.1
  0.0 0.9 %pack.1 = bf16[4,5120]{1,0:T(4,128)(2,1)S(1)} custom-call(bf16[4,4096]{1,0:T(4,128)(2,1)} %queries_ref.1, bf16[4,512]{1,0:T(4,128)(2,1)} %keys_ref.2, bf16[4,512]{1,0:T(4,128)(2,1)} %values_ref.2), custom_call_target="tpu_custom_call" | custom-call | flops 10000000000 | bytes 33554432 | tf_op jit(solution)/shard_map/pack/pallas_call | solution.py:35
  1.0 3.1 %collective-permute-start.2 = (bf16[4,5120]{1,0:T(4,128)(2,1)S(1)}, bf16[4,5120]{1,0:T(4,128)(2,1)S(1)}, u32[]{:S(2)}, u32[]{:S(2)}) collective-permute-start(bf16[4,5120]{1,0:T(4,128)(2,1)S(1)} %pack.1), channel_id=1, source_target_pairs={{12,0},{0,4},{4,8},{8,12},{13,1},{1,5},{5,9},{9,13},{14,2},{2,6},{... | collective-permute-start | bytes 122888 | tf_op jit(solution)/shard_map/ppermute | solution.py:268
  4.0 2.1 %collective-permute-start.1 = (bf16[4,5120]{1,0:T(4,128)(2,1)S(1)}, bf16[4,5120]{1,0:T(4,128)(2,1)S(1)}, u32[]{:S(2)}, u32[]{:S(2)}) collective-permute-start(bf16[4,5120]{1,0:T(4,128)(2,1)S(1)} %pack.1), channel_id=1, source_target_pairs={{4,0},{8,4},{12,8},{0,12},{5,1},{9,5},{13,9},{1,13},{6,2},{10,6},{... | collective-permute-start | bytes 122888 | tf_op jit(solution)/shard_map/ppermute | solution.py:268
  6.1 0.9 %collective-permute-start = (bf16[4,5120]{1,0:T(4,128)(2,1)S(1)}, bf16[4,5120]{1,0:T(4,128)(2,1)S(1)}, u32[]{:S(2)}, u32[]{:S(2)}) collective-permute-start(bf16[4,5120]{1,0:T(4,128)(2,1)S(1)} %pack.1), channel_id=1, source_target_pairs={{8,0},{12,4},{0,8},{4,12},{9,1},{13,5},{1,9},{5,13},{10,2},{14,6},... | collective-permute-start | bytes 122888 | tf_op jit(solution)/shard_map/ppermute | solution.py:268
  7.7 0.0 copy-done.2
  7.7 0.0 copy-done
  7.7 0.0 copy-done.1
  7.8 0.0 copy-start.3
  7.8 2.8 %prefill.1.near_ref = bf16[1168,128]{1,0:T(8,128)(2,1)S(1)} custom-call(s32[1]{0:T(128)S(6)} %copy.9.lengths_ref, bf16[1,4096,512]{2,1,0:T(8,128)(2,1)S(1)} %copy-done, bf16[1,4096,512]{2,1,0:T(8,128)(2,1)S(1)} %copy-done.1, bf16[4,128,128]{2,1,0:T(8,128)(2,1)S(1)} %copy-done.2), custom_call_target="tpu_custom_call" | custom-call | flops 1073741824 | bytes 8388608 | tf_op jit(solution)/shard_map/prefill/pallas_call | solution.py:136
  10.5 0.1 collective-permute-start.3
  10.7 0.0 collective-permute-done.2
  10.7 0.0 collective-permute-done.1
  10.7 0.3 %collective-permute-done = bf16[4,5120]{1,0:T(4,128)(2,1)S(1)} collective-permute-done((bf16[4,5120]{1,0:T(4,128)(2,1)S(1)}, bf16[4,5120]{1,0:T(4,128)(2,1)S(1)}, u32[]{:S(2)}, u32[]{:S(2)}) %collective-permute-start) | collective-permute-done | bytes 40992 | tf_op jit(solution)/shard_map/ppermute | solution.py:268
  11.0 0.1 pad_maximum_fusion.rows_ref
  11.1 0.9 %begin.1 = (bf16[4,128,128]{2,1,0:T(8,128)(2,1)S(1)}, bf16[4,128,128]{2,1,0:T(8,128)(2,1)S(1)}, f32[4,128,128]{2,1,0:T(8,128)S(1)}, f32[4,128,128]{2,1,0:T(8,128)S(1)}, f32[4,128,128]{2,1,0:T(8,128)S(1)}) custom-call(bf16[16,5120]{1,0:T(8,128)(2,1)S(1)} %pad_maximum_fusion.rows_ref, bf16[4,128,128]{2,1,0:T(8,128)(2,1)S(1)} %copy-done.2, ...), custom_call_target="tpu_custom_call" | custom-call | flops 62914560 | bytes 327680 | tf_op jit(solution)/shard_map/begin/pallas_call | solution.py:232
  12.0 0.2 collective-permute-done.3.far_ref
  12.2 0.7 %end.1 = (bf16[4,4096]{1,0:T(4,128)(2,1)S(1)}, bf16[4,4096]{1,0:T(4,128)(2,1)S(1)}, bf16[4,4096]{1,0:T(4,128)(2,1)S(1)}, bf16[4,4096]{1,0:T(4,128)(2,1)S(1)}) custom-call(bf16[4,128,128]{2,1,0:T(8,128)(2,1)S(1)} %get-tuple-element.14.query_ref, bf16[4,128,128]{2,1,0:T(8,128)(2,1)S(1)} %get-tuple-element.15.phi_ref, ...), custom_call_target="tpu_custom_call" | custom-call | flops 33554432 | bytes 262144 | tf_op jit(solution)/shard_map/end/pallas_call | solution.py:247
  13.0 1.6 %collective-permute-start.4 = (bf16[4,4096]{1,0:T(4,128)(2,1)S(1)}, bf16[4,4096]{1,0:T(4,128)(2,1)S(1)}, u32[]{:S(2)}, u32[]{:S(2)}) collective-permute-start(bf16[4,4096]{1,0:T(4,128)(2,1)S(1)} %get-tuple-element.19), channel_id=1, source_target_pairs={{0,4},{4,8},{8,12},{12,0},{1,5},{5,9},{9,13},{13,1},{2,6},{6,10},{... | collective-permute-start | bytes 98312 | tf_op jit(solution)/shard_map/ppermute | solution.py:280
  14.6 1.1 %collective-permute-start.5 = (bf16[4,4096]{1,0:T(4,128)(2,1)S(1)}, bf16[4,4096]{1,0:T(4,128)(2,1)S(1)}, u32[]{:S(2)}, u32[]{:S(2)}) collective-permute-start(bf16[4,4096]{1,0:T(4,128)(2,1)S(1)} %get-tuple-element.20), channel_id=1, source_target_pairs={{0,8},{4,12},{8,0},{12,4},{1,9},{5,13},{9,1},{13,5},{2,10},{6,14},... | collective-permute-start | bytes 98312 | tf_op jit(solution)/shard_map/ppermute | solution.py:280
  15.7 2.2 %collective-permute-start.6 = (bf16[4,4096]{1,0:T(4,128)(2,1)S(1)}, bf16[4,4096]{1,0:T(4,128)(2,1)S(1)}, u32[]{:S(2)}, u32[]{:S(2)}) collective-permute-start(bf16[4,4096]{1,0:T(4,128)(2,1)S(1)} %get-tuple-element.21), channel_id=1, source_target_pairs={{0,12},{4,0},{8,4},{12,8},{1,13},{5,1},{9,5},{13,9},{2,14},{6,2},{... | collective-permute-start | bytes 98312 | tf_op jit(solution)/shard_map/ppermute | solution.py:280
  17.9 0.0 copy-done.3
  17.9 0.1 broadcast_compare_fusion.2
  18.0 1.0 %collective-permute-done.4 = bf16[4,4096]{1,0:T(4,128)(2,1)S(1)} collective-permute-done((bf16[4,4096]{1,0:T(4,128)(2,1)S(1)}, bf16[4,4096]{1,0:T(4,128)(2,1)S(1)}, u32[]{:S(2)}, u32[]{:S(2)}) %collective-permute-start.4) | collective-permute-done | bytes 32800 | tf_op jit(solution)/shard_map/ppermute | solution.py:280
  19.0 1.1 %collective-permute-done.5 = bf16[4,4096]{1,0:T(4,128)(2,1)S(1)} collective-permute-done((bf16[4,4096]{1,0:T(4,128)(2,1)S(1)}, bf16[4,4096]{1,0:T(4,128)(2,1)S(1)}, u32[]{:S(2)}, u32[]{:S(2)}) %collective-permute-start.5) | collective-permute-done | bytes 32800 | tf_op jit(solution)/shard_map/ppermute | solution.py:280
  20.1 0.0 collective-permute-done.6
  20.1 0.7 %select_select_fusion = bf16[4,4096]{1,0:T(4,128)(2,1)} fusion(bf16[4,4096]{1,0:T(4,128)(2,1)S(1)} %collective-permute-done.4, bf16[4,4096]{1,0:T(4,128)(2,1)S(1)} %collective-permute-done.5, bf16[4,4096]{1,0:T(4,128)(2,1)S(1)} %collective-permute-done.6, bf16[4,4096]{1,0:T(4,128)(2,1)S(1)} %get-tuple-element.22, pred[4]{0:T(512)(128)(4,1)S(1)} %get-tuple-element.25, ...), kind=kLoop, calls=%fused_computation.1 | loop fusion | flops 49152 | bytes 163852 | tf_op jit(solution)/shard_map/jit(_where)/select_n | solution.py:281
Async XLA Ops:
  0.0 7.7 %copy-start.2 = (bf16[4,128,128]{2,1,0:T(8,128)(2,1)S(1)}, bf16[4,128,128]{2,1,0:T(8,128)(2,1)}, u32[]{:S(2)}) copy-start(bf16[4,128,128]{2,1,0:T(8,128)(2,1)} %weight_ref.3) | copy-start | bytes 393220
  0.0 7.7 %copy-start = (bf16[1,4096,512]{2,1,0:T(8,128)(2,1)S(1)}, bf16[1,4096,512]{2,1,0:T(8,128)(2,1)}, u32[]{:S(2)}) copy-start(bf16[1,4096,512]{2,1,0:T(8,128)(2,1)} %keys_ref.3) | copy-start | bytes 12582916
  0.0 7.7 %copy-start.1 = (bf16[1,4096,512]{2,1,0:T(8,128)(2,1)S(1)}, bf16[1,4096,512]{2,1,0:T(8,128)(2,1)}, u32[]{:S(2)}) copy-start(bf16[1,4096,512]{2,1,0:T(8,128)(2,1)} %values_ref.3) | copy-start | bytes 12582916
  1.0 9.7 %collective-permute-start.2 = (bf16[4,5120]{1,0:T(4,128)(2,1)S(1)}, bf16[4,5120]{1,0:T(4,128)(2,1)S(1)}, u32[]{:S(2)}, u32[]{:S(2)}) collective-permute-start(bf16[4,5120]{1,0:T(4,128)(2,1)S(1)} %pack.1), channel_id=1, source_target_pairs={{12,0},{0,4},{4,8},{8,12},{13,1},{1,5},{5,9},{9,13},{14,2},{2,6},{... | collective-permute-start | bytes 122888 | tf_op jit(solution)/shard_map/ppermute | solution.py:268
  4.0 6.7 %collective-permute-start.1 = (bf16[4,5120]{1,0:T(4,128)(2,1)S(1)}, bf16[4,5120]{1,0:T(4,128)(2,1)S(1)}, u32[]{:S(2)}, u32[]{:S(2)}) collective-permute-start(bf16[4,5120]{1,0:T(4,128)(2,1)S(1)} %pack.1), channel_id=1, source_target_pairs={{4,0},{8,4},{12,8},{0,12},{5,1},{9,5},{13,9},{1,13},{6,2},{10,6},{... | collective-permute-start | bytes 122888 | tf_op jit(solution)/shard_map/ppermute | solution.py:268
  6.1 4.9 %collective-permute-start = (bf16[4,5120]{1,0:T(4,128)(2,1)S(1)}, bf16[4,5120]{1,0:T(4,128)(2,1)S(1)}, u32[]{:S(2)}, u32[]{:S(2)}) collective-permute-start(bf16[4,5120]{1,0:T(4,128)(2,1)S(1)} %pack.1), channel_id=1, source_target_pairs={{8,0},{12,4},{0,8},{4,12},{9,1},{13,5},{1,9},{5,13},{10,2},{14,6},... | collective-permute-start | bytes 122888 | tf_op jit(solution)/shard_map/ppermute | solution.py:268
  7.8 10.2 %copy-start.3 = (s32[32]{0:T(128)S(1)}, s32[32]{0:T(128)}, u32[]{:S(2)}) copy-start(s32[32]{0:T(128)} %param.15) | copy-start | bytes 388
  10.5 1.7 %collective-permute-start.3 = (bf16[1168,128]{1,0:T(8,128)(2,1)S(1)}, bf16[1168,128]{1,0:T(8,128)(2,1)S(1)}, u32[]{:S(2)}, u32[]{:S(2)}) collective-permute-start(bf16[1168,128]{1,0:T(8,128)(2,1)S(1)} %prefill.1.near_ref), channel_id=1, source_target_pairs={{0,1},{1,0},{2,3},{3,2},{4,5},{5,4},{6,7},{7,6},{8,9},{9,8},{10,11... | collective-permute-start | bytes 897032 | tf_op jit(solution)/shard_map/ppermute | solution.py:270
  13.0 6.1 %collective-permute-start.4 = (bf16[4,4096]{1,0:T(4,128)(2,1)S(1)}, bf16[4,4096]{1,0:T(4,128)(2,1)S(1)}, u32[]{:S(2)}, u32[]{:S(2)}) collective-permute-start(bf16[4,4096]{1,0:T(4,128)(2,1)S(1)} %get-tuple-element.19), channel_id=1, source_target_pairs={{0,4},{4,8},{8,12},{12,0},{1,5},{5,9},{9,13},{13,1},{2,6},{6,10},{... | collective-permute-start | bytes 98312 | tf_op jit(solution)/shard_map/ppermute | solution.py:280
  14.6 5.5 %collective-permute-start.5 = (bf16[4,4096]{1,0:T(4,128)(2,1)S(1)}, bf16[4,4096]{1,0:T(4,128)(2,1)S(1)}, u32[]{:S(2)}, u32[]{:S(2)}) collective-permute-start(bf16[4,4096]{1,0:T(4,128)(2,1)S(1)} %get-tuple-element.20), channel_id=1, source_target_pairs={{0,8},{4,12},{8,0},{12,4},{1,9},{5,13},{9,1},{13,5},{2,10},{6,14},... | collective-permute-start | bytes 98312 | tf_op jit(solution)/shard_map/ppermute | solution.py:280
  15.7 4.4 %collective-permute-start.6 = (bf16[4,4096]{1,0:T(4,128)(2,1)S(1)}, bf16[4,4096]{1,0:T(4,128)(2,1)S(1)}, u32[]{:S(2)}, u32[]{:S(2)}) collective-permute-start(bf16[4,4096]{1,0:T(4,128)(2,1)S(1)} %get-tuple-element.21), channel_id=1, source_target_pairs={{0,12},{4,0},{8,4},{12,8},{1,13},{5,1},{9,5},{13,9},{2,14},{6,2},{... | collective-permute-start | bytes 98312 | tf_op jit(solution)/shard_map/ppermute | solution.py:280

commit v21 on v20

--- a/solution.py
+++ b/solution.py
@@ -12,6 +12,18 @@
 EPS = 1e-06
 BLOCK = 256
 NT = (((1,), (1,)), ((), ()))
+
+
+def paired(sects):
+    return sects & (sects - 1) == 0
+
+
+def shifted(sect, k, sects):
+    return (sect + k) % sects
+
+
+def partner(sect, k, sects):
+    return sect ^ k if paired(sects) else shifted(sect, k, sects)
 
 
 def feature(proj):
@@ -262,23 +274,29 @@
 ):
     sub = lax.axis_index("sub")
     sect = lax.axis_index("sect")
-    shifts = list(range(1, sects))
-    shifts[:2] = shifts[:2][::-1]
+    steps = list(range(1, sects))
+    steps[:2] = steps[:2][::-1]
     mine = pack(queries, new_keys, new_values)
-    blocks = [mine] + [lax.ppermute(mine, "sect", [((i + k) % sects, i) for i in range(sects)]) for k in shifts]
+    ask = shifted if sects == 4 else partner
+    asked = {k: lax.ppermute(mine, "sect", [(ask(i, k, sects), i) for i in range(sects)]) for k in steps}
+    if sects == 4:
+        odd = (sect & 1) == 1
+        asked[1], asked[3] = jnp.where(odd, asked[3], asked[1]), jnp.where(odd, asked[1], asked[3])
+    blocks = [mine] + [asked[k] for k in steps]
     near = prefill(prompt_keys, prompt_values, feature_weight, lengths)
     far = lax.ppermute(near, "sub", [(0, 1), (1, 0)])
     started = begin(jnp.concatenate(blocks, axis=0), feature_weight, near)
     results = end(started, far, *queries.shape, sects)
-    results = dict(zip([0] + shifts, results))
+    results = dict(zip([0] + steps, results))
 
     count = queries.shape[0]
     first_row = (sect * lax.axis_size("sub") + sub) * count
     prompts = lax.dynamic_slice_in_dim(row_prompt, first_row, count, 0)
     out = results[0]
-    for k in range(sects - 1, 0, -1):
-        result = lax.ppermute(results[k], "sect", [(i, (i + k) % sects) for i in range(sects)])
-        out = jnp.where((prompts == (sect - k) % sects)[:, None], result, out)
+    for k in range(1, sects):
+        result = lax.ppermute(results[k], "sect", [(i, partner(i, k, sects)) for i in range(sects)])
+        source = partner(sect, k if paired(sects) else sects - k, sects)
+        out = jnp.where((prompts == source)[:, None], result, out)
     return out
 
 

time: 21 us -> 21.2 us (level)
  waiting for transfers between devices: 2.63 us -> 3.37 us
  starting transfers between devices: 11.1 us -> 10.6 us
    ppermute x6, waiting for transfers between devices: 2.43 us -> 3.17 us  [the longest x3 2.84 us: body(): lax.ppermute(results[k], 'sect', [(i, partner(i, k, sects)) for i in rang...]
    ppermute x6, starting transfers between devices: 11.1 us -> 10.6 us  [the longest x3 6.12 us: body(): lax.ppermute(mine, 'sect', [(ask(i, k, sects), i) for i in range(sects)])]
    select_n x1 -> x2, other arithmetic: 0.71 us -> 0.75 us  [the longest x1 0.71 us: body(): out = jnp.where((prompts == source)[:, None], result, out)]
  transfers between devices with their start and end apart: 7 -> 7, of which waited for: 4 -> 5; matrix products, arithmetic and copies ran while one was open for 1% -> 1% of each run, Pallas kernels for 17% -> 17%
where the time goes in v21:
time: 21.2 us; the launch traced here: 21 us
  starting transfers between devices  10.6 us (50%)
  Pallas kernels  5.32 us (25%)
  waiting for transfers between devices  3.37 us (16%)
  other arithmetic  0.93 us (4%)
  between operations  0.76 us (4%)
    ppermute x3, starting transfers between devices, body(): lax.ppermute(mine, 'sect', [(ask(i, k, sects), i) for i in range(sects)])  6.12 us
    ppermute x3, starting transfers between devices, body(): lax.ppermute(results[k], 'sect', [(i, partner(i, k, sects)) for i in rang...  4.45 us
    ppermute x3, waiting for transfers between devices, body(): lax.ppermute(results[k], 'sect', [(i, partner(i, k, sects)) for i in rang...  2.84 us
    pallas_call x1, Pallas kernels, prefill(): pl.pallas_call(prefill_kernel, in_specs=[pl.BlockSpec(memory_space=pltpu....  2.77 us
    pallas_call x1, Pallas kernels, pack(): pl.pallas_call(pack_kernel, in_specs=[pl.BlockSpec(memory_space=pltpu.Mem...  0.94 us
    pallas_call x1, Pallas kernels, begin(): pl.pallas_call(begin_kernel, in_specs=[vmem] * 3, out_specs=[vmem] * 5, o...  0.86 us
    pallas_call x1, Pallas kernels, end(): pl.pallas_call(end_kernel, in_specs=[vmem] * 6, out_specs=[vmem] * parts,...  0.75 us
    select_n x1, other arithmetic, body(): out = jnp.where((prompts == source)[:, None], result, out)  0.71 us
  transfers between devices with their start and end apart: 7, of which 5 were waited for; matrix products, arithmetic and copies ran while one was open for 1% of the time, Pallas kernels for 17%

profile of v21, /device:TPU:0, one launch (start us, length us, event | category | flops | bytes accessed | tf_op | source)
XLA Modules:
  0.0 21.0 jit_solution(14628915595814995431)
XLA Ops:
  0.0 0.0 copy-start.2
  0.0 0.0 copy-start
  0.0 0.0 copy-start.1
  0.0 0.9 %pack.1 = bf16[4,5120]{1,0:T(4,128)(2,1)S(1)} custom-call(bf16[4,4096]{1,0:T(4,128)(2,1)} %queries_ref.1, bf16[4,512]{1,0:T(4,128)(2,1)} %keys_ref.2, bf16[4,512]{1,0:T(4,128)(2,1)} %values_ref.2), custom_call_target="tpu_custom_call" | custom-call | flops 10000000000 | bytes 33554432 | tf_op jit(solution)/shard_map/pack/pallas_call | solution.py:47
  1.0 3.1 %collective-permute-start.1 = (bf16[4,5120]{1,0:T(4,128)(2,1)S(1)}, bf16[4,5120]{1,0:T(4,128)(2,1)S(1)}, u32[]{:S(2)}, u32[]{:S(2)}) collective-permute-start(bf16[4,5120]{1,0:T(4,128)(2,1)S(1)} %pack.1), channel_id=1, source_target_pairs={{12,0},{0,4},{4,8},{8,12},{13,1},{1,5},{5,9},{9,13},{14,2},{2,6},{... | collective-permute-start | bytes 122888 | tf_op jit(solution)/shard_map/ppermute | solution.py:281
  4.0 2.1 %collective-permute-start.2 = (bf16[4,5120]{1,0:T(4,128)(2,1)S(1)}, bf16[4,5120]{1,0:T(4,128)(2,1)S(1)}, u32[]{:S(2)}, u32[]{:S(2)}) collective-permute-start(bf16[4,5120]{1,0:T(4,128)(2,1)S(1)} %pack.1), channel_id=1, source_target_pairs={{4,0},{8,4},{12,8},{0,12},{5,1},{9,5},{13,9},{1,13},{6,2},{10,6},{... | collective-permute-start | bytes 122888 | tf_op jit(solution)/shard_map/ppermute | solution.py:281
  6.1 0.9 %collective-permute-start = (bf16[4,5120]{1,0:T(4,128)(2,1)S(1)}, bf16[4,5120]{1,0:T(4,128)(2,1)S(1)}, u32[]{:S(2)}, u32[]{:S(2)}) collective-permute-start(bf16[4,5120]{1,0:T(4,128)(2,1)S(1)} %pack.1), channel_id=1, source_target_pairs={{8,0},{12,4},{0,8},{4,12},{9,1},{13,5},{1,9},{5,13},{10,2},{14,6},... | collective-permute-start | bytes 122888 | tf_op jit(solution)/shard_map/ppermute | solution.py:281
  7.7 0.0 copy-done.2
  7.7 0.0 copy-done
  7.7 0.0 copy-done.1
  7.8 0.0 copy-start.3
  7.8 2.8 %prefill.1.near_ref = bf16[1168,128]{1,0:T(8,128)(2,1)S(1)} custom-call(s32[1]{0:T(128)S(6)} %copy.9.lengths_ref, bf16[1,4096,512]{2,1,0:T(8,128)(2,1)S(1)} %copy-done, bf16[1,4096,512]{2,1,0:T(8,128)(2,1)S(1)} %copy-done.1, bf16[4,128,128]{2,1,0:T(8,128)(2,1)S(1)} %copy-done.2), custom_call_target="tpu_custom_call" | custom-call | flops 1073741824 | bytes 8388608 | tf_op jit(solution)/shard_map/prefill/pallas_call | solution.py:148
  10.5 0.1 collective-permute-start.3
  10.6 0.0 collective-permute-done.1
  10.6 0.0 collective-permute-done.2
  10.7 0.3 %collective-permute-done = bf16[4,5120]{1,0:T(4,128)(2,1)S(1)} collective-permute-done((bf16[4,5120]{1,0:T(4,128)(2,1)S(1)}, bf16[4,5120]{1,0:T(4,128)(2,1)S(1)}, u32[]{:S(2)}, u32[]{:S(2)}) %collective-permute-start) | collective-permute-done | bytes 40992 | tf_op jit(solution)/shard_map/ppermute | solution.py:281
  11.0 0.1 pad_maximum_fusion.rows_ref
  11.1 0.9 %begin.1 = (bf16[4,128,128]{2,1,0:T(8,128)(2,1)S(1)}, bf16[4,128,128]{2,1,0:T(8,128)(2,1)S(1)}, f32[4,128,128]{2,1,0:T(8,128)S(1)}, f32[4,128,128]{2,1,0:T(8,128)S(1)}, f32[4,128,128]{2,1,0:T(8,128)S(1)}) custom-call(bf16[16,5120]{1,0:T(8,128)(2,1)S(1)} %pad_maximum_fusion.rows_ref, bf16[4,128,128]{2,1,0:T(8,128)(2,1)S(1)} %copy-done.2, ...), custom_call_target="tpu_custom_call" | custom-call | flops 62914560 | bytes 327680 | tf_op jit(solution)/shard_map/begin/pallas_call | solution.py:244
  12.0 0.2 collective-permute-done.3.far_ref
  12.2 0.7 %end.1 = (bf16[4,4096]{1,0:T(4,128)(2,1)S(1)}, bf16[4,4096]{1,0:T(4,128)(2,1)S(1)}, bf16[4,4096]{1,0:T(4,128)(2,1)S(1)}, bf16[4,4096]{1,0:T(4,128)(2,1)S(1)}) custom-call(bf16[4,128,128]{2,1,0:T(8,128)(2,1)S(1)} %get-tuple-element.14.query_ref, bf16[4,128,128]{2,1,0:T(8,128)(2,1)S(1)} %get-tuple-element.15.phi_ref, ...), custom_call_target="tpu_custom_call" | custom-call | flops 33554432 | bytes 262144 | tf_op jit(solution)/shard_map/end/pallas_call | solution.py:259
  13.0 2.2 %collective-permute-start.4 = (bf16[4,4096]{1,0:T(4,128)(2,1)S(1)}, bf16[4,4096]{1,0:T(4,128)(2,1)S(1)}, u32[]{:S(2)}, u32[]{:S(2)}) collective-permute-start(bf16[4,4096]{1,0:T(4,128)(2,1)S(1)} %get-tuple-element.19), channel_id=1, source_target_pairs={{0,12},{4,8},{8,4},{12,0},{1,13},{5,9},{9,5},{13,1},{2,14},{6,10},... | collective-permute-start | bytes 98312 | tf_op jit(solution)/shard_map/ppermute | solution.py:297
  15.1 1.0 %collective-permute-start.5 = (bf16[4,4096]{1,0:T(4,128)(2,1)S(1)}, bf16[4,4096]{1,0:T(4,128)(2,1)S(1)}, u32[]{:S(2)}, u32[]{:S(2)}) collective-permute-start(bf16[4,4096]{1,0:T(4,128)(2,1)S(1)} %get-tuple-element.20), channel_id=1, source_target_pairs={{0,8},{4,12},{8,0},{12,4},{1,9},{5,13},{9,1},{13,5},{2,10},{6,14},... | collective-permute-start | bytes 98312 | tf_op jit(solution)/shard_map/ppermute | solution.py:297
  16.1 1.3 %collective-permute-start.6 = (bf16[4,4096]{1,0:T(4,128)(2,1)S(1)}, bf16[4,4096]{1,0:T(4,128)(2,1)S(1)}, u32[]{:S(2)}, u32[]{:S(2)}) collective-permute-start(bf16[4,4096]{1,0:T(4,128)(2,1)S(1)} %get-tuple-element.21), channel_id=1, source_target_pairs={{0,4},{4,0},{8,12},{12,8},{1,5},{5,1},{9,13},{13,9},{2,6},{6,2},{1... | collective-permute-start | bytes 98312 | tf_op jit(solution)/shard_map/ppermute | solution.py:297
  17.4 0.0 copy-done.3
  17.4 0.1 broadcast_compare_fusion.2
  17.5 1.6 %collective-permute-done.4 = bf16[4,4096]{1,0:T(4,128)(2,1)S(1)} collective-permute-done((bf16[4,4096]{1,0:T(4,128)(2,1)S(1)}, bf16[4,4096]{1,0:T(4,128)(2,1)S(1)}, u32[]{:S(2)}, u32[]{:S(2)}) %collective-permute-start.4) | collective-permute-done | bytes 32800 | tf_op jit(solution)/shard_map/ppermute | solution.py:297
  19.1 1.2 %collective-permute-done.5 = bf16[4,4096]{1,0:T(4,128)(2,1)S(1)} collective-permute-done((bf16[4,4096]{1,0:T(4,128)(2,1)S(1)}, bf16[4,4096]{1,0:T(4,128)(2,1)S(1)}, u32[]{:S(2)}, u32[]{:S(2)}) %collective-permute-start.5) | collective-permute-done | bytes 32800 | tf_op jit(solution)/shard_map/ppermute | solution.py:297
  20.3 0.1 collective-permute-done.6
  20.3 0.7 %select_select_fusion = bf16[4,4096]{1,0:T(4,128)(2,1)} fusion(bf16[4,4096]{1,0:T(4,128)(2,1)S(1)} %collective-permute-done.4, bf16[4,4096]{1,0:T(4,128)(2,1)S(1)} %collective-permute-done.5, bf16[4,4096]{1,0:T(4,128)(2,1)S(1)} %collective-permute-done.6, bf16[4,4096]{1,0:T(4,128)(2,1)S(1)} %get-tuple-element.22, pred[4]{0:T(512)(128)(4,1)S(1)} %get-tuple-element.27, ...), kind=kLoop, calls=%fused_computation.3 | loop fusion | flops 49152 | bytes 163852 | tf_op jit(solution)/shard_map/jit(_where)/select_n | solution.py:299
  (1 shorter events, 0.0 us)
Async XLA Ops:
  0.0 7.7 %copy-start.2 = (bf16[4,128,128]{2,1,0:T(8,128)(2,1)S(1)}, bf16[4,128,128]{2,1,0:T(8,128)(2,1)}, u32[]{:S(2)}) copy-start(bf16[4,128,128]{2,1,0:T(8,128)(2,1)} %weight_ref.3) | copy-start | bytes 393220
  0.0 7.7 %copy-start = (bf16[1,4096,512]{2,1,0:T(8,128)(2,1)S(1)}, bf16[1,4096,512]{2,1,0:T(8,128)(2,1)}, u32[]{:S(2)}) copy-start(bf16[1,4096,512]{2,1,0:T(8,128)(2,1)} %keys_ref.3) | copy-start | bytes 12582916
  0.0 7.7 %copy-start.1 = (bf16[1,4096,512]{2,1,0:T(8,128)(2,1)S(1)}, bf16[1,4096,512]{2,1,0:T(8,128)(2,1)}, u32[]{:S(2)}) copy-start(bf16[1,4096,512]{2,1,0:T(8,128)(2,1)} %values_ref.3) | copy-start | bytes 12582916
  1.0 9.7 %collective-permute-start.1 = (bf16[4,5120]{1,0:T(4,128)(2,1)S(1)}, bf16[4,5120]{1,0:T(4,128)(2,1)S(1)}, u32[]{:S(2)}, u32[]{:S(2)}) collective-permute-start(bf16[4,5120]{1,0:T(4,128)(2,1)S(1)} %pack.1), channel_id=1, source_target_pairs={{12,0},{0,4},{4,8},{8,12},{13,1},{1,5},{5,9},{9,13},{14,2},{2,6},{... | collective-permute-start | bytes 122888 | tf_op jit(solution)/shard_map/ppermute | solution.py:281
  4.0 6.6 %collective-permute-start.2 = (bf16[4,5120]{1,0:T(4,128)(2,1)S(1)}, bf16[4,5120]{1,0:T(4,128)(2,1)S(1)}, u32[]{:S(2)}, u32[]{:S(2)}) collective-permute-start(bf16[4,5120]{1,0:T(4,128)(2,1)S(1)} %pack.1), channel_id=1, source_target_pairs={{4,0},{8,4},{12,8},{0,12},{5,1},{9,5},{13,9},{1,13},{6,2},{10,6},{... | collective-permute-start | bytes 122888 | tf_op jit(solution)/shard_map/ppermute | solution.py:281
  6.1 4.9 %collective-permute-start = (bf16[4,5120]{1,0:T(4,128)(2,1)S(1)}, bf16[4,5120]{1,0:T(4,128)(2,1)S(1)}, u32[]{:S(2)}, u32[]{:S(2)}) collective-permute-start(bf16[4,5120]{1,0:T(4,128)(2,1)S(1)} %pack.1), channel_id=1, source_target_pairs={{8,0},{12,4},{0,8},{4,12},{9,1},{13,5},{1,9},{5,13},{10,2},{14,6},... | collective-permute-start | bytes 122888 | tf_op jit(solution)/shard_map/ppermute | solution.py:281
  7.8 9.7 %copy-start.3 = (s32[32]{0:T(128)S(1)}, s32[32]{0:T(128)}, u32[]{:S(2)}) copy-start(s32[32]{0:T(128)} %param.15) | copy-start | bytes 388
  10.5 1.7 %collective-permute-start.3 = (bf16[1168,128]{1,0:T(8,128)(2,1)S(1)}, bf16[1168,128]{1,0:T(8,128)(2,1)S(1)}, u32[]{:S(2)}, u32[]{:S(2)}) collective-permute-start(bf16[1168,128]{1,0:T(8,128)(2,1)S(1)} %prefill.1.near_ref), channel_id=1, source_target_pairs={{0,1},{1,0},{2,3},{3,2},{4,5},{5,4},{6,7},{7,6},{8,9},{9,8},{10,11... | collective-permute-start | bytes 897032 | tf_op jit(solution)/shard_map/ppermute | solution.py:287
  13.0 6.1 %collective-permute-start.4 = (bf16[4,4096]{1,0:T(4,128)(2,1)S(1)}, bf16[4,4096]{1,0:T(4,128)(2,1)S(1)}, u32[]{:S(2)}, u32[]{:S(2)}) collective-permute-start(bf16[4,4096]{1,0:T(4,128)(2,1)S(1)} %get-tuple-element.19), channel_id=1, source_target_pairs={{0,12},{4,8},{8,4},{12,0},{1,13},{5,9},{9,5},{13,1},{2,14},{6,10},... | collective-permute-start | bytes 98312 | tf_op jit(solution)/shard_map/ppermute | solution.py:297
  15.1 5.2 %collective-permute-start.5 = (bf16[4,4096]{1,0:T(4,128)(2,1)S(1)}, bf16[4,4096]{1,0:T(4,128)(2,1)S(1)}, u32[]{:S(2)}, u32[]{:S(2)}) collective-permute-start(bf16[4,4096]{1,0:T(4,128)(2,1)S(1)} %get-tuple-element.20), channel_id=1, source_target_pairs={{0,8},{4,12},{8,0},{12,4},{1,9},{5,13},{9,1},{13,5},{2,10},{6,14},... | collective-permute-start | bytes 98312 | tf_op jit(solution)/shard_map/ppermute | solution.py:297
  16.1 4.3 %collective-permute-start.6 = (bf16[4,4096]{1,0:T(4,128)(2,1)S(1)}, bf16[4,4096]{1,0:T(4,128)(2,1)S(1)}, u32[]{:S(2)}, u32[]{:S(2)}) collective-permute-start(bf16[4,4096]{1,0:T(4,128)(2,1)S(1)} %get-tuple-element.21), channel_id=1, source_target_pairs={{0,4},{4,0},{8,12},{12,8},{1,5},{5,1},{9,13},{13,9},{2,6},{6,2},{1... | collective-permute-start | bytes 98312 | tf_op jit(solution)/shard_map/ppermute | solution.py:297

commit v22 on v21

--- a/solution.py
+++ b/solution.py
@@ -220,19 +220,16 @@
         scale_ref[g] = jnp.broadcast_to(scale, num.shape)
 
 
-def end_kernel(query_ref, phi_ref, num_ref, den_ref, scale_ref, far_ref, *out_refs):
-    heads, asked, head_size = query_ref.shape
-    each, width = out_refs[0].shape
-    group = width // (heads * head_size)
-    count = asked // group
+def end_kernel(each, query_ref, phi_ref, num_ref, den_ref, scale_ref, far_ref, *out_refs):
+    heads, asked, _ = query_ref.shape
+    block = out_refs[0].shape[0] // heads
+    count = each * len(out_refs)
     for g in range(heads):
         num, den = share(query_ref[g], phi_ref[g], scale_ref[g][:, :1], far_ref, g, heads)
-        result = ((num_ref[g] + num) / (den_ref[g] + den)).astype(jnp.bfloat16)
-        for h in range(group):
-            at = (g * group + h) * head_size
-            for k, out_ref in enumerate(out_refs):
-                start = h * count + k * each
-                out_ref[:, at : at + head_size] = result[start : start + each]
+        result = (num_ref[g] + num) / (den_ref[g] + den)
+        for k, out_ref in enumerate(out_refs):
+            rows = [result[h * count + k * each : h * count + (k + 1) * each] for h in range(asked // count)]
+            out_ref[g * block : (g + 1) * block, :] = jnp.concatenate(rows, axis=0).astype(jnp.bfloat16)
 
 
 def begin(rows, weight, near):
@@ -255,12 +252,13 @@
 
 
 def end(started, far, count, width, parts):
+    head_size = started[0].shape[2]
     vmem = pl.BlockSpec(memory_space=pltpu.VMEM)
     return pl.pallas_call(
-        end_kernel,
+        functools.partial(end_kernel, count),
         in_specs=[vmem] * 6,
         out_specs=[vmem] * parts,
-        out_shape=[jax.ShapeDtypeStruct((count, width), jnp.bfloat16)] * parts,
+        out_shape=[jax.ShapeDtypeStruct((count * width // head_size, head_size), jnp.bfloat16)] * parts,
         compiler_params=pltpu.CompilerParams(vmem_limit_bytes=32 * 1024 * 1024),
         cost_estimate=pl.CostEstimate(
             flops=4 * started[0].size * 128, bytes_accessed=4 * started[0].size, transcendentals=started[0].size
@@ -269,10 +267,41 @@
     )(*started, far)
 
 
+def finish_kernel(prompts_ref, *refs):
+    block_refs, out_ref = refs[:-1], refs[-1]
+    each, width = out_ref.shape
+    rows, head_size = block_refs[0].shape
+    sects = len(block_refs)
+    sect = lax.axis_index("sect")
+    first = (sect * lax.axis_size("sub") + lax.axis_index("sub")) * each
+    shape = (rows, prompts_ref.shape[1])
+    row = first + lax.rem(lax.broadcasted_iota(jnp.int32, shape, 0), each)
+    lane = lax.broadcasted_iota(jnp.int32, shape, 1)
+    prompt = jnp.sum(jnp.where(lane == row, prompts_ref[...], 0), axis=1, keepdims=True)
+    chosen = block_refs[0][...].astype(jnp.float32)
+    for k, ref in zip(range(sects - 1, 0, -1), block_refs[1:]):
+        source = partner(sect, k if paired(sects) else sects - k, sects)
+        chosen = jnp.where(prompt == source, ref[...].astype(jnp.float32), chosen)
+    for head in range(width // head_size):
+        part = chosen[head * each : (head + 1) * each].astype(jnp.bfloat16)
+        out_ref[:, head * head_size : (head + 1) * head_size] = part
+
+
+def finish(row_prompt, blocks, shape):
+    vmem = pl.BlockSpec(memory_space=pltpu.VMEM)
+    return pl.pallas_call(
+        finish_kernel,
+        in_specs=[vmem] * (1 + len(blocks)),
+        out_specs=vmem,
+        out_shape=jax.ShapeDtypeStruct(shape, jnp.bfloat16),
+        compiler_params=pltpu.CompilerParams(vmem_limit_bytes=8 * 1024 * 1024),
+        name="finish",
+    )(row_prompt.reshape(1, -1), *blocks)
+
+
 def body(
     sects, prompt_keys, prompt_values, lengths, feature_weight, queries, new_keys, new_values, row_prompt
 ):
-    sub = lax.axis_index("sub")
     sect = lax.axis_index("sect")
     steps = list(range(1, sects))
     steps[:2] = steps[:2][::-1]
@@ -289,15 +318,11 @@
     results = end(started, far, *queries.shape, sects)
     results = dict(zip([0] + steps, results))
 
-    count = queries.shape[0]
-    first_row = (sect * lax.axis_size("sub") + sub) * count
-    prompts = lax.dynamic_slice_in_dim(row_prompt, first_row, count, 0)
-    out = results[0]
-    for k in range(1, sects):
-        result = lax.ppermute(results[k], "sect", [(i, partner(i, k, sects)) for i in range(sects)])
-        source = partner(sect, k if paired(sects) else sects - k, sects)
-        out = jnp.where((prompts == source)[:, None], result, out)
-    return out
+    back = [
+        lax.ppermute(results[k], "sect", [(i, partner(i, k, sects)) for i in range(sects)])
+        for k in range(sects - 1, 0, -1)
+    ]
+    return finish(row_prompt, [results[0]] + back, queries.shape)
 
 
 def solution(mesh):

time: 21.2 us -> 21.3 us (level)
  other arithmetic: 0.93 us -> 0.14 us
  Pallas kernels: 5.32 us -> 6.07 us
    pallas_call x1 -> x2, Pallas kernels: 0.75 us -> 1.5 us  [the longest x1 0.75 us: finish(): pl.pallas_call(finish_kernel, in_specs=[vmem] * (1 + len(blocks)), out_sp...]
    select_n x1 -> x0, other arithmetic: 0.71 us -> none  [body(): out = jnp.where((prompts == source)[:, None], result, out)]
where the time goes in v22:
time: 21.3 us; the launch traced here: 21.1 us
  starting transfers between devices  10.6 us (50%)
  Pallas kernels  6.07 us (28%)
  waiting for transfers between devices  3.46 us (16%)
  between operations  0.76 us (4%)
    ppermute x3, starting transfers between devices, body(): lax.ppermute(mine, 'sect', [(ask(i, k, sects), i) for i in range(sects)])  6.12 us
    ppermute x3, starting transfers between devices, body(): lax.ppermute(results[k], 'sect', [(i, partner(i, k, sects)) for i in rang...  4.45 us
    ppermute x3, waiting for transfers between devices, body(): lax.ppermute(results[k], 'sect', [(i, partner(i, k, sects)) for i in rang...  2.92 us
    pallas_call x1, Pallas kernels, prefill(): pl.pallas_call(prefill_kernel, in_specs=[pl.BlockSpec(memory_space=pltpu....  2.77 us
    pallas_call x1, Pallas kernels, pack(): pl.pallas_call(pack_kernel, in_specs=[pl.BlockSpec(memory_space=pltpu.Mem...  0.94 us
    pallas_call x1, Pallas kernels, begin(): pl.pallas_call(begin_kernel, in_specs=[vmem] * 3, out_specs=[vmem] * 5, o...  0.86 us
    pallas_call x1, Pallas kernels, finish(): pl.pallas_call(finish_kernel, in_specs=[vmem] * (1 + len(blocks)), out_sp...  0.75 us
    pallas_call x1, Pallas kernels, end(): pl.pallas_call(functools.partial(end_kernel, count), in_specs=[vmem] * 6,...  0.74 us
  transfers between devices with their start and end apart: 7, of which 5 were waited for; matrix products, arithmetic and copies ran while one was open for 1% of the time, Pallas kernels for 17%

profile of v22, /device:TPU:0, one launch (start us, length us, event | category | flops | bytes accessed | tf_op | source)
XLA Modules:
  0.0 21.1 jit_solution(13960849336927487920)
XLA Ops:
  0.0 0.0 copy-start.2
  0.0 0.0 copy-start
  0.0 0.0 copy-start.1
  0.0 0.9 %pack.1 = bf16[4,5120]{1,0:T(4,128)(2,1)S(1)} custom-call(bf16[4,4096]{1,0:T(4,128)(2,1)} %queries_ref.1, bf16[4,512]{1,0:T(4,128)(2,1)} %keys_ref.2, bf16[4,512]{1,0:T(4,128)(2,1)} %values_ref.2), custom_call_target="tpu_custom_call" | custom-call | flops 10000000000 | bytes 33554432 | tf_op jit(solution)/shard_map/pack/pallas_call | solution.py:47
  1.0 3.1 %collective-permute-start.1 = (bf16[4,5120]{1,0:T(4,128)(2,1)S(1)}, bf16[4,5120]{1,0:T(4,128)(2,1)S(1)}, u32[]{:S(2)}, u32[]{:S(2)}) collective-permute-start(bf16[4,5120]{1,0:T(4,128)(2,1)S(1)} %pack.1), channel_id=1, source_target_pairs={{12,0},{0,4},{4,8},{8,12},{13,1},{1,5},{5,9},{9,13},{14,2},{2,6},{... | collective-permute-start | bytes 122888 | tf_op jit(solution)/shard_map/ppermute | solution.py:310
  4.0 2.1 %collective-permute-start.2 = (bf16[4,5120]{1,0:T(4,128)(2,1)S(1)}, bf16[4,5120]{1,0:T(4,128)(2,1)S(1)}, u32[]{:S(2)}, u32[]{:S(2)}) collective-permute-start(bf16[4,5120]{1,0:T(4,128)(2,1)S(1)} %pack.1), channel_id=1, source_target_pairs={{4,0},{8,4},{12,8},{0,12},{5,1},{9,5},{13,9},{1,13},{6,2},{10,6},{... | collective-permute-start | bytes 122888 | tf_op jit(solution)/shard_map/ppermute | solution.py:310
  6.1 0.9 %collective-permute-start = (bf16[4,5120]{1,0:T(4,128)(2,1)S(1)}, bf16[4,5120]{1,0:T(4,128)(2,1)S(1)}, u32[]{:S(2)}, u32[]{:S(2)}) collective-permute-start(bf16[4,5120]{1,0:T(4,128)(2,1)S(1)} %pack.1), channel_id=1, source_target_pairs={{8,0},{12,4},{0,8},{4,12},{9,1},{13,5},{1,9},{5,13},{10,2},{14,6},... | collective-permute-start | bytes 122888 | tf_op jit(solution)/shard_map/ppermute | solution.py:310
  7.7 0.0 copy-done.2
  7.7 0.0 copy-done
  7.7 0.0 copy-done.1
  7.8 0.0 copy-start.3
  7.8 2.8 %prefill.1.near_ref = bf16[1168,128]{1,0:T(8,128)(2,1)S(1)} custom-call(s32[1]{0:T(128)S(6)} %copy.9.lengths_ref, bf16[1,4096,512]{2,1,0:T(8,128)(2,1)S(1)} %copy-done, bf16[1,4096,512]{2,1,0:T(8,128)(2,1)S(1)} %copy-done.1, bf16[4,128,128]{2,1,0:T(8,128)(2,1)S(1)} %copy-done.2), custom_call_target="tpu_custom_call" | custom-call | flops 1073741824 | bytes 8388608 | tf_op jit(solution)/shard_map/prefill/pallas_call | solution.py:148
  10.5 0.1 collective-permute-start.3
  10.6 0.0 collective-permute-done.1
  10.6 0.0 collective-permute-done.2
  10.7 0.3 %collective-permute-done = bf16[4,5120]{1,0:T(4,128)(2,1)S(1)} collective-permute-done((bf16[4,5120]{1,0:T(4,128)(2,1)S(1)}, bf16[4,5120]{1,0:T(4,128)(2,1)S(1)}, u32[]{:S(2)}, u32[]{:S(2)}) %collective-permute-start) | collective-permute-done | bytes 40992 | tf_op jit(solution)/shard_map/ppermute | solution.py:310
  11.0 0.1 pad_maximum_fusion.rows_ref
  11.1 0.9 %begin.1 = (bf16[4,128,128]{2,1,0:T(8,128)(2,1)S(1)}, bf16[4,128,128]{2,1,0:T(8,128)(2,1)S(1)}, f32[4,128,128]{2,1,0:T(8,128)S(1)}, f32[4,128,128]{2,1,0:T(8,128)S(1)}, f32[4,128,128]{2,1,0:T(8,128)S(1)}) custom-call(bf16[16,5120]{1,0:T(8,128)(2,1)S(1)} %pad_maximum_fusion.rows_ref, bf16[4,128,128]{2,1,0:T(8,128)(2,1)S(1)} %copy-done.2, ...), custom_call_target="tpu_custom_call" | custom-call | flops 62914560 | bytes 327680 | tf_op jit(solution)/shard_map/begin/pallas_call | solution.py:241
  12.0 0.2 collective-permute-done.3.far_ref
  12.2 0.7 %end.1 = (bf16[128,128]{1,0:T(8,128)(2,1)S(1)}, bf16[128,128]{1,0:T(8,128)(2,1)S(1)}, bf16[128,128]{1,0:T(8,128)(2,1)S(1)}, bf16[128,128]{1,0:T(8,128)(2,1)S(1)}) custom-call(bf16[4,128,128]{2,1,0:T(8,128)(2,1)S(1)} %get-tuple-element.14.query_ref, bf16[4,128,128]{2,1,0:T(8,128)(2,1)S(1)} %get-tuple-element.15.phi_ref, ...), custom_call_target="tpu_custom_call" | custom-call | flops 33554432 | bytes 262144 | tf_op jit(solution)/shard_map/end/pallas_call | solution.py:257
  13.0 2.2 %collective-permute-start.4 = (bf16[128,128]{1,0:T(8,128)(2,1)S(1)}, bf16[128,128]{1,0:T(8,128)(2,1)S(1)}, u32[]{:S(2)}, u32[]{:S(2)}) collective-permute-start(bf16[128,128]{1,0:T(8,128)(2,1)S(1)} %get-tuple-element.20), channel_id=1, source_target_pairs={{0,12},{4,8},{8,4},{12,0},{1,13},{5,9},{9,5},{13,1},{2,14},{6,10},... | collective-permute-start | bytes 98312 | tf_op jit(solution)/shard_map/ppermute | solution.py:322
  15.1 1.0 %collective-permute-start.5 = (bf16[128,128]{1,0:T(8,128)(2,1)S(1)}, bf16[128,128]{1,0:T(8,128)(2,1)S(1)}, u32[]{:S(2)}, u32[]{:S(2)}) collective-permute-start(bf16[128,128]{1,0:T(8,128)(2,1)S(1)} %get-tuple-element.21), channel_id=1, source_target_pairs={{0,8},{4,12},{8,0},{12,4},{1,9},{5,13},{9,1},{13,5},{2,10},{6,14},... | collective-permute-start | bytes 98312 | tf_op jit(solution)/shard_map/ppermute | solution.py:322
  16.1 1.3 %collective-permute-start.6 = (bf16[128,128]{1,0:T(8,128)(2,1)S(1)}, bf16[128,128]{1,0:T(8,128)(2,1)S(1)}, u32[]{:S(2)}, u32[]{:S(2)}) collective-permute-start(bf16[128,128]{1,0:T(8,128)(2,1)S(1)} %get-tuple-element.22), channel_id=1, source_target_pairs={{0,4},{4,0},{8,12},{12,8},{1,5},{5,1},{9,13},{13,9},{2,6},{6,2},{1... | collective-permute-start | bytes 98312 | tf_op jit(solution)/shard_map/ppermute | solution.py:322
  17.4 1.7 %collective-permute-done.4.refs_1_ = bf16[128,128]{1,0:T(8,128)(2,1)S(1)} collective-permute-done((bf16[128,128]{1,0:T(8,128)(2,1)S(1)}, bf16[128,128]{1,0:T(8,128)(2,1)S(1)}, u32[]{:S(2)}, u32[]{:S(2)}) %collective-permute-start.4) | collective-permute-done | bytes 32800 | tf_op jit(solution)/shard_map/ppermute | solution.py:322
  19.1 1.2 %collective-permute-done.5.refs_2_ = bf16[128,128]{1,0:T(8,128)(2,1)S(1)} collective-permute-done((bf16[128,128]{1,0:T(8,128)(2,1)S(1)}, bf16[128,128]{1,0:T(8,128)(2,1)S(1)}, u32[]{:S(2)}, u32[]{:S(2)}) %collective-permute-start.5) | collective-permute-done | bytes 32800 | tf_op jit(solution)/shard_map/ppermute | solution.py:322
  20.3 0.1 collective-permute-done.6.refs_3_
  20.3 0.0 copy-done.3
  20.3 0.8 %finish.1 = bf16[4,4096]{1,0:T(4,128)(2,1)} custom-call(s32[1,32]{1,0:T(1,128)S(1)} %bitcast.1, bf16[128,128]{1,0:T(8,128)(2,1)S(1)} %get-tuple-element.19.refs_0_, bf16[128,128]{1,0:T(8,128)(2,1)S(1)} %collective-permute-done.4.refs_1_, bf16[128,128]{1,0:T(8,128)(2,1)S(1)} %collective-permute-done.5.refs_2_, bf16[128,128]{1,0:T(8,128)(2,1)S(1)} %collective-permute-done.6.refs_3_), custom_call_target="tpu_custom_call" | custom-call | tf_op jit(solution)/shard_map/finish/pallas_call | solution.py:292
  (1 shorter events, 0.0 us)
Async XLA Ops:
  0.0 7.7 %copy-start.2 = (bf16[4,128,128]{2,1,0:T(8,128)(2,1)S(1)}, bf16[4,128,128]{2,1,0:T(8,128)(2,1)}, u32[]{:S(2)}) copy-start(bf16[4,128,128]{2,1,0:T(8,128)(2,1)} %weight_ref.3) | copy-start | bytes 393220
  0.0 7.7 %copy-start = (bf16[1,4096,512]{2,1,0:T(8,128)(2,1)S(1)}, bf16[1,4096,512]{2,1,0:T(8,128)(2,1)}, u32[]{:S(2)}) copy-start(bf16[1,4096,512]{2,1,0:T(8,128)(2,1)} %keys_ref.3) | copy-start | bytes 12582916
  0.0 7.7 %copy-start.1 = (bf16[1,4096,512]{2,1,0:T(8,128)(2,1)S(1)}, bf16[1,4096,512]{2,1,0:T(8,128)(2,1)}, u32[]{:S(2)}) copy-start(bf16[1,4096,512]{2,1,0:T(8,128)(2,1)} %values_ref.3) | copy-start | bytes 12582916
  1.0 9.7 %collective-permute-start.1 = (bf16[4,5120]{1,0:T(4,128)(2,1)S(1)}, bf16[4,5120]{1,0:T(4,128)(2,1)S(1)}, u32[]{:S(2)}, u32[]{:S(2)}) collective-permute-start(bf16[4,5120]{1,0:T(4,128)(2,1)S(1)} %pack.1), channel_id=1, source_target_pairs={{12,0},{0,4},{4,8},{8,12},{13,1},{1,5},{5,9},{9,13},{14,2},{2,6},{... | collective-permute-start | bytes 122888 | tf_op jit(solution)/shard_map/ppermute | solution.py:310
  4.0 6.6 %collective-permute-start.2 = (bf16[4,5120]{1,0:T(4,128)(2,1)S(1)}, bf16[4,5120]{1,0:T(4,128)(2,1)S(1)}, u32[]{:S(2)}, u32[]{:S(2)}) collective-permute-start(bf16[4,5120]{1,0:T(4,128)(2,1)S(1)} %pack.1), channel_id=1, source_target_pairs={{4,0},{8,4},{12,8},{0,12},{5,1},{9,5},{13,9},{1,13},{6,2},{10,6},{... | collective-permute-start | bytes 122888 | tf_op jit(solution)/shard_map/ppermute | solution.py:310
  6.1 4.9 %collective-permute-start = (bf16[4,5120]{1,0:T(4,128)(2,1)S(1)}, bf16[4,5120]{1,0:T(4,128)(2,1)S(1)}, u32[]{:S(2)}, u32[]{:S(2)}) collective-permute-start(bf16[4,5120]{1,0:T(4,128)(2,1)S(1)} %pack.1), channel_id=1, source_target_pairs={{8,0},{12,4},{0,8},{4,12},{9,1},{13,5},{1,9},{5,13},{10,2},{14,6},... | collective-permute-start | bytes 122888 | tf_op jit(solution)/shard_map/ppermute | solution.py:310
  7.8 12.6 %copy-start.3 = (s32[32]{0:T(128)S(1)}, s32[32]{0:T(128)}, u32[]{:S(2)}) copy-start(s32[32]{0:T(128)} %param.15) | copy-start | bytes 388
  10.5 1.7 %collective-permute-start.3 = (bf16[1168,128]{1,0:T(8,128)(2,1)S(1)}, bf16[1168,128]{1,0:T(8,128)(2,1)S(1)}, u32[]{:S(2)}, u32[]{:S(2)}) collective-permute-start(bf16[1168,128]{1,0:T(8,128)(2,1)S(1)} %prefill.1.near_ref), channel_id=1, source_target_pairs={{0,1},{1,0},{2,3},{3,2},{4,5},{5,4},{6,7},{7,6},{8,9},{9,8},{10,11... | collective-permute-start | bytes 897032 | tf_op jit(solution)/shard_map/ppermute | solution.py:316
  13.0 6.1 %collective-permute-start.4 = (bf16[128,128]{1,0:T(8,128)(2,1)S(1)}, bf16[128,128]{1,0:T(8,128)(2,1)S(1)}, u32[]{:S(2)}, u32[]{:S(2)}) collective-permute-start(bf16[128,128]{1,0:T(8,128)(2,1)S(1)} %get-tuple-element.20), channel_id=1, source_target_pairs={{0,12},{4,8},{8,4},{12,0},{1,13},{5,9},{9,5},{13,1},{2,14},{6,10},... | collective-permute-start | bytes 98312 | tf_op jit(solution)/shard_map/ppermute | solution.py:322
  15.1 5.2 %collective-permute-start.5 = (bf16[128,128]{1,0:T(8,128)(2,1)S(1)}, bf16[128,128]{1,0:T(8,128)(2,1)S(1)}, u32[]{:S(2)}, u32[]{:S(2)}) collective-permute-start(bf16[128,128]{1,0:T(8,128)(2,1)S(1)} %get-tuple-element.21), channel_id=1, source_target_pairs={{0,8},{4,12},{8,0},{12,4},{1,9},{5,13},{9,1},{13,5},{2,10},{6,14},... | collective-permute-start | bytes 98312 | tf_op jit(solution)/shard_map/ppermute | solution.py:322
  16.1 4.3 %collective-permute-start.6 = (bf16[128,128]{1,0:T(8,128)(2,1)S(1)}, bf16[128,128]{1,0:T(8,128)(2,1)S(1)}, u32[]{:S(2)}, u32[]{:S(2)}) collective-permute-start(bf16[128,128]{1,0:T(8,128)(2,1)S(1)} %get-tuple-element.22), channel_id=1, source_target_pairs={{0,4},{4,0},{8,12},{12,8},{1,5},{5,1},{9,13},{13,9},{2,6},{6,2},{1... | collective-permute-start | bytes 98312 | tf_op jit(solution)/shard_map/ppermute | solution.py:322

commit v23 on v21

--- a/solution.py
+++ b/solution.py
@@ -195,6 +195,7 @@
     group = (rows_ref.shape[1] - 2 * heads * head_size) // (heads * head_size)
     keys_at = heads * group * head_size
     values_at = keys_at + heads * head_size
+    ready = []
     for g in range(heads):
         query = jnp.concatenate(
             [
@@ -213,10 +214,12 @@
         own_weight = jnp.exp(own_score)
         num, den = share(query, phi, scale, near_ref, g, heads)
         num += own_weight.astype(jnp.bfloat16).astype(jnp.float32) * jnp.concatenate([own_value] * group, axis=0)
+        ready.append((query, phi, num, den + own_weight, scale))
+    for g, (query, phi, num, den, scale) in enumerate(ready):
         query_ref[g] = query
         phi_ref[g] = phi
         num_ref[g] = num
-        den_ref[g] = jnp.broadcast_to(den + own_weight, num.shape)
+        den_ref[g] = jnp.broadcast_to(den, num.shape)
         scale_ref[g] = jnp.broadcast_to(scale, num.shape)
 
 
@@ -225,9 +228,11 @@
     each, width = out_refs[0].shape
     group = width // (heads * head_size)
     count = asked // group
+    ready = []
     for g in range(heads):
         num, den = share(query_ref[g], phi_ref[g], scale_ref[g][:, :1], far_ref, g, heads)
-        result = ((num_ref[g] + num) / (den_ref[g] + den)).astype(jnp.bfloat16)
+        ready.append(((num_ref[g] + num) / (den_ref[g] + den)).astype(jnp.bfloat16))
+    for g, result in enumerate(ready):
         for h in range(group):
             at = (g * group + h) * head_size
             for k, out_ref in enumerate(out_refs):

time: 21.2 us -> 21.2 us (level)
  no operation moved by 1% of the time
where the time goes in v23:
time: 21.2 us; the launch traced here: 21 us
  starting transfers between devices  10.6 us (50%)
  Pallas kernels  5.31 us (25%)
  waiting for transfers between devices  3.38 us (16%)
  other arithmetic  0.93 us (4%)
  between operations  0.76 us (4%)
    ppermute x3, starting transfers between devices, body(): lax.ppermute(mine, 'sect', [(ask(i, k, sects), i) for i in range(sects)])  6.12 us
    ppermute x3, starting transfers between devices, body(): lax.ppermute(results[k], 'sect', [(i, partner(i, k, sects)) for i in rang...  4.45 us
    ppermute x3, waiting for transfers between devices, body(): lax.ppermute(results[k], 'sect', [(i, partner(i, k, sects)) for i in rang...  2.84 us
    pallas_call x1, Pallas kernels, prefill(): pl.pallas_call(prefill_kernel, in_specs=[pl.BlockSpec(memory_space=pltpu....  2.77 us
    pallas_call x1, Pallas kernels, pack(): pl.pallas_call(pack_kernel, in_specs=[pl.BlockSpec(memory_space=pltpu.Mem...  0.94 us
    pallas_call x1, Pallas kernels, begin(): pl.pallas_call(begin_kernel, in_specs=[vmem] * 3, out_specs=[vmem] * 5, o...  0.86 us
    pallas_call x1, Pallas kernels, end(): pl.pallas_call(end_kernel, in_specs=[vmem] * 6, out_specs=[vmem] * parts,...  0.75 us
    select_n x1, other arithmetic, body(): out = jnp.where((prompts == source)[:, None], result, out)  0.71 us
  transfers between devices with their start and end apart: 7, of which 5 were waited for; matrix products, arithmetic and copies ran while one was open for 1% of the time, Pallas kernels for 17%

profile of v23, /device:TPU:0, one launch (start us, length us, event | category | flops | bytes accessed | tf_op | source)
XLA Modules:
  0.0 21.0 jit_solution(12824218987441758694)
XLA Ops:
  0.0 0.0 copy-start.2
  0.0 0.0 copy-start
  0.0 0.0 copy-start.1
  0.0 0.9 %pack.1 = bf16[4,5120]{1,0:T(4,128)(2,1)S(1)} custom-call(bf16[4,4096]{1,0:T(4,128)(2,1)} %queries_ref.1, bf16[4,512]{1,0:T(4,128)(2,1)} %keys_ref.2, bf16[4,512]{1,0:T(4,128)(2,1)} %values_ref.2), custom_call_target="tpu_custom_call" | custom-call | flops 10000000000 | bytes 33554432 | tf_op jit(solution)/shard_map/pack/pallas_call | solution.py:47
  1.0 3.1 %collective-permute-start.1 = (bf16[4,5120]{1,0:T(4,128)(2,1)S(1)}, bf16[4,5120]{1,0:T(4,128)(2,1)S(1)}, u32[]{:S(2)}, u32[]{:S(2)}) collective-permute-start(bf16[4,5120]{1,0:T(4,128)(2,1)S(1)} %pack.1), channel_id=1, source_target_pairs={{12,0},{0,4},{4,8},{8,12},{13,1},{1,5},{5,9},{9,13},{14,2},{2,6},{... | collective-permute-start | bytes 122888 | tf_op jit(solution)/shard_map/ppermute | solution.py:286
  4.0 2.1 %collective-permute-start.2 = (bf16[4,5120]{1,0:T(4,128)(2,1)S(1)}, bf16[4,5120]{1,0:T(4,128)(2,1)S(1)}, u32[]{:S(2)}, u32[]{:S(2)}) collective-permute-start(bf16[4,5120]{1,0:T(4,128)(2,1)S(1)} %pack.1), channel_id=1, source_target_pairs={{4,0},{8,4},{12,8},{0,12},{5,1},{9,5},{13,9},{1,13},{6,2},{10,6},{... | collective-permute-start | bytes 122888 | tf_op jit(solution)/shard_map/ppermute | solution.py:286
  6.1 0.9 %collective-permute-start = (bf16[4,5120]{1,0:T(4,128)(2,1)S(1)}, bf16[4,5120]{1,0:T(4,128)(2,1)S(1)}, u32[]{:S(2)}, u32[]{:S(2)}) collective-permute-start(bf16[4,5120]{1,0:T(4,128)(2,1)S(1)} %pack.1), channel_id=1, source_target_pairs={{8,0},{12,4},{0,8},{4,12},{9,1},{13,5},{1,9},{5,13},{10,2},{14,6},... | collective-permute-start | bytes 122888 | tf_op jit(solution)/shard_map/ppermute | solution.py:286
  7.7 0.0 copy-done.2
  7.7 0.0 copy-done
  7.7 0.0 copy-done.1
  7.8 0.0 copy-start.3
  7.8 2.8 %prefill.1.near_ref = bf16[1168,128]{1,0:T(8,128)(2,1)S(1)} custom-call(s32[1]{0:T(128)S(6)} %copy.9.lengths_ref, bf16[1,4096,512]{2,1,0:T(8,128)(2,1)S(1)} %copy-done, bf16[1,4096,512]{2,1,0:T(8,128)(2,1)S(1)} %copy-done.1, bf16[4,128,128]{2,1,0:T(8,128)(2,1)S(1)} %copy-done.2), custom_call_target="tpu_custom_call" | custom-call | flops 1073741824 | bytes 8388608 | tf_op jit(solution)/shard_map/prefill/pallas_call | solution.py:148
  10.5 0.1 collective-permute-start.3
  10.6 0.0 collective-permute-done.1
  10.6 0.0 collective-permute-done.2
  10.7 0.3 %collective-permute-done = bf16[4,5120]{1,0:T(4,128)(2,1)S(1)} collective-permute-done((bf16[4,5120]{1,0:T(4,128)(2,1)S(1)}, bf16[4,5120]{1,0:T(4,128)(2,1)S(1)}, u32[]{:S(2)}, u32[]{:S(2)}) %collective-permute-start) | collective-permute-done | bytes 40992 | tf_op jit(solution)/shard_map/ppermute | solution.py:286
  11.0 0.1 pad_maximum_fusion.rows_ref
  11.1 0.9 %begin.1 = (bf16[4,128,128]{2,1,0:T(8,128)(2,1)S(1)}, bf16[4,128,128]{2,1,0:T(8,128)(2,1)S(1)}, f32[4,128,128]{2,1,0:T(8,128)S(1)}, f32[4,128,128]{2,1,0:T(8,128)S(1)}, f32[4,128,128]{2,1,0:T(8,128)S(1)}) custom-call(bf16[16,5120]{1,0:T(8,128)(2,1)S(1)} %pad_maximum_fusion.rows_ref, bf16[4,128,128]{2,1,0:T(8,128)(2,1)S(1)} %copy-done.2, ...), custom_call_target="tpu_custom_call" | custom-call | flops 62914560 | bytes 327680 | tf_op jit(solution)/shard_map/begin/pallas_call | solution.py:249
  12.0 0.2 collective-permute-done.3.far_ref
  12.2 0.7 %end.1 = (bf16[4,4096]{1,0:T(4,128)(2,1)S(1)}, bf16[4,4096]{1,0:T(4,128)(2,1)S(1)}, bf16[4,4096]{1,0:T(4,128)(2,1)S(1)}, bf16[4,4096]{1,0:T(4,128)(2,1)S(1)}) custom-call(bf16[4,128,128]{2,1,0:T(8,128)(2,1)S(1)} %get-tuple-element.14.query_ref, bf16[4,128,128]{2,1,0:T(8,128)(2,1)S(1)} %get-tuple-element.15.phi_ref, ...), custom_call_target="tpu_custom_call" | custom-call | flops 33554432 | bytes 262144 | tf_op jit(solution)/shard_map/end/pallas_call | solution.py:264
  13.0 2.2 %collective-permute-start.4 = (bf16[4,4096]{1,0:T(4,128)(2,1)S(1)}, bf16[4,4096]{1,0:T(4,128)(2,1)S(1)}, u32[]{:S(2)}, u32[]{:S(2)}) collective-permute-start(bf16[4,4096]{1,0:T(4,128)(2,1)S(1)} %get-tuple-element.19), channel_id=1, source_target_pairs={{0,12},{4,8},{8,4},{12,0},{1,13},{5,9},{9,5},{13,1},{2,14},{6,10},... | collective-permute-start | bytes 98312 | tf_op jit(solution)/shard_map/ppermute | solution.py:302
  15.1 1.0 %collective-permute-start.5 = (bf16[4,4096]{1,0:T(4,128)(2,1)S(1)}, bf16[4,4096]{1,0:T(4,128)(2,1)S(1)}, u32[]{:S(2)}, u32[]{:S(2)}) collective-permute-start(bf16[4,4096]{1,0:T(4,128)(2,1)S(1)} %get-tuple-element.20), channel_id=1, source_target_pairs={{0,8},{4,12},{8,0},{12,4},{1,9},{5,13},{9,1},{13,5},{2,10},{6,14},... | collective-permute-start | bytes 98312 | tf_op jit(solution)/shard_map/ppermute | solution.py:302
  16.1 1.3 %collective-permute-start.6 = (bf16[4,4096]{1,0:T(4,128)(2,1)S(1)}, bf16[4,4096]{1,0:T(4,128)(2,1)S(1)}, u32[]{:S(2)}, u32[]{:S(2)}) collective-permute-start(bf16[4,4096]{1,0:T(4,128)(2,1)S(1)} %get-tuple-element.21), channel_id=1, source_target_pairs={{0,4},{4,0},{8,12},{12,8},{1,5},{5,1},{9,13},{13,9},{2,6},{6,2},{1... | collective-permute-start | bytes 98312 | tf_op jit(solution)/shard_map/ppermute | solution.py:302
  17.4 0.0 copy-done.3
  17.4 0.1 broadcast_compare_fusion.2
  17.5 1.6 %collective-permute-done.4 = bf16[4,4096]{1,0:T(4,128)(2,1)S(1)} collective-permute-done((bf16[4,4096]{1,0:T(4,128)(2,1)S(1)}, bf16[4,4096]{1,0:T(4,128)(2,1)S(1)}, u32[]{:S(2)}, u32[]{:S(2)}) %collective-permute-start.4) | collective-permute-done | bytes 32800 | tf_op jit(solution)/shard_map/ppermute | solution.py:302
  19.1 1.2 %collective-permute-done.5 = bf16[4,4096]{1,0:T(4,128)(2,1)S(1)} collective-permute-done((bf16[4,4096]{1,0:T(4,128)(2,1)S(1)}, bf16[4,4096]{1,0:T(4,128)(2,1)S(1)}, u32[]{:S(2)}, u32[]{:S(2)}) %collective-permute-start.5) | collective-permute-done | bytes 32800 | tf_op jit(solution)/shard_map/ppermute | solution.py:302
  20.3 0.1 collective-permute-done.6
  20.3 0.7 %select_select_fusion = bf16[4,4096]{1,0:T(4,128)(2,1)} fusion(bf16[4,4096]{1,0:T(4,128)(2,1)S(1)} %collective-permute-done.4, bf16[4,4096]{1,0:T(4,128)(2,1)S(1)} %collective-permute-done.5, bf16[4,4096]{1,0:T(4,128)(2,1)S(1)} %collective-permute-done.6, bf16[4,4096]{1,0:T(4,128)(2,1)S(1)} %get-tuple-element.22, pred[4]{0:T(512)(128)(4,1)S(1)} %get-tuple-element.27, ...), kind=kLoop, calls=%fused_computation.3 | loop fusion | flops 49152 | bytes 163852 | tf_op jit(solution)/shard_map/jit(_where)/select_n | solution.py:304
  (1 shorter events, 0.0 us)
Async XLA Ops:
  0.0 7.7 %copy-start.2 = (bf16[4,128,128]{2,1,0:T(8,128)(2,1)S(1)}, bf16[4,128,128]{2,1,0:T(8,128)(2,1)}, u32[]{:S(2)}) copy-start(bf16[4,128,128]{2,1,0:T(8,128)(2,1)} %weight_ref.3) | copy-start | bytes 393220
  0.0 7.7 %copy-start = (bf16[1,4096,512]{2,1,0:T(8,128)(2,1)S(1)}, bf16[1,4096,512]{2,1,0:T(8,128)(2,1)}, u32[]{:S(2)}) copy-start(bf16[1,4096,512]{2,1,0:T(8,128)(2,1)} %keys_ref.3) | copy-start | bytes 12582916
  0.0 7.7 %copy-start.1 = (bf16[1,4096,512]{2,1,0:T(8,128)(2,1)S(1)}, bf16[1,4096,512]{2,1,0:T(8,128)(2,1)}, u32[]{:S(2)}) copy-start(bf16[1,4096,512]{2,1,0:T(8,128)(2,1)} %values_ref.3) | copy-start | bytes 12582916
  1.0 9.7 %collective-permute-start.1 = (bf16[4,5120]{1,0:T(4,128)(2,1)S(1)}, bf16[4,5120]{1,0:T(4,128)(2,1)S(1)}, u32[]{:S(2)}, u32[]{:S(2)}) collective-permute-start(bf16[4,5120]{1,0:T(4,128)(2,1)S(1)} %pack.1), channel_id=1, source_target_pairs={{12,0},{0,4},{4,8},{8,12},{13,1},{1,5},{5,9},{9,13},{14,2},{2,6},{... | collective-permute-start | bytes 122888 | tf_op jit(solution)/shard_map/ppermute | solution.py:286
  4.0 6.6 %collective-permute-start.2 = (bf16[4,5120]{1,0:T(4,128)(2,1)S(1)}, bf16[4,5120]{1,0:T(4,128)(2,1)S(1)}, u32[]{:S(2)}, u32[]{:S(2)}) collective-permute-start(bf16[4,5120]{1,0:T(4,128)(2,1)S(1)} %pack.1), channel_id=1, source_target_pairs={{4,0},{8,4},{12,8},{0,12},{5,1},{9,5},{13,9},{1,13},{6,2},{10,6},{... | collective-permute-start | bytes 122888 | tf_op jit(solution)/shard_map/ppermute | solution.py:286
  6.1 4.9 %collective-permute-start = (bf16[4,5120]{1,0:T(4,128)(2,1)S(1)}, bf16[4,5120]{1,0:T(4,128)(2,1)S(1)}, u32[]{:S(2)}, u32[]{:S(2)}) collective-permute-start(bf16[4,5120]{1,0:T(4,128)(2,1)S(1)} %pack.1), channel_id=1, source_target_pairs={{8,0},{12,4},{0,8},{4,12},{9,1},{13,5},{1,9},{5,13},{10,2},{14,6},... | collective-permute-start | bytes 122888 | tf_op jit(solution)/shard_map/ppermute | solution.py:286
  7.8 9.7 %copy-start.3 = (s32[32]{0:T(128)S(1)}, s32[32]{0:T(128)}, u32[]{:S(2)}) copy-start(s32[32]{0:T(128)} %param.15) | copy-start | bytes 388
  10.5 1.7 %collective-permute-start.3 = (bf16[1168,128]{1,0:T(8,128)(2,1)S(1)}, bf16[1168,128]{1,0:T(8,128)(2,1)S(1)}, u32[]{:S(2)}, u32[]{:S(2)}) collective-permute-start(bf16[1168,128]{1,0:T(8,128)(2,1)S(1)} %prefill.1.near_ref), channel_id=1, source_target_pairs={{0,1},{1,0},{2,3},{3,2},{4,5},{5,4},{6,7},{7,6},{8,9},{9,8},{10,11... | collective-permute-start | bytes 897032 | tf_op jit(solution)/shard_map/ppermute | solution.py:292
  13.0 6.1 %collective-permute-start.4 = (bf16[4,4096]{1,0:T(4,128)(2,1)S(1)}, bf16[4,4096]{1,0:T(4,128)(2,1)S(1)}, u32[]{:S(2)}, u32[]{:S(2)}) collective-permute-start(bf16[4,4096]{1,0:T(4,128)(2,1)S(1)} %get-tuple-element.19), channel_id=1, source_target_pairs={{0,12},{4,8},{8,4},{12,0},{1,13},{5,9},{9,5},{13,1},{2,14},{6,10},... | collective-permute-start | bytes 98312 | tf_op jit(solution)/shard_map/ppermute | solution.py:302
  15.1 5.2 %collective-permute-start.5 = (bf16[4,4096]{1,0:T(4,128)(2,1)S(1)}, bf16[4,4096]{1,0:T(4,128)(2,1)S(1)}, u32[]{:S(2)}, u32[]{:S(2)}) collective-permute-start(bf16[4,4096]{1,0:T(4,128)(2,1)S(1)} %get-tuple-element.20), channel_id=1, source_target_pairs={{0,8},{4,12},{8,0},{12,4},{1,9},{5,13},{9,1},{13,5},{2,10},{6,14},... | collective-permute-start | bytes 98312 | tf_op jit(solution)/shard_map/ppermute | solution.py:302
  16.1 4.3 %collective-permute-start.6 = (bf16[4,4096]{1,0:T(4,128)(2,1)S(1)}, bf16[4,4096]{1,0:T(4,128)(2,1)S(1)}, u32[]{:S(2)}, u32[]{:S(2)}) collective-permute-start(bf16[4,4096]{1,0:T(4,128)(2,1)S(1)} %get-tuple-element.21), channel_id=1, source_target_pairs={{0,4},{4,0},{8,12},{12,8},{1,5},{5,1},{9,13},{13,9},{2,6},{6,2},{1... | collective-permute-start | bytes 98312 | tf_op jit(solution)/shard_map/ppermute | solution.py:302

commit v24 on v23

--- a/solution.py
+++ b/solution.py
@@ -170,24 +170,35 @@
     )
 
 
+def halves(wide):
+    high = wide.astype(jnp.bfloat16)
+    return high, (wide - high.astype(jnp.float32)).astype(jnp.bfloat16)
+
+
 def share(query, phi, scale, ref, g, heads):
     head_size = query.shape[1]
     feats = phi.shape[1]
     tile_at = heads * feats
     tile = ref[tile_at : tile_at + 16, :].astype(jnp.float32)
     linear = jnp.dot(phi, ref[g * feats : (g + 1) * feats, :], preferred_element_type=jnp.float32)
+    norms = jnp.broadcast_to(tile[g : g + 1], (head_size, feats)).astype(jnp.bfloat16)
+    linear_den = lax.dot_general(phi, norms, NT, preferred_element_type=jnp.float32)
     at = tile_at + 16 + g * SLAB
     keys = ref[at : at + SLAB, :]
     at += heads * SLAB
     values = ref[at : at + SLAB, :]
     keys_wide = keys.astype(jnp.float32)
-    key_scale = lax.rsqrt(jnp.mean((keys_wide * keys_wide).T, axis=0, keepdims=True) + EPS)
-    score = lax.dot_general(query, keys, NT, preferred_element_type=jnp.float32) * scale * key_scale
-    weights = jnp.exp(score) * tile[MASK_ROW : MASK_ROW + 1, :SLAB]
+    ones = jnp.ones((16, head_size), jnp.bfloat16)
+    squares = [
+        lax.dot_general(ones, part, NT, preferred_element_type=jnp.float32) for part in halves(keys_wide * keys_wide)
+    ]
+    key_scale = lax.rsqrt((squares[0] + squares[1])[:1] * (1.0 / head_size) + EPS)
+    score = lax.dot_general(query, keys, NT, preferred_element_type=jnp.float32) * scale[:, :SLAB] * key_scale
+    weights = (jnp.exp(score) * tile[MASK_ROW : MASK_ROW + 1, :SLAB]).astype(jnp.bfloat16)
     back = 1.0 / (feats * feats)
-    num = linear * back + jnp.dot(weights.astype(jnp.bfloat16), values, preferred_element_type=jnp.float32)
-    den = jnp.sum(weights, axis=-1, keepdims=True)
-    return num, den + jnp.sum(phi.astype(jnp.float32) * tile[g : g + 1], axis=-1, keepdims=True) * back
+    num = linear * back + jnp.dot(weights, values, preferred_element_type=jnp.float32)
+    ones = jnp.ones((SLAB, head_size), jnp.bfloat16)
+    return num, linear_den * back + jnp.dot(weights, ones, preferred_element_type=jnp.float32)
 
 
 def begin_kernel(rows_ref, weight_ref, near_ref, query_ref, phi_ref, num_ref, den_ref, scale_ref):
@@ -212,6 +223,7 @@
         own_key = own_key * lax.rsqrt(jnp.mean(own_key * own_key, axis=-1, keepdims=True) + EPS)
         own_score = jnp.sum(wide * jnp.concatenate([own_key] * group, axis=0), axis=-1, keepdims=True) * scale
         own_weight = jnp.exp(own_score)
+        scale = jnp.broadcast_to(scale, query.shape)
         num, den = share(query, phi, scale, near_ref, g, heads)
         num += own_weight.astype(jnp.bfloat16).astype(jnp.float32) * jnp.concatenate([own_value] * group, axis=0)
         ready.append((query, phi, num, den + own_weight, scale))
@@ -219,8 +231,8 @@
         query_ref[g] = query
         phi_ref[g] = phi
         num_ref[g] = num
-        den_ref[g] = jnp.broadcast_to(den, num.shape)
-        scale_ref[g] = jnp.broadcast_to(scale, num.shape)
+        den_ref[g] = den
+        scale_ref[g] = scale
 
 
 def end_kernel(query_ref, phi_ref, num_ref, den_ref, scale_ref, far_ref, *out_refs):
@@ -230,7 +242,7 @@
     count = asked // group
     ready = []
     for g in range(heads):
-        num, den = share(query_ref[g], phi_ref[g], scale_ref[g][:, :1], far_ref, g, heads)
+        num, den = share(query_ref[g], phi_ref[g], scale_ref[g], far_ref, g, heads)
         ready.append(((num_ref[g] + num) / (den_ref[g] + den)).astype(jnp.bfloat16))
     for g, result in enumerate(ready):
         for h in range(group):

time: 21.2 us -> 21.6 us (1.019)
  Pallas kernels: 5.31 us -> 6.07 us
  waiting for transfers between devices: 3.38 us -> 2.97 us
    pallas_call x1, Pallas kernels: 0.86 us -> 1.38 us  [begin(): pl.pallas_call(begin_kernel, in_specs=[vmem] * 3, out_specs=[vmem] * 5, o...]
    pallas_call x1, Pallas kernels: 0.75 us -> 0.98 us  [end(): pl.pallas_call(end_kernel, in_specs=[vmem] * 6, out_specs=[vmem] * parts,...]
  transfers between devices with their start and end apart: 7 -> 7, of which waited for: 5 -> 3; matrix products, arithmetic and copies ran while one was open for 1% -> 1% of each run, Pallas kernels for 17% -> 19%
where the time goes in v24:
time: 21.6 us; the launch traced here: 21.4 us
  starting transfers between devices  10.6 us (49%)
  Pallas kernels  6.07 us (28%)
  waiting for transfers between devices  2.97 us (14%)
  other arithmetic  0.93 us (4%)
  between operations  0.76 us (4%)
    ppermute x3, starting transfers between devices, body(): lax.ppermute(mine, 'sect', [(ask(i, k, sects), i) for i in range(sects)])  6.12 us
    ppermute x3, starting transfers between devices, body(): lax.ppermute(results[k], 'sect', [(i, partner(i, k, sects)) for i in rang...  4.45 us
    pallas_call x1, Pallas kernels, prefill(): pl.pallas_call(prefill_kernel, in_specs=[pl.BlockSpec(memory_space=pltpu....  2.77 us
    ppermute x3, waiting for transfers between devices, body(): lax.ppermute(results[k], 'sect', [(i, partner(i, k, sects)) for i in rang...  2.64 us
    pallas_call x1, Pallas kernels, begin(): pl.pallas_call(begin_kernel, in_specs=[vmem] * 3, out_specs=[vmem] * 5, o...  1.38 us
    pallas_call x1, Pallas kernels, end(): pl.pallas_call(end_kernel, in_specs=[vmem] * 6, out_specs=[vmem] * parts,...  0.98 us
    pallas_call x1, Pallas kernels, pack(): pl.pallas_call(pack_kernel, in_specs=[pl.BlockSpec(memory_space=pltpu.Mem...  0.94 us
    select_n x1, other arithmetic, body(): out = jnp.where((prompts == source)[:, None], result, out)  0.71 us
  transfers between devices with their start and end apart: 7, of which 3 were waited for; matrix products, arithmetic and copies ran while one was open for 1% of the time, Pallas kernels for 19%

profile of v24, /device:TPU:0, one launch (start us, length us, event | category | flops | bytes accessed | tf_op | source)
XLA Modules:
  0.0 21.4 jit_solution(14786942230160394533)
XLA Ops:
  0.0 0.0 copy-start.2
  0.0 0.0 copy-start
  0.0 0.0 copy-start.1
  0.0 0.9 %pack.1 = bf16[4,5120]{1,0:T(4,128)(2,1)S(1)} custom-call(bf16[4,4096]{1,0:T(4,128)(2,1)} %queries_ref.1, bf16[4,512]{1,0:T(4,128)(2,1)} %keys_ref.2, bf16[4,512]{1,0:T(4,128)(2,1)} %values_ref.2), custom_call_target="tpu_custom_call" | custom-call | flops 10000000000 | bytes 33554432 | tf_op jit(solution)/shard_map/pack/pallas_call | solution.py:47
  1.0 3.1 %collective-permute-start.1 = (bf16[4,5120]{1,0:T(4,128)(2,1)S(1)}, bf16[4,5120]{1,0:T(4,128)(2,1)S(1)}, u32[]{:S(2)}, u32[]{:S(2)}) collective-permute-start(bf16[4,5120]{1,0:T(4,128)(2,1)S(1)} %pack.1), channel_id=1, source_target_pairs={{12,0},{0,4},{4,8},{8,12},{13,1},{1,5},{5,9},{9,13},{14,2},{2,6},{... | collective-permute-start | bytes 122888 | tf_op jit(solution)/shard_map/ppermute | solution.py:298
  4.0 2.1 %collective-permute-start.2 = (bf16[4,5120]{1,0:T(4,128)(2,1)S(1)}, bf16[4,5120]{1,0:T(4,128)(2,1)S(1)}, u32[]{:S(2)}, u32[]{:S(2)}) collective-permute-start(bf16[4,5120]{1,0:T(4,128)(2,1)S(1)} %pack.1), channel_id=1, source_target_pairs={{4,0},{8,4},{12,8},{0,12},{5,1},{9,5},{13,9},{1,13},{6,2},{10,6},{... | collective-permute-start | bytes 122888 | tf_op jit(solution)/shard_map/ppermute | solution.py:298
  6.1 0.9 %collective-permute-start = (bf16[4,5120]{1,0:T(4,128)(2,1)S(1)}, bf16[4,5120]{1,0:T(4,128)(2,1)S(1)}, u32[]{:S(2)}, u32[]{:S(2)}) collective-permute-start(bf16[4,5120]{1,0:T(4,128)(2,1)S(1)} %pack.1), channel_id=1, source_target_pairs={{8,0},{12,4},{0,8},{4,12},{9,1},{13,5},{1,9},{5,13},{10,2},{14,6},... | collective-permute-start | bytes 122888 | tf_op jit(solution)/shard_map/ppermute | solution.py:298
  7.7 0.0 copy-done.2
  7.7 0.0 copy-done
  7.7 0.0 copy-done.1
  7.8 0.0 copy-start.3
  7.8 2.8 %prefill.1.near_ref = bf16[1168,128]{1,0:T(8,128)(2,1)S(1)} custom-call(s32[1]{0:T(128)S(6)} %copy.9.lengths_ref, bf16[1,4096,512]{2,1,0:T(8,128)(2,1)S(1)} %copy-done, bf16[1,4096,512]{2,1,0:T(8,128)(2,1)S(1)} %copy-done.1, bf16[4,128,128]{2,1,0:T(8,128)(2,1)S(1)} %copy-done.2), custom_call_target="tpu_custom_call" | custom-call | flops 1073741824 | bytes 8388608 | tf_op jit(solution)/shard_map/prefill/pallas_call | solution.py:148
  10.5 0.1 collective-permute-start.3
  10.6 0.0 collective-permute-done.1
  10.6 0.0 collective-permute-done.2
  10.7 0.3 %collective-permute-done = bf16[4,5120]{1,0:T(4,128)(2,1)S(1)} collective-permute-done((bf16[4,5120]{1,0:T(4,128)(2,1)S(1)}, bf16[4,5120]{1,0:T(4,128)(2,1)S(1)}, u32[]{:S(2)}, u32[]{:S(2)}) %collective-permute-start) | collective-permute-done | bytes 40992 | tf_op jit(solution)/shard_map/ppermute | solution.py:298
  11.0 0.1 pad_maximum_fusion.rows_ref
  11.1 1.4 %begin.1 = (bf16[4,128,128]{2,1,0:T(8,128)(2,1)S(1)}, bf16[4,128,128]{2,1,0:T(8,128)(2,1)S(1)}, f32[4,128,128]{2,1,0:T(8,128)S(1)}, f32[4,128,128]{2,1,0:T(8,128)S(1)}, f32[4,128,128]{2,1,0:T(8,128)S(1)}) custom-call(bf16[16,5120]{1,0:T(8,128)(2,1)S(1)} %pad_maximum_fusion.rows_ref, bf16[4,128,128]{2,1,0:T(8,128)(2,1)S(1)} %copy-done.2, ...), custom_call_target="tpu_custom_call" | custom-call | flops 62914560 | bytes 327680 | tf_op jit(solution)/shard_map/begin/pallas_call | solution.py:261
  12.5 0.0 collective-permute-done.3.far_ref
  12.5 1.0 %end.1 = (bf16[4,4096]{1,0:T(4,128)(2,1)S(1)}, bf16[4,4096]{1,0:T(4,128)(2,1)S(1)}, bf16[4,4096]{1,0:T(4,128)(2,1)S(1)}, bf16[4,4096]{1,0:T(4,128)(2,1)S(1)}) custom-call(bf16[4,128,128]{2,1,0:T(8,128)(2,1)S(1)} %get-tuple-element.14.query_ref, bf16[4,128,128]{2,1,0:T(8,128)(2,1)S(1)} %get-tuple-element.15.phi_ref, ...), custom_call_target="tpu_custom_call" | custom-call | flops 33554432 | bytes 262144 | tf_op jit(solution)/shard_map/end/pallas_call | solution.py:276
  13.5 2.3 %collective-permute-start.4 = (bf16[4,4096]{1,0:T(4,128)(2,1)S(1)}, bf16[4,4096]{1,0:T(4,128)(2,1)S(1)}, u32[]{:S(2)}, u32[]{:S(2)}) collective-permute-start(bf16[4,4096]{1,0:T(4,128)(2,1)S(1)} %get-tuple-element.19), channel_id=1, source_target_pairs={{0,12},{4,8},{8,4},{12,0},{1,13},{5,9},{9,5},{13,1},{2,14},{6,10},... | collective-permute-start | bytes 98312 | tf_op jit(solution)/shard_map/ppermute | solution.py:314
  15.9 0.4 %collective-permute-start.5 = (bf16[4,4096]{1,0:T(4,128)(2,1)S(1)}, bf16[4,4096]{1,0:T(4,128)(2,1)S(1)}, u32[]{:S(2)}, u32[]{:S(2)}) collective-permute-start(bf16[4,4096]{1,0:T(4,128)(2,1)S(1)} %get-tuple-element.20), channel_id=1, source_target_pairs={{0,8},{4,12},{8,0},{12,4},{1,9},{5,13},{9,1},{13,5},{2,10},{6,14},... | collective-permute-start | bytes 98312 | tf_op jit(solution)/shard_map/ppermute | solution.py:314
  16.3 1.7 %collective-permute-start.6 = (bf16[4,4096]{1,0:T(4,128)(2,1)S(1)}, bf16[4,4096]{1,0:T(4,128)(2,1)S(1)}, u32[]{:S(2)}, u32[]{:S(2)}) collective-permute-start(bf16[4,4096]{1,0:T(4,128)(2,1)S(1)} %get-tuple-element.21), channel_id=1, source_target_pairs={{0,4},{4,0},{8,12},{12,8},{1,5},{5,1},{9,13},{13,9},{2,6},{6,2},{1... | collective-permute-start | bytes 98312 | tf_op jit(solution)/shard_map/ppermute | solution.py:314
  18.0 0.0 copy-done.3
  18.0 0.1 broadcast_compare_fusion.2
  18.0 1.6 %collective-permute-done.4 = bf16[4,4096]{1,0:T(4,128)(2,1)S(1)} collective-permute-done((bf16[4,4096]{1,0:T(4,128)(2,1)S(1)}, bf16[4,4096]{1,0:T(4,128)(2,1)S(1)}, u32[]{:S(2)}, u32[]{:S(2)}) %collective-permute-start.4) | collective-permute-done | bytes 32800 | tf_op jit(solution)/shard_map/ppermute | solution.py:314
  19.6 1.0 %collective-permute-done.5 = bf16[4,4096]{1,0:T(4,128)(2,1)S(1)} collective-permute-done((bf16[4,4096]{1,0:T(4,128)(2,1)S(1)}, bf16[4,4096]{1,0:T(4,128)(2,1)S(1)}, u32[]{:S(2)}, u32[]{:S(2)}) %collective-permute-start.5) | collective-permute-done | bytes 32800 | tf_op jit(solution)/shard_map/ppermute | solution.py:314
  20.7 0.0 collective-permute-done.6
  20.7 0.7 %select_select_fusion = bf16[4,4096]{1,0:T(4,128)(2,1)} fusion(bf16[4,4096]{1,0:T(4,128)(2,1)S(1)} %collective-permute-done.4, bf16[4,4096]{1,0:T(4,128)(2,1)S(1)} %collective-permute-done.5, bf16[4,4096]{1,0:T(4,128)(2,1)S(1)} %collective-permute-done.6, bf16[4,4096]{1,0:T(4,128)(2,1)S(1)} %get-tuple-element.22, pred[4]{0:T(512)(128)(4,1)S(1)} %get-tuple-element.27, ...), kind=kLoop, calls=%fused_computation.3 | loop fusion | flops 49152 | bytes 163852 | tf_op jit(solution)/shard_map/jit(_where)/select_n | solution.py:316
  (1 shorter events, 0.0 us)
Async XLA Ops:
  0.0 7.7 %copy-start.2 = (bf16[4,128,128]{2,1,0:T(8,128)(2,1)S(1)}, bf16[4,128,128]{2,1,0:T(8,128)(2,1)}, u32[]{:S(2)}) copy-start(bf16[4,128,128]{2,1,0:T(8,128)(2,1)} %weight_ref.3) | copy-start | bytes 393220
  0.0 7.7 %copy-start = (bf16[1,4096,512]{2,1,0:T(8,128)(2,1)S(1)}, bf16[1,4096,512]{2,1,0:T(8,128)(2,1)}, u32[]{:S(2)}) copy-start(bf16[1,4096,512]{2,1,0:T(8,128)(2,1)} %keys_ref.3) | copy-start | bytes 12582916
  0.0 7.7 %copy-start.1 = (bf16[1,4096,512]{2,1,0:T(8,128)(2,1)S(1)}, bf16[1,4096,512]{2,1,0:T(8,128)(2,1)}, u32[]{:S(2)}) copy-start(bf16[1,4096,512]{2,1,0:T(8,128)(2,1)} %values_ref.3) | copy-start | bytes 12582916
  1.0 9.7 %collective-permute-start.1 = (bf16[4,5120]{1,0:T(4,128)(2,1)S(1)}, bf16[4,5120]{1,0:T(4,128)(2,1)S(1)}, u32[]{:S(2)}, u32[]{:S(2)}) collective-permute-start(bf16[4,5120]{1,0:T(4,128)(2,1)S(1)} %pack.1), channel_id=1, source_target_pairs={{12,0},{0,4},{4,8},{8,12},{13,1},{1,5},{5,9},{9,13},{14,2},{2,6},{... | collective-permute-start | bytes 122888 | tf_op jit(solution)/shard_map/ppermute | solution.py:298
  4.0 6.6 %collective-permute-start.2 = (bf16[4,5120]{1,0:T(4,128)(2,1)S(1)}, bf16[4,5120]{1,0:T(4,128)(2,1)S(1)}, u32[]{:S(2)}, u32[]{:S(2)}) collective-permute-start(bf16[4,5120]{1,0:T(4,128)(2,1)S(1)} %pack.1), channel_id=1, source_target_pairs={{4,0},{8,4},{12,8},{0,12},{5,1},{9,5},{13,9},{1,13},{6,2},{10,6},{... | collective-permute-start | bytes 122888 | tf_op jit(solution)/shard_map/ppermute | solution.py:298
  6.1 4.9 %collective-permute-start = (bf16[4,5120]{1,0:T(4,128)(2,1)S(1)}, bf16[4,5120]{1,0:T(4,128)(2,1)S(1)}, u32[]{:S(2)}, u32[]{:S(2)}) collective-permute-start(bf16[4,5120]{1,0:T(4,128)(2,1)S(1)} %pack.1), channel_id=1, source_target_pairs={{8,0},{12,4},{0,8},{4,12},{9,1},{13,5},{1,9},{5,13},{10,2},{14,6},... | collective-permute-start | bytes 122888 | tf_op jit(solution)/shard_map/ppermute | solution.py:298
  7.8 10.2 %copy-start.3 = (s32[32]{0:T(128)S(1)}, s32[32]{0:T(128)}, u32[]{:S(2)}) copy-start(s32[32]{0:T(128)} %param.15) | copy-start | bytes 388
  10.5 2.0 %collective-permute-start.3 = (bf16[1168,128]{1,0:T(8,128)(2,1)S(1)}, bf16[1168,128]{1,0:T(8,128)(2,1)S(1)}, u32[]{:S(2)}, u32[]{:S(2)}) collective-permute-start(bf16[1168,128]{1,0:T(8,128)(2,1)S(1)} %prefill.1.near_ref), channel_id=1, source_target_pairs={{0,1},{1,0},{2,3},{3,2},{4,5},{5,4},{6,7},{7,6},{8,9},{9,8},{10,11... | collective-permute-start | bytes 897032 | tf_op jit(solution)/shard_map/ppermute | solution.py:304
  13.5 6.1 %collective-permute-start.4 = (bf16[4,4096]{1,0:T(4,128)(2,1)S(1)}, bf16[4,4096]{1,0:T(4,128)(2,1)S(1)}, u32[]{:S(2)}, u32[]{:S(2)}) collective-permute-start(bf16[4,4096]{1,0:T(4,128)(2,1)S(1)} %get-tuple-element.19), channel_id=1, source_target_pairs={{0,12},{4,8},{8,4},{12,0},{1,13},{5,9},{9,5},{13,1},{2,14},{6,10},... | collective-permute-start | bytes 98312 | tf_op jit(solution)/shard_map/ppermute | solution.py:314
  15.9 4.8 %collective-permute-start.5 = (bf16[4,4096]{1,0:T(4,128)(2,1)S(1)}, bf16[4,4096]{1,0:T(4,128)(2,1)S(1)}, u32[]{:S(2)}, u32[]{:S(2)}) collective-permute-start(bf16[4,4096]{1,0:T(4,128)(2,1)S(1)} %get-tuple-element.20), channel_id=1, source_target_pairs={{0,8},{4,12},{8,0},{12,4},{1,9},{5,13},{9,1},{13,5},{2,10},{6,14},... | collective-permute-start | bytes 98312 | tf_op jit(solution)/shard_map/ppermute | solution.py:314
  16.3 4.4 %collective-permute-start.6 = (bf16[4,4096]{1,0:T(4,128)(2,1)S(1)}, bf16[4,4096]{1,0:T(4,128)(2,1)S(1)}, u32[]{:S(2)}, u32[]{:S(2)}) collective-permute-start(bf16[4,4096]{1,0:T(4,128)(2,1)S(1)} %get-tuple-element.21), channel_id=1, source_target_pairs={{0,4},{4,0},{8,12},{12,8},{1,5},{5,1},{9,13},{13,9},{2,6},{6,2},{1... | collective-permute-start | bytes 98312 | tf_op jit(solution)/shard_map/ppermute | solution.py:314

commit v25 on v23

--- a/solution.py
+++ b/solution.py
@@ -81,10 +81,11 @@
     begin = lengths_ref[0] - WINDOW - lax.axis_index("sub") * span
     first = jnp.clip(begin, 0, span - SLAB)
     first = pl.multiple_of(first - lax.rem(first, 16), 16)
+    part = feats + SLAB
     slabs = []
     for i, source in enumerate((keys_ref, values_ref)):
         for g in range(heads):
-            at = heads * feats + 16 + (i * heads + g) * SLAB
+            at = g * part + feats if i else heads * part + 16 + g * SLAB
             slabs.append(
                 pltpu.make_async_copy(
                     source.at[0, pl.ds(first, SLAB), g * head_size : (g + 1) * head_size],
@@ -125,18 +126,19 @@
             project(c + 1)
         collect(c)
 
+    back = 1.0 / (feats * feats)
     tile = []
     for g in range(heads):
         half = g % 2
-        part = state_ref[g // 2, half * feats : (half + 1) * feats, half * head_size : (half + 1) * head_size]
-        out_ref[g * feats : (g + 1) * feats, :] = part.astype(jnp.bfloat16)
+        state = state_ref[g // 2, half * feats : (half + 1) * feats, half * head_size : (half + 1) * head_size]
+        out_ref[g * part : g * part + feats, :] = (state * back).astype(jnp.bfloat16)
         sums = norm_ref[g // 2, half * feats : (half + 1) * feats, :]
-        tile.append(jnp.sum(sums.T, axis=0, keepdims=True))
+        tile.append(jnp.sum(sums.T, axis=0, keepdims=True) * back)
     slot = first + lax.broadcasted_iota(jnp.int32, (1, head_size), 1)
     tile.append(jnp.zeros((MASK_ROW - heads, head_size), jnp.float32))
     tile.append(jnp.where((slot >= begin) & (slot < begin + WINDOW), 1.0, 0.0))
     tile.append(jnp.zeros((15 - MASK_ROW, head_size), jnp.float32))
-    out_ref[heads * feats : heads * feats + 16, :] = jnp.concatenate(tile, axis=0).astype(jnp.bfloat16)
+    out_ref[heads * part : heads * part + 16, :] = jnp.concatenate(tile, axis=0).astype(jnp.bfloat16)
     for slab in slabs:
         slab.wait()
 
@@ -173,21 +175,20 @@
 def share(query, phi, scale, ref, g, heads):
     head_size = query.shape[1]
     feats = phi.shape[1]
-    tile_at = heads * feats
+    part = feats + SLAB
+    tile_at = heads * part
     tile = ref[tile_at : tile_at + 16, :].astype(jnp.float32)
-    linear = jnp.dot(phi, ref[g * feats : (g + 1) * feats, :], preferred_element_type=jnp.float32)
     at = tile_at + 16 + g * SLAB
     keys = ref[at : at + SLAB, :]
-    at += heads * SLAB
-    values = ref[at : at + SLAB, :]
     keys_wide = keys.astype(jnp.float32)
     key_scale = lax.rsqrt(jnp.mean((keys_wide * keys_wide).T, axis=0, keepdims=True) + EPS)
-    score = lax.dot_general(query, keys, NT, preferred_element_type=jnp.float32) * scale * key_scale
+    score = lax.dot_general(query, keys, NT, preferred_element_type=jnp.float32) * scale[:, :SLAB] * key_scale
     weights = jnp.exp(score) * tile[MASK_ROW : MASK_ROW + 1, :SLAB]
-    back = 1.0 / (feats * feats)
-    num = linear * back + jnp.dot(weights.astype(jnp.bfloat16), values, preferred_element_type=jnp.float32)
-    den = jnp.sum(weights, axis=-1, keepdims=True)
-    return num, den + jnp.sum(phi.astype(jnp.float32) * tile[g : g + 1], axis=-1, keepdims=True) * back
+    both = jnp.concatenate([phi, weights.astype(jnp.bfloat16)], axis=1)
+    num = jnp.dot(both, ref[g * part : (g + 1) * part, :], preferred_element_type=jnp.float32)
+    rest = jnp.zeros((query.shape[0], feats - SLAB), jnp.float32)
+    den = phi.astype(jnp.float32) * tile[g : g + 1] + jnp.concatenate([weights, rest], axis=1)
+    return num, jnp.sum(den, axis=-1, keepdims=True)
 
 
 def begin_kernel(rows_ref, weight_ref, near_ref, query_ref, phi_ref, num_ref, den_ref, scale_ref):
@@ -212,6 +213,7 @@
         own_key = own_key * lax.rsqrt(jnp.mean(own_key * own_key, axis=-1, keepdims=True) + EPS)
         own_score = jnp.sum(wide * jnp.concatenate([own_key] * group, axis=0), axis=-1, keepdims=True) * scale
         own_weight = jnp.exp(own_score)
+        scale = jnp.broadcast_to(scale, query.shape)
         num, den = share(query, phi, scale, near_ref, g, heads)
         num += own_weight.astype(jnp.bfloat16).astype(jnp.float32) * jnp.concatenate([own_value] * group, axis=0)
         ready.append((query, phi, num, den + own_weight, scale))
@@ -220,7 +222,7 @@
         phi_ref[g] = phi
         num_ref[g] = num
         den_ref[g] = jnp.broadcast_to(den, num.shape)
-        scale_ref[g] = jnp.broadcast_to(scale, num.shape)
+        scale_ref[g] = scale
 
 
 def end_kernel(query_ref, phi_ref, num_ref, den_ref, scale_ref, far_ref, *out_refs):
@@ -230,7 +232,7 @@
     count = asked // group
     ready = []
     for g in range(heads):
-        num, den = share(query_ref[g], phi_ref[g], scale_ref[g][:, :1], far_ref, g, heads)
+        num, den = share(query_ref[g], phi_ref[g], scale_ref[g], far_ref, g, heads)
         ready.append(((num_ref[g] + num) / (den_ref[g] + den)).astype(jnp.bfloat16))
     for g, result in enumerate(ready):
         for h in range(group):

time: 21.2 us -> 20.9 us (0.986)
  Pallas kernels: 5.31 us -> 4.89 us
    pallas_call x1, Pallas kernels: 0.75 us -> 0.51 us  [end(): pl.pallas_call(end_kernel, in_specs=[vmem] * 6, out_specs=[vmem] * parts,...]
where the time goes in v25:
time: 20.9 us; the launch traced here: 20.7 us
  starting transfers between devices  10.6 us (51%)
  Pallas kernels  4.89 us (23%)
  waiting for transfers between devices  3.48 us (17%)
  other arithmetic  0.93 us (4%)
  between operations  0.76 us (4%)
    ppermute x3, starting transfers between devices, body(): lax.ppermute(mine, 'sect', [(ask(i, k, sects), i) for i in range(sects)])  6.12 us
    ppermute x3, starting transfers between devices, body(): lax.ppermute(results[k], 'sect', [(i, partner(i, k, sects)) for i in rang...  4.45 us
    pallas_call x1, Pallas kernels, prefill(): pl.pallas_call(prefill_kernel, in_specs=[pl.BlockSpec(memory_space=pltpu....  2.77 us
    ppermute x3, waiting for transfers between devices, body(): lax.ppermute(results[k], 'sect', [(i, partner(i, k, sects)) for i in rang...  2.76 us
    pallas_call x1, Pallas kernels, pack(): pl.pallas_call(pack_kernel, in_specs=[pl.BlockSpec(memory_space=pltpu.Mem...  0.94 us
    select_n x1, other arithmetic, body(): out = jnp.where((prompts == source)[:, None], result, out)  0.71 us
    pallas_call x1, Pallas kernels, begin(): pl.pallas_call(begin_kernel, in_specs=[vmem] * 3, out_specs=[vmem] * 5, o...  0.67 us
    pallas_call x1, Pallas kernels, end(): pl.pallas_call(end_kernel, in_specs=[vmem] * 6, out_specs=[vmem] * parts,...  0.51 us
  transfers between devices with their start and end apart: 7, of which 5 were waited for; matrix products, arithmetic and copies ran while one was open for 1% of the time, Pallas kernels for 17%

profile of v25, /device:TPU:0, one launch (start us, length us, event | category | flops | bytes accessed | tf_op | source)
XLA Modules:
  0.0 20.7 jit_solution(1815388401261088495)
XLA Ops:
  0.0 0.0 copy-start.2
  0.0 0.0 copy-start
  0.0 0.0 copy-start.1
  0.0 0.9 %pack.1 = bf16[4,5120]{1,0:T(4,128)(2,1)S(1)} custom-call(bf16[4,4096]{1,0:T(4,128)(2,1)} %queries_ref.1, bf16[4,512]{1,0:T(4,128)(2,1)} %keys_ref.2, bf16[4,512]{1,0:T(4,128)(2,1)} %values_ref.2), custom_call_target="tpu_custom_call" | custom-call | flops 10000000000 | bytes 33554432 | tf_op jit(solution)/shard_map/pack/pallas_call | solution.py:47
  1.0 3.1 %collective-permute-start.1 = (bf16[4,5120]{1,0:T(4,128)(2,1)S(1)}, bf16[4,5120]{1,0:T(4,128)(2,1)S(1)}, u32[]{:S(2)}, u32[]{:S(2)}) collective-permute-start(bf16[4,5120]{1,0:T(4,128)(2,1)S(1)} %pack.1), channel_id=1, source_target_pairs={{12,0},{0,4},{4,8},{8,12},{13,1},{1,5},{5,9},{9,13},{14,2},{2,6},{... | collective-permute-start | bytes 122888 | tf_op jit(solution)/shard_map/ppermute | solution.py:288
  4.0 2.1 %collective-permute-start.2 = (bf16[4,5120]{1,0:T(4,128)(2,1)S(1)}, bf16[4,5120]{1,0:T(4,128)(2,1)S(1)}, u32[]{:S(2)}, u32[]{:S(2)}) collective-permute-start(bf16[4,5120]{1,0:T(4,128)(2,1)S(1)} %pack.1), channel_id=1, source_target_pairs={{4,0},{8,4},{12,8},{0,12},{5,1},{9,5},{13,9},{1,13},{6,2},{10,6},{... | collective-permute-start | bytes 122888 | tf_op jit(solution)/shard_map/ppermute | solution.py:288
  6.1 0.9 %collective-permute-start = (bf16[4,5120]{1,0:T(4,128)(2,1)S(1)}, bf16[4,5120]{1,0:T(4,128)(2,1)S(1)}, u32[]{:S(2)}, u32[]{:S(2)}) collective-permute-start(bf16[4,5120]{1,0:T(4,128)(2,1)S(1)} %pack.1), channel_id=1, source_target_pairs={{8,0},{12,4},{0,8},{4,12},{9,1},{13,5},{1,9},{5,13},{10,2},{14,6},... | collective-permute-start | bytes 122888 | tf_op jit(solution)/shard_map/ppermute | solution.py:288
  7.7 0.0 copy-done.2
  7.7 0.0 copy-done
  7.7 0.0 copy-done.1
  7.8 0.0 copy-start.3
  7.8 2.8 %prefill.1.near_ref = bf16[1168,128]{1,0:T(8,128)(2,1)S(1)} custom-call(s32[1]{0:T(128)S(6)} %copy.9.lengths_ref, bf16[1,4096,512]{2,1,0:T(8,128)(2,1)S(1)} %copy-done, bf16[1,4096,512]{2,1,0:T(8,128)(2,1)S(1)} %copy-done.1, bf16[4,128,128]{2,1,0:T(8,128)(2,1)S(1)} %copy-done.2), custom_call_target="tpu_custom_call" | custom-call | flops 1073741824 | bytes 8388608 | tf_op jit(solution)/shard_map/prefill/pallas_call | solution.py:150
  10.5 0.1 collective-permute-start.3
  10.6 0.0 collective-permute-done.1
  10.6 0.0 collective-permute-done.2
  10.7 0.3 %collective-permute-done = bf16[4,5120]{1,0:T(4,128)(2,1)S(1)} collective-permute-done((bf16[4,5120]{1,0:T(4,128)(2,1)S(1)}, bf16[4,5120]{1,0:T(4,128)(2,1)S(1)}, u32[]{:S(2)}, u32[]{:S(2)}) %collective-permute-start) | collective-permute-done | bytes 40992 | tf_op jit(solution)/shard_map/ppermute | solution.py:288
  11.0 0.1 pad_maximum_fusion.rows_ref
  11.1 0.7 %begin.1 = (bf16[4,128,128]{2,1,0:T(8,128)(2,1)S(1)}, bf16[4,128,128]{2,1,0:T(8,128)(2,1)S(1)}, f32[4,128,128]{2,1,0:T(8,128)S(1)}, f32[4,128,128]{2,1,0:T(8,128)S(1)}, f32[4,128,128]{2,1,0:T(8,128)S(1)}) custom-call(bf16[16,5120]{1,0:T(8,128)(2,1)S(1)} %pad_maximum_fusion.rows_ref, bf16[4,128,128]{2,1,0:T(8,128)(2,1)S(1)} %copy-done.2, ...), custom_call_target="tpu_custom_call" | custom-call | flops 62914560 | bytes 327680 | tf_op jit(solution)/shard_map/begin/pallas_call | solution.py:251
  11.8 0.4 %collective-permute-done.3.far_ref = bf16[1168,128]{1,0:T(8,128)(2,1)S(1)} collective-permute-done((bf16[1168,128]{1,0:T(8,128)(2,1)S(1)}, bf16[1168,128]{1,0:T(8,128)(2,1)S(1)}, u32[]{:S(2)}, u32[]{:S(2)}) %collective-permute-start.3) | collective-permute-done | bytes 299040 | tf_op jit(solution)/shard_map/ppermute | solution.py:294
  12.2 0.5 %end.1 = (bf16[4,4096]{1,0:T(4,128)(2,1)S(1)}, bf16[4,4096]{1,0:T(4,128)(2,1)S(1)}, bf16[4,4096]{1,0:T(4,128)(2,1)S(1)}, bf16[4,4096]{1,0:T(4,128)(2,1)S(1)}) custom-call(bf16[4,128,128]{2,1,0:T(8,128)(2,1)S(1)} %get-tuple-element.14.query_ref, bf16[4,128,128]{2,1,0:T(8,128)(2,1)S(1)} %get-tuple-element.15.phi_ref, ...), custom_call_target="tpu_custom_call" | custom-call | flops 33554432 | bytes 262144 | tf_op jit(solution)/shard_map/end/pallas_call | solution.py:266
  12.7 2.0 %collective-permute-start.4 = (bf16[4,4096]{1,0:T(4,128)(2,1)S(1)}, bf16[4,4096]{1,0:T(4,128)(2,1)S(1)}, u32[]{:S(2)}, u32[]{:S(2)}) collective-permute-start(bf16[4,4096]{1,0:T(4,128)(2,1)S(1)} %get-tuple-element.19), channel_id=1, source_target_pairs={{0,12},{4,8},{8,4},{12,0},{1,13},{5,9},{9,5},{13,1},{2,14},{6,10},... | collective-permute-start | bytes 98312 | tf_op jit(solution)/shard_map/ppermute | solution.py:304
  14.7 1.1 %collective-permute-start.5 = (bf16[4,4096]{1,0:T(4,128)(2,1)S(1)}, bf16[4,4096]{1,0:T(4,128)(2,1)S(1)}, u32[]{:S(2)}, u32[]{:S(2)}) collective-permute-start(bf16[4,4096]{1,0:T(4,128)(2,1)S(1)} %get-tuple-element.20), channel_id=1, source_target_pairs={{0,8},{4,12},{8,0},{12,4},{1,9},{5,13},{9,1},{13,5},{2,10},{6,14},... | collective-permute-start | bytes 98312 | tf_op jit(solution)/shard_map/ppermute | solution.py:304
  15.8 1.3 %collective-permute-start.6 = (bf16[4,4096]{1,0:T(4,128)(2,1)S(1)}, bf16[4,4096]{1,0:T(4,128)(2,1)S(1)}, u32[]{:S(2)}, u32[]{:S(2)}) collective-permute-start(bf16[4,4096]{1,0:T(4,128)(2,1)S(1)} %get-tuple-element.21), channel_id=1, source_target_pairs={{0,4},{4,0},{8,12},{12,8},{1,5},{5,1},{9,13},{13,9},{2,6},{6,2},{1... | collective-permute-start | bytes 98312 | tf_op jit(solution)/shard_map/ppermute | solution.py:304
  17.2 0.0 copy-done.3
  17.2 0.1 broadcast_compare_fusion.2
  17.3 1.6 %collective-permute-done.4 = bf16[4,4096]{1,0:T(4,128)(2,1)S(1)} collective-permute-done((bf16[4,4096]{1,0:T(4,128)(2,1)S(1)}, bf16[4,4096]{1,0:T(4,128)(2,1)S(1)}, u32[]{:S(2)}, u32[]{:S(2)}) %collective-permute-start.4) | collective-permute-done | bytes 32800 | tf_op jit(solution)/shard_map/ppermute | solution.py:304
  18.8 1.1 %collective-permute-done.5 = bf16[4,4096]{1,0:T(4,128)(2,1)S(1)} collective-permute-done((bf16[4,4096]{1,0:T(4,128)(2,1)S(1)}, bf16[4,4096]{1,0:T(4,128)(2,1)S(1)}, u32[]{:S(2)}, u32[]{:S(2)}) %collective-permute-start.5) | collective-permute-done | bytes 32800 | tf_op jit(solution)/shard_map/ppermute | solution.py:304
  20.0 0.1 collective-permute-done.6
  20.0 0.7 %select_select_fusion = bf16[4,4096]{1,0:T(4,128)(2,1)} fusion(bf16[4,4096]{1,0:T(4,128)(2,1)S(1)} %collective-permute-done.4, bf16[4,4096]{1,0:T(4,128)(2,1)S(1)} %collective-permute-done.5, bf16[4,4096]{1,0:T(4,128)(2,1)S(1)} %collective-permute-done.6, bf16[4,4096]{1,0:T(4,128)(2,1)S(1)} %get-tuple-element.22, pred[4]{0:T(512)(128)(4,1)S(1)} %get-tuple-element.27, ...), kind=kLoop, calls=%fused_computation.3 | loop fusion | flops 49152 | bytes 163852 | tf_op jit(solution)/shard_map/jit(_where)/select_n | solution.py:306
  (1 shorter events, 0.0 us)
Async XLA Ops:
  0.0 7.7 %copy-start.2 = (bf16[4,128,128]{2,1,0:T(8,128)(2,1)S(1)}, bf16[4,128,128]{2,1,0:T(8,128)(2,1)}, u32[]{:S(2)}) copy-start(bf16[4,128,128]{2,1,0:T(8,128)(2,1)} %weight_ref.3) | copy-start | bytes 393220
  0.0 7.7 %copy-start = (bf16[1,4096,512]{2,1,0:T(8,128)(2,1)S(1)}, bf16[1,4096,512]{2,1,0:T(8,128)(2,1)}, u32[]{:S(2)}) copy-start(bf16[1,4096,512]{2,1,0:T(8,128)(2,1)} %keys_ref.3) | copy-start | bytes 12582916
  0.0 7.7 %copy-start.1 = (bf16[1,4096,512]{2,1,0:T(8,128)(2,1)S(1)}, bf16[1,4096,512]{2,1,0:T(8,128)(2,1)}, u32[]{:S(2)}) copy-start(bf16[1,4096,512]{2,1,0:T(8,128)(2,1)} %values_ref.3) | copy-start | bytes 12582916
  1.0 9.7 %collective-permute-start.1 = (bf16[4,5120]{1,0:T(4,128)(2,1)S(1)}, bf16[4,5120]{1,0:T(4,128)(2,1)S(1)}, u32[]{:S(2)}, u32[]{:S(2)}) collective-permute-start(bf16[4,5120]{1,0:T(4,128)(2,1)S(1)} %pack.1), channel_id=1, source_target_pairs={{12,0},{0,4},{4,8},{8,12},{13,1},{1,5},{5,9},{9,13},{14,2},{2,6},{... | collective-permute-start | bytes 122888 | tf_op jit(solution)/shard_map/ppermute | solution.py:288
  4.0 6.6 %collective-permute-start.2 = (bf16[4,5120]{1,0:T(4,128)(2,1)S(1)}, bf16[4,5120]{1,0:T(4,128)(2,1)S(1)}, u32[]{:S(2)}, u32[]{:S(2)}) collective-permute-start(bf16[4,5120]{1,0:T(4,128)(2,1)S(1)} %pack.1), channel_id=1, source_target_pairs={{4,0},{8,4},{12,8},{0,12},{5,1},{9,5},{13,9},{1,13},{6,2},{10,6},{... | collective-permute-start | bytes 122888 | tf_op jit(solution)/shard_map/ppermute | solution.py:288
  6.1 4.9 %collective-permute-start = (bf16[4,5120]{1,0:T(4,128)(2,1)S(1)}, bf16[4,5120]{1,0:T(4,128)(2,1)S(1)}, u32[]{:S(2)}, u32[]{:S(2)}) collective-permute-start(bf16[4,5120]{1,0:T(4,128)(2,1)S(1)} %pack.1), channel_id=1, source_target_pairs={{8,0},{12,4},{0,8},{4,12},{9,1},{13,5},{1,9},{5,13},{10,2},{14,6},... | collective-permute-start | bytes 122888 | tf_op jit(solution)/shard_map/ppermute | solution.py:288
  7.8 9.4 %copy-start.3 = (s32[32]{0:T(128)S(1)}, s32[32]{0:T(128)}, u32[]{:S(2)}) copy-start(s32[32]{0:T(128)} %param.15) | copy-start | bytes 388
  10.5 1.7 %collective-permute-start.3 = (bf16[1168,128]{1,0:T(8,128)(2,1)S(1)}, bf16[1168,128]{1,0:T(8,128)(2,1)S(1)}, u32[]{:S(2)}, u32[]{:S(2)}) collective-permute-start(bf16[1168,128]{1,0:T(8,128)(2,1)S(1)} %prefill.1.near_ref), channel_id=1, source_target_pairs={{0,1},{1,0},{2,3},{3,2},{4,5},{5,4},{6,7},{7,6},{8,9},{9,8},{10,11... | collective-permute-start | bytes 897032 | tf_op jit(solution)/shard_map/ppermute | solution.py:294
  12.7 6.1 %collective-permute-start.4 = (bf16[4,4096]{1,0:T(4,128)(2,1)S(1)}, bf16[4,4096]{1,0:T(4,128)(2,1)S(1)}, u32[]{:S(2)}, u32[]{:S(2)}) collective-permute-start(bf16[4,4096]{1,0:T(4,128)(2,1)S(1)} %get-tuple-element.19), channel_id=1, source_target_pairs={{0,12},{4,8},{8,4},{12,0},{1,13},{5,9},{9,5},{13,1},{2,14},{6,10},... | collective-permute-start | bytes 98312 | tf_op jit(solution)/shard_map/ppermute | solution.py:304
  14.7 5.3 %collective-permute-start.5 = (bf16[4,4096]{1,0:T(4,128)(2,1)S(1)}, bf16[4,4096]{1,0:T(4,128)(2,1)S(1)}, u32[]{:S(2)}, u32[]{:S(2)}) collective-permute-start(bf16[4,4096]{1,0:T(4,128)(2,1)S(1)} %get-tuple-element.20), channel_id=1, source_target_pairs={{0,8},{4,12},{8,0},{12,4},{1,9},{5,13},{9,1},{13,5},{2,10},{6,14},... | collective-permute-start | bytes 98312 | tf_op jit(solution)/shard_map/ppermute | solution.py:304
  15.8 4.2 %collective-permute-start.6 = (bf16[4,4096]{1,0:T(4,128)(2,1)S(1)}, bf16[4,4096]{1,0:T(4,128)(2,1)S(1)}, u32[]{:S(2)}, u32[]{:S(2)}) collective-permute-start(bf16[4,4096]{1,0:T(4,128)(2,1)S(1)} %get-tuple-element.21), channel_id=1, source_target_pairs={{0,4},{4,0},{8,12},{12,8},{1,5},{5,1},{9,13},{13,9},{2,6},{6,2},{1... | collective-permute-start | bytes 98312 | tf_op jit(solution)/shard_map/ppermute | solution.py:304

commit v26 on v25

--- a/solution.py
+++ b/solution.py
@@ -75,8 +75,7 @@
     wide_ref[...] = jnp.zeros_like(wide_ref)
     for g in range(heads):
         half = g % 2
-        turned = weight_ref[g].astype(jnp.float32).T.astype(jnp.bfloat16)
-        wide_ref[g // 2, half * feats : (half + 1) * feats, half * head_size : (half + 1) * head_size] = turned
+        wide_ref[g // 2, half * head_size : (half + 1) * head_size, half * feats : (half + 1) * feats] = weight_ref[g]
 
     begin = lengths_ref[0] - WINDOW - lax.axis_index("sub") * span
     first = jnp.clip(begin, 0, span - SLAB)
@@ -97,13 +96,9 @@
 
     def project(c):
         for j in range(pairs):
-            proj = lax.dot_general(
-                wide_ref[j],
-                keys_at[c * BLOCK : (c + 1) * BLOCK, j * 2 * head_size : (j + 1) * 2 * head_size],
-                NT,
-                preferred_element_type=jnp.float32,
-            )
-            proj_ref[c % 2, j] = proj.astype(jnp.bfloat16)
+            keys = keys_at[c * BLOCK : (c + 1) * BLOCK, j * 2 * head_size : (j + 1) * 2 * head_size]
+            proj = jnp.dot(keys, wide_ref[j], preferred_element_type=jnp.float32)
+            proj_ref[c % 2, j] = proj.astype(jnp.bfloat16).T
 
     def collect(c):
         position = c * BLOCK + lax.broadcasted_iota(jnp.int32, (1, BLOCK), 1)

time: 20.9 us -> 21.3 us (1.019)
  Pallas kernels: 4.89 us -> 5.35 us
    pallas_call x1, Pallas kernels: 2.77 us -> 3.24 us  [prefill(): pl.pallas_call(prefill_kernel, in_specs=[pl.BlockSpec(memory_space=pltpu....]
    ppermute x3, waiting for transfers between devices: 0.33 us -> 0.01 us  [body(): lax.ppermute(mine, 'sect', [(ask(i, k, sects), i) for i in range(sects)])]
    ppermute x1, waiting for transfers between devices: 0.39 us -> 0.7 us  [body(): far = lax.ppermute(near, 'sub', [(0, 1), (1, 0)])]
  transfers between devices with their start and end apart: 7 -> 7, of which waited for: 5 -> 4; matrix products, arithmetic and copies ran while one was open for 1% -> 1% of each run, Pallas kernels for 17% -> 19%
where the time goes in v26:
time: 21.3 us; the launch traced here: 21.1 us
  starting transfers between devices  10.6 us (50%)
  Pallas kernels  5.35 us (25%)
  waiting for transfers between devices  3.39 us (16%)
  other arithmetic  0.93 us (4%)
  between operations  0.77 us (4%)
    ppermute x3, starting transfers between devices, body(): lax.ppermute(mine, 'sect', [(ask(i, k, sects), i) for i in range(sects)])  6.12 us
    ppermute x3, starting transfers between devices, body(): lax.ppermute(results[k], 'sect', [(i, partner(i, k, sects)) for i in rang...  4.45 us
    pallas_call x1, Pallas kernels, prefill(): pl.pallas_call(prefill_kernel, in_specs=[pl.BlockSpec(memory_space=pltpu....  3.24 us
    ppermute x3, waiting for transfers between devices, body(): lax.ppermute(results[k], 'sect', [(i, partner(i, k, sects)) for i in rang...  2.68 us
    pallas_call x1, Pallas kernels, pack(): pl.pallas_call(pack_kernel, in_specs=[pl.BlockSpec(memory_space=pltpu.Mem...  0.94 us
    select_n x1, other arithmetic, body(): out = jnp.where((prompts == source)[:, None], result, out)  0.71 us
    ppermute x1, waiting for transfers between devices, body(): far = lax.ppermute(near, 'sub', [(0, 1), (1, 0)])  0.7 us
    pallas_call x1, Pallas kernels, begin(): pl.pallas_call(begin_kernel, in_specs=[vmem] * 3, out_specs=[vmem] * 5, o...  0.67 us
  transfers between devices with their start and end apart: 7, of which 4 were waited for; matrix products, arithmetic and copies ran while one was open for 1% of the time, Pallas kernels for 19%

profile of v26, /device:TPU:0, one launch (start us, length us, event | category | flops | bytes accessed | tf_op | source)
XLA Modules:
  0.0 21.1 jit_solution(13767632695575181659)
XLA Ops:
  0.0 0.0 copy-start.2
  0.0 0.0 copy-start
  0.0 0.0 copy-start.1
  0.0 0.9 %pack.1 = bf16[4,5120]{1,0:T(4,128)(2,1)S(1)} custom-call(bf16[4,4096]{1,0:T(4,128)(2,1)} %queries_ref.1, bf16[4,512]{1,0:T(4,128)(2,1)} %keys_ref.2, bf16[4,512]{1,0:T(4,128)(2,1)} %values_ref.2), custom_call_target="tpu_custom_call" | custom-call | flops 10000000000 | bytes 33554432 | tf_op jit(solution)/shard_map/pack/pallas_call | solution.py:47
  1.0 3.1 %collective-permute-start.1 = (bf16[4,5120]{1,0:T(4,128)(2,1)S(1)}, bf16[4,5120]{1,0:T(4,128)(2,1)S(1)}, u32[]{:S(2)}, u32[]{:S(2)}) collective-permute-start(bf16[4,5120]{1,0:T(4,128)(2,1)S(1)} %pack.1), channel_id=1, source_target_pairs={{12,0},{0,4},{4,8},{8,12},{13,1},{1,5},{5,9},{9,13},{14,2},{2,6},{... | collective-permute-start | bytes 122888 | tf_op jit(solution)/shard_map/ppermute | solution.py:283
  4.0 2.1 %collective-permute-start.2 = (bf16[4,5120]{1,0:T(4,128)(2,1)S(1)}, bf16[4,5120]{1,0:T(4,128)(2,1)S(1)}, u32[]{:S(2)}, u32[]{:S(2)}) collective-permute-start(bf16[4,5120]{1,0:T(4,128)(2,1)S(1)} %pack.1), channel_id=1, source_target_pairs={{4,0},{8,4},{12,8},{0,12},{5,1},{9,5},{13,9},{1,13},{6,2},{10,6},{... | collective-permute-start | bytes 122888 | tf_op jit(solution)/shard_map/ppermute | solution.py:283
  6.1 0.9 %collective-permute-start = (bf16[4,5120]{1,0:T(4,128)(2,1)S(1)}, bf16[4,5120]{1,0:T(4,128)(2,1)S(1)}, u32[]{:S(2)}, u32[]{:S(2)}) collective-permute-start(bf16[4,5120]{1,0:T(4,128)(2,1)S(1)} %pack.1), channel_id=1, source_target_pairs={{8,0},{12,4},{0,8},{4,12},{9,1},{13,5},{1,9},{5,13},{10,2},{14,6},... | collective-permute-start | bytes 122888 | tf_op jit(solution)/shard_map/ppermute | solution.py:283
  7.7 0.0 copy-done.2
  7.7 0.0 copy-done
  7.7 0.0 copy-done.1
  7.8 0.0 copy-start.3
  7.8 3.2 %prefill.1.near_ref = bf16[1168,128]{1,0:T(8,128)(2,1)S(1)} custom-call(s32[1]{0:T(128)S(6)} %copy.9.lengths_ref, bf16[1,4096,512]{2,1,0:T(8,128)(2,1)S(1)} %copy-done, bf16[1,4096,512]{2,1,0:T(8,128)(2,1)S(1)} %copy-done.1, bf16[4,128,128]{2,1,0:T(8,128)(2,1)S(1)} %copy-done.2), custom_call_target="tpu_custom_call" | custom-call | flops 1073741824 | bytes 8388608 | tf_op jit(solution)/shard_map/prefill/pallas_call | solution.py:145
  11.0 0.1 collective-permute-start.3
  11.1 0.0 collective-permute-done.1
  11.1 0.0 collective-permute-done.2
  11.2 0.0 collective-permute-done
  11.2 0.1 pad_maximum_fusion.rows_ref
  11.3 0.7 %begin.1 = (bf16[4,128,128]{2,1,0:T(8,128)(2,1)S(1)}, bf16[4,128,128]{2,1,0:T(8,128)(2,1)S(1)}, f32[4,128,128]{2,1,0:T(8,128)S(1)}, f32[4,128,128]{2,1,0:T(8,128)S(1)}, f32[4,128,128]{2,1,0:T(8,128)S(1)}) custom-call(bf16[16,5120]{1,0:T(8,128)(2,1)S(1)} %pad_maximum_fusion.rows_ref, bf16[4,128,128]{2,1,0:T(8,128)(2,1)S(1)} %copy-done.2, ...), custom_call_target="tpu_custom_call" | custom-call | flops 62914560 | bytes 327680 | tf_op jit(solution)/shard_map/begin/pallas_call | solution.py:246
  12.0 0.7 %collective-permute-done.3.far_ref = bf16[1168,128]{1,0:T(8,128)(2,1)S(1)} collective-permute-done((bf16[1168,128]{1,0:T(8,128)(2,1)S(1)}, bf16[1168,128]{1,0:T(8,128)(2,1)S(1)}, u32[]{:S(2)}, u32[]{:S(2)}) %collective-permute-start.3) | collective-permute-done | bytes 299040 | tf_op jit(solution)/shard_map/ppermute | solution.py:289
  12.7 0.5 %end.1 = (bf16[4,4096]{1,0:T(4,128)(2,1)S(1)}, bf16[4,4096]{1,0:T(4,128)(2,1)S(1)}, bf16[4,4096]{1,0:T(4,128)(2,1)S(1)}, bf16[4,4096]{1,0:T(4,128)(2,1)S(1)}) custom-call(bf16[4,128,128]{2,1,0:T(8,128)(2,1)S(1)} %get-tuple-element.14.query_ref, bf16[4,128,128]{2,1,0:T(8,128)(2,1)S(1)} %get-tuple-element.15.phi_ref, ...), custom_call_target="tpu_custom_call" | custom-call | flops 33554432 | bytes 262144 | tf_op jit(solution)/shard_map/end/pallas_call | solution.py:261
  13.2 1.5 %collective-permute-start.4 = (bf16[4,4096]{1,0:T(4,128)(2,1)S(1)}, bf16[4,4096]{1,0:T(4,128)(2,1)S(1)}, u32[]{:S(2)}, u32[]{:S(2)}) collective-permute-start(bf16[4,4096]{1,0:T(4,128)(2,1)S(1)} %get-tuple-element.19), channel_id=1, source_target_pairs={{0,12},{4,8},{8,4},{12,0},{1,13},{5,9},{9,5},{13,1},{2,14},{6,10},... | collective-permute-start | bytes 98312 | tf_op jit(solution)/shard_map/ppermute | solution.py:299
  14.7 1.6 %collective-permute-start.5 = (bf16[4,4096]{1,0:T(4,128)(2,1)S(1)}, bf16[4,4096]{1,0:T(4,128)(2,1)S(1)}, u32[]{:S(2)}, u32[]{:S(2)}) collective-permute-start(bf16[4,4096]{1,0:T(4,128)(2,1)S(1)} %get-tuple-element.20), channel_id=1, source_target_pairs={{0,8},{4,12},{8,0},{12,4},{1,9},{5,13},{9,1},{13,5},{2,10},{6,14},... | collective-permute-start | bytes 98312 | tf_op jit(solution)/shard_map/ppermute | solution.py:299
  16.3 1.3 %collective-permute-start.6 = (bf16[4,4096]{1,0:T(4,128)(2,1)S(1)}, bf16[4,4096]{1,0:T(4,128)(2,1)S(1)}, u32[]{:S(2)}, u32[]{:S(2)}) collective-permute-start(bf16[4,4096]{1,0:T(4,128)(2,1)S(1)} %get-tuple-element.21), channel_id=1, source_target_pairs={{0,4},{4,0},{8,12},{12,8},{1,5},{5,1},{9,13},{13,9},{2,6},{6,2},{1... | collective-permute-start | bytes 98312 | tf_op jit(solution)/shard_map/ppermute | solution.py:299
  17.6 0.0 copy-done.3
  17.6 0.1 broadcast_compare_fusion.2
  17.7 1.6 %collective-permute-done.4 = bf16[4,4096]{1,0:T(4,128)(2,1)S(1)} collective-permute-done((bf16[4,4096]{1,0:T(4,128)(2,1)S(1)}, bf16[4,4096]{1,0:T(4,128)(2,1)S(1)}, u32[]{:S(2)}, u32[]{:S(2)}) %collective-permute-start.4) | collective-permute-done | bytes 32800 | tf_op jit(solution)/shard_map/ppermute | solution.py:299
  19.3 1.0 %collective-permute-done.5 = bf16[4,4096]{1,0:T(4,128)(2,1)S(1)} collective-permute-done((bf16[4,4096]{1,0:T(4,128)(2,1)S(1)}, bf16[4,4096]{1,0:T(4,128)(2,1)S(1)}, u32[]{:S(2)}, u32[]{:S(2)}) %collective-permute-start.5) | collective-permute-done | bytes 32800 | tf_op jit(solution)/shard_map/ppermute | solution.py:299
  20.3 0.1 collective-permute-done.6
  20.4 0.7 %select_select_fusion = bf16[4,4096]{1,0:T(4,128)(2,1)} fusion(bf16[4,4096]{1,0:T(4,128)(2,1)S(1)} %collective-permute-done.4, bf16[4,4096]{1,0:T(4,128)(2,1)S(1)} %collective-permute-done.5, bf16[4,4096]{1,0:T(4,128)(2,1)S(1)} %collective-permute-done.6, bf16[4,4096]{1,0:T(4,128)(2,1)S(1)} %get-tuple-element.22, pred[4]{0:T(512)(128)(4,1)S(1)} %get-tuple-element.27, ...), kind=kLoop, calls=%fused_computation.3 | loop fusion | flops 49152 | bytes 163852 | tf_op jit(solution)/shard_map/jit(_where)/select_n | solution.py:301
  (1 shorter events, 0.0 us)
Async XLA Ops:
  0.0 7.7 %copy-start.2 = (bf16[4,128,128]{2,1,0:T(8,128)(2,1)S(1)}, bf16[4,128,128]{2,1,0:T(8,128)(2,1)}, u32[]{:S(2)}) copy-start(bf16[4,128,128]{2,1,0:T(8,128)(2,1)} %weight_ref.3) | copy-start | bytes 393220
  0.0 7.7 %copy-start = (bf16[1,4096,512]{2,1,0:T(8,128)(2,1)S(1)}, bf16[1,4096,512]{2,1,0:T(8,128)(2,1)}, u32[]{:S(2)}) copy-start(bf16[1,4096,512]{2,1,0:T(8,128)(2,1)} %keys_ref.3) | copy-start | bytes 12582916
  0.0 7.7 %copy-start.1 = (bf16[1,4096,512]{2,1,0:T(8,128)(2,1)S(1)}, bf16[1,4096,512]{2,1,0:T(8,128)(2,1)}, u32[]{:S(2)}) copy-start(bf16[1,4096,512]{2,1,0:T(8,128)(2,1)} %values_ref.3) | copy-start | bytes 12582916
  1.0 10.1 %collective-permute-start.1 = (bf16[4,5120]{1,0:T(4,128)(2,1)S(1)}, bf16[4,5120]{1,0:T(4,128)(2,1)S(1)}, u32[]{:S(2)}, u32[]{:S(2)}) collective-permute-start(bf16[4,5120]{1,0:T(4,128)(2,1)S(1)} %pack.1), channel_id=1, source_target_pairs={{12,0},{0,4},{4,8},{8,12},{13,1},{1,5},{5,9},{9,13},{14,2},{2,6},{... | collective-permute-start | bytes 122888 | tf_op jit(solution)/shard_map/ppermute | solution.py:283
  4.0 7.1 %collective-permute-start.2 = (bf16[4,5120]{1,0:T(4,128)(2,1)S(1)}, bf16[4,5120]{1,0:T(4,128)(2,1)S(1)}, u32[]{:S(2)}, u32[]{:S(2)}) collective-permute-start(bf16[4,5120]{1,0:T(4,128)(2,1)S(1)} %pack.1), channel_id=1, source_target_pairs={{4,0},{8,4},{12,8},{0,12},{5,1},{9,5},{13,9},{1,13},{6,2},{10,6},{... | collective-permute-start | bytes 122888 | tf_op jit(solution)/shard_map/ppermute | solution.py:283
  6.1 5.0 %collective-permute-start = (bf16[4,5120]{1,0:T(4,128)(2,1)S(1)}, bf16[4,5120]{1,0:T(4,128)(2,1)S(1)}, u32[]{:S(2)}, u32[]{:S(2)}) collective-permute-start(bf16[4,5120]{1,0:T(4,128)(2,1)S(1)} %pack.1), channel_id=1, source_target_pairs={{8,0},{12,4},{0,8},{4,12},{9,1},{13,5},{1,9},{5,13},{10,2},{14,6},... | collective-permute-start | bytes 122888 | tf_op jit(solution)/shard_map/ppermute | solution.py:283
  7.8 9.9 %copy-start.3 = (s32[32]{0:T(128)S(1)}, s32[32]{0:T(128)}, u32[]{:S(2)}) copy-start(s32[32]{0:T(128)} %param.15) | copy-start | bytes 388
  11.0 1.7 %collective-permute-start.3 = (bf16[1168,128]{1,0:T(8,128)(2,1)S(1)}, bf16[1168,128]{1,0:T(8,128)(2,1)S(1)}, u32[]{:S(2)}, u32[]{:S(2)}) collective-permute-start(bf16[1168,128]{1,0:T(8,128)(2,1)S(1)} %prefill.1.near_ref), channel_id=1, source_target_pairs={{0,1},{1,0},{2,3},{3,2},{4,5},{5,4},{6,7},{7,6},{8,9},{9,8},{10,11... | collective-permute-start | bytes 897032 | tf_op jit(solution)/shard_map/ppermute | solution.py:289
  13.2 6.1 %collective-permute-start.4 = (bf16[4,4096]{1,0:T(4,128)(2,1)S(1)}, bf16[4,4096]{1,0:T(4,128)(2,1)S(1)}, u32[]{:S(2)}, u32[]{:S(2)}) collective-permute-start(bf16[4,4096]{1,0:T(4,128)(2,1)S(1)} %get-tuple-element.19), channel_id=1, source_target_pairs={{0,12},{4,8},{8,4},{12,0},{1,13},{5,9},{9,5},{13,1},{2,14},{6,10},... | collective-permute-start | bytes 98312 | tf_op jit(solution)/shard_map/ppermute | solution.py:299
  14.7 5.7 %collective-permute-start.5 = (bf16[4,4096]{1,0:T(4,128)(2,1)S(1)}, bf16[4,4096]{1,0:T(4,128)(2,1)S(1)}, u32[]{:S(2)}, u32[]{:S(2)}) collective-permute-start(bf16[4,4096]{1,0:T(4,128)(2,1)S(1)} %get-tuple-element.20), channel_id=1, source_target_pairs={{0,8},{4,12},{8,0},{12,4},{1,9},{5,13},{9,1},{13,5},{2,10},{6,14},... | collective-permute-start | bytes 98312 | tf_op jit(solution)/shard_map/ppermute | solution.py:299
  16.3 4.1 %collective-permute-start.6 = (bf16[4,4096]{1,0:T(4,128)(2,1)S(1)}, bf16[4,4096]{1,0:T(4,128)(2,1)S(1)}, u32[]{:S(2)}, u32[]{:S(2)}) collective-permute-start(bf16[4,4096]{1,0:T(4,128)(2,1)S(1)} %get-tuple-element.21), channel_id=1, source_target_pairs={{0,4},{4,0},{8,12},{12,8},{1,5},{5,1},{9,13},{13,9},{2,6},{6,2},{1... | collective-permute-start | bytes 98312 | tf_op jit(solution)/shard_map/ppermute | solution.py:299

commit v27 on v25

--- a/solution.py
+++ b/solution.py
@@ -103,28 +103,35 @@
                 NT,
                 preferred_element_type=jnp.float32,
             )
-            proj_ref[c % 2, j] = proj.astype(jnp.bfloat16)
-
-    def collect(c):
-        position = c * BLOCK + lax.broadcasted_iota(jnp.int32, (1, BLOCK), 1)
-        live = jnp.where(position < begin, 1.0, 0.0).astype(jnp.bfloat16)
+            proj_ref[c % 4, j] = proj.astype(jnp.bfloat16)
+
+    def collect(first_chunk):
         for j in range(pairs):
-            mapped = feature(proj_ref[c % 2, j]) * live
-            some = [mapped[:, k * 128 : (k + 1) * 128] for k in range(BLOCK // 128)]
-            while len(some) > 1:
-                some = [x + y for x, y in zip(some[::2], some[1::2])]
-            norm_ref[j] += some[0].astype(jnp.float32)
-            state_ref[j] += jnp.dot(
-                mapped,
-                values_at[c * BLOCK : (c + 1) * BLOCK, j * 2 * head_size : (j + 1) * 2 * head_size],
-                preferred_element_type=jnp.float32,
-            )
-
-    project(0)
-    for c in range(chunks):
-        if c + 1 < chunks:
+            sums, parts = [], []
+            for c in (first_chunk, first_chunk + 1):
+                position = c * BLOCK + lax.broadcasted_iota(jnp.int32, (1, BLOCK), 1)
+                live = jnp.where(position < begin, 1.0, 0.0).astype(jnp.bfloat16)
+                mapped = feature(proj_ref[c % 4, j]) * live
+                some = [mapped[:, k * 128 : (k + 1) * 128] for k in range(BLOCK // 128)]
+                while len(some) > 1:
+                    some = [x + y for x, y in zip(some[::2], some[1::2])]
+                sums.append(some[0].astype(jnp.float32))
+                parts.append(
+                    jnp.dot(
+                        mapped,
+                        values_at[c * BLOCK : (c + 1) * BLOCK, j * 2 * head_size : (j + 1) * 2 * head_size],
+                        preferred_element_type=jnp.float32,
+                    )
+                )
+            norm_ref[j] += sums[0] + sums[1]
+            state_ref[j] += parts[0] + parts[1]
+
+    for c in range(0, chunks + 2, 2):
+        if c < chunks:
+            project(c)
             project(c + 1)
-        collect(c)
+        if c > 0:
+            collect(c - 2)
 
     back = 1.0 / (feats * feats)
     tile = []
@@ -154,7 +161,7 @@
         out_shape=jax.ShapeDtypeStruct((heads * feats + 16 + 2 * heads * SLAB, head_size), jnp.bfloat16),
         scratch_shapes=[
             pltpu.VMEM((heads // 2, 2 * feats, 2 * head_size), jnp.bfloat16),
-            pltpu.VMEM((2, heads // 2, 2 * feats, BLOCK), jnp.bfloat16),
+            pltpu.VMEM((4, heads // 2, 2 * feats, BLOCK), jnp.bfloat16),
             pltpu.VMEM((heads // 2, 2 * feats, 2 * head_size), jnp.float32),
             pltpu.VMEM((heads // 2, 2 * feats, 128), jnp.float32),
             pltpu.SemaphoreType.DMA((2, heads)),

time: 20.9 us -> 21.1 us (level)
  Pallas kernels: 4.89 us -> 5.21 us
    pallas_call x1, Pallas kernels: 2.77 us -> 3.1 us  [prefill(): pl.pallas_call(prefill_kernel, in_specs=[pl.BlockSpec(memory_space=pltpu....]
    ppermute x3, waiting for transfers between devices: 0.33 us -> 0.01 us  [body(): lax.ppermute(mine, 'sect', [(ask(i, k, sects), i) for i in range(sects)])]
    ppermute x1, waiting for transfers between devices: 0.39 us -> 0.7 us  [body(): far = lax.ppermute(near, 'sub', [(0, 1), (1, 0)])]
  transfers between devices with their start and end apart: 7 -> 7, of which waited for: 5 -> 3; matrix products, arithmetic and copies ran while one was open for 1% -> 1% of each run, Pallas kernels for 17% -> 18%
where the time goes in v27:
time: 21.1 us; the launch traced here: 21 us
  starting transfers between devices  10.6 us (50%)
  Pallas kernels  5.21 us (25%)
  waiting for transfers between devices  3.38 us (16%)
  other arithmetic  0.93 us (4%)
  between operations  0.77 us (4%)
    ppermute x3, starting transfers between devices, body(): lax.ppermute(mine, 'sect', [(ask(i, k, sects), i) for i in range(sects)])  6.12 us
    ppermute x3, starting transfers between devices, body(): lax.ppermute(results[k], 'sect', [(i, partner(i, k, sects)) for i in rang...  4.45 us
    pallas_call x1, Pallas kernels, prefill(): pl.pallas_call(prefill_kernel, in_specs=[pl.BlockSpec(memory_space=pltpu....  3.1 us
    ppermute x3, waiting for transfers between devices, body(): lax.ppermute(results[k], 'sect', [(i, partner(i, k, sects)) for i in rang...  2.67 us
    pallas_call x1, Pallas kernels, pack(): pl.pallas_call(pack_kernel, in_specs=[pl.BlockSpec(memory_space=pltpu.Mem...  0.94 us
    select_n x1, other arithmetic, body(): out = jnp.where((prompts == source)[:, None], result, out)  0.71 us
    ppermute x1, waiting for transfers between devices, body(): far = lax.ppermute(near, 'sub', [(0, 1), (1, 0)])  0.7 us
    pallas_call x1, Pallas kernels, begin(): pl.pallas_call(begin_kernel, in_specs=[vmem] * 3, out_specs=[vmem] * 5, o...  0.67 us
  transfers between devices with their start and end apart: 7, of which 3 were waited for; matrix products, arithmetic and copies ran while one was open for 1% of the time, Pallas kernels for 18%

profile of v27, /device:TPU:0, one launch (start us, length us, event | category | flops | bytes accessed | tf_op | source)
XLA Modules:
  0.0 21.0 jit_solution(5128511560791015940)
XLA Ops:
  0.0 0.0 copy-start.2
  0.0 0.0 copy-start
  0.0 0.0 copy-start.1
  0.0 0.9 %pack.1 = bf16[4,5120]{1,0:T(4,128)(2,1)S(1)} custom-call(bf16[4,4096]{1,0:T(4,128)(2,1)} %queries_ref.1, bf16[4,512]{1,0:T(4,128)(2,1)} %keys_ref.2, bf16[4,512]{1,0:T(4,128)(2,1)} %values_ref.2), custom_call_target="tpu_custom_call" | custom-call | flops 10000000000 | bytes 33554432 | tf_op jit(solution)/shard_map/pack/pallas_call | solution.py:47
  1.0 3.1 %collective-permute-start.1 = (bf16[4,5120]{1,0:T(4,128)(2,1)S(1)}, bf16[4,5120]{1,0:T(4,128)(2,1)S(1)}, u32[]{:S(2)}, u32[]{:S(2)}) collective-permute-start(bf16[4,5120]{1,0:T(4,128)(2,1)S(1)} %pack.1), channel_id=1, source_target_pairs={{12,0},{0,4},{4,8},{8,12},{13,1},{1,5},{5,9},{9,13},{14,2},{2,6},{... | collective-permute-start | bytes 122888 | tf_op jit(solution)/shard_map/ppermute | solution.py:295
  4.0 2.1 %collective-permute-start.2 = (bf16[4,5120]{1,0:T(4,128)(2,1)S(1)}, bf16[4,5120]{1,0:T(4,128)(2,1)S(1)}, u32[]{:S(2)}, u32[]{:S(2)}) collective-permute-start(bf16[4,5120]{1,0:T(4,128)(2,1)S(1)} %pack.1), channel_id=1, source_target_pairs={{4,0},{8,4},{12,8},{0,12},{5,1},{9,5},{13,9},{1,13},{6,2},{10,6},{... | collective-permute-start | bytes 122888 | tf_op jit(solution)/shard_map/ppermute | solution.py:295
  6.1 0.9 %collective-permute-start = (bf16[4,5120]{1,0:T(4,128)(2,1)S(1)}, bf16[4,5120]{1,0:T(4,128)(2,1)S(1)}, u32[]{:S(2)}, u32[]{:S(2)}) collective-permute-start(bf16[4,5120]{1,0:T(4,128)(2,1)S(1)} %pack.1), channel_id=1, source_target_pairs={{8,0},{12,4},{0,8},{4,12},{9,1},{13,5},{1,9},{5,13},{10,2},{14,6},... | collective-permute-start | bytes 122888 | tf_op jit(solution)/shard_map/ppermute | solution.py:295
  7.7 0.0 copy-done.2
  7.7 0.0 copy-done
  7.7 0.0 copy-done.1
  7.8 0.0 copy-start.3
  7.8 3.1 %prefill.1.near_ref = bf16[1168,128]{1,0:T(8,128)(2,1)S(1)} custom-call(s32[1]{0:T(128)S(6)} %copy.9.lengths_ref, bf16[1,4096,512]{2,1,0:T(8,128)(2,1)S(1)} %copy-done, bf16[1,4096,512]{2,1,0:T(8,128)(2,1)S(1)} %copy-done.1, bf16[4,128,128]{2,1,0:T(8,128)(2,1)S(1)} %copy-done.2), custom_call_target="tpu_custom_call" | custom-call | flops 1073741824 | bytes 8388608 | tf_op jit(solution)/shard_map/prefill/pallas_call | solution.py:157
  10.9 0.1 collective-permute-start.3
  11.0 0.0 collective-permute-done.1
  11.0 0.0 collective-permute-done.2
  11.0 0.0 collective-permute-done
  11.0 0.1 pad_maximum_fusion.rows_ref
  11.1 0.7 %begin.1 = (bf16[4,128,128]{2,1,0:T(8,128)(2,1)S(1)}, bf16[4,128,128]{2,1,0:T(8,128)(2,1)S(1)}, f32[4,128,128]{2,1,0:T(8,128)S(1)}, f32[4,128,128]{2,1,0:T(8,128)S(1)}, f32[4,128,128]{2,1,0:T(8,128)S(1)}) custom-call(bf16[16,5120]{1,0:T(8,128)(2,1)S(1)} %pad_maximum_fusion.rows_ref, bf16[4,128,128]{2,1,0:T(8,128)(2,1)S(1)} %copy-done.2, ...), custom_call_target="tpu_custom_call" | custom-call | flops 62914560 | bytes 327680 | tf_op jit(solution)/shard_map/begin/pallas_call | solution.py:258
  11.8 0.7 %collective-permute-done.3.far_ref = bf16[1168,128]{1,0:T(8,128)(2,1)S(1)} collective-permute-done((bf16[1168,128]{1,0:T(8,128)(2,1)S(1)}, bf16[1168,128]{1,0:T(8,128)(2,1)S(1)}, u32[]{:S(2)}, u32[]{:S(2)}) %collective-permute-start.3) | collective-permute-done | bytes 299040 | tf_op jit(solution)/shard_map/ppermute | solution.py:301
  12.5 0.5 %end.1 = (bf16[4,4096]{1,0:T(4,128)(2,1)S(1)}, bf16[4,4096]{1,0:T(4,128)(2,1)S(1)}, bf16[4,4096]{1,0:T(4,128)(2,1)S(1)}, bf16[4,4096]{1,0:T(4,128)(2,1)S(1)}) custom-call(bf16[4,128,128]{2,1,0:T(8,128)(2,1)S(1)} %get-tuple-element.14.query_ref, bf16[4,128,128]{2,1,0:T(8,128)(2,1)S(1)} %get-tuple-element.15.phi_ref, ...), custom_call_target="tpu_custom_call" | custom-call | flops 33554432 | bytes 262144 | tf_op jit(solution)/shard_map/end/pallas_call | solution.py:273
  13.0 1.6 %collective-permute-start.4 = (bf16[4,4096]{1,0:T(4,128)(2,1)S(1)}, bf16[4,4096]{1,0:T(4,128)(2,1)S(1)}, u32[]{:S(2)}, u32[]{:S(2)}) collective-permute-start(bf16[4,4096]{1,0:T(4,128)(2,1)S(1)} %get-tuple-element.19), channel_id=1, source_target_pairs={{0,12},{4,8},{8,4},{12,0},{1,13},{5,9},{9,5},{13,1},{2,14},{6,10},... | collective-permute-start | bytes 98312 | tf_op jit(solution)/shard_map/ppermute | solution.py:311
  14.7 1.5 %collective-permute-start.5 = (bf16[4,4096]{1,0:T(4,128)(2,1)S(1)}, bf16[4,4096]{1,0:T(4,128)(2,1)S(1)}, u32[]{:S(2)}, u32[]{:S(2)}) collective-permute-start(bf16[4,4096]{1,0:T(4,128)(2,1)S(1)} %get-tuple-element.20), channel_id=1, source_target_pairs={{0,8},{4,12},{8,0},{12,4},{1,9},{5,13},{9,1},{13,5},{2,10},{6,14},... | collective-permute-start | bytes 98312 | tf_op jit(solution)/shard_map/ppermute | solution.py:311
  16.1 1.3 %collective-permute-start.6 = (bf16[4,4096]{1,0:T(4,128)(2,1)S(1)}, bf16[4,4096]{1,0:T(4,128)(2,1)S(1)}, u32[]{:S(2)}, u32[]{:S(2)}) collective-permute-start(bf16[4,4096]{1,0:T(4,128)(2,1)S(1)} %get-tuple-element.21), channel_id=1, source_target_pairs={{0,4},{4,0},{8,12},{12,8},{1,5},{5,1},{9,13},{13,9},{2,6},{6,2},{1... | collective-permute-start | bytes 98312 | tf_op jit(solution)/shard_map/ppermute | solution.py:311
  17.5 0.0 copy-done.3
  17.5 0.1 broadcast_compare_fusion.2
  17.6 1.6 %collective-permute-done.4 = bf16[4,4096]{1,0:T(4,128)(2,1)S(1)} collective-permute-done((bf16[4,4096]{1,0:T(4,128)(2,1)S(1)}, bf16[4,4096]{1,0:T(4,128)(2,1)S(1)}, u32[]{:S(2)}, u32[]{:S(2)}) %collective-permute-start.4) | collective-permute-done | bytes 32800 | tf_op jit(solution)/shard_map/ppermute | solution.py:311
  19.2 1.0 %collective-permute-done.5 = bf16[4,4096]{1,0:T(4,128)(2,1)S(1)} collective-permute-done((bf16[4,4096]{1,0:T(4,128)(2,1)S(1)}, bf16[4,4096]{1,0:T(4,128)(2,1)S(1)}, u32[]{:S(2)}, u32[]{:S(2)}) %collective-permute-start.5) | collective-permute-done | bytes 32800 | tf_op jit(solution)/shard_map/ppermute | solution.py:311
  20.2 0.0 collective-permute-done.6
  20.2 0.7 %select_select_fusion = bf16[4,4096]{1,0:T(4,128)(2,1)} fusion(bf16[4,4096]{1,0:T(4,128)(2,1)S(1)} %collective-permute-done.4, bf16[4,4096]{1,0:T(4,128)(2,1)S(1)} %collective-permute-done.5, bf16[4,4096]{1,0:T(4,128)(2,1)S(1)} %collective-permute-done.6, bf16[4,4096]{1,0:T(4,128)(2,1)S(1)} %get-tuple-element.22, pred[4]{0:T(512)(128)(4,1)S(1)} %get-tuple-element.27, ...), kind=kLoop, calls=%fused_computation.3 | loop fusion | flops 49152 | bytes 163852 | tf_op jit(solution)/shard_map/jit(_where)/select_n | solution.py:313
  (1 shorter events, 0.0 us)
Async XLA Ops:
  0.0 7.7 %copy-start.2 = (bf16[4,128,128]{2,1,0:T(8,128)(2,1)S(1)}, bf16[4,128,128]{2,1,0:T(8,128)(2,1)}, u32[]{:S(2)}) copy-start(bf16[4,128,128]{2,1,0:T(8,128)(2,1)} %weight_ref.3) | copy-start | bytes 393220
  0.0 7.7 %copy-start = (bf16[1,4096,512]{2,1,0:T(8,128)(2,1)S(1)}, bf16[1,4096,512]{2,1,0:T(8,128)(2,1)}, u32[]{:S(2)}) copy-start(bf16[1,4096,512]{2,1,0:T(8,128)(2,1)} %keys_ref.3) | copy-start | bytes 12582916
  0.0 7.7 %copy-start.1 = (bf16[1,4096,512]{2,1,0:T(8,128)(2,1)S(1)}, bf16[1,4096,512]{2,1,0:T(8,128)(2,1)}, u32[]{:S(2)}) copy-start(bf16[1,4096,512]{2,1,0:T(8,128)(2,1)} %values_ref.3) | copy-start | bytes 12582916
  1.0 10.0 %collective-permute-start.1 = (bf16[4,5120]{1,0:T(4,128)(2,1)S(1)}, bf16[4,5120]{1,0:T(4,128)(2,1)S(1)}, u32[]{:S(2)}, u32[]{:S(2)}) collective-permute-start(bf16[4,5120]{1,0:T(4,128)(2,1)S(1)} %pack.1), channel_id=1, source_target_pairs={{12,0},{0,4},{4,8},{8,12},{13,1},{1,5},{5,9},{9,13},{14,2},{2,6},{... | collective-permute-start | bytes 122888 | tf_op jit(solution)/shard_map/ppermute | solution.py:295
  4.0 6.9 %collective-permute-start.2 = (bf16[4,5120]{1,0:T(4,128)(2,1)S(1)}, bf16[4,5120]{1,0:T(4,128)(2,1)S(1)}, u32[]{:S(2)}, u32[]{:S(2)}) collective-permute-start(bf16[4,5120]{1,0:T(4,128)(2,1)S(1)} %pack.1), channel_id=1, source_target_pairs={{4,0},{8,4},{12,8},{0,12},{5,1},{9,5},{13,9},{1,13},{6,2},{10,6},{... | collective-permute-start | bytes 122888 | tf_op jit(solution)/shard_map/ppermute | solution.py:295
  6.1 4.9 %collective-permute-start = (bf16[4,5120]{1,0:T(4,128)(2,1)S(1)}, bf16[4,5120]{1,0:T(4,128)(2,1)S(1)}, u32[]{:S(2)}, u32[]{:S(2)}) collective-permute-start(bf16[4,5120]{1,0:T(4,128)(2,1)S(1)} %pack.1), channel_id=1, source_target_pairs={{8,0},{12,4},{0,8},{4,12},{9,1},{13,5},{1,9},{5,13},{10,2},{14,6},... | collective-permute-start | bytes 122888 | tf_op jit(solution)/shard_map/ppermute | solution.py:295
  7.8 9.7 %copy-start.3 = (s32[32]{0:T(128)S(1)}, s32[32]{0:T(128)}, u32[]{:S(2)}) copy-start(s32[32]{0:T(128)} %param.15) | copy-start | bytes 388
  10.9 1.7 %collective-permute-start.3 = (bf16[1168,128]{1,0:T(8,128)(2,1)S(1)}, bf16[1168,128]{1,0:T(8,128)(2,1)S(1)}, u32[]{:S(2)}, u32[]{:S(2)}) collective-permute-start(bf16[1168,128]{1,0:T(8,128)(2,1)S(1)} %prefill.1.near_ref), channel_id=1, source_target_pairs={{0,1},{1,0},{2,3},{3,2},{4,5},{5,4},{6,7},{7,6},{8,9},{9,8},{10,11... | collective-permute-start | bytes 897032 | tf_op jit(solution)/shard_map/ppermute | solution.py:301
  13.0 6.1 %collective-permute-start.4 = (bf16[4,4096]{1,0:T(4,128)(2,1)S(1)}, bf16[4,4096]{1,0:T(4,128)(2,1)S(1)}, u32[]{:S(2)}, u32[]{:S(2)}) collective-permute-start(bf16[4,4096]{1,0:T(4,128)(2,1)S(1)} %get-tuple-element.19), channel_id=1, source_target_pairs={{0,12},{4,8},{8,4},{12,0},{1,13},{5,9},{9,5},{13,1},{2,14},{6,10},... | collective-permute-start | bytes 98312 | tf_op jit(solution)/shard_map/ppermute | solution.py:311
  14.7 5.5 %collective-permute-start.5 = (bf16[4,4096]{1,0:T(4,128)(2,1)S(1)}, bf16[4,4096]{1,0:T(4,128)(2,1)S(1)}, u32[]{:S(2)}, u32[]{:S(2)}) collective-permute-start(bf16[4,4096]{1,0:T(4,128)(2,1)S(1)} %get-tuple-element.20), channel_id=1, source_target_pairs={{0,8},{4,12},{8,0},{12,4},{1,9},{5,13},{9,1},{13,5},{2,10},{6,14},... | collective-permute-start | bytes 98312 | tf_op jit(solution)/shard_map/ppermute | solution.py:311
  16.1 4.1 %collective-permute-start.6 = (bf16[4,4096]{1,0:T(4,128)(2,1)S(1)}, bf16[4,4096]{1,0:T(4,128)(2,1)S(1)}, u32[]{:S(2)}, u32[]{:S(2)}) collective-permute-start(bf16[4,4096]{1,0:T(4,128)(2,1)S(1)} %get-tuple-element.21), channel_id=1, source_target_pairs={{0,4},{4,0},{8,12},{12,8},{1,5},{5,1},{9,13},{13,9},{2,6},{6,2},{1... | collective-permute-start | bytes 98312 | tf_op jit(solution)/shard_map/ppermute | solution.py:311

commit v28 on v26

--- a/solution.py
+++ b/solution.py
@@ -75,7 +75,8 @@
     wide_ref[...] = jnp.zeros_like(wide_ref)
     for g in range(heads):
         half = g % 2
-        wide_ref[g // 2, half * head_size : (half + 1) * head_size, half * feats : (half + 1) * feats] = weight_ref[g]
+        turned = weight_ref[g].astype(jnp.float32).T.astype(jnp.bfloat16)
+        wide_ref[g // 2, half * feats : (half + 1) * feats, half * head_size : (half + 1) * head_size] = turned
 
     begin = lengths_ref[0] - WINDOW - lax.axis_index("sub") * span
     first = jnp.clip(begin, 0, span - SLAB)
@@ -94,32 +95,36 @@
             )
             slabs[-1].start()
 
-    def project(c):
-        for j in range(pairs):
-            keys = keys_at[c * BLOCK : (c + 1) * BLOCK, j * 2 * head_size : (j + 1) * 2 * head_size]
-            proj = jnp.dot(keys, wide_ref[j], preferred_element_type=jnp.float32)
-            proj_ref[c % 2, j] = proj.astype(jnp.bfloat16).T
-
-    def collect(c):
+    def project(unit):
+        c, j = divmod(unit, pairs)
+        proj = lax.dot_general(
+            wide_ref[j],
+            keys_at[c * BLOCK : (c + 1) * BLOCK, j * 2 * head_size : (j + 1) * 2 * head_size],
+            NT,
+            preferred_element_type=jnp.float32,
+        )
+        proj_ref[unit % 2] = proj.astype(jnp.bfloat16)
+
+    def collect(unit):
+        c, j = divmod(unit, pairs)
         position = c * BLOCK + lax.broadcasted_iota(jnp.int32, (1, BLOCK), 1)
         live = jnp.where(position < begin, 1.0, 0.0).astype(jnp.bfloat16)
-        for j in range(pairs):
-            mapped = feature(proj_ref[c % 2, j]) * live
-            some = [mapped[:, k * 128 : (k + 1) * 128] for k in range(BLOCK // 128)]
-            while len(some) > 1:
-                some = [x + y for x, y in zip(some[::2], some[1::2])]
-            norm_ref[j] += some[0].astype(jnp.float32)
-            state_ref[j] += jnp.dot(
-                mapped,
-                values_at[c * BLOCK : (c + 1) * BLOCK, j * 2 * head_size : (j + 1) * 2 * head_size],
-                preferred_element_type=jnp.float32,
-            )
+        mapped = feature(proj_ref[unit % 2]) * live
+        some = [mapped[:, k * 128 : (k + 1) * 128] for k in range(BLOCK // 128)]
+        while len(some) > 1:
+            some = [x + y for x, y in zip(some[::2], some[1::2])]
+        norm_ref[j] += some[0].astype(jnp.float32)
+        state_ref[j] += jnp.dot(
+            mapped,
+            values_at[c * BLOCK : (c + 1) * BLOCK, j * 2 * head_size : (j + 1) * 2 * head_size],
+            preferred_element_type=jnp.float32,
+        )
 
     project(0)
-    for c in range(chunks):
-        if c + 1 < chunks:
-            project(c + 1)
-        collect(c)
+    for unit in range(chunks * pairs):
+        if unit + 1 < chunks * pairs:
+            project(unit + 1)
+        collect(unit)
 
     back = 1.0 / (feats * feats)
     tile = []
@@ -149,7 +154,7 @@
         out_shape=jax.ShapeDtypeStruct((heads * feats + 16 + 2 * heads * SLAB, head_size), jnp.bfloat16),
         scratch_shapes=[
             pltpu.VMEM((heads // 2, 2 * feats, 2 * head_size), jnp.bfloat16),
-            pltpu.VMEM((2, heads // 2, 2 * feats, BLOCK), jnp.bfloat16),
+            pltpu.VMEM((2, 2 * feats, BLOCK), jnp.bfloat16),
             pltpu.VMEM((heads // 2, 2 * feats, 2 * head_size), jnp.float32),
             pltpu.VMEM((heads // 2, 2 * feats, 128), jnp.float32),
             pltpu.SemaphoreType.DMA((2, heads)),

time: 21.3 us -> 20.9 us (0.981)
  Pallas kernels: 5.35 us -> 4.84 us
    pallas_call x1, Pallas kernels: 3.24 us -> 2.72 us  [prefill(): pl.pallas_call(prefill_kernel, in_specs=[pl.BlockSpec(memory_space=pltpu....]
    ppermute x3, waiting for transfers between devices: 0.01 us -> 0.38 us  [body(): lax.ppermute(mine, 'sect', [(ask(i, k, sects), i) for i in range(sects)])]
    ppermute x1, waiting for transfers between devices: 0.7 us -> 0.34 us  [body(): far = lax.ppermute(near, 'sub', [(0, 1), (1, 0)])]
  transfers between devices with their start and end apart: 7 -> 7, of which waited for: 4 -> 4; matrix products, arithmetic and copies ran while one was open for 1% -> 1% of each run, Pallas kernels for 19% -> 16%
where the time goes in v28:
time: 20.9 us; the launch traced here: 20.7 us
  starting transfers between devices  10.6 us (51%)
  Pallas kernels  4.84 us (23%)
  waiting for transfers between devices  3.53 us (17%)
  other arithmetic  0.93 us (4%)
  between operations  0.76 us (4%)
    ppermute x3, starting transfers between devices, body(): lax.ppermute(mine, 'sect', [(ask(i, k, sects), i) for i in range(sects)])  6.12 us
    ppermute x3, starting transfers between devices, body(): lax.ppermute(results[k], 'sect', [(i, partner(i, k, sects)) for i in rang...  4.45 us
    ppermute x3, waiting for transfers between devices, body(): lax.ppermute(results[k], 'sect', [(i, partner(i, k, sects)) for i in rang...  2.81 us
    pallas_call x1, Pallas kernels, prefill(): pl.pallas_call(prefill_kernel, in_specs=[pl.BlockSpec(memory_space=pltpu....  2.72 us
    pallas_call x1, Pallas kernels, pack(): pl.pallas_call(pack_kernel, in_specs=[pl.BlockSpec(memory_space=pltpu.Mem...  0.94 us
    select_n x1, other arithmetic, body(): out = jnp.where((prompts == source)[:, None], result, out)  0.71 us
    pallas_call x1, Pallas kernels, begin(): pl.pallas_call(begin_kernel, in_specs=[vmem] * 3, out_specs=[vmem] * 5, o...  0.67 us
    pallas_call x1, Pallas kernels, end(): pl.pallas_call(end_kernel, in_specs=[vmem] * 6, out_specs=[vmem] * parts,...  0.51 us
  transfers between devices with their start and end apart: 7, of which 4 were waited for; matrix products, arithmetic and copies ran while one was open for 1% of the time, Pallas kernels for 16%

profile of v28, /device:TPU:0, one launch (start us, length us, event | category | flops | bytes accessed | tf_op | source)
XLA Modules:
  0.0 20.7 jit_solution(12243078717007338187)
XLA Ops:
  0.0 0.0 copy-start.2
  0.0 0.0 copy-start
  0.0 0.0 copy-start.1
  0.0 0.9 %pack.1 = bf16[4,5120]{1,0:T(4,128)(2,1)S(1)} custom-call(bf16[4,4096]{1,0:T(4,128)(2,1)} %queries_ref.1, bf16[4,512]{1,0:T(4,128)(2,1)} %keys_ref.2, bf16[4,512]{1,0:T(4,128)(2,1)} %values_ref.2), custom_call_target="tpu_custom_call" | custom-call | flops 10000000000 | bytes 33554432 | tf_op jit(solution)/shard_map/pack/pallas_call | solution.py:47
  1.0 3.1 %collective-permute-start.1 = (bf16[4,5120]{1,0:T(4,128)(2,1)S(1)}, bf16[4,5120]{1,0:T(4,128)(2,1)S(1)}, u32[]{:S(2)}, u32[]{:S(2)}) collective-permute-start(bf16[4,5120]{1,0:T(4,128)(2,1)S(1)} %pack.1), channel_id=1, source_target_pairs={{12,0},{0,4},{4,8},{8,12},{13,1},{1,5},{5,9},{9,13},{14,2},{2,6},{... | collective-permute-start | bytes 122888 | tf_op jit(solution)/shard_map/ppermute | solution.py:288
  4.0 2.1 %collective-permute-start.2 = (bf16[4,5120]{1,0:T(4,128)(2,1)S(1)}, bf16[4,5120]{1,0:T(4,128)(2,1)S(1)}, u32[]{:S(2)}, u32[]{:S(2)}) collective-permute-start(bf16[4,5120]{1,0:T(4,128)(2,1)S(1)} %pack.1), channel_id=1, source_target_pairs={{4,0},{8,4},{12,8},{0,12},{5,1},{9,5},{13,9},{1,13},{6,2},{10,6},{... | collective-permute-start | bytes 122888 | tf_op jit(solution)/shard_map/ppermute | solution.py:288
  6.1 0.9 %collective-permute-start = (bf16[4,5120]{1,0:T(4,128)(2,1)S(1)}, bf16[4,5120]{1,0:T(4,128)(2,1)S(1)}, u32[]{:S(2)}, u32[]{:S(2)}) collective-permute-start(bf16[4,5120]{1,0:T(4,128)(2,1)S(1)} %pack.1), channel_id=1, source_target_pairs={{8,0},{12,4},{0,8},{4,12},{9,1},{13,5},{1,9},{5,13},{10,2},{14,6},... | collective-permute-start | bytes 122888 | tf_op jit(solution)/shard_map/ppermute | solution.py:288
  7.7 0.0 copy-done.2
  7.7 0.0 copy-done
  7.7 0.0 copy-done.1
  7.8 0.0 copy-start.3
  7.8 2.7 %prefill.1.near_ref = bf16[1168,128]{1,0:T(8,128)(2,1)S(1)} custom-call(s32[1]{0:T(128)S(6)} %copy.9.lengths_ref, bf16[1,4096,512]{2,1,0:T(8,128)(2,1)S(1)} %copy-done, bf16[1,4096,512]{2,1,0:T(8,128)(2,1)S(1)} %copy-done.1, bf16[4,128,128]{2,1,0:T(8,128)(2,1)S(1)} %copy-done.2), custom_call_target="tpu_custom_call" | custom-call | flops 1073741824 | bytes 8388608 | tf_op jit(solution)/shard_map/prefill/pallas_call | solution.py:150
  10.5 0.1 collective-permute-start.3
  10.6 0.0 collective-permute-done.1
  10.6 0.0 collective-permute-done.2
  10.6 0.4 %collective-permute-done = bf16[4,5120]{1,0:T(4,128)(2,1)S(1)} collective-permute-done((bf16[4,5120]{1,0:T(4,128)(2,1)S(1)}, bf16[4,5120]{1,0:T(4,128)(2,1)S(1)}, u32[]{:S(2)}, u32[]{:S(2)}) %collective-permute-start) | collective-permute-done | bytes 40992 | tf_op jit(solution)/shard_map/ppermute | solution.py:288
  11.0 0.1 pad_maximum_fusion.rows_ref
  11.1 0.7 %begin.1 = (bf16[4,128,128]{2,1,0:T(8,128)(2,1)S(1)}, bf16[4,128,128]{2,1,0:T(8,128)(2,1)S(1)}, f32[4,128,128]{2,1,0:T(8,128)S(1)}, f32[4,128,128]{2,1,0:T(8,128)S(1)}, f32[4,128,128]{2,1,0:T(8,128)S(1)}) custom-call(bf16[16,5120]{1,0:T(8,128)(2,1)S(1)} %pad_maximum_fusion.rows_ref, bf16[4,128,128]{2,1,0:T(8,128)(2,1)S(1)} %copy-done.2, ...), custom_call_target="tpu_custom_call" | custom-call | flops 62914560 | bytes 327680 | tf_op jit(solution)/shard_map/begin/pallas_call | solution.py:251
  11.8 0.3 %collective-permute-done.3.far_ref = bf16[1168,128]{1,0:T(8,128)(2,1)S(1)} collective-permute-done((bf16[1168,128]{1,0:T(8,128)(2,1)S(1)}, bf16[1168,128]{1,0:T(8,128)(2,1)S(1)}, u32[]{:S(2)}, u32[]{:S(2)}) %collective-permute-start.3) | collective-permute-done | bytes 299040 | tf_op jit(solution)/shard_map/ppermute | solution.py:294
  12.1 0.5 %end.1 = (bf16[4,4096]{1,0:T(4,128)(2,1)S(1)}, bf16[4,4096]{1,0:T(4,128)(2,1)S(1)}, bf16[4,4096]{1,0:T(4,128)(2,1)S(1)}, bf16[4,4096]{1,0:T(4,128)(2,1)S(1)}) custom-call(bf16[4,128,128]{2,1,0:T(8,128)(2,1)S(1)} %get-tuple-element.14.query_ref, bf16[4,128,128]{2,1,0:T(8,128)(2,1)S(1)} %get-tuple-element.15.phi_ref, ...), custom_call_target="tpu_custom_call" | custom-call | flops 33554432 | bytes 262144 | tf_op jit(solution)/shard_map/end/pallas_call | solution.py:266
  12.7 2.0 %collective-permute-start.4 = (bf16[4,4096]{1,0:T(4,128)(2,1)S(1)}, bf16[4,4096]{1,0:T(4,128)(2,1)S(1)}, u32[]{:S(2)}, u32[]{:S(2)}) collective-permute-start(bf16[4,4096]{1,0:T(4,128)(2,1)S(1)} %get-tuple-element.19), channel_id=1, source_target_pairs={{0,12},{4,8},{8,4},{12,0},{1,13},{5,9},{9,5},{13,1},{2,14},{6,10},... | collective-permute-start | bytes 98312 | tf_op jit(solution)/shard_map/ppermute | solution.py:304
  14.7 1.1 %collective-permute-start.5 = (bf16[4,4096]{1,0:T(4,128)(2,1)S(1)}, bf16[4,4096]{1,0:T(4,128)(2,1)S(1)}, u32[]{:S(2)}, u32[]{:S(2)}) collective-permute-start(bf16[4,4096]{1,0:T(4,128)(2,1)S(1)} %get-tuple-element.20), channel_id=1, source_target_pairs={{0,8},{4,12},{8,0},{12,4},{1,9},{5,13},{9,1},{13,5},{2,10},{6,14},... | collective-permute-start | bytes 98312 | tf_op jit(solution)/shard_map/ppermute | solution.py:304
  15.8 1.3 %collective-permute-start.6 = (bf16[4,4096]{1,0:T(4,128)(2,1)S(1)}, bf16[4,4096]{1,0:T(4,128)(2,1)S(1)}, u32[]{:S(2)}, u32[]{:S(2)}) collective-permute-start(bf16[4,4096]{1,0:T(4,128)(2,1)S(1)} %get-tuple-element.21), channel_id=1, source_target_pairs={{0,4},{4,0},{8,12},{12,8},{1,5},{5,1},{9,13},{13,9},{2,6},{6,2},{1... | collective-permute-start | bytes 98312 | tf_op jit(solution)/shard_map/ppermute | solution.py:304
  17.1 0.0 copy-done.3
  17.1 0.1 broadcast_compare_fusion.2
  17.2 1.6 %collective-permute-done.4 = bf16[4,4096]{1,0:T(4,128)(2,1)S(1)} collective-permute-done((bf16[4,4096]{1,0:T(4,128)(2,1)S(1)}, bf16[4,4096]{1,0:T(4,128)(2,1)S(1)}, u32[]{:S(2)}, u32[]{:S(2)}) %collective-permute-start.4) | collective-permute-done | bytes 32800 | tf_op jit(solution)/shard_map/ppermute | solution.py:304
  18.8 1.2 %collective-permute-done.5 = bf16[4,4096]{1,0:T(4,128)(2,1)S(1)} collective-permute-done((bf16[4,4096]{1,0:T(4,128)(2,1)S(1)}, bf16[4,4096]{1,0:T(4,128)(2,1)S(1)}, u32[]{:S(2)}, u32[]{:S(2)}) %collective-permute-start.5) | collective-permute-done | bytes 32800 | tf_op jit(solution)/shard_map/ppermute | solution.py:304
  20.0 0.0 collective-permute-done.6
  20.0 0.7 %select_select_fusion = bf16[4,4096]{1,0:T(4,128)(2,1)} fusion(bf16[4,4096]{1,0:T(4,128)(2,1)S(1)} %collective-permute-done.4, bf16[4,4096]{1,0:T(4,128)(2,1)S(1)} %collective-permute-done.5, bf16[4,4096]{1,0:T(4,128)(2,1)S(1)} %collective-permute-done.6, bf16[4,4096]{1,0:T(4,128)(2,1)S(1)} %get-tuple-element.22, pred[4]{0:T(512)(128)(4,1)S(1)} %get-tuple-element.27, ...), kind=kLoop, calls=%fused_computation.3 | loop fusion | flops 49152 | bytes 163852 | tf_op jit(solution)/shard_map/jit(_where)/select_n | solution.py:306
  (1 shorter events, 0.0 us)
Async XLA Ops:
  0.0 7.7 %copy-start.2 = (bf16[4,128,128]{2,1,0:T(8,128)(2,1)S(1)}, bf16[4,128,128]{2,1,0:T(8,128)(2,1)}, u32[]{:S(2)}) copy-start(bf16[4,128,128]{2,1,0:T(8,128)(2,1)} %weight_ref.3) | copy-start | bytes 393220
  0.0 7.7 %copy-start = (bf16[1,4096,512]{2,1,0:T(8,128)(2,1)S(1)}, bf16[1,4096,512]{2,1,0:T(8,128)(2,1)}, u32[]{:S(2)}) copy-start(bf16[1,4096,512]{2,1,0:T(8,128)(2,1)} %keys_ref.3) | copy-start | bytes 12582916
  0.0 7.7 %copy-start.1 = (bf16[1,4096,512]{2,1,0:T(8,128)(2,1)S(1)}, bf16[1,4096,512]{2,1,0:T(8,128)(2,1)}, u32[]{:S(2)}) copy-start(bf16[1,4096,512]{2,1,0:T(8,128)(2,1)} %values_ref.3) | copy-start | bytes 12582916
  1.0 9.6 %collective-permute-start.1 = (bf16[4,5120]{1,0:T(4,128)(2,1)S(1)}, bf16[4,5120]{1,0:T(4,128)(2,1)S(1)}, u32[]{:S(2)}, u32[]{:S(2)}) collective-permute-start(bf16[4,5120]{1,0:T(4,128)(2,1)S(1)} %pack.1), channel_id=1, source_target_pairs={{12,0},{0,4},{4,8},{8,12},{13,1},{1,5},{5,9},{9,13},{14,2},{2,6},{... | collective-permute-start | bytes 122888 | tf_op jit(solution)/shard_map/ppermute | solution.py:288
  4.0 6.6 %collective-permute-start.2 = (bf16[4,5120]{1,0:T(4,128)(2,1)S(1)}, bf16[4,5120]{1,0:T(4,128)(2,1)S(1)}, u32[]{:S(2)}, u32[]{:S(2)}) collective-permute-start(bf16[4,5120]{1,0:T(4,128)(2,1)S(1)} %pack.1), channel_id=1, source_target_pairs={{4,0},{8,4},{12,8},{0,12},{5,1},{9,5},{13,9},{1,13},{6,2},{10,6},{... | collective-permute-start | bytes 122888 | tf_op jit(solution)/shard_map/ppermute | solution.py:288
  6.1 4.9 %collective-permute-start = (bf16[4,5120]{1,0:T(4,128)(2,1)S(1)}, bf16[4,5120]{1,0:T(4,128)(2,1)S(1)}, u32[]{:S(2)}, u32[]{:S(2)}) collective-permute-start(bf16[4,5120]{1,0:T(4,128)(2,1)S(1)} %pack.1), channel_id=1, source_target_pairs={{8,0},{12,4},{0,8},{4,12},{9,1},{13,5},{1,9},{5,13},{10,2},{14,6},... | collective-permute-start | bytes 122888 | tf_op jit(solution)/shard_map/ppermute | solution.py:288
  7.8 9.4 %copy-start.3 = (s32[32]{0:T(128)S(1)}, s32[32]{0:T(128)}, u32[]{:S(2)}) copy-start(s32[32]{0:T(128)} %param.15) | copy-start | bytes 388
  10.5 1.7 %collective-permute-start.3 = (bf16[1168,128]{1,0:T(8,128)(2,1)S(1)}, bf16[1168,128]{1,0:T(8,128)(2,1)S(1)}, u32[]{:S(2)}, u32[]{:S(2)}) collective-permute-start(bf16[1168,128]{1,0:T(8,128)(2,1)S(1)} %prefill.1.near_ref), channel_id=1, source_target_pairs={{0,1},{1,0},{2,3},{3,2},{4,5},{5,4},{6,7},{7,6},{8,9},{9,8},{10,11... | collective-permute-start | bytes 897032 | tf_op jit(solution)/shard_map/ppermute | solution.py:294
  12.7 6.1 %collective-permute-start.4 = (bf16[4,4096]{1,0:T(4,128)(2,1)S(1)}, bf16[4,4096]{1,0:T(4,128)(2,1)S(1)}, u32[]{:S(2)}, u32[]{:S(2)}) collective-permute-start(bf16[4,4096]{1,0:T(4,128)(2,1)S(1)} %get-tuple-element.19), channel_id=1, source_target_pairs={{0,12},{4,8},{8,4},{12,0},{1,13},{5,9},{9,5},{13,1},{2,14},{6,10},... | collective-permute-start | bytes 98312 | tf_op jit(solution)/shard_map/ppermute | solution.py:304
  14.7 5.3 %collective-permute-start.5 = (bf16[4,4096]{1,0:T(4,128)(2,1)S(1)}, bf16[4,4096]{1,0:T(4,128)(2,1)S(1)}, u32[]{:S(2)}, u32[]{:S(2)}) collective-permute-start(bf16[4,4096]{1,0:T(4,128)(2,1)S(1)} %get-tuple-element.20), channel_id=1, source_target_pairs={{0,8},{4,12},{8,0},{12,4},{1,9},{5,13},{9,1},{13,5},{2,10},{6,14},... | collective-permute-start | bytes 98312 | tf_op jit(solution)/shard_map/ppermute | solution.py:304
  15.8 4.2 %collective-permute-start.6 = (bf16[4,4096]{1,0:T(4,128)(2,1)S(1)}, bf16[4,4096]{1,0:T(4,128)(2,1)S(1)}, u32[]{:S(2)}, u32[]{:S(2)}) collective-permute-start(bf16[4,4096]{1,0:T(4,128)(2,1)S(1)} %get-tuple-element.21), channel_id=1, source_target_pairs={{0,4},{4,0},{8,12},{12,8},{1,5},{5,1},{9,13},{13,9},{2,6},{6,2},{1... | collective-permute-start | bytes 98312 | tf_op jit(solution)/shard_map/ppermute | solution.py:304

commit v29 on v28

--- a/solution.py
+++ b/solution.py
@@ -62,21 +62,17 @@
 
 def prefill_kernel(
     lengths_ref, keys_ref, values_ref, weight_ref, out_ref,
-    wide_ref, proj_ref, state_ref, norm_ref,
+    turned_ref, proj_ref, state_ref, norm_ref,
     slab_sem,
 ):
     heads, head_size, feats = weight_ref.shape
-    pairs = heads // 2
     span = keys_ref.shape[1]
     keys_at, values_at = keys_ref.at[0], values_ref.at[0]
     chunks = span // BLOCK
     state_ref[...] = jnp.zeros_like(state_ref)
     norm_ref[...] = jnp.zeros_like(norm_ref)
-    wide_ref[...] = jnp.zeros_like(wide_ref)
     for g in range(heads):
-        half = g % 2
-        turned = weight_ref[g].astype(jnp.float32).T.astype(jnp.bfloat16)
-        wide_ref[g // 2, half * feats : (half + 1) * feats, half * head_size : (half + 1) * head_size] = turned
+        turned_ref[g] = weight_ref[g].astype(jnp.float32).T.astype(jnp.bfloat16)
 
     begin = lengths_ref[0] - WINDOW - lax.axis_index("sub") * span
     first = jnp.clip(begin, 0, span - SLAB)
@@ -96,43 +92,34 @@
             slabs[-1].start()
 
     def project(unit):
-        c, j = divmod(unit, pairs)
-        proj = lax.dot_general(
-            wide_ref[j],
-            keys_at[c * BLOCK : (c + 1) * BLOCK, j * 2 * head_size : (j + 1) * 2 * head_size],
-            NT,
-            preferred_element_type=jnp.float32,
-        )
+        c, g = divmod(unit, heads)
+        keys = keys_at[c * BLOCK : (c + 1) * BLOCK, g * head_size : (g + 1) * head_size]
+        proj = lax.dot_general(turned_ref[g], keys, NT, preferred_element_type=jnp.float32)
         proj_ref[unit % 2] = proj.astype(jnp.bfloat16)
 
     def collect(unit):
-        c, j = divmod(unit, pairs)
+        c, g = divmod(unit, heads)
         position = c * BLOCK + lax.broadcasted_iota(jnp.int32, (1, BLOCK), 1)
         live = jnp.where(position < begin, 1.0, 0.0).astype(jnp.bfloat16)
         mapped = feature(proj_ref[unit % 2]) * live
         some = [mapped[:, k * 128 : (k + 1) * 128] for k in range(BLOCK // 128)]
         while len(some) > 1:
             some = [x + y for x, y in zip(some[::2], some[1::2])]
-        norm_ref[j] += some[0].astype(jnp.float32)
-        state_ref[j] += jnp.dot(
-            mapped,
-            values_at[c * BLOCK : (c + 1) * BLOCK, j * 2 * head_size : (j + 1) * 2 * head_size],
-            preferred_element_type=jnp.float32,
-        )
+        norm_ref[g] += some[0].astype(jnp.float32)
+        values = values_at[c * BLOCK : (c + 1) * BLOCK, g * head_size : (g + 1) * head_size]
+        state_ref[g] += jnp.dot(mapped, values, preferred_element_type=jnp.float32)
 
     project(0)
-    for unit in range(chunks * pairs):
-        if unit + 1 < chunks * pairs:
+    for unit in range(chunks * heads):
+        if unit + 1 < chunks * heads:
             project(unit + 1)
         collect(unit)
 
     back = 1.0 / (feats * feats)
     tile = []
     for g in range(heads):
-        half = g % 2
-        state = state_ref[g // 2, half * feats : (half + 1) * feats, half * head_size : (half + 1) * head_size]
-        out_ref[g * part : g * part + feats, :] = (state * back).astype(jnp.bfloat16)
-        sums = norm_ref[g // 2, half * feats : (half + 1) * feats, :]
+        out_ref[g * part : g * part + feats, :] = (state_ref[g] * back).astype(jnp.bfloat16)
+        sums = norm_ref[g]
         tile.append(jnp.sum(sums.T, axis=0, keepdims=True) * back)
     slot = first + lax.broadcasted_iota(jnp.int32, (1, head_size), 1)
     tile.append(jnp.zeros((MASK_ROW - heads, head_size), jnp.float32))
@@ -153,10 +140,10 @@
         out_specs=vmem,
         out_shape=jax.ShapeDtypeStruct((heads * feats + 16 + 2 * heads * SLAB, head_size), jnp.bfloat16),
         scratch_shapes=[
-            pltpu.VMEM((heads // 2, 2 * feats, 2 * head_size), jnp.bfloat16),
-            pltpu.VMEM((2, 2 * feats, BLOCK), jnp.bfloat16),
-            pltpu.VMEM((heads // 2, 2 * feats, 2 * head_size), jnp.float32),
-            pltpu.VMEM((heads // 2, 2 * feats, 128), jnp.float32),
+            pltpu.VMEM((heads, feats, head_size), jnp.bfloat16),
+            pltpu.VMEM((2, feats, BLOCK), jnp.bfloat16),
+            pltpu.VMEM((heads, feats, head_size), jnp.float32),
+            pltpu.VMEM((heads, feats, 128), jnp.float32),
             pltpu.SemaphoreType.DMA((2, heads)),
         ],
         compiler_params=pltpu.CompilerParams(vmem_limit_bytes=16 * 1024 * 1024),

time: 20.9 us -> 20.9 us (level)
  transfers between devices with their start and end apart: 7 -> 7, of which waited for: 4 -> 5; matrix products, arithmetic and copies ran while one was open for 1% -> 1% of each run, Pallas kernels for 16% -> 16%
where the time goes in v29:
time: 20.9 us; the launch traced here: 20.7 us
  starting transfers between devices  10.6 us (51%)
  Pallas kernels  4.82 us (23%)
  waiting for transfers between devices  3.56 us (17%)
  other arithmetic  0.93 us (4%)
  between operations  0.76 us (4%)
    ppermute x3, starting transfers between devices, body(): lax.ppermute(mine, 'sect', [(ask(i, k, sects), i) for i in range(sects)])  6.12 us
    ppermute x3, starting transfers between devices, body(): lax.ppermute(results[k], 'sect', [(i, partner(i, k, sects)) for i in rang...  4.45 us
    ppermute x3, waiting for transfers between devices, body(): lax.ppermute(results[k], 'sect', [(i, partner(i, k, sects)) for i in rang...  2.84 us
    pallas_call x1, Pallas kernels, prefill(): pl.pallas_call(prefill_kernel, in_specs=[pl.BlockSpec(memory_space=pltpu....  2.7 us
    pallas_call x1, Pallas kernels, pack(): pl.pallas_call(pack_kernel, in_specs=[pl.BlockSpec(memory_space=pltpu.Mem...  0.94 us
    select_n x1, other arithmetic, body(): out = jnp.where((prompts == source)[:, None], result, out)  0.71 us
    pallas_call x1, Pallas kernels, begin(): pl.pallas_call(begin_kernel, in_specs=[vmem] * 3, out_specs=[vmem] * 5, o...  0.67 us
    pallas_call x1, Pallas kernels, end(): pl.pallas_call(end_kernel, in_specs=[vmem] * 6, out_specs=[vmem] * parts,...  0.51 us
  transfers between devices with their start and end apart: 7, of which 5 were waited for; matrix products, arithmetic and copies ran while one was open for 1% of the time, Pallas kernels for 16%

profile of v29, /device:TPU:0, one launch (start us, length us, event | category | flops | bytes accessed | tf_op | source)
XLA Modules:
  0.0 20.7 jit_solution(4304952520712460014)
XLA Ops:
  0.0 0.0 copy-start.2
  0.0 0.0 copy-start
  0.0 0.0 copy-start.1
  0.0 0.9 %pack.1 = bf16[4,5120]{1,0:T(4,128)(2,1)S(1)} custom-call(bf16[4,4096]{1,0:T(4,128)(2,1)} %queries_ref.1, bf16[4,512]{1,0:T(4,128)(2,1)} %keys_ref.2, bf16[4,512]{1,0:T(4,128)(2,1)} %values_ref.2), custom_call_target="tpu_custom_call" | custom-call | flops 10000000000 | bytes 33554432 | tf_op jit(solution)/shard_map/pack/pallas_call | solution.py:47
  1.0 3.1 %collective-permute-start.1 = (bf16[4,5120]{1,0:T(4,128)(2,1)S(1)}, bf16[4,5120]{1,0:T(4,128)(2,1)S(1)}, u32[]{:S(2)}, u32[]{:S(2)}) collective-permute-start(bf16[4,5120]{1,0:T(4,128)(2,1)S(1)} %pack.1), channel_id=1, source_target_pairs={{12,0},{0,4},{4,8},{8,12},{13,1},{1,5},{5,9},{9,13},{14,2},{2,6},{... | collective-permute-start | bytes 122888 | tf_op jit(solution)/shard_map/ppermute | solution.py:275
  4.0 2.1 %collective-permute-start.2 = (bf16[4,5120]{1,0:T(4,128)(2,1)S(1)}, bf16[4,5120]{1,0:T(4,128)(2,1)S(1)}, u32[]{:S(2)}, u32[]{:S(2)}) collective-permute-start(bf16[4,5120]{1,0:T(4,128)(2,1)S(1)} %pack.1), channel_id=1, source_target_pairs={{4,0},{8,4},{12,8},{0,12},{5,1},{9,5},{13,9},{1,13},{6,2},{10,6},{... | collective-permute-start | bytes 122888 | tf_op jit(solution)/shard_map/ppermute | solution.py:275
  6.1 0.9 %collective-permute-start = (bf16[4,5120]{1,0:T(4,128)(2,1)S(1)}, bf16[4,5120]{1,0:T(4,128)(2,1)S(1)}, u32[]{:S(2)}, u32[]{:S(2)}) collective-permute-start(bf16[4,5120]{1,0:T(4,128)(2,1)S(1)} %pack.1), channel_id=1, source_target_pairs={{8,0},{12,4},{0,8},{4,12},{9,1},{13,5},{1,9},{5,13},{10,2},{14,6},... | collective-permute-start | bytes 122888 | tf_op jit(solution)/shard_map/ppermute | solution.py:275
  7.7 0.0 copy-done.2
  7.7 0.0 copy-done
  7.7 0.0 copy-done.1
  7.8 0.0 copy-start.3
  7.8 2.7 %prefill.1.near_ref = bf16[1168,128]{1,0:T(8,128)(2,1)S(1)} custom-call(s32[1]{0:T(128)S(6)} %copy.9.lengths_ref, bf16[1,4096,512]{2,1,0:T(8,128)(2,1)S(1)} %copy-done, bf16[1,4096,512]{2,1,0:T(8,128)(2,1)S(1)} %copy-done.1, bf16[4,128,128]{2,1,0:T(8,128)(2,1)S(1)} %copy-done.2), custom_call_target="tpu_custom_call" | custom-call | flops 1073741824 | bytes 8388608 | tf_op jit(solution)/shard_map/prefill/pallas_call | solution.py:137
  10.5 0.1 collective-permute-start.3
  10.6 0.0 collective-permute-done.1
  10.6 0.0 collective-permute-done.2
  10.6 0.4 %collective-permute-done = bf16[4,5120]{1,0:T(4,128)(2,1)S(1)} collective-permute-done((bf16[4,5120]{1,0:T(4,128)(2,1)S(1)}, bf16[4,5120]{1,0:T(4,128)(2,1)S(1)}, u32[]{:S(2)}, u32[]{:S(2)}) %collective-permute-start) | collective-permute-done | bytes 40992 | tf_op jit(solution)/shard_map/ppermute | solution.py:275
  11.0 0.1 pad_maximum_fusion.rows_ref
  11.1 0.7 %begin.1 = (bf16[4,128,128]{2,1,0:T(8,128)(2,1)S(1)}, bf16[4,128,128]{2,1,0:T(8,128)(2,1)S(1)}, f32[4,128,128]{2,1,0:T(8,128)S(1)}, f32[4,128,128]{2,1,0:T(8,128)S(1)}, f32[4,128,128]{2,1,0:T(8,128)S(1)}) custom-call(bf16[16,5120]{1,0:T(8,128)(2,1)S(1)} %pad_maximum_fusion.rows_ref, bf16[4,128,128]{2,1,0:T(8,128)(2,1)S(1)} %copy-done.2, ...), custom_call_target="tpu_custom_call" | custom-call | flops 62914560 | bytes 327680 | tf_op jit(solution)/shard_map/begin/pallas_call | solution.py:238
  11.8 0.3 %collective-permute-done.3.far_ref = bf16[1168,128]{1,0:T(8,128)(2,1)S(1)} collective-permute-done((bf16[1168,128]{1,0:T(8,128)(2,1)S(1)}, bf16[1168,128]{1,0:T(8,128)(2,1)S(1)}, u32[]{:S(2)}, u32[]{:S(2)}) %collective-permute-start.3) | collective-permute-done | bytes 299040 | tf_op jit(solution)/shard_map/ppermute | solution.py:281
  12.1 0.5 %end.1 = (bf16[4,4096]{1,0:T(4,128)(2,1)S(1)}, bf16[4,4096]{1,0:T(4,128)(2,1)S(1)}, bf16[4,4096]{1,0:T(4,128)(2,1)S(1)}, bf16[4,4096]{1,0:T(4,128)(2,1)S(1)}) custom-call(bf16[4,128,128]{2,1,0:T(8,128)(2,1)S(1)} %get-tuple-element.14.query_ref, bf16[4,128,128]{2,1,0:T(8,128)(2,1)S(1)} %get-tuple-element.15.phi_ref, ...), custom_call_target="tpu_custom_call" | custom-call | flops 33554432 | bytes 262144 | tf_op jit(solution)/shard_map/end/pallas_call | solution.py:253
  12.6 2.0 %collective-permute-start.4 = (bf16[4,4096]{1,0:T(4,128)(2,1)S(1)}, bf16[4,4096]{1,0:T(4,128)(2,1)S(1)}, u32[]{:S(2)}, u32[]{:S(2)}) collective-permute-start(bf16[4,4096]{1,0:T(4,128)(2,1)S(1)} %get-tuple-element.19), channel_id=1, source_target_pairs={{0,12},{4,8},{8,4},{12,0},{1,13},{5,9},{9,5},{13,1},{2,14},{6,10},... | collective-permute-start | bytes 98312 | tf_op jit(solution)/shard_map/ppermute | solution.py:291
  14.7 1.1 %collective-permute-start.5 = (bf16[4,4096]{1,0:T(4,128)(2,1)S(1)}, bf16[4,4096]{1,0:T(4,128)(2,1)S(1)}, u32[]{:S(2)}, u32[]{:S(2)}) collective-permute-start(bf16[4,4096]{1,0:T(4,128)(2,1)S(1)} %get-tuple-element.20), channel_id=1, source_target_pairs={{0,8},{4,12},{8,0},{12,4},{1,9},{5,13},{9,1},{13,5},{2,10},{6,14},... | collective-permute-start | bytes 98312 | tf_op jit(solution)/shard_map/ppermute | solution.py:291
  15.7 1.3 %collective-permute-start.6 = (bf16[4,4096]{1,0:T(4,128)(2,1)S(1)}, bf16[4,4096]{1,0:T(4,128)(2,1)S(1)}, u32[]{:S(2)}, u32[]{:S(2)}) collective-permute-start(bf16[4,4096]{1,0:T(4,128)(2,1)S(1)} %get-tuple-element.21), channel_id=1, source_target_pairs={{0,4},{4,0},{8,12},{12,8},{1,5},{5,1},{9,13},{13,9},{2,6},{6,2},{1... | collective-permute-start | bytes 98312 | tf_op jit(solution)/shard_map/ppermute | solution.py:291
  17.1 0.0 copy-done.3
  17.1 0.1 broadcast_compare_fusion.2
  17.2 1.6 %collective-permute-done.4 = bf16[4,4096]{1,0:T(4,128)(2,1)S(1)} collective-permute-done((bf16[4,4096]{1,0:T(4,128)(2,1)S(1)}, bf16[4,4096]{1,0:T(4,128)(2,1)S(1)}, u32[]{:S(2)}, u32[]{:S(2)}) %collective-permute-start.4) | collective-permute-done | bytes 32800 | tf_op jit(solution)/shard_map/ppermute | solution.py:291
  18.8 1.2 %collective-permute-done.5 = bf16[4,4096]{1,0:T(4,128)(2,1)S(1)} collective-permute-done((bf16[4,4096]{1,0:T(4,128)(2,1)S(1)}, bf16[4,4096]{1,0:T(4,128)(2,1)S(1)}, u32[]{:S(2)}, u32[]{:S(2)}) %collective-permute-start.5) | collective-permute-done | bytes 32800 | tf_op jit(solution)/shard_map/ppermute | solution.py:291
  20.0 0.1 collective-permute-done.6
  20.0 0.7 %select_select_fusion = bf16[4,4096]{1,0:T(4,128)(2,1)} fusion(bf16[4,4096]{1,0:T(4,128)(2,1)S(1)} %collective-permute-done.4, bf16[4,4096]{1,0:T(4,128)(2,1)S(1)} %collective-permute-done.5, bf16[4,4096]{1,0:T(4,128)(2,1)S(1)} %collective-permute-done.6, bf16[4,4096]{1,0:T(4,128)(2,1)S(1)} %get-tuple-element.22, pred[4]{0:T(512)(128)(4,1)S(1)} %get-tuple-element.27, ...), kind=kLoop, calls=%fused_computation.3 | loop fusion | flops 49152 | bytes 163852 | tf_op jit(solution)/shard_map/jit(_where)/select_n | solution.py:293
  (1 shorter events, 0.0 us)
Async XLA Ops:
  0.0 7.7 %copy-start.2 = (bf16[4,128,128]{2,1,0:T(8,128)(2,1)S(1)}, bf16[4,128,128]{2,1,0:T(8,128)(2,1)}, u32[]{:S(2)}) copy-start(bf16[4,128,128]{2,1,0:T(8,128)(2,1)} %weight_ref.3) | copy-start | bytes 393220
  0.0 7.7 %copy-start = (bf16[1,4096,512]{2,1,0:T(8,128)(2,1)S(1)}, bf16[1,4096,512]{2,1,0:T(8,128)(2,1)}, u32[]{:S(2)}) copy-start(bf16[1,4096,512]{2,1,0:T(8,128)(2,1)} %keys_ref.3) | copy-start | bytes 12582916
  0.0 7.7 %copy-start.1 = (bf16[1,4096,512]{2,1,0:T(8,128)(2,1)S(1)}, bf16[1,4096,512]{2,1,0:T(8,128)(2,1)}, u32[]{:S(2)}) copy-start(bf16[1,4096,512]{2,1,0:T(8,128)(2,1)} %values_ref.3) | copy-start | bytes 12582916
  1.0 9.6 %collective-permute-start.1 = (bf16[4,5120]{1,0:T(4,128)(2,1)S(1)}, bf16[4,5120]{1,0:T(4,128)(2,1)S(1)}, u32[]{:S(2)}, u32[]{:S(2)}) collective-permute-start(bf16[4,5120]{1,0:T(4,128)(2,1)S(1)} %pack.1), channel_id=1, source_target_pairs={{12,0},{0,4},{4,8},{8,12},{13,1},{1,5},{5,9},{9,13},{14,2},{2,6},{... | collective-permute-start | bytes 122888 | tf_op jit(solution)/shard_map/ppermute | solution.py:275
  4.0 6.5 %collective-permute-start.2 = (bf16[4,5120]{1,0:T(4,128)(2,1)S(1)}, bf16[4,5120]{1,0:T(4,128)(2,1)S(1)}, u32[]{:S(2)}, u32[]{:S(2)}) collective-permute-start(bf16[4,5120]{1,0:T(4,128)(2,1)S(1)} %pack.1), channel_id=1, source_target_pairs={{4,0},{8,4},{12,8},{0,12},{5,1},{9,5},{13,9},{1,13},{6,2},{10,6},{... | collective-permute-start | bytes 122888 | tf_op jit(solution)/shard_map/ppermute | solution.py:275
  6.1 4.9 %collective-permute-start = (bf16[4,5120]{1,0:T(4,128)(2,1)S(1)}, bf16[4,5120]{1,0:T(4,128)(2,1)S(1)}, u32[]{:S(2)}, u32[]{:S(2)}) collective-permute-start(bf16[4,5120]{1,0:T(4,128)(2,1)S(1)} %pack.1), channel_id=1, source_target_pairs={{8,0},{12,4},{0,8},{4,12},{9,1},{13,5},{1,9},{5,13},{10,2},{14,6},... | collective-permute-start | bytes 122888 | tf_op jit(solution)/shard_map/ppermute | solution.py:275
  7.8 9.3 %copy-start.3 = (s32[32]{0:T(128)S(1)}, s32[32]{0:T(128)}, u32[]{:S(2)}) copy-start(s32[32]{0:T(128)} %param.15) | copy-start | bytes 388
  10.5 1.7 %collective-permute-start.3 = (bf16[1168,128]{1,0:T(8,128)(2,1)S(1)}, bf16[1168,128]{1,0:T(8,128)(2,1)S(1)}, u32[]{:S(2)}, u32[]{:S(2)}) collective-permute-start(bf16[1168,128]{1,0:T(8,128)(2,1)S(1)} %prefill.1.near_ref), channel_id=1, source_target_pairs={{0,1},{1,0},{2,3},{3,2},{4,5},{5,4},{6,7},{7,6},{8,9},{9,8},{10,11... | collective-permute-start | bytes 897032 | tf_op jit(solution)/shard_map/ppermute | solution.py:281
  12.6 6.1 %collective-permute-start.4 = (bf16[4,4096]{1,0:T(4,128)(2,1)S(1)}, bf16[4,4096]{1,0:T(4,128)(2,1)S(1)}, u32[]{:S(2)}, u32[]{:S(2)}) collective-permute-start(bf16[4,4096]{1,0:T(4,128)(2,1)S(1)} %get-tuple-element.19), channel_id=1, source_target_pairs={{0,12},{4,8},{8,4},{12,0},{1,13},{5,9},{9,5},{13,1},{2,14},{6,10},... | collective-permute-start | bytes 98312 | tf_op jit(solution)/shard_map/ppermute | solution.py:291
  14.7 5.3 %collective-permute-start.5 = (bf16[4,4096]{1,0:T(4,128)(2,1)S(1)}, bf16[4,4096]{1,0:T(4,128)(2,1)S(1)}, u32[]{:S(2)}, u32[]{:S(2)}) collective-permute-start(bf16[4,4096]{1,0:T(4,128)(2,1)S(1)} %get-tuple-element.20), channel_id=1, source_target_pairs={{0,8},{4,12},{8,0},{12,4},{1,9},{5,13},{9,1},{13,5},{2,10},{6,14},... | collective-permute-start | bytes 98312 | tf_op jit(solution)/shard_map/ppermute | solution.py:291
  15.7 4.3 %collective-permute-start.6 = (bf16[4,4096]{1,0:T(4,128)(2,1)S(1)}, bf16[4,4096]{1,0:T(4,128)(2,1)S(1)}, u32[]{:S(2)}, u32[]{:S(2)}) collective-permute-start(bf16[4,4096]{1,0:T(4,128)(2,1)S(1)} %get-tuple-element.21), channel_id=1, source_target_pairs={{0,4},{4,0},{8,12},{12,8},{1,5},{5,1},{9,13},{13,9},{2,6},{6,2},{1... | collective-permute-start | bytes 98312 | tf_op jit(solution)/shard_map/ppermute | solution.py:291

commit v30 on v29

--- a/solution.py
+++ b/solution.py
@@ -10,7 +10,7 @@
 WINDOW = 64
 TAU = 10.0
 EPS = 1e-06
-BLOCK = 256
+BLOCK = 512
 NT = (((1,), (1,)), ((), ()))
 
 

time: 20.9 us -> 21.6 us (1.033)
  Pallas kernels: 4.82 us -> 5.7 us
    pallas_call x1, Pallas kernels: 2.7 us -> 3.59 us  [prefill(): pl.pallas_call(prefill_kernel, in_specs=[pl.BlockSpec(memory_space=pltpu....]
    ppermute x3, waiting for transfers between devices: 0.41 us -> 0.01 us  [body(): lax.ppermute(mine, 'sect', [(ask(i, k, sects), i) for i in range(sects)])]
    ppermute x1, waiting for transfers between devices: 0.31 us -> 0.7 us  [body(): far = lax.ppermute(near, 'sub', [(0, 1), (1, 0)])]
  transfers between devices with their start and end apart: 7 -> 7, of which waited for: 5 -> 4; matrix products, arithmetic and copies ran while one was open for 1% -> 1% of each run, Pallas kernels for 16% -> 20%
where the time goes in v30:
time: 21.6 us; the launch traced here: 21.5 us
  starting transfers between devices  10.6 us (49%)
  Pallas kernels  5.7 us (26%)
  waiting for transfers between devices  3.39 us (16%)
  other arithmetic  0.93 us (4%)
  between operations  0.77 us (4%)
    ppermute x3, starting transfers between devices, body(): lax.ppermute(mine, 'sect', [(ask(i, k, sects), i) for i in range(sects)])  6.12 us
    ppermute x3, starting transfers between devices, body(): lax.ppermute(results[k], 'sect', [(i, partner(i, k, sects)) for i in rang...  4.45 us
    pallas_call x1, Pallas kernels, prefill(): pl.pallas_call(prefill_kernel, in_specs=[pl.BlockSpec(memory_space=pltpu....  3.59 us
    ppermute x3, waiting for transfers between devices, body(): lax.ppermute(results[k], 'sect', [(i, partner(i, k, sects)) for i in rang...  2.69 us
    pallas_call x1, Pallas kernels, pack(): pl.pallas_call(pack_kernel, in_specs=[pl.BlockSpec(memory_space=pltpu.Mem...  0.94 us
    select_n x1, other arithmetic, body(): out = jnp.where((prompts == source)[:, None], result, out)  0.71 us
    ppermute x1, waiting for transfers between devices, body(): far = lax.ppermute(near, 'sub', [(0, 1), (1, 0)])  0.7 us
    pallas_call x1, Pallas kernels, begin(): pl.pallas_call(begin_kernel, in_specs=[vmem] * 3, out_specs=[vmem] * 5, o...  0.67 us
  transfers between devices with their start and end apart: 7, of which 4 were waited for; matrix products, arithmetic and copies ran while one was open for 1% of the time, Pallas kernels for 20%

profile of v30, /device:TPU:0, one launch (start us, length us, event | category | flops | bytes accessed | tf_op | source)
XLA Modules:
  0.0 21.5 jit_solution(4730637175954629567)
XLA Ops:
  0.0 0.0 copy-start.2
  0.0 0.0 copy-start
  0.0 0.0 copy-start.1
  0.0 0.9 %pack.1 = bf16[4,5120]{1,0:T(4,128)(2,1)S(1)} custom-call(bf16[4,4096]{1,0:T(4,128)(2,1)} %queries_ref.1, bf16[4,512]{1,0:T(4,128)(2,1)} %keys_ref.2, bf16[4,512]{1,0:T(4,128)(2,1)} %values_ref.2), custom_call_target="tpu_custom_call" | custom-call | flops 10000000000 | bytes 33554432 | tf_op jit(solution)/shard_map/pack/pallas_call | solution.py:47
  1.0 3.1 %collective-permute-start.1 = (bf16[4,5120]{1,0:T(4,128)(2,1)S(1)}, bf16[4,5120]{1,0:T(4,128)(2,1)S(1)}, u32[]{:S(2)}, u32[]{:S(2)}) collective-permute-start(bf16[4,5120]{1,0:T(4,128)(2,1)S(1)} %pack.1), channel_id=1, source_target_pairs={{12,0},{0,4},{4,8},{8,12},{13,1},{1,5},{5,9},{9,13},{14,2},{2,6},{... | collective-permute-start | bytes 122888 | tf_op jit(solution)/shard_map/ppermute | solution.py:275
  4.0 2.1 %collective-permute-start.2 = (bf16[4,5120]{1,0:T(4,128)(2,1)S(1)}, bf16[4,5120]{1,0:T(4,128)(2,1)S(1)}, u32[]{:S(2)}, u32[]{:S(2)}) collective-permute-start(bf16[4,5120]{1,0:T(4,128)(2,1)S(1)} %pack.1), channel_id=1, source_target_pairs={{4,0},{8,4},{12,8},{0,12},{5,1},{9,5},{13,9},{1,13},{6,2},{10,6},{... | collective-permute-start | bytes 122888 | tf_op jit(solution)/shard_map/ppermute | solution.py:275
  6.1 0.9 %collective-permute-start = (bf16[4,5120]{1,0:T(4,128)(2,1)S(1)}, bf16[4,5120]{1,0:T(4,128)(2,1)S(1)}, u32[]{:S(2)}, u32[]{:S(2)}) collective-permute-start(bf16[4,5120]{1,0:T(4,128)(2,1)S(1)} %pack.1), channel_id=1, source_target_pairs={{8,0},{12,4},{0,8},{4,12},{9,1},{13,5},{1,9},{5,13},{10,2},{14,6},... | collective-permute-start | bytes 122888 | tf_op jit(solution)/shard_map/ppermute | solution.py:275
  7.7 0.0 copy-done.2
  7.7 0.0 copy-done
  7.7 0.0 copy-done.1
  7.8 0.0 copy-start.3
  7.8 3.6 %prefill.1.near_ref = bf16[1168,128]{1,0:T(8,128)(2,1)S(1)} custom-call(s32[1]{0:T(128)S(6)} %copy.9.lengths_ref, bf16[1,4096,512]{2,1,0:T(8,128)(2,1)S(1)} %copy-done, bf16[1,4096,512]{2,1,0:T(8,128)(2,1)S(1)} %copy-done.1, bf16[4,128,128]{2,1,0:T(8,128)(2,1)S(1)} %copy-done.2), custom_call_target="tpu_custom_call" | custom-call | flops 1073741824 | bytes 8388608 | tf_op jit(solution)/shard_map/prefill/pallas_call | solution.py:137
  11.4 0.1 collective-permute-start.3
  11.4 0.0 collective-permute-done.1
  11.5 0.0 collective-permute-done.2
  11.5 0.0 collective-permute-done
  11.5 0.1 pad_maximum_fusion.rows_ref
  11.6 0.7 %begin.1 = (bf16[4,128,128]{2,1,0:T(8,128)(2,1)S(1)}, bf16[4,128,128]{2,1,0:T(8,128)(2,1)S(1)}, f32[4,128,128]{2,1,0:T(8,128)S(1)}, f32[4,128,128]{2,1,0:T(8,128)S(1)}, f32[4,128,128]{2,1,0:T(8,128)S(1)}) custom-call(bf16[16,5120]{1,0:T(8,128)(2,1)S(1)} %pad_maximum_fusion.rows_ref, bf16[4,128,128]{2,1,0:T(8,128)(2,1)S(1)} %copy-done.2, ...), custom_call_target="tpu_custom_call" | custom-call | flops 62914560 | bytes 327680 | tf_op jit(solution)/shard_map/begin/pallas_call | solution.py:238
  12.3 0.7 %collective-permute-done.3.far_ref = bf16[1168,128]{1,0:T(8,128)(2,1)S(1)} collective-permute-done((bf16[1168,128]{1,0:T(8,128)(2,1)S(1)}, bf16[1168,128]{1,0:T(8,128)(2,1)S(1)}, u32[]{:S(2)}, u32[]{:S(2)}) %collective-permute-start.3) | collective-permute-done | bytes 299040 | tf_op jit(solution)/shard_map/ppermute | solution.py:281
  13.0 0.5 %end.1 = (bf16[4,4096]{1,0:T(4,128)(2,1)S(1)}, bf16[4,4096]{1,0:T(4,128)(2,1)S(1)}, bf16[4,4096]{1,0:T(4,128)(2,1)S(1)}, bf16[4,4096]{1,0:T(4,128)(2,1)S(1)}) custom-call(bf16[4,128,128]{2,1,0:T(8,128)(2,1)S(1)} %get-tuple-element.14.query_ref, bf16[4,128,128]{2,1,0:T(8,128)(2,1)S(1)} %get-tuple-element.15.phi_ref, ...), custom_call_target="tpu_custom_call" | custom-call | flops 33554432 | bytes 262144 | tf_op jit(solution)/shard_map/end/pallas_call | solution.py:253
  13.5 1.4 %collective-permute-start.4 = (bf16[4,4096]{1,0:T(4,128)(2,1)S(1)}, bf16[4,4096]{1,0:T(4,128)(2,1)S(1)}, u32[]{:S(2)}, u32[]{:S(2)}) collective-permute-start(bf16[4,4096]{1,0:T(4,128)(2,1)S(1)} %get-tuple-element.19), channel_id=1, source_target_pairs={{0,12},{4,8},{8,4},{12,0},{1,13},{5,9},{9,5},{13,1},{2,14},{6,10},... | collective-permute-start | bytes 98312 | tf_op jit(solution)/shard_map/ppermute | solution.py:291
  14.9 1.7 %collective-permute-start.5 = (bf16[4,4096]{1,0:T(4,128)(2,1)S(1)}, bf16[4,4096]{1,0:T(4,128)(2,1)S(1)}, u32[]{:S(2)}, u32[]{:S(2)}) collective-permute-start(bf16[4,4096]{1,0:T(4,128)(2,1)S(1)} %get-tuple-element.20), channel_id=1, source_target_pairs={{0,8},{4,12},{8,0},{12,4},{1,9},{5,13},{9,1},{13,5},{2,10},{6,14},... | collective-permute-start | bytes 98312 | tf_op jit(solution)/shard_map/ppermute | solution.py:291
  16.6 1.3 %collective-permute-start.6 = (bf16[4,4096]{1,0:T(4,128)(2,1)S(1)}, bf16[4,4096]{1,0:T(4,128)(2,1)S(1)}, u32[]{:S(2)}, u32[]{:S(2)}) collective-permute-start(bf16[4,4096]{1,0:T(4,128)(2,1)S(1)} %get-tuple-element.21), channel_id=1, source_target_pairs={{0,4},{4,0},{8,12},{12,8},{1,5},{5,1},{9,13},{13,9},{2,6},{6,2},{1... | collective-permute-start | bytes 98312 | tf_op jit(solution)/shard_map/ppermute | solution.py:291
  18.0 0.0 copy-done.3
  18.0 0.1 broadcast_compare_fusion.2
  18.1 1.6 %collective-permute-done.4 = bf16[4,4096]{1,0:T(4,128)(2,1)S(1)} collective-permute-done((bf16[4,4096]{1,0:T(4,128)(2,1)S(1)}, bf16[4,4096]{1,0:T(4,128)(2,1)S(1)}, u32[]{:S(2)}, u32[]{:S(2)}) %collective-permute-start.4) | collective-permute-done | bytes 32800 | tf_op jit(solution)/shard_map/ppermute | solution.py:291
  19.7 1.0 %collective-permute-done.5 = bf16[4,4096]{1,0:T(4,128)(2,1)S(1)} collective-permute-done((bf16[4,4096]{1,0:T(4,128)(2,1)S(1)}, bf16[4,4096]{1,0:T(4,128)(2,1)S(1)}, u32[]{:S(2)}, u32[]{:S(2)}) %collective-permute-start.5) | collective-permute-done | bytes 32800 | tf_op jit(solution)/shard_map/ppermute | solution.py:291
  20.7 0.1 collective-permute-done.6
  20.8 0.7 %select_select_fusion = bf16[4,4096]{1,0:T(4,128)(2,1)} fusion(bf16[4,4096]{1,0:T(4,128)(2,1)S(1)} %collective-permute-done.4, bf16[4,4096]{1,0:T(4,128)(2,1)S(1)} %collective-permute-done.5, bf16[4,4096]{1,0:T(4,128)(2,1)S(1)} %collective-permute-done.6, bf16[4,4096]{1,0:T(4,128)(2,1)S(1)} %get-tuple-element.22, pred[4]{0:T(512)(128)(4,1)S(1)} %get-tuple-element.27, ...), kind=kLoop, calls=%fused_computation.3 | loop fusion | flops 49152 | bytes 163852 | tf_op jit(solution)/shard_map/jit(_where)/select_n | solution.py:293
  (1 shorter events, 0.0 us)
Async XLA Ops:
  0.0 7.7 %copy-start.2 = (bf16[4,128,128]{2,1,0:T(8,128)(2,1)S(1)}, bf16[4,128,128]{2,1,0:T(8,128)(2,1)}, u32[]{:S(2)}) copy-start(bf16[4,128,128]{2,1,0:T(8,128)(2,1)} %weight_ref.3) | copy-start | bytes 393220
  0.0 7.7 %copy-start = (bf16[1,4096,512]{2,1,0:T(8,128)(2,1)S(1)}, bf16[1,4096,512]{2,1,0:T(8,128)(2,1)}, u32[]{:S(2)}) copy-start(bf16[1,4096,512]{2,1,0:T(8,128)(2,1)} %keys_ref.3) | copy-start | bytes 12582916
  0.0 7.7 %copy-start.1 = (bf16[1,4096,512]{2,1,0:T(8,128)(2,1)S(1)}, bf16[1,4096,512]{2,1,0:T(8,128)(2,1)}, u32[]{:S(2)}) copy-start(bf16[1,4096,512]{2,1,0:T(8,128)(2,1)} %values_ref.3) | copy-start | bytes 12582916
  1.0 10.5 %collective-permute-start.1 = (bf16[4,5120]{1,0:T(4,128)(2,1)S(1)}, bf16[4,5120]{1,0:T(4,128)(2,1)S(1)}, u32[]{:S(2)}, u32[]{:S(2)}) collective-permute-start(bf16[4,5120]{1,0:T(4,128)(2,1)S(1)} %pack.1), channel_id=1, source_target_pairs={{12,0},{0,4},{4,8},{8,12},{13,1},{1,5},{5,9},{9,13},{14,2},{2,6},{... | collective-permute-start | bytes 122888 | tf_op jit(solution)/shard_map/ppermute | solution.py:275
  4.0 7.4 %collective-permute-start.2 = (bf16[4,5120]{1,0:T(4,128)(2,1)S(1)}, bf16[4,5120]{1,0:T(4,128)(2,1)S(1)}, u32[]{:S(2)}, u32[]{:S(2)}) collective-permute-start(bf16[4,5120]{1,0:T(4,128)(2,1)S(1)} %pack.1), channel_id=1, source_target_pairs={{4,0},{8,4},{12,8},{0,12},{5,1},{9,5},{13,9},{1,13},{6,2},{10,6},{... | collective-permute-start | bytes 122888 | tf_op jit(solution)/shard_map/ppermute | solution.py:275
  6.1 5.4 %collective-permute-start = (bf16[4,5120]{1,0:T(4,128)(2,1)S(1)}, bf16[4,5120]{1,0:T(4,128)(2,1)S(1)}, u32[]{:S(2)}, u32[]{:S(2)}) collective-permute-start(bf16[4,5120]{1,0:T(4,128)(2,1)S(1)} %pack.1), channel_id=1, source_target_pairs={{8,0},{12,4},{0,8},{4,12},{9,1},{13,5},{1,9},{5,13},{10,2},{14,6},... | collective-permute-start | bytes 122888 | tf_op jit(solution)/shard_map/ppermute | solution.py:275
  7.8 10.2 %copy-start.3 = (s32[32]{0:T(128)S(1)}, s32[32]{0:T(128)}, u32[]{:S(2)}) copy-start(s32[32]{0:T(128)} %param.15) | copy-start | bytes 388
  11.4 1.7 %collective-permute-start.3 = (bf16[1168,128]{1,0:T(8,128)(2,1)S(1)}, bf16[1168,128]{1,0:T(8,128)(2,1)S(1)}, u32[]{:S(2)}, u32[]{:S(2)}) collective-permute-start(bf16[1168,128]{1,0:T(8,128)(2,1)S(1)} %prefill.1.near_ref), channel_id=1, source_target_pairs={{0,1},{1,0},{2,3},{3,2},{4,5},{5,4},{6,7},{7,6},{8,9},{9,8},{10,11... | collective-permute-start | bytes 897032 | tf_op jit(solution)/shard_map/ppermute | solution.py:281
  13.5 6.1 %collective-permute-start.4 = (bf16[4,4096]{1,0:T(4,128)(2,1)S(1)}, bf16[4,4096]{1,0:T(4,128)(2,1)S(1)}, u32[]{:S(2)}, u32[]{:S(2)}) collective-permute-start(bf16[4,4096]{1,0:T(4,128)(2,1)S(1)} %get-tuple-element.19), channel_id=1, source_target_pairs={{0,12},{4,8},{8,4},{12,0},{1,13},{5,9},{9,5},{13,1},{2,14},{6,10},... | collective-permute-start | bytes 98312 | tf_op jit(solution)/shard_map/ppermute | solution.py:291
  14.9 5.8 %collective-permute-start.5 = (bf16[4,4096]{1,0:T(4,128)(2,1)S(1)}, bf16[4,4096]{1,0:T(4,128)(2,1)S(1)}, u32[]{:S(2)}, u32[]{:S(2)}) collective-permute-start(bf16[4,4096]{1,0:T(4,128)(2,1)S(1)} %get-tuple-element.20), channel_id=1, source_target_pairs={{0,8},{4,12},{8,0},{12,4},{1,9},{5,13},{9,1},{13,5},{2,10},{6,14},... | collective-permute-start | bytes 98312 | tf_op jit(solution)/shard_map/ppermute | solution.py:291
  16.6 4.1 %collective-permute-start.6 = (bf16[4,4096]{1,0:T(4,128)(2,1)S(1)}, bf16[4,4096]{1,0:T(4,128)(2,1)S(1)}, u32[]{:S(2)}, u32[]{:S(2)}) collective-permute-start(bf16[4,4096]{1,0:T(4,128)(2,1)S(1)} %get-tuple-element.21), channel_id=1, source_target_pairs={{0,4},{4,0},{8,12},{12,8},{1,5},{5,1},{9,13},{13,9},{2,6},{6,2},{1... | collective-permute-start | bytes 98312 | tf_op jit(solution)/shard_map/ppermute | solution.py:291
